TPU v7x, 32 devices: a whole 2x2x4 slice. The times are simulated.
32 devices in a mesh: groups: 2 (over y), expert: 4 (over x, core), tensor: 4 (over z).
Axes of the slice: x: 2, y: 2, z: 4, core: 2. Of those that a mesh axis runs over, the one named last changes fastest.
Arguments:
- residual: bfloat16 [512, 7168], P(('groups', 'expert'), 'tensor'), parts along dimension 0
- attn_partial: bfloat16 [4, 512, 7168], P('tensor', ('groups', 'expert')), parts along dimension 1, may hold values from -4 to 4
- norm_gain: bfloat16 [7168], P('tensor'), may hold values from 0.25 to 1.75
- expert_ids: int32 [512, 2], P(('groups', 'expert')), parts along dimension 0, may hold values from 0 to 3, all different within a row; in each aligned block of 64 rows (0 to 63, 64 to 127, ...) at most 40 rows name the same one
- route_scores: float32 [512, 2], P(('groups', 'expert')), parts along dimension 0, may hold values from 0.05 to 1
- w_gate: bfloat16 [4, 7168, 2048], P('expert', 'tensor'), may hold values from -0.0625 to 0.0625
- w_down: bfloat16 [4, 2048, 7168], P('expert', None, 'tensor'), may hold values from -0.125 to 0.125
Outputs:
- stream: bfloat16 [512, 7168], P(('groups', 'expert'), 'tensor'), parts along dimension 0
- moe_out: bfloat16 [512, 7168], P(('groups', 'expert'), 'tensor'), parts along dimension 0
There are 2 independent parts, one for each index of `groups`. A program takes and returns all parts, laid end to end along the dimension named above; an argument that names none is the same for every part. Nothing has to cross between parts.
Inputs may be any that keep to these rules, and one draw needn't show every extreme that they name: `expert_ids`: in each device's block of 64 tokens no expert is named by more than 40 rows, a bound that some block reaches; a token names 2 different experts.
All inputs are finite; a program needn't handle non-finite values.
Results may differ from a plain program's by a relative error of at most 0.018.
Values may be sent and summed in bfloat16 or wider, within the bound.
No kernel may reach another device: no remote copies, remote signals or barrier semaphores. Data moves between devices by JAX's collectives and lax.ppermute only.
A program may use at most 64 MiB of HBM per device.

v0:
```python
import jax
import jax.numpy as jnp
from jax import lax
from jax.sharding import PartitionSpec as P


def local(residual, attn_partial, norm_gain, expert_ids, route_scores, w_gate, w_down):
    tok_rows = residual.shape[0]
    width_share = residual.shape[1]
    n_tensor = lax.axis_size("tensor")
    n_expert = lax.axis_size("expert")
    top_count = expert_ids.shape[1]
    capacity = tok_rows * top_count // n_expert * 5 // 4
    partial_value = attn_partial[0].astype(jnp.float32)
    summed = lax.psum_scatter(
        partial_value.astype(jnp.bfloat16), "tensor", scatter_dimension=1, tiled=True
    ).astype(jnp.float32)
    stream_f = residual.astype(jnp.float32) + summed
    squared = lax.psum(jnp.sum(stream_f * stream_f, axis=1), "tensor")
    inverse = lax.rsqrt(squared / (width_share * n_tensor) + 1e-06)
    normed = (stream_f * inverse[:, None] * norm_gain.astype(jnp.float32)).astype(jnp.bfloat16)
    weights = 2.827 * route_scores / jnp.sum(route_scores, axis=1, keepdims=True)
    flat_ids = expert_ids.reshape(-1)
    onehot = (flat_ids[:, None] == jnp.arange(n_expert, dtype=jnp.int32)[None, :]).astype(jnp.int32)
    position = jnp.sum((jnp.cumsum(onehot, axis=0) - 1) * onehot, axis=1)
    slot = flat_ids * capacity + position
    token_of = jnp.arange(tok_rows * top_count, dtype=jnp.int32) // top_count
    outgoing = (
        jnp.zeros((n_expert * capacity, width_share), jnp.bfloat16).at[slot].set(normed[token_of])
    )
    outgoing = outgoing.reshape(n_expert, capacity, width_share)
    gate_local = w_gate[0]
    down_local = w_down[0]
    arrived = lax.all_to_all(outgoing, "expert", split_axis=0, concat_axis=0, tiled=True)
    count = arrived.shape[1]
    rows_flat = arrived.reshape(n_expert * count, width_share)
    partial_gate = jnp.dot(rows_flat, gate_local, preferred_element_type=jnp.float32)
    rounded = lax.optimization_barrier(partial_gate.astype(jnp.bfloat16)).astype(jnp.float32)
    gate_full = lax.psum(rounded.astype(jnp.bfloat16), "tensor").astype(jnp.float32)
    hidden_full = jax.nn.silu(gate_full).astype(jnp.bfloat16)
    produced = jnp.dot(hidden_full, down_local, preferred_element_type=jnp.float32)
    result = produced.astype(jnp.bfloat16).reshape(n_expert, count, width_share)
    returned = lax.all_to_all(result, "expert", split_axis=0, concat_axis=0, tiled=True)
    returned_flat = returned.reshape(n_expert * capacity, width_share)
    picked = returned_flat[slot].astype(jnp.float32).reshape(tok_rows, top_count, width_share)
    moe_out = jnp.sum(picked * weights[:, :, None], axis=1).astype(jnp.bfloat16)
    return (stream_f.astype(jnp.bfloat16), moe_out)


def solution(mesh):
    return jax.shard_map(
        local,
        mesh=mesh,
        in_specs=(
            P(("groups", "expert"), "tensor"),
            P("tensor", ("groups", "expert"), None),
            P("tensor"),
            P(("groups", "expert"), None),
            P(("groups", "expert"), None),
            P("expert", "tensor", None),
            P("expert", None, "tensor"),
        ),
        out_specs=(P(("groups", "expert"), "tensor"), P(("groups", "expert"), "tensor")),
        check_vma=False,
    )
```

profile of v0, /device:TPU:0, one launch (start us, length us, event | category | flops | bytes accessed | tf_op | source)
XLA Modules:
  0.0 137.5 jit_solution(8746131907202802008)
XLA Ops:
  7.2 0.0 copy-start
  7.2 0.0 reduce-scatter.2.cloned.1.call-start
  7.2 0.7 reduce-scatter.2.cloned.1.call-update
  7.9 0.0 all-reduce.2.cloned.1.call-start
  8.0 0.7 convert_element_type.48
  8.6 0.8 copy.13
  9.4 0.7 broadcast_multiply_fusion
  10.1 0.1 copy.12
  10.2 0.1 mul.58
  10.3 0.1 eq.15
  10.5 0.1 fusion.20
  10.6 0.2 reduce_window_sum.11
  10.8 0.2 select_reduce_fusion
  10.9 27.2 %reduce-scatter.2.cloned.1.call-done = bf16[64,1792]{1,0:T(8,128)(2,1)} async-done(((bf16[64,7168]{1,0:T(8,128)(2,1)}), bf16[64,1792]{1,0:T(8,128)(2,1)}) %reduce-scatter.2.cloned.1.call-update) | async-done | bytes 229392 | tf_op jit(solution)/shard_map/reduce_scatter | solution.py:15
  38.2 0.0 copy-done
  38.2 1.1 multiply_reduce_fusion.1
  39.3 9.7 %psum.14 = f32[64]{0:T(128)S(1)} all-reduce(f32[64]{0:T(128)S(1)} %multiply_reduce_fusion.1), channel_id=1, replica_groups=mesh['groups'=2,'expert'=4,'tensor'=4] {'tensor'}, use_global_device_ids=true, to_apply=%region_4.0 | all-reduce | flops 64 | bytes 512 | tf_op jit(solution)/shard_map/psum | solution.py:19
  49.0 1.7 %multiply_convert_fusion = (bf16[64,1792]{1,0:T(8,128)(2,1)S(1)}, bf16[64,1792]{1,0:T(8,128)(2,1)}) fusion(bf16[64,1792]{1,0:T(8,128)(2,1)} %reduce-scatter.2.cloned.1.call-done, bf16[64,1792]{1,0:T(8,128)(2,1)S(1)} %copy-done, f32[1792]{0:T(1024)S(1)} %convert_element_type.48, f32[64]{0:T(128)S(1)} %add_rsqrt_fusion), kind=kLoop, calls=%fused_computation.19 | loop fusion | flops 802816 | bytes 924928 | tf_op jit(solution)/shard_map/convert_element_type | solution.py:21
  50.7 2.9 %scatter_custom_fusion = bf16[160,1792]{1,0:T(8,128)(2,1)S(1)} fusion(s32[128]{0:T(128)S(1)} %fusion.22, bf16[64,1792]{1,0:T(8,128)(2,1)S(1)} %get-tuple-element.2, s32[1024]{0:T(1024)S(1)} %pad_clamp_fusion.1, bf16[]{:T(256)} %constant.32.clone.1), kind=kCustom, calls=%fused_computation.17 | custom fusion | bytes 573442 | tf_op jit(solution)/shard_map/scatter | solution.py:29
  53.6 11.9 %all_to_all.10 = bf16[4,40,1792]{2,1,0:T(8,128)(2,1)S(1)} all-to-all(bf16[4,40,1792]{2,1,0:T(8,128)(2,1)S(1)} %bitcast.25), channel_id=1, replica_groups=mesh['groups'=2,'expert'=4,'tensor'=4] {'expert'}, dimensions={0} | all-to-all | bytes 1146880 | tf_op jit(solution)/shard_map/all_to_all | solution.py:34
  65.5 5.4 %fusion.4 = bf16[160,2048]{1,0:T(8,128)(2,1)} fusion(bf16[160,1792]{1,0:T(8,128)(2,1)S(1)} %bitcast.27, bf16[1,1792,2048]{2,1,0:T(8,128)(2,1)} %param.12), kind=kOutput, calls=%fused_computation.7 | convolution fusion | flops 1174732800 | bytes 8568832 | tf_op jit(solution)/shard_map/dot_general | solution.py:37
  70.9 0.0 all-reduce.2.cloned.1.call-update
  70.9 0.0 copy-start.1
  70.9 38.0 %all-reduce.2.cloned.1.call-done = bf16[160,2048]{1,0:T(8,128)(2,1)} async-done(((bf16[160,2048]{1,0:T(8,128)(2,1)}), bf16[160,2048]{1,0:T(8,128)(2,1)}) %all-reduce.2.cloned.1.call-update) | async-done | bytes 655376 | tf_op jit(solution)/shard_map/psum | solution.py:39
  108.9 5.6 %fusion.7 = bf16[160,1792]{1,0:T(8,128)(2,1)} fusion(bf16[1,2048,1792]{2,1,0:T(8,128)(2,1)} %param.13, bf16[160,2048]{1,0:T(8,128)(2,1)} %all-reduce.2.cloned.1.call-done), kind=kOutput, calls=%fused_computation.8 | convolution fusion | flops 1176657920 | bytes 8568832 | tf_op jit(solution)/shard_map/dot_general | solution.py:41
  114.5 3.5 %all-to-all-start.1 = ((bf16[4,40,1792]{2,1,0:T(8,128)(2,1)}), bf16[4,40,1792]{2,1,0:T(8,128)(2,1)S(1)}, u32[]{:S(2)}, u32[]{:S(2)}) async-start(bf16[4,40,1792]{2,1,0:T(8,128)(2,1)} %bitcast.8), calls=%async_computation.2 | async-start | bytes 1146880 | tf_op jit(solution)/shard_map/all_to_all | solution.py:43
  118.0 0.0 copy-done.1
  118.1 0.1 copy.14
  118.2 9.2 %all-to-all-done.1 = bf16[4,40,1792]{2,1,0:T(8,128)(2,1)S(1)} async-done(((bf16[4,40,1792]{2,1,0:T(8,128)(2,1)}), bf16[4,40,1792]{2,1,0:T(8,128)(2,1)S(1)}, u32[]{:S(2)}, u32[]{:S(2)}) %all-to-all-start.1) | async-done | bytes 573472 | tf_op jit(solution)/shard_map/all_to_all | solution.py:43
  127.4 0.9 gather_fusion
  128.3 0.4 reshape.101
  128.7 2.0 %multiply_reduce_fusion = bf16[64,1792]{1,0:T(8,128)(2,1)} fusion(f32[64,2,1792]{2,1,0:T(2,128)S(1)} %reshape.101, f32[64,2]{1,0:T(8,128)S(1)} %copy.14), kind=kLoop, calls=%fused_computation.15 | loop fusion | flops 344064 | bytes 1147392 | tf_op jit(solution)/shard_map/reduce_sum | solution.py:46
  (7 shorter events, 0.1 us)
Async XLA Ops:
  7.2 31.0 %copy-start = (bf16[64,1792]{1,0:T(8,128)(2,1)S(1)}, bf16[64,1792]{1,0:T(8,128)(2,1)}, u32[]{:S(2)}) copy-start(bf16[64,1792]{1,0:T(8,128)(2,1)} %param.7) | copy-start | bytes 688132
  7.2 31.0 %reduce-scatter.2.cloned.1.call-start = ((), (), s32[]{:S(2)}) async-start(), calls=%async_computation.3 | async-start | bytes 1146880 | tf_op jit(solution)/shard_map/reduce_scatter | solution.py:15
  7.9 101.0 %all-reduce.2.cloned.1.call-start = ((), (), s32[]{:S(2)}) async-start(), calls=%async_computation.4 | async-start | bytes 1310720 | tf_op jit(solution)/shard_map/psum | solution.py:39
  70.9 47.1 %copy-start.1 = (f32[64,2]{0,1:T(2,128)S(1)}, f32[64,2]{0,1:T(2,128)}, u32[]{:S(2)}) copy-start(f32[64,2]{0,1:T(2,128)} %param.11) | copy-start | bytes 1540
  114.5 12.8 %all-to-all-start.1 = ((bf16[4,40,1792]{2,1,0:T(8,128)(2,1)}), bf16[4,40,1792]{2,1,0:T(8,128)(2,1)S(1)}, u32[]{:S(2)}, u32[]{:S(2)}) async-start(bf16[4,40,1792]{2,1,0:T(8,128)(2,1)} %bitcast.8), calls=%async_computation.2 | async-start | bytes 1146880 | tf_op jit(solution)/shard_map/all_to_all | solution.py:43
Sparse Core Ops, SparseCore 0:
  10.3 27.7 reduce-scatter.1
  71.0 37.8 all-reduce.1
where the time goes:
time: 138 us
  waiting for transfers between devices  75.1 us (54%)
  blocking collectives  21.7 us (16%)
  between operations  14.1 us (10%)
  matrix products  11 us (8%)
  other arithmetic  6.62 us (5%)
  local copies, waits for them, and re-layouts  5.51 us (4%)
  starting transfers between devices  3.55 us (3%)
    psum x1, waiting for transfers between devices, local(): lax.psum(rounded.astype(jnp.bfloat16), 'tensor').astype(jnp.float32)  38 us
    reduce_scatter x1, waiting for transfers between devices, local(): lax.psum_scatter(partial_value.astype(jnp.bfloat16), 'tensor', scatter_di...  27.2 us
    all_to_all x1, blocking collectives, local(): lax.all_to_all(outgoing, 'expert', split_axis=0, concat_axis=0, tiled=True)  11.9 us
    psum x1, blocking collectives, local(): squared = lax.psum(jnp.sum(stream_f * stream_f, axis=1), 'tensor')  9.72 us
    all_to_all x1, waiting for transfers between devices, local(): lax.all_to_all(result, 'expert', split_axis=0, concat_axis=0, tiled=True)  9.19 us
    dot_general x1, matrix products, local(): jnp.dot(hidden_full, down_local, preferred_element_type=jnp.float32)  5.62 us
    dot_general x1, matrix products, local(): jnp.dot(rows_flat, gate_local, preferred_element_type=jnp.float32)  5.38 us
    all_to_all x1, starting transfers between devices, local(): lax.all_to_all(result, 'expert', split_axis=0, concat_axis=0, tiled=True)  3.47 us
  transfers between devices with their start and end apart: 3, of which 3 were waited for; matrix products, arithmetic and copies ran while one was open for 2% of the time, Pallas kernels for 0%

commit v1 on v0

v1 whole, which is shorter than its diff:
```python
import functools

import jax
import jax.numpy as jnp
from jax import lax
from jax.experimental import pallas as pl
from jax.experimental.pallas import tpu as pltpu
from jax.sharding import PartitionSpec as P

EXTRA = 8


def partners(n):
    return list(range(n - 1, -1, -1))


def exchange(value, axis, step):
    n = lax.axis_size(axis)
    return lax.ppermute(value, axis, [(i, i ^ step) for i in range(n)])


def params(mib=24):
    return pltpu.CompilerParams(vmem_limit_bytes=mib << 20)


def whole():
    return pl.BlockSpec(memory_space=pltpu.VMEM)


def scalar():
    return pl.BlockSpec(memory_space=pltpu.SMEM)


def routing_kernel(n, cap, me_ref, ids_ref, idst_ref, scores_ref, select_ref, high_ref, low_ref):
    me = me_ref[0]
    tokens, top = ids_ref.shape
    f32, bf16 = jnp.float32, jnp.bfloat16
    row = lax.broadcasted_iota(jnp.int32, (tokens, tokens), 0)
    col = lax.broadcasted_iota(jnp.int32, (tokens, tokens), 1)
    before_t = jnp.where(row < col, 1.0, 0.0).astype(bf16)
    before = jnp.where(col < row, 1.0, 0.0).astype(bf16)
    scores = scores_ref[...]
    weights = 2.827 * scores / jnp.sum(scores, axis=1, keepdims=True)
    slot_t = lax.broadcasted_iota(jnp.int32, (cap, tokens), 0)
    slot = lax.broadcasted_iota(jnp.int32, (tokens, cap), 1)
    selects, highs, lows = [], [], []
    for k in range(n):
        expert = me ^ k
        named_t = jnp.zeros((1, tokens), f32)
        named = jnp.zeros((tokens, 1), f32)
        weight = jnp.zeros((tokens, 1), f32)
        for j in range(top):
            hit = jnp.where(ids_ref[:, j : j + 1] == expert, 1.0, 0.0)
            named_t += jnp.where(idst_ref[j : j + 1, :] == expert, 1.0, 0.0)
            named += hit
            weight += hit * weights[:, j : j + 1]
        place_t = jnp.dot(
            jnp.broadcast_to(named_t, (8, tokens)).astype(bf16), before_t, preferred_element_type=f32
        )[0:1, :].astype(jnp.int32)
        place = jnp.dot(
            before, jnp.broadcast_to(named, (tokens, 128)).astype(bf16), preferred_element_type=f32
        )[:, 0:1].astype(jnp.int32)
        selects.append(jnp.where(place_t == slot_t, jnp.broadcast_to(named_t, slot_t.shape), 0.0))
        full = jnp.where(place == slot, jnp.broadcast_to(weight, slot.shape), 0.0)
        high = full.astype(bf16).astype(f32)
        highs.append(high)
        lows.append(full - high)
    select_ref[...] = jnp.concatenate(selects, axis=0).astype(bf16)
    high_ref[...] = jnp.concatenate(highs, axis=1).astype(bf16)
    low_ref[...] = jnp.concatenate(lows, axis=1).astype(bf16)


def pack_kernel(n_tensor, n, cap, residual_ref, select_ref, *refs):
    parts, stream_ref, outs = refs[:n_tensor], refs[n_tensor], refs[n_tensor + 1 :]
    total = residual_ref[...].astype(jnp.float32)
    for part in parts:
        total += part[...].astype(jnp.float32)
    stream = total.astype(jnp.bfloat16)
    stream_ref[...] = stream
    packed = jnp.dot(select_ref[...], stream, preferred_element_type=jnp.float32)
    for k in range(n):
        outs[k][...] = packed[k * cap : (k + 1) * cap, :].astype(jnp.bfloat16)


def prepare_kernel(n, gain_ref, *refs):
    pieces, lhs_ref, squares_ref = refs[:n], refs[n], refs[n + 1]
    rows = jnp.concatenate([p[...].astype(jnp.float32) for p in pieces], axis=0)
    squared = (rows * rows).astype(jnp.bfloat16)
    ones = jnp.ones((8, rows.shape[1]), jnp.bfloat16)
    sums = lax.dot_general(ones, squared, (((1,), (1,)), ((), ())), preferred_element_type=jnp.float32)
    high = sums.astype(jnp.bfloat16).astype(jnp.float32)
    low = sums - high
    which = lax.broadcasted_iota(jnp.int32, sums.shape, 0)
    squares_ref[...] = jnp.where(which == 0, high, jnp.where(which == 1, low, 0.0))
    lhs_ref[...] = (rows * gain_ref[...].astype(jnp.float32)).astype(jnp.bfloat16)


def gate_kernel(block_ref, lhs_ref, squares_ref, w_ref, out_ref):
    rows = lhs_ref.shape[0]
    width = out_ref.shape[1]
    product = jnp.dot(lhs_ref[...], w_ref[0], preferred_element_type=jnp.float32)
    squares = squares_ref[...]
    if rows <= width:
        extra = jnp.concatenate([squares, jnp.zeros((EXTRA, width - rows), jnp.float32)], axis=1)
    else:
        extra = jnp.concatenate(
            [squares[0:2, i : i + width] for i in range(0, rows, width)]
            + [jnp.zeros((extra_rows(rows, width) - 2 * (rows // width), width), jnp.float32)],
            axis=0,
        )
    out_ref[...] = jnp.concatenate([product, extra], axis=0).astype(jnp.bfloat16)


def extra_rows(rows, width):
    return EXTRA if rows <= width else -(-2 * (rows // width) // 8) * 8


def activate_kernel(n, rows, features, *refs):
    parts, out_ref = refs[:n], refs[n]
    f32, bf16 = jnp.float32, jnp.bfloat16
    width = out_ref.shape[1]
    total, squares = None, None
    for part in parts:
        value = part[...].astype(f32)
        gate = value[:rows]
        extra = value[rows:]
        total = gate if total is None else total + gate
        squares = extra if squares is None else squares + extra
    columns = []
    if rows <= width:
        line = squares[0:1, :rows] + squares[1:2, :rows]
    else:
        line = jnp.concatenate(
            [squares[2 * i : 2 * i + 1] + squares[2 * i + 1 : 2 * i + 2] for i in range(rows // width)], axis=1
        )
    inverse = lax.rsqrt(line / features + 1e-06)
    column = jnp.transpose(jnp.broadcast_to(inverse, (8, rows)))[:, 0:1]
    gate = total * column
    out_ref[...] = (gate / (1.0 + jnp.exp(-gate))).astype(bf16)


def down_kernel(n_tensor, n, cap, block_ref, w_ref, *refs):
    pieces, outs = refs[:n_tensor], refs[n_tensor:]
    width = pieces[0].shape[1]
    total = None
    for k in range(n_tensor):
        start = pl.multiple_of((block_ref[0] ^ k) * width, width)
        term = jnp.dot(pieces[k][...], w_ref[0, pl.ds(start, width), :], preferred_element_type=jnp.float32)
        total = term if total is None else total + term
    for k in range(n):
        outs[k][...] = total[k * cap : (k + 1) * cap, :].astype(jnp.bfloat16)


def combine_kernel(n, high_ref, low_ref, *refs):
    pieces, out_ref = refs[:n], refs[n]
    rows = jnp.concatenate([p[...].astype(jnp.float32) for p in pieces], axis=0).astype(jnp.bfloat16)
    total = jnp.dot(high_ref[...], rows, preferred_element_type=jnp.float32)
    total += jnp.dot(low_ref[...], rows, preferred_element_type=jnp.float32)
    out_ref[...] = total.astype(jnp.bfloat16)


def local(residual, attn_partial, norm_gain, expert_ids, route_scores, w_gate, w_down):
    bf16, f32 = jnp.bfloat16, jnp.float32
    tokens, share = residual.shape
    nt, ne = lax.axis_size("tensor"), lax.axis_size("expert")
    z, me = lax.axis_index("tensor"), lax.axis_index("expert")
    top = expert_ids.shape[1]
    cap = tokens * top // ne * 5 // 4
    rows = ne * cap
    ff = w_gate.shape[2] // nt
    me_arr = jnp.full((1,), me, jnp.int32)
    z_arr = jnp.full((1,), z, jnp.int32)
    sds = jax.ShapeDtypeStruct

    parts = {}
    for k in partners(nt):
        block = lax.dynamic_slice(attn_partial[0], (0, (z ^ k) * share), (tokens, share))
        parts[k] = exchange(block, "tensor", k) if k else block

    select, high, low = pl.pallas_call(
        functools.partial(routing_kernel, ne, cap),
        out_shape=(sds((rows, tokens), bf16), sds((tokens, rows), bf16), sds((tokens, rows), bf16)),
        in_specs=[scalar(), whole(), whole(), whole()],
        out_specs=(whole(),) * 3,
        compiler_params=params(),
        name="routing",
    )(me_arr, expert_ids, expert_ids.T, route_scores)

    packed = pl.pallas_call(
        functools.partial(pack_kernel, nt, ne, cap),
        out_shape=(sds((tokens, share), bf16),) + (sds((cap, share), bf16),) * ne,
        in_specs=[whole()] * (2 + nt),
        out_specs=(whole(),) * (1 + ne),
        compiler_params=params(),
        name="pack",
    )(residual, select, *[parts[k] for k in range(nt)])
    stream, outgoing = packed[0], packed[1:]

    arrived = {}
    for k in partners(ne):
        arrived[k] = exchange(outgoing[k], "expert", k) if k else outgoing[k]

    lhs, squares = pl.pallas_call(
        functools.partial(prepare_kernel, ne),
        out_shape=(sds((rows, share), bf16), sds((8, rows), f32)),
        in_specs=[whole()] * (1 + ne),
        out_specs=(whole(),) * 2,
        compiler_params=params(),
        name="prepare",
    )(norm_gain[None, :], *[arrived[k] for k in range(ne)])

    tall = rows + extra_rows(rows, ff)
    gates = {}
    for k in partners(nt):
        partial_gate = pl.pallas_call(
            gate_kernel,
            out_shape=sds((tall, ff), bf16),
            grid_spec=pltpu.PrefetchScalarGridSpec(
                num_scalar_prefetch=1,
                grid=(1,),
                in_specs=[
                    pl.BlockSpec((rows, share), lambda i, b: (0, 0)),
                    pl.BlockSpec((8, rows), lambda i, b: (0, 0)),
                    pl.BlockSpec((1, share, ff), lambda i, b: (0, 0, b[0])),
                ],
                out_specs=pl.BlockSpec((tall, ff), lambda i, b: (0, 0)),
            ),
            compiler_params=params(),
            cost_estimate=pl.CostEstimate(
                flops=2 * rows * share * ff, bytes_accessed=2 * (share * ff + rows * share), transcendentals=0
            ),
            name="gate",
        )(z_arr ^ k, lhs, squares, w_gate)
        gates[k] = exchange(partial_gate, "tensor", k) if k else partial_gate

    hidden_own = pl.pallas_call(
        functools.partial(activate_kernel, nt, rows, float(share * nt)),
        out_shape=sds((rows, ff), bf16),
        in_specs=[whole()] * nt,
        out_specs=whole(),
        compiler_params=params(),
        name="activate",
    )(*[gates[k] for k in range(nt)])
    hidden = {}
    for k in partners(nt):
        hidden[k] = exchange(hidden_own, "tensor", k) if k else hidden_own

    produced = pl.pallas_call(
        functools.partial(down_kernel, nt, ne, cap),
        out_shape=(sds((cap, share), bf16),) * ne,
        in_specs=[scalar(), whole()] + [whole()] * nt,
        out_specs=(whole(),) * ne,
        compiler_params=params(),
        name="down",
    )(z_arr, w_down, *[hidden[k] for k in range(nt)])
    returned = {}
    for k in partners(ne):
        returned[k] = exchange(produced[k], "expert", k) if k else produced[k]

    moe_out = pl.pallas_call(
        functools.partial(combine_kernel, ne),
        out_shape=sds((tokens, share), bf16),
        in_specs=[whole()] * (2 + ne),
        out_specs=whole(),
        compiler_params=params(),
        name="combine",
    )(high, low, *[returned[k] for k in range(ne)])
    return stream, moe_out


def solution(mesh):
    return jax.shard_map(
        local,
        mesh=mesh,
        in_specs=(
            P(("groups", "expert"), "tensor"),
            P("tensor", ("groups", "expert"), None),
            P("tensor"),
            P(("groups", "expert"), None),
            P(("groups", "expert"), None),
            P("expert", "tensor", None),
            P("expert", None, "tensor"),
        ),
        out_specs=(P(("groups", "expert"), "tensor"), P(("groups", "expert"), "tensor")),
        check_vma=False,
    )
```

time: 138 us -> 85.7 us (0.62)
  waiting for transfers between devices: 75.1 us -> 51.1 us
  blocking collectives: 21.7 us -> 0 us
  starting transfers between devices: 3.55 us -> 18.9 us
  between operations: 14.1 us -> 0.79 us
  matrix products: 11 us -> 0 us
  other arithmetic: 6.62 us -> 0.01 us
  Pallas kernels: 0 us -> 6.16 us
  local copies, waits for them, and re-layouts: 5.51 us -> 8.36 us
    ppermute x0 -> x15, waiting for transfers between devices: none -> 51.1 us  [exchange(): return lax.ppermute(value, axis, [(i, i ^ step) for i in range(n)])]
    psum x1 -> x0, waiting for transfers between devices: 38 us -> none  [local(): lax.psum(rounded.astype(jnp.bfloat16), 'tensor').astype(jnp.float32)]
    reduce_scatter x1 -> x0, waiting for transfers between devices: 27.2 us -> none  [local(): lax.psum_scatter(partial_value.astype(jnp.bfloat16), 'tensor', scatter_di...]
    ppermute x0 -> x15, starting transfers between devices: none -> 18.9 us  [exchange(): return lax.ppermute(value, axis, [(i, i ^ step) for i in range(n)])]
    all_to_all x1 -> x0, blocking collectives: 11.9 us -> none  [local(): lax.all_to_all(outgoing, 'expert', split_axis=0, concat_axis=0, tiled=True)]
    dot_general x2 -> x0, matrix products: 11 us -> none  [the longest x1 5.62 us: local(): jnp.dot(hidden_full, down_local, preferred_element_type=jnp.float32)]
    psum x1 -> x0, blocking collectives: 9.72 us -> none  [local(): squared = lax.psum(jnp.sum(stream_f * stream_f, axis=1), 'tensor')]
    all_to_all x1 -> x0, waiting for transfers between devices: 9.19 us -> none  [local(): lax.all_to_all(result, 'expert', split_axis=0, concat_axis=0, tiled=True)]
  transfers between devices with their start and end apart: 3 -> 15, of which waited for: 3 -> 10; matrix products, arithmetic and copies ran while one was open for 2% -> 3% of each run, Pallas kernels for 0% -> 2%
where the time goes in v1:
time: 85.7 us; the launch traced here: 85.3 us
  waiting for transfers between devices  51.1 us (60%)
  starting transfers between devices  18.9 us (22%)
  local copies, waits for them, and re-layouts  8.36 us (10%)
  Pallas kernels  6.16 us (7%)
    ppermute x15, waiting for transfers between devices, exchange(): return lax.ppermute(value, axis, [(i, i ^ step) for i in range(n)])  51.1 us
    ppermute x15, starting transfers between devices, exchange(): return lax.ppermute(value, axis, [(i, i ^ step) for i in range(n)])  18.9 us
    unnamed x16, local copies, waits for them, and re-layouts  6.32 us
    pallas_call x4, Pallas kernels, local(): pl.pallas_call(gate_kernel, out_shape=sds((tall, ff), bf16), grid_spec=pl...  1.87 us
  transfers between devices with their start and end apart: 15, of which 10 were waited for; matrix products, arithmetic and copies ran while one was open for 3% of the time, Pallas kernels for 2%

profile of v1, /device:TPU:0, one launch (start us, length us, event | category | flops | bytes accessed | tf_op | source)
XLA Modules:
  0.0 85.3 jit_solution(16475928147105802894)
XLA Ops:
  0.7 1.4 %dynamic-slice_bitcast_fusion = (bf16[64,1792]{1,0:T(8,128)(2,1)S(1)}, bf16[64,1792]{1,0:T(8,128)(2,1)S(1)}, bf16[64,1792]{1,0:T(8,128)(2,1)S(1)}, bf16[64,1792]{1,0:T(8,128)(2,1)S(1)}) fusion(bf16[1,64,7168]{2,1,0:T(8,128)(2,1)} %param.8, s32[]{:T(128)S(6)} %select_n.15, s32[]{:T(128)S(6)} %select_n.13, s32[]{:T(128)S(6)} %select_n.12, s32[]{:T(128)S(6)} %select_n.14), kind=kLoop, calls=%fused_computation | loop fusion | bytes 1835024 | tf_op jit(solution)/shard_map/dynamic_slice | solution.py:177
  2.0 3.1 %collective-permute-start = (bf16[64,1792]{1,0:T(8,128)(2,1)S(1)}, bf16[64,1792]{1,0:T(8,128)(2,1)S(1)}, u32[]{:S(2)}, u32[]{:S(2)}) collective-permute-start(bf16[64,1792]{1,0:T(8,128)(2,1)S(1)} %get-tuple-element.31), channel_id=1, source_target_pairs={{0,1},{1,0},{2,3},{3,2},{4,5},{5,4},{6,7},{7,6},{8,9},{9,8},{10,11... | collective-permute-start | bytes 688136 | tf_op jit(solution)/shard_map/ppermute | solution.py:19
  5.1 2.6 %collective-permute-start.1 = (bf16[64,1792]{1,0:T(8,128)(2,1)S(1)}, bf16[64,1792]{1,0:T(8,128)(2,1)S(1)}, u32[]{:S(2)}, u32[]{:S(2)}) collective-permute-start(bf16[64,1792]{1,0:T(8,128)(2,1)S(1)} %get-tuple-element.33), channel_id=1, source_target_pairs={{0,2},{1,3},{2,0},{3,1},{4,6},{5,7},{6,4},{7,5},{8,10},{9,11},{10,... | collective-permute-start | bytes 688136 | tf_op jit(solution)/shard_map/ppermute | solution.py:19
  7.7 0.8 copy.10.scores_ref
  8.5 0.8 copy.9.ids_ref
  9.2 0.7 copy-done.2
  9.9 0.5 routing.1
  10.4 4.4 %collective-permute-done.refs_1_ = bf16[64,1792]{1,0:T(8,128)(2,1)S(1)} collective-permute-done((bf16[64,1792]{1,0:T(8,128)(2,1)S(1)}, bf16[64,1792]{1,0:T(8,128)(2,1)S(1)}, u32[]{:S(2)}, u32[]{:S(2)}) %collective-permute-start) | collective-permute-done | bytes 229408 | tf_op jit(solution)/shard_map/ppermute | solution.py:19
  14.8 9.5 %collective-permute-done.1.refs_2_ = bf16[64,1792]{1,0:T(8,128)(2,1)S(1)} collective-permute-done((bf16[64,1792]{1,0:T(8,128)(2,1)S(1)}, bf16[64,1792]{1,0:T(8,128)(2,1)S(1)}, u32[]{:S(2)}, u32[]{:S(2)}) %collective-permute-start.1) | collective-permute-done | bytes 229408 | tf_op jit(solution)/shard_map/ppermute | solution.py:19
  24.4 0.9 %copy-done.1 = bf16[64,1792]{1,0:T(8,128)(2,1)S(1)} copy-done((bf16[64,1792]{1,0:T(8,128)(2,1)S(1)}, bf16[64,1792]{1,0:T(8,128)(2,1)}, u32[]{:S(2)}) %copy-start.1) | copy-done | bytes 229400
  25.3 0.9 %pack.1 = (bf16[64,1792]{1,0:T(8,128)(2,1)}, bf16[40,1792]{1,0:T(8,128)(2,1)S(1)}, bf16[40,1792]{1,0:T(8,128)(2,1)S(1)}, bf16[40,1792]{1,0:T(8,128)(2,1)S(1)}, bf16[40,1792]{1,0:T(8,128)(2,1)S(1)}) custom-call(bf16[64,1792]{1,0:T(8,128)(2,1)S(1)} %copy-done.1, bf16[160,64]{1,0:T(8,128)(2,1)S(1)} %get-tuple-element.16.select_ref, ...), custom_call_target="tpu_custom_call" | custom-call | tf_op jit(solution)/shard_map/pack/pallas_call | solution.py:189
  26.2 1.5 %collective-permute-start.4 = (bf16[40,1792]{1,0:T(8,128)(2,1)S(1)}, bf16[40,1792]{1,0:T(8,128)(2,1)S(1)}, u32[]{:S(2)}, u32[]{:S(2)}) collective-permute-start(bf16[40,1792]{1,0:T(8,128)(2,1)S(1)} %get-tuple-element.22), channel_id=1, source_target_pairs={{0,8},{4,12},{8,0},{12,4},{1,9},{5,13},{9,1},{13,5},{2,10},{6,14},... | collective-permute-start | bytes 430088 | tf_op jit(solution)/shard_map/ppermute | solution.py:19
  27.7 0.4 collective-permute-start.5
  28.1 0.7 broadcast_in_dim.11.gain_ref
  28.7 0.0 collective-permute-done.3.refs_1_
  28.7 4.0 %collective-permute-done.4.refs_2_ = bf16[40,1792]{1,0:T(8,128)(2,1)S(1)} collective-permute-done((bf16[40,1792]{1,0:T(8,128)(2,1)S(1)}, bf16[40,1792]{1,0:T(8,128)(2,1)S(1)}, u32[]{:S(2)}, u32[]{:S(2)}) %collective-permute-start.4) | collective-permute-done | bytes 143392 | tf_op jit(solution)/shard_map/ppermute | solution.py:19
  32.7 2.3 %collective-permute-done.5.refs_3_ = bf16[40,1792]{1,0:T(8,128)(2,1)S(1)} collective-permute-done((bf16[40,1792]{1,0:T(8,128)(2,1)S(1)}, bf16[40,1792]{1,0:T(8,128)(2,1)S(1)}, u32[]{:S(2)}, u32[]{:S(2)}) %collective-permute-start.5) | collective-permute-done | bytes 143392 | tf_op jit(solution)/shard_map/ppermute | solution.py:19
  35.0 0.2 prepare.1
  35.3 0.0 copy-start
  35.3 3.1 %copy-done = bf16[1,1792,2048]{2,1,0:T(8,128)(2,1)S(1)} copy-done((bf16[1,1792,2048]{2,1,0:T(8,128)(2,1)S(1)}, bf16[1,1792,2048]{2,1,0:T(8,128)(2,1)}, u32[]{:S(2)}) %copy-start) | copy-done | bytes 7340056
  38.4 0.5 gate.7
  38.9 0.0 slice-start
  38.9 2.5 %collective-permute-start.8 = (bf16[168,512]{1,0:T(8,128)(2,1)S(1)}, bf16[168,512]{1,0:T(8,128)(2,1)S(1)}, u32[]{:S(2)}, u32[]{:S(2)}) collective-permute-start(bf16[168,512]{1,0:T(8,128)(2,1)S(1)} %gate.7), channel_id=1, source_target_pairs={{0,3},{1,2},{2,1},{3,0},{4,7},{5,6},{6,5},{7,4},{8,11},{9,10},{10,... | collective-permute-start | bytes 516104 | tf_op jit(solution)/shard_map/ppermute | solution.py:19
  41.5 0.5 gate.6
  41.9 0.0 slice-start.1
  41.9 0.0 slice-start.2
  42.0 3.1 %collective-permute-start.7 = (bf16[168,512]{1,0:T(8,128)(2,1)S(1)}, bf16[168,512]{1,0:T(8,128)(2,1)S(1)}, u32[]{:S(2)}, u32[]{:S(2)}) collective-permute-start(bf16[168,512]{1,0:T(8,128)(2,1)S(1)} %gate.6), channel_id=1, source_target_pairs={{0,2},{1,3},{2,0},{3,1},{4,6},{5,7},{6,4},{7,5},{8,10},{9,11},{10,... | collective-permute-start | bytes 516104 | tf_op jit(solution)/shard_map/ppermute | solution.py:19
  45.1 0.5 gate.5
  45.6 0.0 slice-start.3
  45.6 0.2 collective-permute-start.6
  45.8 0.5 gate.4.refs_0_
  46.3 1.1 %collective-permute-done.8.refs_3_ = bf16[168,512]{1,0:T(8,128)(2,1)S(1)} collective-permute-done((bf16[168,512]{1,0:T(8,128)(2,1)S(1)}, bf16[168,512]{1,0:T(8,128)(2,1)S(1)}, u32[]{:S(2)}, u32[]{:S(2)}) %collective-permute-start.8) | collective-permute-done | bytes 172064 | tf_op jit(solution)/shard_map/ppermute | solution.py:19
  47.4 11.0 %collective-permute-done.7.refs_2_ = bf16[168,512]{1,0:T(8,128)(2,1)S(1)} collective-permute-done((bf16[168,512]{1,0:T(8,128)(2,1)S(1)}, bf16[168,512]{1,0:T(8,128)(2,1)S(1)}, u32[]{:S(2)}, u32[]{:S(2)}) %collective-permute-start.7) | collective-permute-done | bytes 172064 | tf_op jit(solution)/shard_map/ppermute | solution.py:19
  58.3 0.0 collective-permute-done.6.refs_1_
  58.3 0.3 activate.1.refs_0_
  58.6 0.1 collective-permute-start.10
  58.7 2.5 %collective-permute-start.11 = (bf16[160,512]{1,0:T(8,128)(2,1)S(1)}, bf16[160,512]{1,0:T(8,128)(2,1)S(1)}, u32[]{:S(2)}, u32[]{:S(2)}) collective-permute-start(bf16[160,512]{1,0:T(8,128)(2,1)S(1)} %activate.1.refs_0_), channel_id=1, source_target_pairs={{0,3},{1,2},{2,1},{3,0},{4,7},{5,6},{6,5},{7,4},{8,11},{9,10},{10,... | collective-permute-start | bytes 491528 | tf_op jit(solution)/shard_map/ppermute | solution.py:19
  61.2 0.9 %collective-permute-start.9 = (bf16[160,512]{1,0:T(8,128)(2,1)S(1)}, bf16[160,512]{1,0:T(8,128)(2,1)S(1)}, u32[]{:S(2)}, u32[]{:S(2)}) collective-permute-start(bf16[160,512]{1,0:T(8,128)(2,1)S(1)} %activate.1.refs_0_), channel_id=1, source_target_pairs={{0,1},{1,0},{2,3},{3,2},{4,5},{5,4},{6,7},{7,6},{8,9},{9,8},{10,11... | collective-permute-start | bytes 491528 | tf_op jit(solution)/shard_map/ppermute | solution.py:19
  62.2 10.5 %collective-permute-done.10.refs_2_ = bf16[160,512]{1,0:T(8,128)(2,1)S(1)} collective-permute-done((bf16[160,512]{1,0:T(8,128)(2,1)S(1)}, bf16[160,512]{1,0:T(8,128)(2,1)S(1)}, u32[]{:S(2)}, u32[]{:S(2)}) %collective-permute-start.10) | collective-permute-done | bytes 163872 | tf_op jit(solution)/shard_map/ppermute | solution.py:19
  72.7 0.0 collective-permute-done.11.refs_3_
  72.7 1.3 %collective-permute-done.9.refs_1_ = bf16[160,512]{1,0:T(8,128)(2,1)S(1)} collective-permute-done((bf16[160,512]{1,0:T(8,128)(2,1)S(1)}, bf16[160,512]{1,0:T(8,128)(2,1)S(1)}, u32[]{:S(2)}, u32[]{:S(2)}) %collective-permute-start.9) | collective-permute-done | bytes 163872 | tf_op jit(solution)/shard_map/ppermute | solution.py:19
  74.0 1.4 %down.1 = (bf16[40,1792]{1,0:T(8,128)(2,1)S(1)}, bf16[40,1792]{1,0:T(8,128)(2,1)S(1)}, bf16[40,1792]{1,0:T(8,128)(2,1)S(1)}, bf16[40,1792]{1,0:T(8,128)(2,1)S(1)}) custom-call(s32[1]{0:T(128)} %bitcast.6.block_ref, bf16[1,2048,1792]{2,1,0:T(8,128)(2,1)S(1)} %bitcast.14, bf16[160,512]{1,0:T(8,128)(2,1)S(1)} %activate.1.refs_0_, ...), custom_call_target="tpu_custom_call" | custom-call | tf_op jit(solution)/shard_map/down/pallas_call | solution.py:248
  75.4 0.1 collective-permute-start.12
  75.5 1.6 %collective-permute-start.13 = (bf16[40,1792]{1,0:T(8,128)(2,1)S(1)}, bf16[40,1792]{1,0:T(8,128)(2,1)S(1)}, u32[]{:S(2)}, u32[]{:S(2)}) collective-permute-start(bf16[40,1792]{1,0:T(8,128)(2,1)S(1)} %get-tuple-element.28), channel_id=1, source_target_pairs={{0,8},{4,12},{8,0},{12,4},{1,9},{5,13},{9,1},{13,5},{2,10},{6,14},... | collective-permute-start | bytes 430088 | tf_op jit(solution)/shard_map/ppermute | solution.py:19
  77.1 0.3 collective-permute-start.14
  77.4 4.8 %collective-permute-done.13.refs_2_ = bf16[40,1792]{1,0:T(8,128)(2,1)S(1)} collective-permute-done((bf16[40,1792]{1,0:T(8,128)(2,1)S(1)}, bf16[40,1792]{1,0:T(8,128)(2,1)S(1)}, u32[]{:S(2)}, u32[]{:S(2)}) %collective-permute-start.13) | collective-permute-done | bytes 143392 | tf_op jit(solution)/shard_map/ppermute | solution.py:19
  82.1 2.2 %collective-permute-done.14.refs_3_ = bf16[40,1792]{1,0:T(8,128)(2,1)S(1)} collective-permute-done((bf16[40,1792]{1,0:T(8,128)(2,1)S(1)}, bf16[40,1792]{1,0:T(8,128)(2,1)S(1)}, u32[]{:S(2)}, u32[]{:S(2)}) %collective-permute-start.14) | collective-permute-done | bytes 143392 | tf_op jit(solution)/shard_map/ppermute | solution.py:19
  84.3 1.0 %combine.1 = bf16[64,1792]{1,0:T(8,128)(2,1)} custom-call(bf16[64,160]{1,0:T(8,128)(2,1)S(1)} %get-tuple-element.18.high_ref, bf16[64,160]{1,0:T(8,128)(2,1)S(1)} %get-tuple-element.19.low_ref, bf16[40,1792]{1,0:T(8,128)(2,1)S(1)} %get-tuple-element.26.refs_0_, bf16[40,1792]{1,0:T(8,128)(2,1)S(1)} %collective-permute-done.12.refs_1_, ...), custom_call_target="tpu_custom_call" | custom-call | tf_op jit(solution)/shard_map/combine/pallas_call | solution.py:260
  (12 shorter events, 0.0 us)
Async XLA Ops:
  2.0 12.8 %collective-permute-start = (bf16[64,1792]{1,0:T(8,128)(2,1)S(1)}, bf16[64,1792]{1,0:T(8,128)(2,1)S(1)}, u32[]{:S(2)}, u32[]{:S(2)}) collective-permute-start(bf16[64,1792]{1,0:T(8,128)(2,1)S(1)} %get-tuple-element.31), channel_id=1, source_target_pairs={{0,1},{1,0},{2,3},{3,2},{4,5},{5,4},{6,7},{7,6},{8,9},{9,8},{10,11... | collective-permute-start | bytes 688136 | tf_op jit(solution)/shard_map/ppermute | solution.py:19
  5.1 19.3 %collective-permute-start.1 = (bf16[64,1792]{1,0:T(8,128)(2,1)S(1)}, bf16[64,1792]{1,0:T(8,128)(2,1)S(1)}, u32[]{:S(2)}, u32[]{:S(2)}) collective-permute-start(bf16[64,1792]{1,0:T(8,128)(2,1)S(1)} %get-tuple-element.33), channel_id=1, source_target_pairs={{0,2},{1,3},{2,0},{3,1},{4,6},{5,7},{6,4},{7,5},{8,10},{9,11},{10,... | collective-permute-start | bytes 688136 | tf_op jit(solution)/shard_map/ppermute | solution.py:19
  7.7 16.7 %collective-permute-start.2 = (bf16[64,1792]{1,0:T(8,128)(2,1)S(1)}, bf16[64,1792]{1,0:T(8,128)(2,1)S(1)}, u32[]{:S(2)}, u32[]{:S(2)}) collective-permute-start(bf16[64,1792]{1,0:T(8,128)(2,1)S(1)} %get-tuple-element.30), channel_id=1, source_target_pairs={{0,3},{1,2},{2,1},{3,0},{4,7},{5,6},{6,5},{7,4},{8,11},{9,10},{10,... | collective-permute-start | bytes 688136 | tf_op jit(solution)/shard_map/ppermute | solution.py:19
  9.2 0.7 copy-start.2
  24.4 0.9 %copy-start.1 = (bf16[64,1792]{1,0:T(8,128)(2,1)S(1)}, bf16[64,1792]{1,0:T(8,128)(2,1)}, u32[]{:S(2)}) copy-start(bf16[64,1792]{1,0:T(8,128)(2,1)} %residual_ref.1) | copy-start | bytes 688132
  26.2 2.6 %collective-permute-start.3 = (bf16[40,1792]{1,0:T(8,128)(2,1)S(1)}, bf16[40,1792]{1,0:T(8,128)(2,1)S(1)}, u32[]{:S(2)}, u32[]{:S(2)}) collective-permute-start(bf16[40,1792]{1,0:T(8,128)(2,1)S(1)} %get-tuple-element.21), channel_id=1, source_target_pairs={{0,4},{4,0},{8,12},{12,8},{1,5},{5,1},{9,13},{13,9},{2,6},{6,2},{1... | collective-permute-start | bytes 430088 | tf_op jit(solution)/shard_map/ppermute | solution.py:19
  26.2 6.6 %collective-permute-start.4 = (bf16[40,1792]{1,0:T(8,128)(2,1)S(1)}, bf16[40,1792]{1,0:T(8,128)(2,1)S(1)}, u32[]{:S(2)}, u32[]{:S(2)}) collective-permute-start(bf16[40,1792]{1,0:T(8,128)(2,1)S(1)} %get-tuple-element.22), channel_id=1, source_target_pairs={{0,8},{4,12},{8,0},{12,4},{1,9},{5,13},{9,1},{13,5},{2,10},{6,14},... | collective-permute-start | bytes 430088 | tf_op jit(solution)/shard_map/ppermute | solution.py:19
  27.7 7.4 %collective-permute-start.5 = (bf16[40,1792]{1,0:T(8,128)(2,1)S(1)}, bf16[40,1792]{1,0:T(8,128)(2,1)S(1)}, u32[]{:S(2)}, u32[]{:S(2)}) collective-permute-start(bf16[40,1792]{1,0:T(8,128)(2,1)S(1)} %get-tuple-element.23), channel_id=1, source_target_pairs={{0,12},{4,8},{8,4},{12,0},{1,13},{5,9},{9,5},{13,1},{2,14},{6,10},... | collective-permute-start | bytes 430088 | tf_op jit(solution)/shard_map/ppermute | solution.py:19
  35.3 3.1 %copy-start = (bf16[1,1792,2048]{2,1,0:T(8,128)(2,1)S(1)}, bf16[1,1792,2048]{2,1,0:T(8,128)(2,1)}, u32[]{:S(2)}) copy-start(bf16[1,1792,2048]{2,1,0:T(8,128)(2,1)} %w_ref.8) | copy-start | bytes 22020100
  38.9 6.9 %slice-start = ((s8[7340032]{0:T(1024)(128)(4,1)}), s8[4194304]{0:T(1024)(128)(4,1)S(1)}, s32[]{:S(2)}) async-start(s8[7340032]{0:T(1024)(128)(4,1)} %bitcast.11), calls=%async_computation | async-start | bytes 8388608
  38.9 8.5 %collective-permute-start.8 = (bf16[168,512]{1,0:T(8,128)(2,1)S(1)}, bf16[168,512]{1,0:T(8,128)(2,1)S(1)}, u32[]{:S(2)}, u32[]{:S(2)}) collective-permute-start(bf16[168,512]{1,0:T(8,128)(2,1)S(1)} %gate.7), channel_id=1, source_target_pairs={{0,3},{1,2},{2,1},{3,0},{4,7},{5,6},{6,5},{7,4},{8,11},{9,10},{10,... | collective-permute-start | bytes 516104 | tf_op jit(solution)/shard_map/ppermute | solution.py:19
  41.9 3.8 %slice-start.1 = ((s8[7340032]{0:T(1024)(128)(4,1)}), s8[3145728]{0:T(1024)(128)(4,1)S(1)}, s32[]{:S(2)}) async-start(s8[7340032]{0:T(1024)(128)(4,1)} %bitcast.11), calls=%async_computation.1 | async-start | bytes 6291456
  41.9 32.1 %slice-start.2 = ((s8[7340032]{0:T(1024)(128)(4,1)}), s8[4194304]{0:T(1024)(128)(4,1)S(1)}, s32[]{:S(2)}) async-start(s8[7340032]{0:T(1024)(128)(4,1)} %bitcast.13), calls=%async_computation.2 | async-start | bytes 8388608
  42.0 16.4 %collective-permute-start.7 = (bf16[168,512]{1,0:T(8,128)(2,1)S(1)}, bf16[168,512]{1,0:T(8,128)(2,1)S(1)}, u32[]{:S(2)}, u32[]{:S(2)}) collective-permute-start(bf16[168,512]{1,0:T(8,128)(2,1)S(1)} %gate.6), channel_id=1, source_target_pairs={{0,2},{1,3},{2,0},{3,1},{4,6},{5,7},{6,4},{7,5},{8,10},{9,11},{10,... | collective-permute-start | bytes 516104 | tf_op jit(solution)/shard_map/ppermute | solution.py:19
  45.6 28.5 %slice-start.3 = ((s8[7340032]{0:T(1024)(128)(4,1)}), s8[3145728]{0:T(1024)(128)(4,1)S(1)}, s32[]{:S(2)}) async-start(s8[7340032]{0:T(1024)(128)(4,1)} %bitcast.13), calls=%async_computation.3 | async-start | bytes 6291456
  45.6 12.8 %collective-permute-start.6 = (bf16[168,512]{1,0:T(8,128)(2,1)S(1)}, bf16[168,512]{1,0:T(8,128)(2,1)S(1)}, u32[]{:S(2)}, u32[]{:S(2)}) collective-permute-start(bf16[168,512]{1,0:T(8,128)(2,1)S(1)} %gate.5), channel_id=1, source_target_pairs={{0,1},{1,0},{2,3},{3,2},{4,5},{5,4},{6,7},{7,6},{8,9},{9,8},{10,11... | collective-permute-start | bytes 516104 | tf_op jit(solution)/shard_map/ppermute | solution.py:19
  58.6 14.1 %collective-permute-start.10 = (bf16[160,512]{1,0:T(8,128)(2,1)S(1)}, bf16[160,512]{1,0:T(8,128)(2,1)S(1)}, u32[]{:S(2)}, u32[]{:S(2)}) collective-permute-start(bf16[160,512]{1,0:T(8,128)(2,1)S(1)} %activate.1.refs_0_), channel_id=1, source_target_pairs={{0,2},{1,3},{2,0},{3,1},{4,6},{5,7},{6,4},{7,5},{8,10},{9,11},{10,... | collective-permute-start | bytes 491528 | tf_op jit(solution)/shard_map/ppermute | solution.py:19
  58.7 14.0 %collective-permute-start.11 = (bf16[160,512]{1,0:T(8,128)(2,1)S(1)}, bf16[160,512]{1,0:T(8,128)(2,1)S(1)}, u32[]{:S(2)}, u32[]{:S(2)}) collective-permute-start(bf16[160,512]{1,0:T(8,128)(2,1)S(1)} %activate.1.refs_0_), channel_id=1, source_target_pairs={{0,3},{1,2},{2,1},{3,0},{4,7},{5,6},{6,5},{7,4},{8,11},{9,10},{10,... | collective-permute-start | bytes 491528 | tf_op jit(solution)/shard_map/ppermute | solution.py:19
  61.2 12.8 %collective-permute-start.9 = (bf16[160,512]{1,0:T(8,128)(2,1)S(1)}, bf16[160,512]{1,0:T(8,128)(2,1)S(1)}, u32[]{:S(2)}, u32[]{:S(2)}) collective-permute-start(bf16[160,512]{1,0:T(8,128)(2,1)S(1)} %activate.1.refs_0_), channel_id=1, source_target_pairs={{0,1},{1,0},{2,3},{3,2},{4,5},{5,4},{6,7},{7,6},{8,9},{9,8},{10,11... | collective-permute-start | bytes 491528 | tf_op jit(solution)/shard_map/ppermute | solution.py:19
  75.4 1.9 %collective-permute-start.12 = (bf16[40,1792]{1,0:T(8,128)(2,1)S(1)}, bf16[40,1792]{1,0:T(8,128)(2,1)S(1)}, u32[]{:S(2)}, u32[]{:S(2)}) collective-permute-start(bf16[40,1792]{1,0:T(8,128)(2,1)S(1)} %get-tuple-element.27), channel_id=1, source_target_pairs={{0,4},{4,0},{8,12},{12,8},{1,5},{5,1},{9,13},{13,9},{2,6},{6,2},{1... | collective-permute-start | bytes 430088 | tf_op jit(solution)/shard_map/ppermute | solution.py:19
  75.5 6.6 %collective-permute-start.13 = (bf16[40,1792]{1,0:T(8,128)(2,1)S(1)}, bf16[40,1792]{1,0:T(8,128)(2,1)S(1)}, u32[]{:S(2)}, u32[]{:S(2)}) collective-permute-start(bf16[40,1792]{1,0:T(8,128)(2,1)S(1)} %get-tuple-element.28), channel_id=1, source_target_pairs={{0,8},{4,12},{8,0},{12,4},{1,9},{5,13},{9,1},{13,5},{2,10},{6,14},... | collective-permute-start | bytes 430088 | tf_op jit(solution)/shard_map/ppermute | solution.py:19
  77.1 7.2 %collective-permute-start.14 = (bf16[40,1792]{1,0:T(8,128)(2,1)S(1)}, bf16[40,1792]{1,0:T(8,128)(2,1)S(1)}, u32[]{:S(2)}, u32[]{:S(2)}) collective-permute-start(bf16[40,1792]{1,0:T(8,128)(2,1)S(1)} %get-tuple-element.29), channel_id=1, source_target_pairs={{0,12},{4,8},{8,4},{12,0},{1,13},{5,9},{9,5},{13,1},{2,14},{6,10},... | collective-permute-start | bytes 430088 | tf_op jit(solution)/shard_map/ppermute | solution.py:19

commit v2 on v1

v2 whole, which is shorter than its diff:
```python
import functools

import jax
import jax.numpy as jnp
from jax import lax
from jax.experimental import pallas as pl
from jax.experimental.pallas import tpu as pltpu
from jax.sharding import PartitionSpec as P


def partners(n):
    return list(range(n - 1, -1, -1))


def exchange(value, axis, step):
    n = lax.axis_size(axis)
    return lax.ppermute(value, axis, [(i, i ^ step) for i in range(n)])


def params(mib=16):
    return pltpu.CompilerParams(vmem_limit_bytes=mib << 20)


def whole():
    return pl.BlockSpec(memory_space=pltpu.VMEM)


def anywhere():
    return pl.BlockSpec(memory_space=pl.ANY)


def scalar():
    return pl.BlockSpec(memory_space=pltpu.SMEM)


def routing_kernel(n, cap, me_ref, ids_ref, idst_ref, scores_ref, select_ref, high_ref, low_ref):
    me = me_ref[0]
    tokens, top = ids_ref.shape
    f32, bf16 = jnp.float32, jnp.bfloat16
    row = lax.broadcasted_iota(jnp.int32, (tokens, tokens), 0)
    col = lax.broadcasted_iota(jnp.int32, (tokens, tokens), 1)
    before_t = jnp.where(row < col, 1.0, 0.0).astype(bf16)
    before = jnp.where(col < row, 1.0, 0.0).astype(bf16)
    scores = scores_ref[...]
    weights = 2.827 * scores / jnp.sum(scores, axis=1, keepdims=True)
    slot_t = lax.broadcasted_iota(jnp.int32, (cap, tokens), 0)
    slot = lax.broadcasted_iota(jnp.int32, (tokens, cap), 1)
    selects, highs, lows = [], [], []
    for k in range(n):
        expert = me ^ k
        named_t = jnp.zeros((1, tokens), f32)
        named = jnp.zeros((tokens, 1), f32)
        weight = jnp.zeros((tokens, 1), f32)
        for j in range(top):
            hit = jnp.where(ids_ref[:, j : j + 1] == expert, 1.0, 0.0)
            named_t += jnp.where(idst_ref[j : j + 1, :] == expert, 1.0, 0.0)
            named += hit
            weight += hit * weights[:, j : j + 1]
        place_t = jnp.dot(
            jnp.broadcast_to(named_t, (8, tokens)).astype(bf16), before_t, preferred_element_type=f32
        )[0:1, :].astype(jnp.int32)
        place = jnp.dot(
            before, jnp.broadcast_to(named, (tokens, 128)).astype(bf16), preferred_element_type=f32
        )[:, 0:1].astype(jnp.int32)
        selects.append(jnp.where(place_t == slot_t, jnp.broadcast_to(named_t, slot_t.shape), 0.0))
        full = jnp.where(place == slot, jnp.broadcast_to(weight, slot.shape), 0.0)
        high = full.astype(bf16).astype(f32)
        highs.append(high)
        lows.append(full - high)
    select_ref[...] = jnp.concatenate(selects, axis=0).astype(bf16)
    high_ref[...] = jnp.concatenate(highs, axis=1).astype(bf16)
    low_ref[...] = jnp.concatenate(lows, axis=1).astype(bf16)


def fetch_kernel(*refs):
    *pairs, sems = refs
    half = len(pairs) // 2
    copies = [pltpu.make_async_copy(pairs[i], pairs[half + i], sems.at[i]) for i in range(half)]
    for copy in copies:
        copy.start()
    for copy in copies:
        copy.wait()


def add_kernel(n_tensor, cap, ks, residual_ref, select_ref, *refs):
    parts, stream_ref, kept_ref, outs = refs[:n_tensor], *refs[n_tensor : n_tensor + 2], refs[n_tensor + 2 :]
    total = residual_ref[...].astype(jnp.float32)
    for part in parts:
        total += part[...].astype(jnp.float32)
    stream_ref[...] = total.astype(jnp.bfloat16)
    kept_ref[...] = total.astype(jnp.bfloat16)
    pack_kernel(cap, ks, kept_ref, select_ref, *outs)


def pack_kernel(cap, ks, stream_ref, select_ref, *outs):
    first, last = ks[0] * cap, (ks[-1] + 1) * cap
    packed = jnp.dot(select_ref[first:last, :], stream_ref[...], preferred_element_type=jnp.float32)
    for i, out in enumerate(outs):
        out[...] = packed[i * cap : (i + 1) * cap, :].astype(jnp.bfloat16)


def prepare_kernel(n, gain_ref, *refs):
    pieces, lhs_ref, squares_ref = refs[:n], refs[-2], refs[-1]
    rows = jnp.concatenate([p[...].astype(jnp.float32) for p in pieces], axis=0)
    squared = (rows * rows).astype(jnp.bfloat16)
    ones = jnp.ones((8, rows.shape[1]), jnp.bfloat16)
    sums = lax.dot_general(ones, squared, (((1,), (1,)), ((), ())), preferred_element_type=jnp.float32)
    high = sums.astype(jnp.bfloat16).astype(jnp.float32)
    low = sums - high
    which = lax.broadcasted_iota(jnp.int32, sums.shape, 0)
    squares_ref[...] = jnp.where(which == 0, high, jnp.where(which == 1, low, 0.0))
    lhs_ref[...] = (rows * gain_ref[...].astype(jnp.float32)).astype(jnp.bfloat16)


def extra_rows(rows, width):
    return -(-2 * -(-rows // width) // 8) * 8


def gate_kernel(block_ref, lhs_ref, squares_ref, w_ref, *refs):
    out_ref = refs[-1]
    rows = lhs_ref.shape[0]
    width = out_ref.shape[1]
    extra = extra_rows(rows, width)
    product = jnp.dot(lhs_ref[...], w_ref[0], preferred_element_type=jnp.float32)
    squares = squares_ref[...]
    pieces = -(-rows // width)
    if rows % width:
        squares = jnp.concatenate([squares, jnp.zeros((8, width - rows % width), jnp.float32)], axis=1)
    if pieces == 1:
        below = squares
    else:
        below = jnp.concatenate(
            [squares[0:2, i * width : (i + 1) * width] for i in range(pieces)]
            + ([jnp.zeros((extra - 2 * pieces, width), jnp.float32)] if extra > 2 * pieces else []),
            axis=0,
        )
    out_ref[...] = jnp.concatenate([product, below], axis=0).astype(jnp.bfloat16)


def activate_kernel(n, rows, features, *refs):
    parts, out_ref = refs[:n], refs[-1]
    f32, bf16 = jnp.float32, jnp.bfloat16
    width = out_ref.shape[1]
    total, squares = None, None
    for part in parts:
        value = part[...].astype(f32)
        gate = value[:rows]
        extra = value[rows:]
        total = gate if total is None else total + gate
        squares = extra if squares is None else squares + extra
    pieces = -(-rows // width)
    lines = [squares[2 * i : 2 * i + 1] + squares[2 * i + 1 : 2 * i + 2] for i in range(pieces)]
    line = (lines[0] if pieces == 1 else jnp.concatenate(lines, axis=1))[:, :rows]
    inverse = lax.rsqrt(line / features + 1e-06)
    column = jnp.transpose(jnp.broadcast_to(inverse, (8, rows)))[:, 0:1]
    gate = total * column
    out_ref[...] = (gate / (1.0 + jnp.exp(-gate))).astype(bf16)


def down_kernel(n_tensor, n, cap, block_ref, w_ref, *refs):
    pieces, outs = refs[:n_tensor], refs[n_tensor:]
    width = pieces[0].shape[1]
    total = None
    for k in range(n_tensor):
        start = pl.multiple_of((block_ref[0] ^ k) * width, width)
        term = jnp.dot(pieces[k][...], w_ref[0, pl.ds(start, width), :], preferred_element_type=jnp.float32)
        total = term if total is None else total + term
    for k in range(n):
        outs[k][...] = total[k * cap : (k + 1) * cap, :].astype(jnp.bfloat16)


def combine_kernel(n, high_ref, low_ref, *refs):
    pieces, out_ref = refs[:n], refs[n]
    rows = jnp.concatenate([p[...].astype(jnp.float32) for p in pieces], axis=0).astype(jnp.bfloat16)
    total = jnp.dot(high_ref[...], rows, preferred_element_type=jnp.float32)
    total += jnp.dot(low_ref[...], rows, preferred_element_type=jnp.float32)
    out_ref[...] = total.astype(jnp.bfloat16)


def estimate(flops, moved):
    return pl.CostEstimate(flops=int(flops), bytes_accessed=int(moved), transcendentals=0)


def local(residual, attn_partial, norm_gain, expert_ids, route_scores, w_gate, w_down):
    bf16, f32 = jnp.bfloat16, jnp.float32
    tokens, share = residual.shape
    nt, ne = lax.axis_size("tensor"), lax.axis_size("expert")
    z, me = lax.axis_index("tensor"), lax.axis_index("expert")
    top = expert_ids.shape[1]
    cap = tokens * top // ne * 5 // 4
    rows = ne * cap
    ff = w_gate.shape[2] // nt
    me_arr = jnp.full((1,), me, jnp.int32)
    z_arr = jnp.full((1,), z, jnp.int32)
    sds = jax.ShapeDtypeStruct
    near, far = [0, 1], list(range(2, ne))

    parts = {}
    for k in partners(nt):
        block = lax.dynamic_slice(attn_partial[0], (0, (z ^ k) * share), (tokens, share))
        parts[k] = exchange(block, "tensor", k) if k else block

    select, high, low = pl.pallas_call(
        functools.partial(routing_kernel, ne, cap),
        out_shape=(sds((rows, tokens), bf16), sds((tokens, rows), bf16), sds((tokens, rows), bf16)),
        in_specs=[scalar(), whole(), whole(), whole()],
        out_specs=(whole(),) * 3,
        compiler_params=params(),
        cost_estimate=estimate(10**6, 2**16),
        name="routing",
    )(me_arr, expert_ids, expert_ids.T, route_scores)

    fetched = (residual, w_gate)
    residual, w_gate = pl.pallas_call(
        fetch_kernel,
        out_shape=tuple(sds(v.shape, v.dtype) for v in fetched),
        in_specs=[anywhere()] * len(fetched),
        out_specs=(whole(),) * len(fetched),
        scratch_shapes=[pltpu.SemaphoreType.DMA((len(fetched),))],
        compiler_params=params(),
        cost_estimate=estimate(10**6, sum(2 * v.size for v in fetched)),
        name="fetch",
    )(*fetched)

    stream, kept, *near_rows = pl.pallas_call(
        functools.partial(add_kernel, nt, cap, near),
        out_shape=(sds((tokens, share), bf16),) * 2 + (sds((cap, share), bf16),) * len(near),
        in_specs=[whole()] * (2 + nt),
        out_specs=(whole(),) * (2 + len(near)),
        compiler_params=params(),
        cost_estimate=estimate(2 * rows * tokens * share, 4 * tokens * share * nt),
        name="add",
    )(residual, select, *[parts[k] for k in range(nt)])
    arrived = {0: near_rows[0], 1: exchange(near_rows[1], "expert", 1)}
    far_rows = pl.pallas_call(
        functools.partial(pack_kernel, cap, far),
        out_shape=(sds((cap, share), bf16),) * len(far),
        in_specs=[whole()] * 2,
        out_specs=(whole(),) * len(far),
        compiler_params=params(),
        cost_estimate=estimate(2 * rows * tokens * share, 4 * tokens * share),
        name="pack",
    )(kept, select)
    for k, value in zip(far, far_rows):
        arrived[k] = exchange(value, "expert", k)

    def summed_gate(ks, after=None):
        count = len(ks) * cap
        lhs, squares = pl.pallas_call(
            functools.partial(prepare_kernel, len(ks)),
            out_shape=(sds((count, share), bf16), sds((8, count), f32)),
            in_specs=[whole()] * (1 + len(ks)),
            out_specs=(whole(),) * 2,
            compiler_params=params(),
            cost_estimate=estimate(16 * count * share, 4 * count * share),
            name="prepare",
        )(norm_gain[None, :], *[arrived[k] for k in ks])
        tall = count + extra_rows(count, ff)
        gates = {}
        for k in partners(nt):
            earlier = [] if after is None else [after[k or 1]]
            partial_gate = pl.pallas_call(
                gate_kernel,
                out_shape=sds((tall, ff), bf16),
                grid_spec=pltpu.PrefetchScalarGridSpec(
                    num_scalar_prefetch=1,
                    grid=(1,),
                    in_specs=[
                        pl.BlockSpec((count, share), lambda i, b: (0, 0)),
                        pl.BlockSpec((8, count), lambda i, b: (0, 0)),
                        pl.BlockSpec((1, share, ff), lambda i, b: (0, 0, b[0])),
                    ]
                    + [anywhere()] * len(earlier),
                    out_specs=pl.BlockSpec((tall, ff), lambda i, b: (0, 0)),
                ),
                compiler_params=params(),
                cost_estimate=estimate(2 * count * share * ff, 2 * share * ff),
                name="gate",
            )(z_arr ^ k, lhs, squares, w_gate, *earlier)
            gates[k] = exchange(partial_gate, "tensor", k) if k else partial_gate
        return gates

    def gathered_hidden(ks, gates, after=()):
        count = len(ks) * cap
        own = pl.pallas_call(
            functools.partial(activate_kernel, nt, count, float(share * nt)),
            out_shape=sds((count, ff), bf16),
            in_specs=[whole()] * nt + [anywhere()] * len(after),
            out_specs=whole(),
            compiler_params=params(),
            cost_estimate=estimate(20 * count * ff, 2 * count * ff * (nt + 1)),
            name="activate",
        )(*[gates[k] for k in range(nt)], *after)
        return {k: exchange(own, "tensor", k) if k else own for k in partners(nt)}

    def produced(ks, hidden):
        outs = pl.pallas_call(
            functools.partial(down_kernel, nt, len(ks), cap),
            out_shape=(sds((cap, share), bf16),) * len(ks),
            in_specs=[scalar(), whole()] + [whole()] * nt,
            out_specs=(whole(),) * len(ks),
            compiler_params=params(),
            cost_estimate=estimate(2 * len(ks) * cap * share * ff * nt, 2 * share * ff * nt),
            name="down",
        )(z_arr, w_down, *[hidden[k] for k in range(nt)])
        return dict(zip(ks, outs))

    near_gates = summed_gate(near)
    far_gates = summed_gate(far, near_gates)
    far_hidden = gathered_hidden(far, far_gates)
    near_hidden = gathered_hidden(near, near_gates, (far_hidden[3],))
    returned = {}
    for ks, hidden in ((far, far_hidden), (near, near_hidden)):
        for k, value in produced(ks, hidden).items():
            returned[k] = exchange(value, "expert", k) if k else value

    moe_out = pl.pallas_call(
        functools.partial(combine_kernel, ne),
        out_shape=sds((tokens, share), bf16),
        in_specs=[whole()] * (2 + ne),
        out_specs=whole(),
        compiler_params=params(),
        cost_estimate=estimate(4 * rows * tokens * share, 2 * rows * share),
        name="combine",
    )(high, low, *[returned[k] for k in range(ne)])
    return stream, moe_out


def solution(mesh):
    return jax.shard_map(
        local,
        mesh=mesh,
        in_specs=(
            P(("groups", "expert"), "tensor"),
            P("tensor", ("groups", "expert"), None),
            P("tensor"),
            P(("groups", "expert"), None),
            P(("groups", "expert"), None),
            P("expert", "tensor", None),
            P("expert", None, "tensor"),
        ),
        out_specs=(P(("groups", "expert"), "tensor"), P(("groups", "expert"), "tensor")),
        check_vma=False,
    )
```

time: 85.7 us -> 71.9 us (0.84)
  waiting for transfers between devices: 51.1 us -> 21.3 us
  starting transfers between devices: 18.9 us -> 32.1 us
  Pallas kernels: 6.16 us -> 10.5 us
  local copies, waits for them, and re-layouts: 8.36 us -> 6.94 us
    ppermute x15 -> x21, waiting for transfers between devices: 51.1 us -> 21.3 us  [exchange(): return lax.ppermute(value, axis, [(i, i ^ step) for i in range(n)])]
    ppermute x15 -> x21, starting transfers between devices: 18.9 us -> 32.1 us  [exchange(): return lax.ppermute(value, axis, [(i, i ^ step) for i in range(n)])]
    pallas_call x8 -> x17, Pallas kernels: 4.64 us -> 9 us  [the longest x8 3.59 us: summed_gate(): pl.pallas_call(gate_kernel, out_shape=sds((tall, ff), bf16), grid_spec=pl...]
    unnamed x16 -> x14, local copies, waits for them, and re-layouts: 6.32 us -> 5.58 us
  transfers between devices with their start and end apart: 15 -> 21, of which waited for: 10 -> 11; matrix products, arithmetic and copies ran while one was open for 3% -> 2% of each run, Pallas kernels for 2% -> 12%
where the time goes in v2:
time: 71.9 us; the launch traced here: 71.7 us
  starting transfers between devices  32.1 us (45%)
  waiting for transfers between devices  21.3 us (30%)
  Pallas kernels  10.5 us (15%)
  local copies, waits for them, and re-layouts  6.94 us (10%)
  between operations  0.84 us (1%)
    ppermute x21, starting transfers between devices, exchange(): return lax.ppermute(value, axis, [(i, i ^ step) for i in range(n)])  32.1 us
    ppermute x21, waiting for transfers between devices, exchange(): return lax.ppermute(value, axis, [(i, i ^ step) for i in range(n)])  21.3 us
    unnamed x14, local copies, waits for them, and re-layouts  5.58 us
    pallas_call x8, Pallas kernels, summed_gate(): pl.pallas_call(gate_kernel, out_shape=sds((tall, ff), bf16), grid_spec=pl...  3.59 us
    pallas_call x2, Pallas kernels, produced(): pl.pallas_call(functools.partial(down_kernel, nt, len(ks), cap), out_shap...  2.77 us
  transfers between devices with their start and end apart: 21, of which 11 were waited for; matrix products, arithmetic and copies ran while one was open for 2% of the time, Pallas kernels for 12%

profile of v2, /device:TPU:0, one launch (start us, length us, event | category | flops | bytes accessed | tf_op | source)
XLA Modules:
  0.0 71.7 jit_solution(9168524515679884229)
XLA Ops:
  0.7 1.4 %dynamic-slice_bitcast_fusion = (bf16[64,1792]{1,0:T(8,128)(2,1)S(1)}, bf16[64,1792]{1,0:T(8,128)(2,1)S(1)}, bf16[64,1792]{1,0:T(8,128)(2,1)S(1)}, bf16[64,1792]{1,0:T(8,128)(2,1)S(1)}) fusion(bf16[1,64,7168]{2,1,0:T(8,128)(2,1)} %param.8, s32[]{:T(128)S(6)} %select_n.15, s32[]{:T(128)S(6)} %select_n.13, s32[]{:T(128)S(6)} %select_n.12, s32[]{:T(128)S(6)} %select_n.14), kind=kLoop, calls=%fused_computation | loop fusion | bytes 1835024 | tf_op jit(solution)/shard_map/dynamic_slice | solution.py:200
  2.0 3.1 %collective-permute-start = (bf16[64,1792]{1,0:T(8,128)(2,1)S(1)}, bf16[64,1792]{1,0:T(8,128)(2,1)S(1)}, u32[]{:S(2)}, u32[]{:S(2)}) collective-permute-start(bf16[64,1792]{1,0:T(8,128)(2,1)S(1)} %get-tuple-element.41), channel_id=1, source_target_pairs={{0,1},{1,0},{2,3},{3,2},{4,5},{5,4},{6,7},{7,6},{8,9},{9,8},{10,11... | collective-permute-start | bytes 688136 | tf_op jit(solution)/shard_map/ppermute | solution.py:17
  5.1 2.6 %collective-permute-start.1 = (bf16[64,1792]{1,0:T(8,128)(2,1)S(1)}, bf16[64,1792]{1,0:T(8,128)(2,1)S(1)}, u32[]{:S(2)}, u32[]{:S(2)}) collective-permute-start(bf16[64,1792]{1,0:T(8,128)(2,1)S(1)} %get-tuple-element.43), channel_id=1, source_target_pairs={{0,2},{1,3},{2,0},{3,1},{4,6},{5,7},{6,4},{7,5},{8,10},{9,11},{10,... | collective-permute-start | bytes 688136 | tf_op jit(solution)/shard_map/ppermute | solution.py:17
  7.7 0.8 %copy.10.scores_ref = f32[64,2]{1,0:T(8,128)S(1)} copy(f32[64,2]{0,1:T(2,128)} %param.11) | data formatting | bytes 1024 | tf_op args[4]
  8.5 0.8 %copy.9.ids_ref = s32[64,2]{1,0:T(8,128)S(1)} copy(s32[64,2]{0,1:T(2,128)} %param.10) | data formatting | bytes 1024 | tf_op args[3]
  9.2 3.1 %copy-done = bf16[1,1792,2048]{2,1,0:T(8,128)(2,1)S(1)} copy-done((bf16[1,1792,2048]{2,1,0:T(8,128)(2,1)S(1)}, bf16[1,1792,2048]{2,1,0:T(8,128)(2,1)}, u32[]{:S(2)}) %copy-start) | copy-done | bytes 7340056
  12.3 0.9 %copy-done.1 = bf16[64,1792]{1,0:T(8,128)(2,1)S(1)} copy-done((bf16[64,1792]{1,0:T(8,128)(2,1)S(1)}, bf16[64,1792]{1,0:T(8,128)(2,1)}, u32[]{:S(2)}) %copy-start.1) | copy-done | bytes 229400
  13.3 0.8 %fetch.1 = (bf16[64,1792]{1,0:T(8,128)(2,1)S(1)}, bf16[1,1792,2048]{2,1,0:T(8,128)(2,1)S(1)}) custom-call(bf16[64,1792]{1,0:T(8,128)(2,1)S(1)} %copy-done.1, bf16[1,1792,2048]{2,1,0:T(8,128)(2,1)S(1)} %copy-done), custom_call_target="tpu_custom_call" | custom-call | flops 1000000 | bytes 7569408 | tf_op jit(solution)/shard_map/fetch/pallas_call | solution.py:214
  14.1 0.5 routing.1
  14.6 0.3 collective-permute-done.refs_1_
  14.9 9.5 %collective-permute-done.1.refs_2_ = bf16[64,1792]{1,0:T(8,128)(2,1)S(1)} collective-permute-done((bf16[64,1792]{1,0:T(8,128)(2,1)S(1)}, bf16[64,1792]{1,0:T(8,128)(2,1)S(1)}, u32[]{:S(2)}, u32[]{:S(2)}) %collective-permute-start.1) | collective-permute-done | bytes 229408 | tf_op jit(solution)/shard_map/ppermute | solution.py:17
  24.4 0.9 %add.17 = (bf16[64,1792]{1,0:T(8,128)(2,1)}, bf16[64,1792]{1,0:T(8,128)(2,1)S(1)}, bf16[40,1792]{1,0:T(8,128)(2,1)S(1)}, bf16[40,1792]{1,0:T(8,128)(2,1)S(1)}) custom-call(bf16[64,1792]{1,0:T(8,128)(2,1)S(1)} %get-tuple-element.21.residual_ref, bf16[160,64]{1,0:T(8,128)(2,1)S(1)} %get-tuple-element.22.select_ref, ...), custom_call_target="tpu_custom_call" | custom-call | flops 36700160 | bytes 1835008 | tf_op jit(solution)/shard_map/add/pallas_call | solution.py:225
  25.3 0.2 pack.1
  25.5 1.6 %collective-permute-start.7 = (bf16[40,1792]{1,0:T(8,128)(2,1)S(1)}, bf16[40,1792]{1,0:T(8,128)(2,1)S(1)}, u32[]{:S(2)}, u32[]{:S(2)}) collective-permute-start(bf16[40,1792]{1,0:T(8,128)(2,1)S(1)} %get-tuple-element.32), channel_id=1, source_target_pairs={{0,8},{4,12},{8,0},{12,4},{1,9},{5,13},{9,1},{13,5},{2,10},{6,14},... | collective-permute-start | bytes 430088 | tf_op jit(solution)/shard_map/ppermute | solution.py:17
  27.0 0.4 collective-permute-start.8
  27.6 0.5 gate.11
  28.1 2.5 %collective-permute-start.6 = (bf16[88,512]{1,0:T(8,128)(2,1)S(1)}, bf16[88,512]{1,0:T(8,128)(2,1)S(1)}, u32[]{:S(2)}, u32[]{:S(2)}) collective-permute-start(bf16[88,512]{1,0:T(8,128)(2,1)S(1)} %gate.11), channel_id=1, source_target_pairs={{0,3},{1,2},{2,1},{3,0},{4,7},{5,6},{6,5},{7,4},{8,11},{9,10},{10,... | collective-permute-start | bytes 270344 | tf_op jit(solution)/shard_map/ppermute | solution.py:17
  30.6 0.4 gate.10
  31.1 3.1 %collective-permute-start.5 = (bf16[88,512]{1,0:T(8,128)(2,1)S(1)}, bf16[88,512]{1,0:T(8,128)(2,1)S(1)}, u32[]{:S(2)}, u32[]{:S(2)}) collective-permute-start(bf16[88,512]{1,0:T(8,128)(2,1)S(1)} %gate.10), channel_id=1, source_target_pairs={{0,2},{1,3},{2,0},{3,1},{4,6},{5,7},{6,4},{7,5},{8,10},{9,11},{10,... | collective-permute-start | bytes 270344 | tf_op jit(solution)/shard_map/ppermute | solution.py:17
  34.2 0.4 gate.9
  35.0 0.5 gate.15
  35.5 2.4 %collective-permute-start.11 = (bf16[88,512]{1,0:T(8,128)(2,1)S(1)}, bf16[88,512]{1,0:T(8,128)(2,1)S(1)}, u32[]{:S(2)}, u32[]{:S(2)}) collective-permute-start(bf16[88,512]{1,0:T(8,128)(2,1)S(1)} %gate.15), channel_id=1, source_target_pairs={{0,3},{1,2},{2,1},{3,0},{4,7},{5,6},{6,5},{7,4},{8,11},{9,10},{10,... | collective-permute-start | bytes 270344 | tf_op jit(solution)/shard_map/ppermute | solution.py:17
  37.9 3.0 %collective-permute-done.5.refs_0_.refs_2_ = bf16[88,512]{1,0:T(8,128)(2,1)S(1)} collective-permute-done((bf16[88,512]{1,0:T(8,128)(2,1)S(1)}, bf16[88,512]{1,0:T(8,128)(2,1)S(1)}, u32[]{:S(2)}, u32[]{:S(2)}) %collective-permute-start.5) | collective-permute-done | bytes 90144 | tf_op jit(solution)/shard_map/ppermute | solution.py:17
  40.9 0.4 gate.14
  41.4 0.2 collective-permute-start.10
  41.6 0.4 gate.13
  42.1 4.9 %collective-permute-start.9 = (bf16[88,512]{1,0:T(8,128)(2,1)S(1)}, bf16[88,512]{1,0:T(8,128)(2,1)S(1)}, u32[]{:S(2)}, u32[]{:S(2)}) collective-permute-start(bf16[88,512]{1,0:T(8,128)(2,1)S(1)} %gate.13), channel_id=1, source_target_pairs={{0,1},{1,0},{2,3},{3,2},{4,5},{5,4},{6,7},{7,6},{8,9},{9,8},{10,11... | collective-permute-start | bytes 270344 | tf_op jit(solution)/shard_map/ppermute | solution.py:17
  47.0 0.4 gate.12.refs_0_
  47.5 0.7 collective-permute-done.10.refs_2_
  48.2 1.4 %collective-permute-done.9.refs_1_ = bf16[88,512]{1,0:T(8,128)(2,1)S(1)} collective-permute-done((bf16[88,512]{1,0:T(8,128)(2,1)S(1)}, bf16[88,512]{1,0:T(8,128)(2,1)S(1)}, u32[]{:S(2)}, u32[]{:S(2)}) %collective-permute-start.9) | collective-permute-done | bytes 90144 | tf_op jit(solution)/shard_map/ppermute | solution.py:17
  49.5 0.2 activate.2.refs_0_
  49.7 2.8 %collective-permute-start.12 = (bf16[80,512]{1,0:T(8,128)(2,1)S(1)}, bf16[80,512]{1,0:T(8,128)(2,1)S(1)}, u32[]{:S(2)}, u32[]{:S(2)}) collective-permute-start(bf16[80,512]{1,0:T(8,128)(2,1)S(1)} %activate.2.refs_0_), channel_id=1, source_target_pairs={{0,3},{1,2},{2,1},{3,0},{4,7},{5,6},{6,5},{7,4},{8,11},{9,10},{10,... | collective-permute-start | bytes 245768 | tf_op jit(solution)/shard_map/ppermute | solution.py:17
  52.5 1.7 %collective-permute-start.18 = (bf16[80,512]{1,0:T(8,128)(2,1)S(1)}, bf16[80,512]{1,0:T(8,128)(2,1)S(1)}, u32[]{:S(2)}, u32[]{:S(2)}) collective-permute-start(bf16[80,512]{1,0:T(8,128)(2,1)S(1)} %activate.2.refs_0_), channel_id=1, source_target_pairs={{0,2},{1,3},{2,0},{3,1},{4,6},{5,7},{6,4},{7,5},{8,10},{9,11},{10,... | collective-permute-start | bytes 245768 | tf_op jit(solution)/shard_map/ppermute | solution.py:17
  54.2 0.4 gate.8.refs_0_
  54.6 1.5 %collective-permute-done.12.refs_4_.refs_3_ = bf16[80,512]{1,0:T(8,128)(2,1)S(1)} collective-permute-done((bf16[80,512]{1,0:T(8,128)(2,1)S(1)}, bf16[80,512]{1,0:T(8,128)(2,1)S(1)}, u32[]{:S(2)}, u32[]{:S(2)}) %collective-permute-start.12) | collective-permute-done | bytes 81952 | tf_op jit(solution)/shard_map/ppermute | solution.py:17
  56.1 0.2 activate.3.refs_0_
  56.4 2.5 %collective-permute-start.13 = (bf16[80,512]{1,0:T(8,128)(2,1)S(1)}, bf16[80,512]{1,0:T(8,128)(2,1)S(1)}, u32[]{:S(2)}, u32[]{:S(2)}) collective-permute-start(bf16[80,512]{1,0:T(8,128)(2,1)S(1)} %activate.3.refs_0_), channel_id=1, source_target_pairs={{0,1},{1,0},{2,3},{3,2},{4,5},{5,4},{6,7},{7,6},{8,9},{9,8},{10,11... | collective-permute-start | bytes 245768 | tf_op jit(solution)/shard_map/ppermute | solution.py:17
  58.9 1.8 %collective-permute-start.14 = (bf16[80,512]{1,0:T(8,128)(2,1)S(1)}, bf16[80,512]{1,0:T(8,128)(2,1)S(1)}, u32[]{:S(2)}, u32[]{:S(2)}) collective-permute-start(bf16[80,512]{1,0:T(8,128)(2,1)S(1)} %activate.3.refs_0_), channel_id=1, source_target_pairs={{0,2},{1,3},{2,0},{3,1},{4,6},{5,7},{6,4},{7,5},{8,10},{9,11},{10,... | collective-permute-start | bytes 245768 | tf_op jit(solution)/shard_map/ppermute | solution.py:17
  60.7 0.7 collective-permute-start.15
  61.3 0.3 collective-permute-done.18.refs_2_
  61.7 1.4 %down.3 = (bf16[40,1792]{1,0:T(8,128)(2,1)S(1)}, bf16[40,1792]{1,0:T(8,128)(2,1)S(1)}) custom-call(s32[1]{0:T(128)} %bitcast.6.block_ref, bf16[1,2048,1792]{2,1,0:T(8,128)(2,1)S(1)} %bitcast.12, bf16[80,512]{1,0:T(8,128)(2,1)S(1)} %activate.2.refs_0_, bf16[80,512]{1,0:T(8,128)(2,1)S(1)} %collective-permute-done.17.refs_1_, ...), custom_call_target="tpu_custom_call" | custom-call | flops 587202560 | bytes 7340032 | tf_op jit(solution)/shard_map/down/pallas_call | solution.py:297
  63.0 1.6 %collective-permute-start.19 = (bf16[40,1792]{1,0:T(8,128)(2,1)S(1)}, bf16[40,1792]{1,0:T(8,128)(2,1)S(1)}, u32[]{:S(2)}, u32[]{:S(2)}) collective-permute-start(bf16[40,1792]{1,0:T(8,128)(2,1)S(1)} %get-tuple-element.38), channel_id=1, source_target_pairs={{0,8},{4,12},{8,0},{12,4},{1,9},{5,13},{9,1},{13,5},{2,10},{6,14},... | collective-permute-start | bytes 430088 | tf_op jit(solution)/shard_map/ppermute | solution.py:17
  64.6 0.8 %collective-permute-done.14.refs_2_ = bf16[80,512]{1,0:T(8,128)(2,1)S(1)} collective-permute-done((bf16[80,512]{1,0:T(8,128)(2,1)S(1)}, bf16[80,512]{1,0:T(8,128)(2,1)S(1)}, u32[]{:S(2)}, u32[]{:S(2)}) %collective-permute-start.14) | collective-permute-done | bytes 81952 | tf_op jit(solution)/shard_map/ppermute | solution.py:17
  65.4 1.6 %collective-permute-done.15.refs_3_ = bf16[80,512]{1,0:T(8,128)(2,1)S(1)} collective-permute-done((bf16[80,512]{1,0:T(8,128)(2,1)S(1)}, bf16[80,512]{1,0:T(8,128)(2,1)S(1)}, u32[]{:S(2)}, u32[]{:S(2)}) %collective-permute-start.15) | collective-permute-done | bytes 81952 | tf_op jit(solution)/shard_map/ppermute | solution.py:17
  67.0 1.4 %down.2 = (bf16[40,1792]{1,0:T(8,128)(2,1)S(1)}, bf16[40,1792]{1,0:T(8,128)(2,1)S(1)}) custom-call(s32[1]{0:T(128)} %bitcast.6.block_ref, bf16[1,2048,1792]{2,1,0:T(8,128)(2,1)S(1)} %bitcast.12, bf16[80,512]{1,0:T(8,128)(2,1)S(1)} %activate.3.refs_0_, bf16[80,512]{1,0:T(8,128)(2,1)S(1)} %collective-permute-done.13.refs_1_, ...), custom_call_target="tpu_custom_call" | custom-call | flops 587202560 | bytes 7340032 | tf_op jit(solution)/shard_map/down/pallas_call | solution.py:297
  68.5 0.3 collective-permute-done.19.refs_2_
  68.8 1.9 %collective-permute-done.20.refs_3_ = bf16[40,1792]{1,0:T(8,128)(2,1)S(1)} collective-permute-done((bf16[40,1792]{1,0:T(8,128)(2,1)S(1)}, bf16[40,1792]{1,0:T(8,128)(2,1)S(1)}, u32[]{:S(2)}, u32[]{:S(2)}) %collective-permute-start.20) | collective-permute-done | bytes 143392 | tf_op jit(solution)/shard_map/ppermute | solution.py:17
  70.7 1.0 %combine.1 = bf16[64,1792]{1,0:T(8,128)(2,1)} custom-call(bf16[64,160]{1,0:T(8,128)(2,1)S(1)} %get-tuple-element.24.high_ref, bf16[64,160]{1,0:T(8,128)(2,1)S(1)} %get-tuple-element.25.low_ref, bf16[40,1792]{1,0:T(8,128)(2,1)S(1)} %get-tuple-element.36.refs_0_, bf16[40,1792]{1,0:T(8,128)(2,1)S(1)} %collective-permute-done.16.refs_1_, ...), custom_call_target="tpu_custom_call" | custom-call | flops 73400320 | bytes 573440 | tf_op jit(solution)/shard_map/combine/pallas_call | solution.py:317
  (30 shorter events, 0.7 us)
Async XLA Ops:
  0.6 13.4 %copy-start.2 = (s32[64,2]{0,1:T(2,128)S(1)}, s32[64,2]{0,1:T(2,128)}, u32[]{:S(2)}) copy-start(s32[64,2]{0,1:T(2,128)} %param.10) | copy-start | bytes 1540
  0.6 26.8 %copy-start.3 = (bf16[1792]{0:T(1024)(128)(2,1)S(1)}, bf16[1792]{0:T(1024)(128)(2,1)}, u32[]{:S(2)}) copy-start(bf16[1792]{0:T(1024)(128)(2,1)} %param.9) | copy-start | bytes 10756
  2.0 12.8 %collective-permute-start = (bf16[64,1792]{1,0:T(8,128)(2,1)S(1)}, bf16[64,1792]{1,0:T(8,128)(2,1)S(1)}, u32[]{:S(2)}, u32[]{:S(2)}) collective-permute-start(bf16[64,1792]{1,0:T(8,128)(2,1)S(1)} %get-tuple-element.41), channel_id=1, source_target_pairs={{0,1},{1,0},{2,3},{3,2},{4,5},{5,4},{6,7},{7,6},{8,9},{9,8},{10,11... | collective-permute-start | bytes 688136 | tf_op jit(solution)/shard_map/ppermute | solution.py:17
  5.1 19.3 %collective-permute-start.1 = (bf16[64,1792]{1,0:T(8,128)(2,1)S(1)}, bf16[64,1792]{1,0:T(8,128)(2,1)S(1)}, u32[]{:S(2)}, u32[]{:S(2)}) collective-permute-start(bf16[64,1792]{1,0:T(8,128)(2,1)S(1)} %get-tuple-element.43), channel_id=1, source_target_pairs={{0,2},{1,3},{2,0},{3,1},{4,6},{5,7},{6,4},{7,5},{8,10},{9,11},{10,... | collective-permute-start | bytes 688136 | tf_op jit(solution)/shard_map/ppermute | solution.py:17
  7.7 16.7 %collective-permute-start.2 = (bf16[64,1792]{1,0:T(8,128)(2,1)S(1)}, bf16[64,1792]{1,0:T(8,128)(2,1)S(1)}, u32[]{:S(2)}, u32[]{:S(2)}) collective-permute-start(bf16[64,1792]{1,0:T(8,128)(2,1)S(1)} %get-tuple-element.40), channel_id=1, source_target_pairs={{0,3},{1,2},{2,1},{3,0},{4,7},{5,6},{6,5},{7,4},{8,11},{9,10},{10,... | collective-permute-start | bytes 688136 | tf_op jit(solution)/shard_map/ppermute | solution.py:17
  9.2 3.1 %copy-start = (bf16[1,1792,2048]{2,1,0:T(8,128)(2,1)S(1)}, bf16[1,1792,2048]{2,1,0:T(8,128)(2,1)}, u32[]{:S(2)}) copy-start(bf16[1,1792,2048]{2,1,0:T(8,128)(2,1)} %refs_1_.1) | copy-start | bytes 22020100
  12.3 0.9 %copy-start.1 = (bf16[64,1792]{1,0:T(8,128)(2,1)S(1)}, bf16[64,1792]{1,0:T(8,128)(2,1)}, u32[]{:S(2)}) copy-start(bf16[64,1792]{1,0:T(8,128)(2,1)} %refs_0_.1) | copy-start | bytes 688132
  25.3 2.2 %collective-permute-start.3 = (bf16[40,1792]{1,0:T(8,128)(2,1)S(1)}, bf16[40,1792]{1,0:T(8,128)(2,1)S(1)}, u32[]{:S(2)}, u32[]{:S(2)}) collective-permute-start(bf16[40,1792]{1,0:T(8,128)(2,1)S(1)} %get-tuple-element.27), channel_id=1, source_target_pairs={{0,4},{4,0},{8,12},{12,8},{1,5},{5,1},{9,13},{13,9},{2,6},{6,2},{1... | collective-permute-start | bytes 430088 | tf_op jit(solution)/shard_map/ppermute | solution.py:17
  25.5 9.4 %collective-permute-start.7 = (bf16[40,1792]{1,0:T(8,128)(2,1)S(1)}, bf16[40,1792]{1,0:T(8,128)(2,1)S(1)}, u32[]{:S(2)}, u32[]{:S(2)}) collective-permute-start(bf16[40,1792]{1,0:T(8,128)(2,1)S(1)} %get-tuple-element.32), channel_id=1, source_target_pairs={{0,8},{4,12},{8,0},{12,4},{1,9},{5,13},{9,1},{13,5},{2,10},{6,14},... | collective-permute-start | bytes 430088 | tf_op jit(solution)/shard_map/ppermute | solution.py:17
  27.0 7.8 %collective-permute-start.8 = (bf16[40,1792]{1,0:T(8,128)(2,1)S(1)}, bf16[40,1792]{1,0:T(8,128)(2,1)S(1)}, u32[]{:S(2)}, u32[]{:S(2)}) collective-permute-start(bf16[40,1792]{1,0:T(8,128)(2,1)S(1)} %get-tuple-element.33), channel_id=1, source_target_pairs={{0,12},{4,8},{8,4},{12,0},{1,13},{5,9},{9,5},{13,1},{2,14},{6,10},... | collective-permute-start | bytes 430088 | tf_op jit(solution)/shard_map/ppermute | solution.py:17
  28.1 6.9 %collective-permute-start.6 = (bf16[88,512]{1,0:T(8,128)(2,1)S(1)}, bf16[88,512]{1,0:T(8,128)(2,1)S(1)}, u32[]{:S(2)}, u32[]{:S(2)}) collective-permute-start(bf16[88,512]{1,0:T(8,128)(2,1)S(1)} %gate.11), channel_id=1, source_target_pairs={{0,3},{1,2},{2,1},{3,0},{4,7},{5,6},{6,5},{7,4},{8,11},{9,10},{10,... | collective-permute-start | bytes 270344 | tf_op jit(solution)/shard_map/ppermute | solution.py:17
  31.1 9.9 %collective-permute-start.5 = (bf16[88,512]{1,0:T(8,128)(2,1)S(1)}, bf16[88,512]{1,0:T(8,128)(2,1)S(1)}, u32[]{:S(2)}, u32[]{:S(2)}) collective-permute-start(bf16[88,512]{1,0:T(8,128)(2,1)S(1)} %gate.10), channel_id=1, source_target_pairs={{0,2},{1,3},{2,0},{3,1},{4,6},{5,7},{6,4},{7,5},{8,10},{9,11},{10,... | collective-permute-start | bytes 270344 | tf_op jit(solution)/shard_map/ppermute | solution.py:17
  34.6 7.0 %collective-permute-start.4 = (bf16[88,512]{1,0:T(8,128)(2,1)S(1)}, bf16[88,512]{1,0:T(8,128)(2,1)S(1)}, u32[]{:S(2)}, u32[]{:S(2)}) collective-permute-start(bf16[88,512]{1,0:T(8,128)(2,1)S(1)} %gate.9), channel_id=1, source_target_pairs={{0,1},{1,0},{2,3},{3,2},{4,5},{5,4},{6,7},{7,6},{8,9},{9,8},{10,11... | collective-permute-start | bytes 270344 | tf_op jit(solution)/shard_map/ppermute | solution.py:17
  35.5 12.0 %collective-permute-start.11 = (bf16[88,512]{1,0:T(8,128)(2,1)S(1)}, bf16[88,512]{1,0:T(8,128)(2,1)S(1)}, u32[]{:S(2)}, u32[]{:S(2)}) collective-permute-start(bf16[88,512]{1,0:T(8,128)(2,1)S(1)} %gate.15), channel_id=1, source_target_pairs={{0,3},{1,2},{2,1},{3,0},{4,7},{5,6},{6,5},{7,4},{8,11},{9,10},{10,... | collective-permute-start | bytes 270344 | tf_op jit(solution)/shard_map/ppermute | solution.py:17
  41.4 6.8 %collective-permute-start.10 = (bf16[88,512]{1,0:T(8,128)(2,1)S(1)}, bf16[88,512]{1,0:T(8,128)(2,1)S(1)}, u32[]{:S(2)}, u32[]{:S(2)}) collective-permute-start(bf16[88,512]{1,0:T(8,128)(2,1)S(1)} %gate.14), channel_id=1, source_target_pairs={{0,2},{1,3},{2,0},{3,1},{4,6},{5,7},{6,4},{7,5},{8,10},{9,11},{10,... | collective-permute-start | bytes 270344 | tf_op jit(solution)/shard_map/ppermute | solution.py:17
  42.1 19.6 %slice-start = ((s8[7340032]{0:T(1024)(128)(4,1)}), s8[4194304]{0:T(1024)(128)(4,1)S(1)}, s32[]{:S(2)}) async-start(s8[7340032]{0:T(1024)(128)(4,1)} %bitcast.11), calls=%async_computation | async-start | bytes 8388608
  42.1 7.4 %collective-permute-start.9 = (bf16[88,512]{1,0:T(8,128)(2,1)S(1)}, bf16[88,512]{1,0:T(8,128)(2,1)S(1)}, u32[]{:S(2)}, u32[]{:S(2)}) collective-permute-start(bf16[88,512]{1,0:T(8,128)(2,1)S(1)} %gate.13), channel_id=1, source_target_pairs={{0,1},{1,0},{2,3},{3,2},{4,5},{5,4},{6,7},{7,6},{8,9},{9,8},{10,11... | collective-permute-start | bytes 270344 | tf_op jit(solution)/shard_map/ppermute | solution.py:17
  47.5 14.2 %slice-start.1 = ((s8[7340032]{0:T(1024)(128)(4,1)}), s8[3145728]{0:T(1024)(128)(4,1)S(1)}, s32[]{:S(2)}) async-start(s8[7340032]{0:T(1024)(128)(4,1)} %bitcast.11), calls=%async_computation.1 | async-start | bytes 6291456
  49.7 6.4 %collective-permute-start.12 = (bf16[80,512]{1,0:T(8,128)(2,1)S(1)}, bf16[80,512]{1,0:T(8,128)(2,1)S(1)}, u32[]{:S(2)}, u32[]{:S(2)}) collective-permute-start(bf16[80,512]{1,0:T(8,128)(2,1)S(1)} %activate.2.refs_0_), channel_id=1, source_target_pairs={{0,3},{1,2},{2,1},{3,0},{4,7},{5,6},{6,5},{7,4},{8,11},{9,10},{10,... | collective-permute-start | bytes 245768 | tf_op jit(solution)/shard_map/ppermute | solution.py:17
  52.5 8.8 %collective-permute-start.17 = (bf16[80,512]{1,0:T(8,128)(2,1)S(1)}, bf16[80,512]{1,0:T(8,128)(2,1)S(1)}, u32[]{:S(2)}, u32[]{:S(2)}) collective-permute-start(bf16[80,512]{1,0:T(8,128)(2,1)S(1)} %activate.2.refs_0_), channel_id=1, source_target_pairs={{0,1},{1,0},{2,3},{3,2},{4,5},{5,4},{6,7},{7,6},{8,9},{9,8},{10,11... | collective-permute-start | bytes 245768 | tf_op jit(solution)/shard_map/ppermute | solution.py:17
  52.5 9.1 %collective-permute-start.18 = (bf16[80,512]{1,0:T(8,128)(2,1)S(1)}, bf16[80,512]{1,0:T(8,128)(2,1)S(1)}, u32[]{:S(2)}, u32[]{:S(2)}) collective-permute-start(bf16[80,512]{1,0:T(8,128)(2,1)S(1)} %activate.2.refs_0_), channel_id=1, source_target_pairs={{0,2},{1,3},{2,0},{3,1},{4,6},{5,7},{6,4},{7,5},{8,10},{9,11},{10,... | collective-permute-start | bytes 245768 | tf_op jit(solution)/shard_map/ppermute | solution.py:17
  56.4 8.3 %collective-permute-start.13 = (bf16[80,512]{1,0:T(8,128)(2,1)S(1)}, bf16[80,512]{1,0:T(8,128)(2,1)S(1)}, u32[]{:S(2)}, u32[]{:S(2)}) collective-permute-start(bf16[80,512]{1,0:T(8,128)(2,1)S(1)} %activate.3.refs_0_), channel_id=1, source_target_pairs={{0,1},{1,0},{2,3},{3,2},{4,5},{5,4},{6,7},{7,6},{8,9},{9,8},{10,11... | collective-permute-start | bytes 245768 | tf_op jit(solution)/shard_map/ppermute | solution.py:17
  58.9 6.5 %collective-permute-start.14 = (bf16[80,512]{1,0:T(8,128)(2,1)S(1)}, bf16[80,512]{1,0:T(8,128)(2,1)S(1)}, u32[]{:S(2)}, u32[]{:S(2)}) collective-permute-start(bf16[80,512]{1,0:T(8,128)(2,1)S(1)} %activate.3.refs_0_), channel_id=1, source_target_pairs={{0,2},{1,3},{2,0},{3,1},{4,6},{5,7},{6,4},{7,5},{8,10},{9,11},{10,... | collective-permute-start | bytes 245768 | tf_op jit(solution)/shard_map/ppermute | solution.py:17
  60.7 6.3 %collective-permute-start.15 = (bf16[80,512]{1,0:T(8,128)(2,1)S(1)}, bf16[80,512]{1,0:T(8,128)(2,1)S(1)}, u32[]{:S(2)}, u32[]{:S(2)}) collective-permute-start(bf16[80,512]{1,0:T(8,128)(2,1)S(1)} %activate.3.refs_0_), channel_id=1, source_target_pairs={{0,3},{1,2},{2,1},{3,0},{4,7},{5,6},{6,5},{7,4},{8,11},{9,10},{10,... | collective-permute-start | bytes 245768 | tf_op jit(solution)/shard_map/ppermute | solution.py:17
  63.0 5.8 %collective-permute-start.19 = (bf16[40,1792]{1,0:T(8,128)(2,1)S(1)}, bf16[40,1792]{1,0:T(8,128)(2,1)S(1)}, u32[]{:S(2)}, u32[]{:S(2)}) collective-permute-start(bf16[40,1792]{1,0:T(8,128)(2,1)S(1)} %get-tuple-element.38), channel_id=1, source_target_pairs={{0,8},{4,12},{8,0},{12,4},{1,9},{5,13},{9,1},{13,5},{2,10},{6,14},... | collective-permute-start | bytes 430088 | tf_op jit(solution)/shard_map/ppermute | solution.py:17
  64.6 6.0 %collective-permute-start.20 = (bf16[40,1792]{1,0:T(8,128)(2,1)S(1)}, bf16[40,1792]{1,0:T(8,128)(2,1)S(1)}, u32[]{:S(2)}, u32[]{:S(2)}) collective-permute-start(bf16[40,1792]{1,0:T(8,128)(2,1)S(1)} %get-tuple-element.39), channel_id=1, source_target_pairs={{0,12},{4,8},{8,4},{12,0},{1,13},{5,9},{9,5},{13,1},{2,14},{6,10},... | collective-permute-start | bytes 430088 | tf_op jit(solution)/shard_map/ppermute | solution.py:17
  68.4 2.3 %collective-permute-start.16 = (bf16[40,1792]{1,0:T(8,128)(2,1)S(1)}, bf16[40,1792]{1,0:T(8,128)(2,1)S(1)}, u32[]{:S(2)}, u32[]{:S(2)}) collective-permute-start(bf16[40,1792]{1,0:T(8,128)(2,1)S(1)} %get-tuple-element.37), channel_id=1, source_target_pairs={{0,4},{4,0},{8,12},{12,8},{1,5},{5,1},{9,13},{13,9},{2,6},{6,2},{1... | collective-permute-start | bytes 430088 | tf_op jit(solution)/shard_map/ppermute | solution.py:17

commit v3 on v2

--- a/solution.py
+++ b/solution.py
@@ -82,11 +82,23 @@
         copy.wait()
 
 
-def add_kernel(n_tensor, cap, ks, residual_ref, select_ref, *refs):
+def merge_kernel(end_ref, own_ref, passing_ref, relayed_ref, out_ref):
+    @pl.when(end_ref[0] == 1)
+    def _():
+        out_ref[...] = own_ref[...]
+
+    @pl.when(end_ref[0] == 0)
+    def _():
+        total = passing_ref[...].astype(jnp.float32) + relayed_ref[...].astype(jnp.float32)
+        out_ref[...] = total.astype(jnp.bfloat16)
+
+
+def add_kernel(n_tensor, cap, ks, last_ref, residual_ref, select_ref, *refs):
     parts, stream_ref, kept_ref, outs = refs[:n_tensor], *refs[n_tensor : n_tensor + 2], refs[n_tensor + 2 :]
     total = residual_ref[...].astype(jnp.float32)
-    for part in parts:
+    for part in parts[:-1]:
         total += part[...].astype(jnp.float32)
+    total += jnp.where(last_ref[0] == 1, parts[-1][...].astype(jnp.float32), 0.0)
     stream_ref[...] = total.astype(jnp.bfloat16)
     kept_ref[...] = total.astype(jnp.bfloat16)
     pack_kernel(cap, ks, kept_ref, select_ref, *outs)
@@ -161,9 +173,9 @@
     pieces, outs = refs[:n_tensor], refs[n_tensor:]
     width = pieces[0].shape[1]
     total = None
-    for k in range(n_tensor):
+    for i, k in enumerate(partners(n_tensor)):
         start = pl.multiple_of((block_ref[0] ^ k) * width, width)
-        term = jnp.dot(pieces[k][...], w_ref[0, pl.ds(start, width), :], preferred_element_type=jnp.float32)
+        term = jnp.dot(pieces[i][...], w_ref[0, pl.ds(start, width), :], preferred_element_type=jnp.float32)
         total = term if total is None else total + term
     for k in range(n):
         outs[k][...] = total[k * cap : (k + 1) * cap, :].astype(jnp.bfloat16)
@@ -195,10 +207,30 @@
     sds = jax.ShapeDtypeStruct
     near, far = [0, 1], list(range(2, ne))
 
-    parts = {}
-    for k in partners(nt):
-        block = lax.dynamic_slice(attn_partial[0], (0, (z ^ k) * share), (tokens, share))
-        parts[k] = exchange(block, "tensor", k) if k else block
+    def block(k):
+        return lax.dynamic_slice(attn_partial[0], (0, k * share), (tokens, share))
+
+    if nt == 4:
+        end = (z == 0) | (z == 3)
+        end_arr = jnp.where(end, 1, 0).astype(jnp.int32).reshape(1)
+        relayed = exchange(block(jnp.where(end, z ^ 3, z ^ 1)), "tensor", 1)
+        parts = [block(z)]
+        parts.append(lax.ppermute(block(z ^ 3), "tensor", [(1, 2), (2, 1)]))
+        parts.append(lax.ppermute(block(z ^ 2), "tensor", [(0, 2), (3, 1)]))
+        merged = pl.pallas_call(
+            merge_kernel,
+            out_shape=sds((tokens, share), bf16),
+            in_specs=[scalar()] + [whole()] * 3,
+            out_specs=whole(),
+            compiler_params=params(),
+            cost_estimate=estimate(2 * tokens * share, 8 * tokens * share),
+            name="merge",
+        )(end_arr, block(z ^ 1), block(z ^ 2), relayed)
+        parts.append(lax.ppermute(merged, "tensor", [(0, 1), (1, 3), (2, 0), (3, 2)]))
+        parts.append(relayed)
+    else:
+        end_arr = jnp.ones((1,), jnp.int32)
+        parts = [exchange(block(z ^ k), "tensor", k) if k else block(z) for k in partners(nt)]
 
     select, high, low = pl.pallas_call(
         functools.partial(routing_kernel, ne, cap),
@@ -223,14 +255,14 @@
     )(*fetched)
 
     stream, kept, *near_rows = pl.pallas_call(
-        functools.partial(add_kernel, nt, cap, near),
+        functools.partial(add_kernel, len(parts), cap, near),
         out_shape=(sds((tokens, share), bf16),) * 2 + (sds((cap, share), bf16),) * len(near),
-        in_specs=[whole()] * (2 + nt),
+        in_specs=[scalar()] + [whole()] * (2 + len(parts)),
         out_specs=(whole(),) * (2 + len(near)),
         compiler_params=params(),
         cost_estimate=estimate(2 * rows * tokens * share, 4 * tokens * share * nt),
         name="add",
-    )(residual, select, *[parts[k] for k in range(nt)])
+    )(end_arr, residual, select, *parts)
     arrived = {0: near_rows[0], 1: exchange(near_rows[1], "expert", 1)}
     far_rows = pl.pallas_call(
         functools.partial(pack_kernel, cap, far),
@@ -302,7 +334,7 @@
             compiler_params=params(),
             cost_estimate=estimate(2 * len(ks) * cap * share * ff * nt, 2 * share * ff * nt),
             name="down",
-        )(z_arr, w_down, *[hidden[k] for k in range(nt)])
+        )(z_arr, w_down, *[hidden[k] for k in partners(nt)])
         return dict(zip(ks, outs))
 
     near_gates = summed_gate(near)

time: 71.9 us -> 69.9 us (0.972)
  waiting for transfers between devices: 21.3 us -> 17.5 us
  starting transfers between devices: 32.1 us -> 33.4 us
    ppermute x21 -> x19, waiting for transfers between devices: 21.3 us -> 12.2 us  [exchange(): return lax.ppermute(value, axis, [(i, i ^ step) for i in range(n)])]
    ppermute x0 -> x3, starting transfers between devices: none -> 7.39 us  [the longest x1 5.75 us: local(): parts.append(lax.ppermute(block(z ^ 2), 'tensor', [(0, 2), (3, 1)]))]
    ppermute x21 -> x19, starting transfers between devices: 32.1 us -> 26 us  [exchange(): return lax.ppermute(value, axis, [(i, i ^ step) for i in range(n)])]
    ppermute x0 -> x3, waiting for transfers between devices: none -> 5.29 us  [the longest x1 5.28 us: local(): lax.ppermute(merged, 'tensor', [(0, 1), (1, 3), (2, 0), (3, 2)])]
  transfers between devices with their start and end apart: 21 -> 22, of which waited for: 11 -> 10; matrix products, arithmetic and copies ran while one was open for 2% -> 2% of each run, Pallas kernels for 12% -> 12%
where the time goes in v3:
time: 69.9 us; the launch traced here: 69.5 us
  starting transfers between devices  33.4 us (48%)
  waiting for transfers between devices  17.5 us (25%)
  Pallas kernels  10.6 us (15%)
  local copies, waits for them, and re-layouts  7.03 us (10%)
  between operations  0.91 us (1%)
    ppermute x19, starting transfers between devices, exchange(): return lax.ppermute(value, axis, [(i, i ^ step) for i in range(n)])  26 us
    ppermute x19, waiting for transfers between devices, exchange(): return lax.ppermute(value, axis, [(i, i ^ step) for i in range(n)])  12.2 us
    ppermute x1, starting transfers between devices, local(): parts.append(lax.ppermute(block(z ^ 2), 'tensor', [(0, 2), (3, 1)]))  5.75 us
    unnamed x14, local copies, waits for them, and re-layouts  5.58 us
    ppermute x1, waiting for transfers between devices, local(): lax.ppermute(merged, 'tensor', [(0, 1), (1, 3), (2, 0), (3, 2)])  5.28 us
    pallas_call x8, Pallas kernels, summed_gate(): pl.pallas_call(gate_kernel, out_shape=sds((tall, ff), bf16), grid_spec=pl...  3.59 us
    pallas_call x2, Pallas kernels, produced(): pl.pallas_call(functools.partial(down_kernel, nt, len(ks), cap), out_shap...  2.77 us
    dynamic_slice x1, local copies, waits for them, and re-layouts, block(): return lax.dynamic_slice(attn_partial[0], (0, k * share), (tokens, share))  1.44 us
  transfers between devices with their start and end apart: 22, of which 10 were waited for; matrix products, arithmetic and copies ran while one was open for 2% of the time, Pallas kernels for 12%

profile of v3, /device:TPU:0, one launch (start us, length us, event | category | flops | bytes accessed | tf_op | source)
XLA Modules:
  0.0 69.5 jit_solution(6786390247267095817)
XLA Ops:
  0.7 1.4 %dynamic-slice_bitcast_fusion = (bf16[64,1792]{1,0:T(8,128)(2,1)S(1)}, bf16[64,1792]{1,0:T(8,128)(2,1)S(1)}, bf16[64,1792]{1,0:T(8,128)(2,1)S(1)}, bf16[64,1792]{1,0:T(8,128)(2,1)S(1)}, bf16[64,1792]{1,0:T(8,128)(2,1)S(1)}) fusion(bf16[1,64,7168]{2,1,0:T(8,128)(2,1)} %param.8, s32[]{:T(128)S(6)} %select_n.30, s32[]{:T(128)S(6)} %select_n.27, s32[]{:T(128)S(6)} %select_n.26, ...), kind=kLoop, calls=%fused_computation | loop fusion | bytes 2293780 | tf_op jit(solution)/shard_map/dynamic_slice | solution.py:211
  2.1 3.1 %collective-permute-start.2 = (bf16[64,1792]{1,0:T(8,128)(2,1)S(1)}, bf16[64,1792]{1,0:T(8,128)(2,1)S(1)}, u32[]{:S(2)}, u32[]{:S(2)}) collective-permute-start(bf16[64,1792]{1,0:T(8,128)(2,1)S(1)} %get-tuple-element.40), channel_id=1, source_target_pairs={{0,1},{1,0},{2,3},{3,2},{4,5},{5,4},{6,7},{7,6},{8,9},{9,8},{10,11... | collective-permute-start | bytes 688136 | tf_op jit(solution)/shard_map/ppermute | solution.py:17
  5.2 0.7 collective-permute-start
  5.9 5.8 %collective-permute-start.1 = (bf16[64,1792]{1,0:T(8,128)(2,1)S(1)}, bf16[64,1792]{1,0:T(8,128)(2,1)S(1)}, u32[]{:S(2)}, u32[]{:S(2)}) collective-permute-start(bf16[64,1792]{1,0:T(8,128)(2,1)S(1)} %get-tuple-element.41.passing_ref), channel_id=1, source_target_pairs={{0,2},{3,1},{4,6},{7,5},{8,10},{11,9},{12,14},{15,13},{16,18},{19,... | collective-permute-start | bytes 688136 | tf_op jit(solution)/shard_map/ppermute | solution.py:219
  11.7 1.0 %collective-permute-start.3 = (bf16[64,1792]{1,0:T(8,128)(2,1)S(1)}, bf16[64,1792]{1,0:T(8,128)(2,1)S(1)}, u32[]{:S(2)}, u32[]{:S(2)}) collective-permute-start(bf16[64,1792]{1,0:T(8,128)(2,1)S(1)} %merge.1), channel_id=1, source_target_pairs={{0,1},{1,3},{2,0},{3,2},{4,5},{5,7},{6,4},{7,6},{8,9},{9,11},{10,8... | collective-permute-start | bytes 688136 | tf_op jit(solution)/shard_map/ppermute | solution.py:229
  12.7 0.8 %copy.10.scores_ref = f32[64,2]{1,0:T(8,128)S(1)} copy(f32[64,2]{0,1:T(2,128)} %param.11) | data formatting | bytes 1024 | tf_op args[4]
  13.4 0.8 %copy.9.ids_ref = s32[64,2]{1,0:T(8,128)S(1)} copy(s32[64,2]{0,1:T(2,128)} %param.10) | data formatting | bytes 1024 | tf_op args[3]
  14.2 3.1 %copy-done = bf16[1,1792,2048]{2,1,0:T(8,128)(2,1)S(1)} copy-done((bf16[1,1792,2048]{2,1,0:T(8,128)(2,1)S(1)}, bf16[1,1792,2048]{2,1,0:T(8,128)(2,1)}, u32[]{:S(2)}) %copy-start) | copy-done | bytes 7340056
  17.3 0.9 %copy-done.1 = bf16[64,1792]{1,0:T(8,128)(2,1)S(1)} copy-done((bf16[64,1792]{1,0:T(8,128)(2,1)S(1)}, bf16[64,1792]{1,0:T(8,128)(2,1)}, u32[]{:S(2)}) %copy-start.1) | copy-done | bytes 229400
  18.2 0.8 %fetch.1 = (bf16[64,1792]{1,0:T(8,128)(2,1)S(1)}, bf16[1,1792,2048]{2,1,0:T(8,128)(2,1)S(1)}) custom-call(bf16[64,1792]{1,0:T(8,128)(2,1)S(1)} %copy-done.1, bf16[1,1792,2048]{2,1,0:T(8,128)(2,1)S(1)} %copy-done), custom_call_target="tpu_custom_call" | custom-call | flops 1000000 | bytes 7569408 | tf_op jit(solution)/shard_map/fetch/pallas_call | solution.py:246
  19.0 0.5 routing.1
  19.6 5.3 %collective-permute-done.3.refs_3_ = bf16[64,1792]{1,0:T(8,128)(2,1)S(1)} collective-permute-done((bf16[64,1792]{1,0:T(8,128)(2,1)S(1)}, bf16[64,1792]{1,0:T(8,128)(2,1)S(1)}, u32[]{:S(2)}, u32[]{:S(2)}) %collective-permute-start.3) | collective-permute-done | bytes 229408 | tf_op jit(solution)/shard_map/ppermute | solution.py:229
  24.9 0.9 %add.22 = (bf16[64,1792]{1,0:T(8,128)(2,1)}, bf16[64,1792]{1,0:T(8,128)(2,1)S(1)}, bf16[40,1792]{1,0:T(8,128)(2,1)S(1)}, bf16[40,1792]{1,0:T(8,128)(2,1)S(1)}) custom-call(s32[1]{0:T(128)} %bitcast.end_ref.last_ref, bf16[64,1792]{1,0:T(8,128)(2,1)S(1)} %get-tuple-element.21.residual_ref, bf16[160,64]{1,0:T(8,128)(2,1)S(1)} %get-tuple-element.22.select_ref, ...), custom_call_target="tpu_custom_call" | custom-call | flops 36700160 | bytes 1835008 | tf_op jit(solution)/shard_map/add/pallas_call | solution.py:257
  25.8 0.2 pack.1
  26.0 1.6 %collective-permute-start.8 = (bf16[40,1792]{1,0:T(8,128)(2,1)S(1)}, bf16[40,1792]{1,0:T(8,128)(2,1)S(1)}, u32[]{:S(2)}, u32[]{:S(2)}) collective-permute-start(bf16[40,1792]{1,0:T(8,128)(2,1)S(1)} %get-tuple-element.32), channel_id=1, source_target_pairs={{0,8},{4,12},{8,0},{12,4},{1,9},{5,13},{9,1},{13,5},{2,10},{6,14},... | collective-permute-start | bytes 430088 | tf_op jit(solution)/shard_map/ppermute | solution.py:17
  27.6 0.4 collective-permute-start.9
  27.9 0.2 prepare.2
  28.1 0.5 gate.11
  28.6 2.7 %collective-permute-start.7 = (bf16[88,512]{1,0:T(8,128)(2,1)S(1)}, bf16[88,512]{1,0:T(8,128)(2,1)S(1)}, u32[]{:S(2)}, u32[]{:S(2)}) collective-permute-start(bf16[88,512]{1,0:T(8,128)(2,1)S(1)} %gate.11), channel_id=1, source_target_pairs={{0,3},{1,2},{2,1},{3,0},{4,7},{5,6},{6,5},{7,4},{8,11},{9,10},{10,... | collective-permute-start | bytes 270344 | tf_op jit(solution)/shard_map/ppermute | solution.py:17
  31.3 0.4 gate.10
  31.8 0.4 gate.9
  32.3 1.8 %collective-permute-start.5 = (bf16[88,512]{1,0:T(8,128)(2,1)S(1)}, bf16[88,512]{1,0:T(8,128)(2,1)S(1)}, u32[]{:S(2)}, u32[]{:S(2)}) collective-permute-start(bf16[88,512]{1,0:T(8,128)(2,1)S(1)} %gate.9), channel_id=1, source_target_pairs={{0,1},{1,0},{2,3},{3,2},{4,5},{5,4},{6,7},{7,6},{8,9},{9,8},{10,11... | collective-permute-start | bytes 270344 | tf_op jit(solution)/shard_map/ppermute | solution.py:17
  34.1 0.8 %collective-permute-done.9.refs_1_ = bf16[40,1792]{1,0:T(8,128)(2,1)S(1)} collective-permute-done((bf16[40,1792]{1,0:T(8,128)(2,1)S(1)}, bf16[40,1792]{1,0:T(8,128)(2,1)S(1)}, u32[]{:S(2)}, u32[]{:S(2)}) %collective-permute-start.9) | collective-permute-done | bytes 143392 | tf_op jit(solution)/shard_map/ppermute | solution.py:17
  35.1 0.9 %collective-permute-done.7.refs_0_.refs_3_ = bf16[88,512]{1,0:T(8,128)(2,1)S(1)} collective-permute-done((bf16[88,512]{1,0:T(8,128)(2,1)S(1)}, bf16[88,512]{1,0:T(8,128)(2,1)S(1)}, u32[]{:S(2)}, u32[]{:S(2)}) %collective-permute-start.7) | collective-permute-done | bytes 90144 | tf_op jit(solution)/shard_map/ppermute | solution.py:17
  36.0 0.4 gate.15
  36.4 2.7 %collective-permute-start.12 = (bf16[88,512]{1,0:T(8,128)(2,1)S(1)}, bf16[88,512]{1,0:T(8,128)(2,1)S(1)}, u32[]{:S(2)}, u32[]{:S(2)}) collective-permute-start(bf16[88,512]{1,0:T(8,128)(2,1)S(1)} %gate.15), channel_id=1, source_target_pairs={{0,3},{1,2},{2,1},{3,0},{4,7},{5,6},{6,5},{7,4},{8,11},{9,10},{10,... | collective-permute-start | bytes 270344 | tf_op jit(solution)/shard_map/ppermute | solution.py:17
  39.3 0.4 gate.14
  39.7 0.4 collective-permute-start.11
  40.1 0.5 gate.13
  40.6 2.9 %collective-permute-start.10 = (bf16[88,512]{1,0:T(8,128)(2,1)S(1)}, bf16[88,512]{1,0:T(8,128)(2,1)S(1)}, u32[]{:S(2)}, u32[]{:S(2)}) collective-permute-start(bf16[88,512]{1,0:T(8,128)(2,1)S(1)} %gate.13), channel_id=1, source_target_pairs={{0,1},{1,0},{2,3},{3,2},{4,5},{5,4},{6,7},{7,6},{8,9},{9,8},{10,11... | collective-permute-start | bytes 270344 | tf_op jit(solution)/shard_map/ppermute | solution.py:17
  43.5 0.4 gate.12.refs_0_
  43.9 3.2 %collective-permute-done.11.refs_2_ = bf16[88,512]{1,0:T(8,128)(2,1)S(1)} collective-permute-done((bf16[88,512]{1,0:T(8,128)(2,1)S(1)}, bf16[88,512]{1,0:T(8,128)(2,1)S(1)}, u32[]{:S(2)}, u32[]{:S(2)}) %collective-permute-start.11) | collective-permute-done | bytes 90144 | tf_op jit(solution)/shard_map/ppermute | solution.py:17
  47.1 0.7 %collective-permute-done.10.refs_1_ = bf16[88,512]{1,0:T(8,128)(2,1)S(1)} collective-permute-done((bf16[88,512]{1,0:T(8,128)(2,1)S(1)}, bf16[88,512]{1,0:T(8,128)(2,1)S(1)}, u32[]{:S(2)}, u32[]{:S(2)}) %collective-permute-start.10) | collective-permute-done | bytes 90144 | tf_op jit(solution)/shard_map/ppermute | solution.py:17
  47.9 0.2 activate.2.refs_3_
  48.1 2.0 %collective-permute-start.13 = (bf16[80,512]{1,0:T(8,128)(2,1)S(1)}, bf16[80,512]{1,0:T(8,128)(2,1)S(1)}, u32[]{:S(2)}, u32[]{:S(2)}) collective-permute-start(bf16[80,512]{1,0:T(8,128)(2,1)S(1)} %activate.2.refs_3_), channel_id=1, source_target_pairs={{0,3},{1,2},{2,1},{3,0},{4,7},{5,6},{6,5},{7,4},{8,11},{9,10},{10,... | collective-permute-start | bytes 245768 | tf_op jit(solution)/shard_map/ppermute | solution.py:17
  50.1 2.4 %collective-permute-start.19 = (bf16[80,512]{1,0:T(8,128)(2,1)S(1)}, bf16[80,512]{1,0:T(8,128)(2,1)S(1)}, u32[]{:S(2)}, u32[]{:S(2)}) collective-permute-start(bf16[80,512]{1,0:T(8,128)(2,1)S(1)} %activate.2.refs_3_), channel_id=1, source_target_pairs={{0,1},{1,0},{2,3},{3,2},{4,5},{5,4},{6,7},{7,6},{8,9},{9,8},{10,11... | collective-permute-start | bytes 245768 | tf_op jit(solution)/shard_map/ppermute | solution.py:17
  52.5 0.4 gate.8.refs_0_
  53.0 1.9 %collective-permute-done.13.refs_4_.refs_0_ = bf16[80,512]{1,0:T(8,128)(2,1)S(1)} collective-permute-done((bf16[80,512]{1,0:T(8,128)(2,1)S(1)}, bf16[80,512]{1,0:T(8,128)(2,1)S(1)}, u32[]{:S(2)}, u32[]{:S(2)}) %collective-permute-start.13) | collective-permute-done | bytes 81952 | tf_op jit(solution)/shard_map/ppermute | solution.py:17
  54.9 0.2 activate.3.refs_3_
  55.1 2.6 %collective-permute-start.14 = (bf16[80,512]{1,0:T(8,128)(2,1)S(1)}, bf16[80,512]{1,0:T(8,128)(2,1)S(1)}, u32[]{:S(2)}, u32[]{:S(2)}) collective-permute-start(bf16[80,512]{1,0:T(8,128)(2,1)S(1)} %activate.3.refs_3_), channel_id=1, source_target_pairs={{0,3},{1,2},{2,1},{3,0},{4,7},{5,6},{6,5},{7,4},{8,11},{9,10},{10,... | collective-permute-start | bytes 245768 | tf_op jit(solution)/shard_map/ppermute | solution.py:17
  57.7 1.9 %collective-permute-start.16 = (bf16[80,512]{1,0:T(8,128)(2,1)S(1)}, bf16[80,512]{1,0:T(8,128)(2,1)S(1)}, u32[]{:S(2)}, u32[]{:S(2)}) collective-permute-start(bf16[80,512]{1,0:T(8,128)(2,1)S(1)} %activate.3.refs_3_), channel_id=1, source_target_pairs={{0,1},{1,0},{2,3},{3,2},{4,5},{5,4},{6,7},{7,6},{8,9},{9,8},{10,11... | collective-permute-start | bytes 245768 | tf_op jit(solution)/shard_map/ppermute | solution.py:17
  59.6 1.4 %down.3 = (bf16[40,1792]{1,0:T(8,128)(2,1)S(1)}, bf16[40,1792]{1,0:T(8,128)(2,1)S(1)}) custom-call(s32[1]{0:T(128)} %bitcast.8.block_ref, bf16[1,2048,1792]{2,1,0:T(8,128)(2,1)S(1)} %bitcast.15, bf16[80,512]{1,0:T(8,128)(2,1)S(1)} %collective-permute-done.13.refs_4_.refs_0_, bf16[80,512]{1,0:T(8,128)(2,1)S(1)} %collective-permute-done.18.refs_1_, ...), custom_call_target="tpu_custom_call" | custom-call | flops 587202560 | bytes 7340032 | tf_op jit(solution)/shard_map/down/pallas_call | solution.py:329
  61.0 1.5 %collective-permute-start.20 = (bf16[40,1792]{1,0:T(8,128)(2,1)S(1)}, bf16[40,1792]{1,0:T(8,128)(2,1)S(1)}, u32[]{:S(2)}, u32[]{:S(2)}) collective-permute-start(bf16[40,1792]{1,0:T(8,128)(2,1)S(1)} %get-tuple-element.38), channel_id=1, source_target_pairs={{0,8},{4,12},{8,0},{12,4},{1,9},{5,13},{9,1},{13,5},{2,10},{6,14},... | collective-permute-start | bytes 430088 | tf_op jit(solution)/shard_map/ppermute | solution.py:17
  62.4 2.0 %collective-permute-done.15.refs_1_ = bf16[80,512]{1,0:T(8,128)(2,1)S(1)} collective-permute-done((bf16[80,512]{1,0:T(8,128)(2,1)S(1)}, bf16[80,512]{1,0:T(8,128)(2,1)S(1)}, u32[]{:S(2)}, u32[]{:S(2)}) %collective-permute-start.15) | collective-permute-done | bytes 81952 | tf_op jit(solution)/shard_map/ppermute | solution.py:17
  64.5 1.4 %down.2 = (bf16[40,1792]{1,0:T(8,128)(2,1)S(1)}, bf16[40,1792]{1,0:T(8,128)(2,1)S(1)}) custom-call(s32[1]{0:T(128)} %bitcast.8.block_ref, bf16[1,2048,1792]{2,1,0:T(8,128)(2,1)S(1)} %bitcast.15, bf16[80,512]{1,0:T(8,128)(2,1)S(1)} %collective-permute-done.14.refs_0_, bf16[80,512]{1,0:T(8,128)(2,1)S(1)} %collective-permute-done.15.refs_1_, ...), custom_call_target="tpu_custom_call" | custom-call | flops 587202560 | bytes 7340032 | tf_op jit(solution)/shard_map/down/pallas_call | solution.py:329
  65.9 0.9 %collective-permute-done.20.refs_2_ = bf16[40,1792]{1,0:T(8,128)(2,1)S(1)} collective-permute-done((bf16[40,1792]{1,0:T(8,128)(2,1)S(1)}, bf16[40,1792]{1,0:T(8,128)(2,1)S(1)}, u32[]{:S(2)}, u32[]{:S(2)}) %collective-permute-start.20) | collective-permute-done | bytes 143392 | tf_op jit(solution)/shard_map/ppermute | solution.py:17
  66.9 1.6 %collective-permute-done.21.refs_3_ = bf16[40,1792]{1,0:T(8,128)(2,1)S(1)} collective-permute-done((bf16[40,1792]{1,0:T(8,128)(2,1)S(1)}, bf16[40,1792]{1,0:T(8,128)(2,1)S(1)}, u32[]{:S(2)}, u32[]{:S(2)}) %collective-permute-start.21) | collective-permute-done | bytes 143392 | tf_op jit(solution)/shard_map/ppermute | solution.py:17
  68.5 1.0 %combine.1 = bf16[64,1792]{1,0:T(8,128)(2,1)} custom-call(bf16[64,160]{1,0:T(8,128)(2,1)S(1)} %get-tuple-element.24.high_ref, bf16[64,160]{1,0:T(8,128)(2,1)S(1)} %get-tuple-element.25.low_ref, bf16[40,1792]{1,0:T(8,128)(2,1)S(1)} %get-tuple-element.36.refs_0_, bf16[40,1792]{1,0:T(8,128)(2,1)S(1)} %collective-permute-done.17.refs_1_, ...), custom_call_target="tpu_custom_call" | custom-call | flops 73400320 | bytes 573440 | tf_op jit(solution)/shard_map/combine/pallas_call | solution.py:349
  (33 shorter events, 0.6 us)
Async XLA Ops:
  0.6 18.4 %copy-start.2 = (s32[64,2]{0,1:T(2,128)S(1)}, s32[64,2]{0,1:T(2,128)}, u32[]{:S(2)}) copy-start(s32[64,2]{0,1:T(2,128)} %param.10) | copy-start | bytes 1540
  0.6 27.3 %copy-start.3 = (bf16[1792]{0:T(1024)(128)(2,1)S(1)}, bf16[1792]{0:T(1024)(128)(2,1)}, u32[]{:S(2)}) copy-start(bf16[1792]{0:T(1024)(128)(2,1)} %param.9) | copy-start | bytes 10756
  2.1 9.5 %collective-permute-start.2 = (bf16[64,1792]{1,0:T(8,128)(2,1)S(1)}, bf16[64,1792]{1,0:T(8,128)(2,1)S(1)}, u32[]{:S(2)}, u32[]{:S(2)}) collective-permute-start(bf16[64,1792]{1,0:T(8,128)(2,1)S(1)} %get-tuple-element.40), channel_id=1, source_target_pairs={{0,1},{1,0},{2,3},{3,2},{4,5},{5,4},{6,7},{7,6},{8,9},{9,8},{10,11... | collective-permute-start | bytes 688136 | tf_op jit(solution)/shard_map/ppermute | solution.py:17
  5.2 14.3 %collective-permute-start = (bf16[64,1792]{1,0:T(8,128)(2,1)S(1)}, bf16[64,1792]{1,0:T(8,128)(2,1)S(1)}, u32[]{:S(2)}, u32[]{:S(2)}) collective-permute-start(bf16[64,1792]{1,0:T(8,128)(2,1)S(1)} %get-tuple-element.42), channel_id=1, source_target_pairs={{1,2},{2,1},{5,6},{6,5},{9,10},{10,9},{13,14},{14,13},{17,18},{18,... | collective-permute-start | bytes 688136 | tf_op jit(solution)/shard_map/ppermute | solution.py:218
  5.9 13.7 %collective-permute-start.1 = (bf16[64,1792]{1,0:T(8,128)(2,1)S(1)}, bf16[64,1792]{1,0:T(8,128)(2,1)S(1)}, u32[]{:S(2)}, u32[]{:S(2)}) collective-permute-start(bf16[64,1792]{1,0:T(8,128)(2,1)S(1)} %get-tuple-element.41.passing_ref), channel_id=1, source_target_pairs={{0,2},{3,1},{4,6},{7,5},{8,10},{11,9},{12,14},{15,13},{16,18},{19,... | collective-permute-start | bytes 688136 | tf_op jit(solution)/shard_map/ppermute | solution.py:219
  11.7 13.1 %collective-permute-start.3 = (bf16[64,1792]{1,0:T(8,128)(2,1)S(1)}, bf16[64,1792]{1,0:T(8,128)(2,1)S(1)}, u32[]{:S(2)}, u32[]{:S(2)}) collective-permute-start(bf16[64,1792]{1,0:T(8,128)(2,1)S(1)} %merge.1), channel_id=1, source_target_pairs={{0,1},{1,3},{2,0},{3,2},{4,5},{5,7},{6,4},{7,6},{8,9},{9,11},{10,8... | collective-permute-start | bytes 688136 | tf_op jit(solution)/shard_map/ppermute | solution.py:229
  14.2 3.1 %copy-start = (bf16[1,1792,2048]{2,1,0:T(8,128)(2,1)S(1)}, bf16[1,1792,2048]{2,1,0:T(8,128)(2,1)}, u32[]{:S(2)}) copy-start(bf16[1,1792,2048]{2,1,0:T(8,128)(2,1)} %refs_1_.1) | copy-start | bytes 22020100
  17.3 0.9 %copy-start.1 = (bf16[64,1792]{1,0:T(8,128)(2,1)S(1)}, bf16[64,1792]{1,0:T(8,128)(2,1)}, u32[]{:S(2)}) copy-start(bf16[64,1792]{1,0:T(8,128)(2,1)} %refs_0_.1) | copy-start | bytes 688132
  25.8 2.2 %collective-permute-start.4 = (bf16[40,1792]{1,0:T(8,128)(2,1)S(1)}, bf16[40,1792]{1,0:T(8,128)(2,1)S(1)}, u32[]{:S(2)}, u32[]{:S(2)}) collective-permute-start(bf16[40,1792]{1,0:T(8,128)(2,1)S(1)} %get-tuple-element.27), channel_id=1, source_target_pairs={{0,4},{4,0},{8,12},{12,8},{1,5},{5,1},{9,13},{13,9},{2,6},{6,2},{1... | collective-permute-start | bytes 430088 | tf_op jit(solution)/shard_map/ppermute | solution.py:17
  26.0 8.1 %collective-permute-start.8 = (bf16[40,1792]{1,0:T(8,128)(2,1)S(1)}, bf16[40,1792]{1,0:T(8,128)(2,1)S(1)}, u32[]{:S(2)}, u32[]{:S(2)}) collective-permute-start(bf16[40,1792]{1,0:T(8,128)(2,1)S(1)} %get-tuple-element.32), channel_id=1, source_target_pairs={{0,8},{4,12},{8,0},{12,4},{1,9},{5,13},{9,1},{13,5},{2,10},{6,14},... | collective-permute-start | bytes 430088 | tf_op jit(solution)/shard_map/ppermute | solution.py:17
  27.6 7.4 %collective-permute-start.9 = (bf16[40,1792]{1,0:T(8,128)(2,1)S(1)}, bf16[40,1792]{1,0:T(8,128)(2,1)S(1)}, u32[]{:S(2)}, u32[]{:S(2)}) collective-permute-start(bf16[40,1792]{1,0:T(8,128)(2,1)S(1)} %get-tuple-element.33), channel_id=1, source_target_pairs={{0,12},{4,8},{8,4},{12,0},{1,13},{5,9},{9,5},{13,1},{2,14},{6,10},... | collective-permute-start | bytes 430088 | tf_op jit(solution)/shard_map/ppermute | solution.py:17
  28.6 7.4 %collective-permute-start.7 = (bf16[88,512]{1,0:T(8,128)(2,1)S(1)}, bf16[88,512]{1,0:T(8,128)(2,1)S(1)}, u32[]{:S(2)}, u32[]{:S(2)}) collective-permute-start(bf16[88,512]{1,0:T(8,128)(2,1)S(1)} %gate.11), channel_id=1, source_target_pairs={{0,3},{1,2},{2,1},{3,0},{4,7},{5,6},{6,5},{7,4},{8,11},{9,10},{10,... | collective-permute-start | bytes 270344 | tf_op jit(solution)/shard_map/ppermute | solution.py:17
  31.8 7.5 %collective-permute-start.6 = (bf16[88,512]{1,0:T(8,128)(2,1)S(1)}, bf16[88,512]{1,0:T(8,128)(2,1)S(1)}, u32[]{:S(2)}, u32[]{:S(2)}) collective-permute-start(bf16[88,512]{1,0:T(8,128)(2,1)S(1)} %gate.10), channel_id=1, source_target_pairs={{0,2},{1,3},{2,0},{3,1},{4,6},{5,7},{6,4},{7,5},{8,10},{9,11},{10,... | collective-permute-start | bytes 270344 | tf_op jit(solution)/shard_map/ppermute | solution.py:17
  32.3 7.8 %collective-permute-start.5 = (bf16[88,512]{1,0:T(8,128)(2,1)S(1)}, bf16[88,512]{1,0:T(8,128)(2,1)S(1)}, u32[]{:S(2)}, u32[]{:S(2)}) collective-permute-start(bf16[88,512]{1,0:T(8,128)(2,1)S(1)} %gate.9), channel_id=1, source_target_pairs={{0,1},{1,0},{2,3},{3,2},{4,5},{5,4},{6,7},{7,6},{8,9},{9,8},{10,11... | collective-permute-start | bytes 270344 | tf_op jit(solution)/shard_map/ppermute | solution.py:17
  36.4 7.5 %collective-permute-start.12 = (bf16[88,512]{1,0:T(8,128)(2,1)S(1)}, bf16[88,512]{1,0:T(8,128)(2,1)S(1)}, u32[]{:S(2)}, u32[]{:S(2)}) collective-permute-start(bf16[88,512]{1,0:T(8,128)(2,1)S(1)} %gate.15), channel_id=1, source_target_pairs={{0,3},{1,2},{2,1},{3,0},{4,7},{5,6},{6,5},{7,4},{8,11},{9,10},{10,... | collective-permute-start | bytes 270344 | tf_op jit(solution)/shard_map/ppermute | solution.py:17
  39.7 7.4 %collective-permute-start.11 = (bf16[88,512]{1,0:T(8,128)(2,1)S(1)}, bf16[88,512]{1,0:T(8,128)(2,1)S(1)}, u32[]{:S(2)}, u32[]{:S(2)}) collective-permute-start(bf16[88,512]{1,0:T(8,128)(2,1)S(1)} %gate.14), channel_id=1, source_target_pairs={{0,2},{1,3},{2,0},{3,1},{4,6},{5,7},{6,4},{7,5},{8,10},{9,11},{10,... | collective-permute-start | bytes 270344 | tf_op jit(solution)/shard_map/ppermute | solution.py:17
  40.6 19.0 %slice-start = ((s8[7340032]{0:T(1024)(128)(4,1)}), s8[4194304]{0:T(1024)(128)(4,1)S(1)}, s32[]{:S(2)}) async-start(s8[7340032]{0:T(1024)(128)(4,1)} %bitcast.14), calls=%async_computation | async-start | bytes 8388608
  40.6 7.3 %collective-permute-start.10 = (bf16[88,512]{1,0:T(8,128)(2,1)S(1)}, bf16[88,512]{1,0:T(8,128)(2,1)S(1)}, u32[]{:S(2)}, u32[]{:S(2)}) collective-permute-start(bf16[88,512]{1,0:T(8,128)(2,1)S(1)} %gate.13), channel_id=1, source_target_pairs={{0,1},{1,0},{2,3},{3,2},{4,5},{5,4},{6,7},{7,6},{8,9},{9,8},{10,11... | collective-permute-start | bytes 270344 | tf_op jit(solution)/shard_map/ppermute | solution.py:17
  43.9 15.6 %slice-start.1 = ((s8[7340032]{0:T(1024)(128)(4,1)}), s8[3145728]{0:T(1024)(128)(4,1)S(1)}, s32[]{:S(2)}) async-start(s8[7340032]{0:T(1024)(128)(4,1)} %bitcast.14), calls=%async_computation.1 | async-start | bytes 6291456
  48.1 6.8 %collective-permute-start.13 = (bf16[80,512]{1,0:T(8,128)(2,1)S(1)}, bf16[80,512]{1,0:T(8,128)(2,1)S(1)}, u32[]{:S(2)}, u32[]{:S(2)}) collective-permute-start(bf16[80,512]{1,0:T(8,128)(2,1)S(1)} %activate.2.refs_3_), channel_id=1, source_target_pairs={{0,3},{1,2},{2,1},{3,0},{4,7},{5,6},{6,5},{7,4},{8,11},{9,10},{10,... | collective-permute-start | bytes 245768 | tf_op jit(solution)/shard_map/ppermute | solution.py:17
  50.1 9.4 %collective-permute-start.18 = (bf16[80,512]{1,0:T(8,128)(2,1)S(1)}, bf16[80,512]{1,0:T(8,128)(2,1)S(1)}, u32[]{:S(2)}, u32[]{:S(2)}) collective-permute-start(bf16[80,512]{1,0:T(8,128)(2,1)S(1)} %activate.2.refs_3_), channel_id=1, source_target_pairs={{0,2},{1,3},{2,0},{3,1},{4,6},{5,7},{6,4},{7,5},{8,10},{9,11},{10,... | collective-permute-start | bytes 245768 | tf_op jit(solution)/shard_map/ppermute | solution.py:17
  50.1 9.4 %collective-permute-start.19 = (bf16[80,512]{1,0:T(8,128)(2,1)S(1)}, bf16[80,512]{1,0:T(8,128)(2,1)S(1)}, u32[]{:S(2)}, u32[]{:S(2)}) collective-permute-start(bf16[80,512]{1,0:T(8,128)(2,1)S(1)} %activate.2.refs_3_), channel_id=1, source_target_pairs={{0,1},{1,0},{2,3},{3,2},{4,5},{5,4},{6,7},{7,6},{8,9},{9,8},{10,11... | collective-permute-start | bytes 245768 | tf_op jit(solution)/shard_map/ppermute | solution.py:17
  55.1 7.3 %collective-permute-start.14 = (bf16[80,512]{1,0:T(8,128)(2,1)S(1)}, bf16[80,512]{1,0:T(8,128)(2,1)S(1)}, u32[]{:S(2)}, u32[]{:S(2)}) collective-permute-start(bf16[80,512]{1,0:T(8,128)(2,1)S(1)} %activate.3.refs_3_), channel_id=1, source_target_pairs={{0,3},{1,2},{2,1},{3,0},{4,7},{5,6},{6,5},{7,4},{8,11},{9,10},{10,... | collective-permute-start | bytes 245768 | tf_op jit(solution)/shard_map/ppermute | solution.py:17
  57.7 6.8 %collective-permute-start.15 = (bf16[80,512]{1,0:T(8,128)(2,1)S(1)}, bf16[80,512]{1,0:T(8,128)(2,1)S(1)}, u32[]{:S(2)}, u32[]{:S(2)}) collective-permute-start(bf16[80,512]{1,0:T(8,128)(2,1)S(1)} %activate.3.refs_3_), channel_id=1, source_target_pairs={{0,2},{1,3},{2,0},{3,1},{4,6},{5,7},{6,4},{7,5},{8,10},{9,11},{10,... | collective-permute-start | bytes 245768 | tf_op jit(solution)/shard_map/ppermute | solution.py:17
  57.7 6.8 %collective-permute-start.16 = (bf16[80,512]{1,0:T(8,128)(2,1)S(1)}, bf16[80,512]{1,0:T(8,128)(2,1)S(1)}, u32[]{:S(2)}, u32[]{:S(2)}) collective-permute-start(bf16[80,512]{1,0:T(8,128)(2,1)S(1)} %activate.3.refs_3_), channel_id=1, source_target_pairs={{0,1},{1,0},{2,3},{3,2},{4,5},{5,4},{6,7},{7,6},{8,9},{9,8},{10,11... | collective-permute-start | bytes 245768 | tf_op jit(solution)/shard_map/ppermute | solution.py:17
  61.0 5.9 %collective-permute-start.20 = (bf16[40,1792]{1,0:T(8,128)(2,1)S(1)}, bf16[40,1792]{1,0:T(8,128)(2,1)S(1)}, u32[]{:S(2)}, u32[]{:S(2)}) collective-permute-start(bf16[40,1792]{1,0:T(8,128)(2,1)S(1)} %get-tuple-element.38), channel_id=1, source_target_pairs={{0,8},{4,12},{8,0},{12,4},{1,9},{5,13},{9,1},{13,5},{2,10},{6,14},... | collective-permute-start | bytes 430088 | tf_op jit(solution)/shard_map/ppermute | solution.py:17
  62.4 6.0 %collective-permute-start.21 = (bf16[40,1792]{1,0:T(8,128)(2,1)S(1)}, bf16[40,1792]{1,0:T(8,128)(2,1)S(1)}, u32[]{:S(2)}, u32[]{:S(2)}) collective-permute-start(bf16[40,1792]{1,0:T(8,128)(2,1)S(1)} %get-tuple-element.39), channel_id=1, source_target_pairs={{0,12},{4,8},{8,4},{12,0},{1,13},{5,9},{9,5},{13,1},{2,14},{6,10},... | collective-permute-start | bytes 430088 | tf_op jit(solution)/shard_map/ppermute | solution.py:17
  65.8 2.6 %collective-permute-start.17 = (bf16[40,1792]{1,0:T(8,128)(2,1)S(1)}, bf16[40,1792]{1,0:T(8,128)(2,1)S(1)}, u32[]{:S(2)}, u32[]{:S(2)}) collective-permute-start(bf16[40,1792]{1,0:T(8,128)(2,1)S(1)} %get-tuple-element.37), channel_id=1, source_target_pairs={{0,4},{4,0},{8,12},{12,8},{1,5},{5,1},{9,13},{13,9},{2,6},{6,2},{1... | collective-permute-start | bytes 430088 | tf_op jit(solution)/shard_map/ppermute | solution.py:17

commit v4 on v3

--- a/solution.py
+++ b/solution.py
@@ -94,12 +94,11 @@
 
 
 def add_kernel(n_tensor, cap, ks, last_ref, residual_ref, select_ref, *refs):
-    parts, stream_ref, kept_ref, outs = refs[:n_tensor], *refs[n_tensor : n_tensor + 2], refs[n_tensor + 2 :]
+    parts, kept_ref, outs = refs[:n_tensor], refs[n_tensor], refs[n_tensor + 1 :]
     total = residual_ref[...].astype(jnp.float32)
     for part in parts[:-1]:
         total += part[...].astype(jnp.float32)
     total += jnp.where(last_ref[0] == 1, parts[-1][...].astype(jnp.float32), 0.0)
-    stream_ref[...] = total.astype(jnp.bfloat16)
     kept_ref[...] = total.astype(jnp.bfloat16)
     pack_kernel(cap, ks, kept_ref, select_ref, *outs)
 
@@ -109,6 +108,10 @@
     packed = jnp.dot(select_ref[first:last, :], stream_ref[...], preferred_element_type=jnp.float32)
     for i, out in enumerate(outs):
         out[...] = packed[i * cap : (i + 1) * cap, :].astype(jnp.bfloat16)
+
+
+def store_kernel(values_ref, after_ref, out_ref):
+    out_ref[...] = values_ref[...]
 
 
 def prepare_kernel(n, gain_ref, *refs):
@@ -254,11 +257,11 @@
         name="fetch",
     )(*fetched)
 
-    stream, kept, *near_rows = pl.pallas_call(
+    kept, *near_rows = pl.pallas_call(
         functools.partial(add_kernel, len(parts), cap, near),
-        out_shape=(sds((tokens, share), bf16),) * 2 + (sds((cap, share), bf16),) * len(near),
+        out_shape=(sds((tokens, share), bf16),) + (sds((cap, share), bf16),) * len(near),
         in_specs=[scalar()] + [whole()] * (2 + len(parts)),
-        out_specs=(whole(),) * (2 + len(near)),
+        out_specs=(whole(),) * (1 + len(near)),
         compiler_params=params(),
         cost_estimate=estimate(2 * rows * tokens * share, 4 * tokens * share * nt),
         name="add",
@@ -275,6 +278,8 @@
     )(kept, select)
     for k, value in zip(far, far_rows):
         arrived[k] = exchange(value, "expert", k)
+
+    stored = []
 
     def summed_gate(ks, after=None):
         count = len(ks) * cap
@@ -291,6 +296,19 @@
         gates = {}
         for k in partners(nt):
             earlier = [] if after is None else [after[k or 1]]
+            if k == 0 and after is not None:
+                stored.append(
+                    pl.pallas_call(
+                        store_kernel,
+                        out_shape=sds((tokens, share), bf16),
+                        in_specs=[whole(), anywhere()],
+                        out_specs=whole(),
+                        compiler_params=params(),
+                        cost_estimate=estimate(10**6, 4 * tokens * share),
+                        name="store",
+                    )(kept, partial_gate)
+                )
+                earlier.append(stored[0])
             partial_gate = pl.pallas_call(
                 gate_kernel,
                 out_shape=sds((tall, ff), bf16),
@@ -355,7 +373,7 @@
         cost_estimate=estimate(4 * rows * tokens * share, 2 * rows * share),
         name="combine",
     )(high, low, *[returned[k] for k in range(ne)])
-    return stream, moe_out
+    return stored[0], moe_out
 
 
 def solution(mesh):

time: 69.9 us -> 69.3 us (level)
  waiting for transfers between devices: 17.5 us -> 15.8 us
  local copies, waits for them, and re-layouts: 7.03 us -> 7.96 us
    ppermute x19, waiting for transfers between devices: 12.2 us -> 10.5 us  [exchange(): return lax.ppermute(value, axis, [(i, i ^ step) for i in range(n)])]
    unnamed x14 -> x16, local copies, waits for them, and re-layouts: 5.58 us -> 6.52 us
    pallas_call x0 -> x1, Pallas kernels: none -> 0.7 us  [summed_gate(): pl.pallas_call(store_kernel, out_shape=sds((tokens, share), bf16), in_spe...]
  transfers between devices with their start and end apart: 22 -> 22, of which waited for: 10 -> 10; matrix products, arithmetic and copies ran while one was open for 2% -> 2% of each run, Pallas kernels for 12% -> 13%
where the time goes in v4:
time: 69.3 us; the launch traced here: 69 us
  starting transfers between devices  33.6 us (48%)
  waiting for transfers between devices  15.8 us (23%)
  Pallas kernels  10.8 us (16%)
  local copies, waits for them, and re-layouts  7.96 us (11%)
  between operations  0.93 us (1%)
    ppermute x19, starting transfers between devices, exchange(): return lax.ppermute(value, axis, [(i, i ^ step) for i in range(n)])  26.2 us
    ppermute x19, waiting for transfers between devices, exchange(): return lax.ppermute(value, axis, [(i, i ^ step) for i in range(n)])  10.5 us
    unnamed x16, local copies, waits for them, and re-layouts  6.52 us
    ppermute x1, starting transfers between devices, local(): parts.append(lax.ppermute(block(z ^ 2), 'tensor', [(0, 2), (3, 1)]))  5.75 us
    ppermute x1, waiting for transfers between devices, local(): lax.ppermute(merged, 'tensor', [(0, 1), (1, 3), (2, 0), (3, 2)])  5.28 us
    pallas_call x8, Pallas kernels, summed_gate(): pl.pallas_call(gate_kernel, out_shape=sds((tall, ff), bf16), grid_spec=pl...  3.58 us
    pallas_call x2, Pallas kernels, produced(): pl.pallas_call(functools.partial(down_kernel, nt, len(ks), cap), out_shap...  2.78 us
    dynamic_slice x1, local copies, waits for them, and re-layouts, block(): return lax.dynamic_slice(attn_partial[0], (0, k * share), (tokens, share))  1.44 us
  transfers between devices with their start and end apart: 22, of which 10 were waited for; matrix products, arithmetic and copies ran while one was open for 2% of the time, Pallas kernels for 13%

profile of v4, /device:TPU:0, one launch (start us, length us, event | category | flops | bytes accessed | tf_op | source)
XLA Modules:
  0.0 69.0 jit_solution(3507386849034517100)
XLA Ops:
  0.7 1.4 %dynamic-slice_bitcast_fusion = (bf16[64,1792]{1,0:T(8,128)(2,1)S(1)}, bf16[64,1792]{1,0:T(8,128)(2,1)S(1)}, bf16[64,1792]{1,0:T(8,128)(2,1)S(1)}, bf16[64,1792]{1,0:T(8,128)(2,1)S(1)}, bf16[64,1792]{1,0:T(8,128)(2,1)S(1)}) fusion(bf16[1,64,7168]{2,1,0:T(8,128)(2,1)} %param.8, s32[]{:T(128)S(6)} %select_n.30, s32[]{:T(128)S(6)} %select_n.27, s32[]{:T(128)S(6)} %select_n.26, ...), kind=kLoop, calls=%fused_computation | loop fusion | bytes 2293780 | tf_op jit(solution)/shard_map/dynamic_slice | solution.py:214
  2.1 3.1 %collective-permute-start.2 = (bf16[64,1792]{1,0:T(8,128)(2,1)S(1)}, bf16[64,1792]{1,0:T(8,128)(2,1)S(1)}, u32[]{:S(2)}, u32[]{:S(2)}) collective-permute-start(bf16[64,1792]{1,0:T(8,128)(2,1)S(1)} %get-tuple-element.38), channel_id=1, source_target_pairs={{0,1},{1,0},{2,3},{3,2},{4,5},{5,4},{6,7},{7,6},{8,9},{9,8},{10,11... | collective-permute-start | bytes 688136 | tf_op jit(solution)/shard_map/ppermute | solution.py:17
  5.2 0.7 collective-permute-start
  5.9 5.8 %collective-permute-start.1 = (bf16[64,1792]{1,0:T(8,128)(2,1)S(1)}, bf16[64,1792]{1,0:T(8,128)(2,1)S(1)}, u32[]{:S(2)}, u32[]{:S(2)}) collective-permute-start(bf16[64,1792]{1,0:T(8,128)(2,1)S(1)} %get-tuple-element.39.passing_ref), channel_id=1, source_target_pairs={{0,2},{3,1},{4,6},{7,5},{8,10},{11,9},{12,14},{15,13},{16,18},{19,... | collective-permute-start | bytes 688136 | tf_op jit(solution)/shard_map/ppermute | solution.py:222
  11.7 1.0 %collective-permute-start.3 = (bf16[64,1792]{1,0:T(8,128)(2,1)S(1)}, bf16[64,1792]{1,0:T(8,128)(2,1)S(1)}, u32[]{:S(2)}, u32[]{:S(2)}) collective-permute-start(bf16[64,1792]{1,0:T(8,128)(2,1)S(1)} %merge.1), channel_id=1, source_target_pairs={{0,1},{1,3},{2,0},{3,2},{4,5},{5,7},{6,4},{7,6},{8,9},{9,11},{10,8... | collective-permute-start | bytes 688136 | tf_op jit(solution)/shard_map/ppermute | solution.py:232
  12.7 0.8 %copy.10.scores_ref = f32[64,2]{1,0:T(8,128)S(1)} copy(f32[64,2]{0,1:T(2,128)} %param.11) | data formatting | bytes 1024 | tf_op args[4]
  13.4 0.8 %copy.9.ids_ref = s32[64,2]{1,0:T(8,128)S(1)} copy(s32[64,2]{0,1:T(2,128)} %param.10) | data formatting | bytes 1024 | tf_op args[3]
  14.2 3.1 %copy-done = bf16[1,1792,2048]{2,1,0:T(8,128)(2,1)S(1)} copy-done((bf16[1,1792,2048]{2,1,0:T(8,128)(2,1)S(1)}, bf16[1,1792,2048]{2,1,0:T(8,128)(2,1)}, u32[]{:S(2)}) %copy-start) | copy-done | bytes 7340056
  17.3 0.9 %copy-done.2 = bf16[64,1792]{1,0:T(8,128)(2,1)S(1)} copy-done((bf16[64,1792]{1,0:T(8,128)(2,1)S(1)}, bf16[64,1792]{1,0:T(8,128)(2,1)}, u32[]{:S(2)}) %copy-start.2) | copy-done | bytes 229400
  18.2 0.8 %fetch.1 = (bf16[64,1792]{1,0:T(8,128)(2,1)S(1)}, bf16[1,1792,2048]{2,1,0:T(8,128)(2,1)S(1)}) custom-call(bf16[64,1792]{1,0:T(8,128)(2,1)S(1)} %copy-done.2, bf16[1,1792,2048]{2,1,0:T(8,128)(2,1)S(1)} %copy-done), custom_call_target="tpu_custom_call" | custom-call | flops 1000000 | bytes 7569408 | tf_op jit(solution)/shard_map/fetch/pallas_call | solution.py:249
  19.0 0.5 routing.1
  19.6 5.3 %collective-permute-done.3.refs_3_ = bf16[64,1792]{1,0:T(8,128)(2,1)S(1)} collective-permute-done((bf16[64,1792]{1,0:T(8,128)(2,1)S(1)}, bf16[64,1792]{1,0:T(8,128)(2,1)S(1)}, u32[]{:S(2)}, u32[]{:S(2)}) %collective-permute-start.3) | collective-permute-done | bytes 229408 | tf_op jit(solution)/shard_map/ppermute | solution.py:232
  24.9 0.4 add.22
  25.3 0.2 pack.1
  25.5 1.6 %collective-permute-start.4 = (bf16[40,1792]{1,0:T(8,128)(2,1)S(1)}, bf16[40,1792]{1,0:T(8,128)(2,1)S(1)}, u32[]{:S(2)}, u32[]{:S(2)}) collective-permute-start(bf16[40,1792]{1,0:T(8,128)(2,1)S(1)} %get-tuple-element.23), channel_id=1, source_target_pairs={{0,8},{4,12},{8,0},{12,4},{1,9},{5,13},{9,1},{13,5},{2,10},{6,14},... | collective-permute-start | bytes 430088 | tf_op jit(solution)/shard_map/ppermute | solution.py:17
  27.1 0.4 collective-permute-start.5
  27.6 0.5 gate.12
  28.1 2.7 %collective-permute-start.9 = (bf16[88,512]{1,0:T(8,128)(2,1)S(1)}, bf16[88,512]{1,0:T(8,128)(2,1)S(1)}, u32[]{:S(2)}, u32[]{:S(2)}) collective-permute-start(bf16[88,512]{1,0:T(8,128)(2,1)S(1)} %gate.12), channel_id=1, source_target_pairs={{0,3},{1,2},{2,1},{3,0},{4,7},{5,6},{6,5},{7,4},{8,11},{9,10},{10,... | collective-permute-start | bytes 270344 | tf_op jit(solution)/shard_map/ppermute | solution.py:17
  30.8 0.4 gate.11
  31.4 0.4 gate.8
  31.8 1.8 %collective-permute-start.7 = (bf16[88,512]{1,0:T(8,128)(2,1)S(1)}, bf16[88,512]{1,0:T(8,128)(2,1)S(1)}, u32[]{:S(2)}, u32[]{:S(2)}) collective-permute-start(bf16[88,512]{1,0:T(8,128)(2,1)S(1)} %gate.8), channel_id=1, source_target_pairs={{0,1},{1,0},{2,3},{3,2},{4,5},{5,4},{6,7},{7,6},{8,9},{9,8},{10,11... | collective-permute-start | bytes 270344 | tf_op jit(solution)/shard_map/ppermute | solution.py:17
  33.6 0.8 %collective-permute-done.5.refs_1_ = bf16[40,1792]{1,0:T(8,128)(2,1)S(1)} collective-permute-done((bf16[40,1792]{1,0:T(8,128)(2,1)S(1)}, bf16[40,1792]{1,0:T(8,128)(2,1)S(1)}, u32[]{:S(2)}, u32[]{:S(2)}) %collective-permute-start.5) | collective-permute-done | bytes 143392 | tf_op jit(solution)/shard_map/ppermute | solution.py:17
  34.6 0.9 %collective-permute-done.9.refs_0_.refs_3_ = bf16[88,512]{1,0:T(8,128)(2,1)S(1)} collective-permute-done((bf16[88,512]{1,0:T(8,128)(2,1)S(1)}, bf16[88,512]{1,0:T(8,128)(2,1)S(1)}, u32[]{:S(2)}, u32[]{:S(2)}) %collective-permute-start.9) | collective-permute-done | bytes 90144 | tf_op jit(solution)/shard_map/ppermute | solution.py:17
  35.5 0.4 gate.15
  35.9 2.7 %collective-permute-start.12 = (bf16[88,512]{1,0:T(8,128)(2,1)S(1)}, bf16[88,512]{1,0:T(8,128)(2,1)S(1)}, u32[]{:S(2)}, u32[]{:S(2)}) collective-permute-start(bf16[88,512]{1,0:T(8,128)(2,1)S(1)} %gate.15), channel_id=1, source_target_pairs={{0,3},{1,2},{2,1},{3,0},{4,7},{5,6},{6,5},{7,4},{8,11},{9,10},{10,... | collective-permute-start | bytes 270344 | tf_op jit(solution)/shard_map/ppermute | solution.py:17
  38.8 0.4 gate.14
  39.3 0.4 collective-permute-start.11
  39.7 0.4 gate.9.after_ref
  40.1 2.9 %collective-permute-start.10 = (bf16[88,512]{1,0:T(8,128)(2,1)S(1)}, bf16[88,512]{1,0:T(8,128)(2,1)S(1)}, u32[]{:S(2)}, u32[]{:S(2)}) collective-permute-start(bf16[88,512]{1,0:T(8,128)(2,1)S(1)} %gate.9.after_ref), channel_id=1, source_target_pairs={{0,1},{1,0},{2,3},{3,2},{4,5},{5,4},{6,7},{7,6},{8,9},{9,8},{10,11... | collective-permute-start | bytes 270344 | tf_op jit(solution)/shard_map/ppermute | solution.py:17
  43.0 0.7 %store.1.refs_1_ = bf16[64,1792]{1,0:T(8,128)(2,1)} custom-call(bf16[64,1792]{1,0:T(8,128)(2,1)S(1)} %get-tuple-element.22.stream_ref.values_ref, bf16[88,512]{1,0:T(8,128)(2,1)S(1)} %gate.9.after_ref), custom_call_target="tpu_custom_call" | custom-call | flops 1000000 | bytes 458752 | tf_op jit(solution)/shard_map/store/pallas_call | solution.py:301
  43.7 0.9 %copy-done.1 = bf16[64,1792]{1,0:T(8,128)(2,1)S(1)} copy-done((bf16[64,1792]{1,0:T(8,128)(2,1)S(1)}, bf16[64,1792]{1,0:T(8,128)(2,1)}, u32[]{:S(2)}) %copy-start.1) | copy-done | bytes 229400
  44.6 0.4 gate.13.refs_0_
  45.1 1.5 %collective-permute-done.11.refs_2_ = bf16[88,512]{1,0:T(8,128)(2,1)S(1)} collective-permute-done((bf16[88,512]{1,0:T(8,128)(2,1)S(1)}, bf16[88,512]{1,0:T(8,128)(2,1)S(1)}, u32[]{:S(2)}, u32[]{:S(2)}) %collective-permute-start.11) | collective-permute-done | bytes 90144 | tf_op jit(solution)/shard_map/ppermute | solution.py:17
  46.6 0.8 %collective-permute-done.10.refs_1_ = bf16[88,512]{1,0:T(8,128)(2,1)S(1)} collective-permute-done((bf16[88,512]{1,0:T(8,128)(2,1)S(1)}, bf16[88,512]{1,0:T(8,128)(2,1)S(1)}, u32[]{:S(2)}, u32[]{:S(2)}) %collective-permute-start.10) | collective-permute-done | bytes 90144 | tf_op jit(solution)/shard_map/ppermute | solution.py:17
  47.6 2.0 %collective-permute-start.13 = (bf16[80,512]{1,0:T(8,128)(2,1)S(1)}, bf16[80,512]{1,0:T(8,128)(2,1)S(1)}, u32[]{:S(2)}, u32[]{:S(2)}) collective-permute-start(bf16[80,512]{1,0:T(8,128)(2,1)S(1)} %activate.2.refs_3_), channel_id=1, source_target_pairs={{0,3},{1,2},{2,1},{3,0},{4,7},{5,6},{6,5},{7,4},{8,11},{9,10},{10,... | collective-permute-start | bytes 245768 | tf_op jit(solution)/shard_map/ppermute | solution.py:17
  49.6 2.4 %collective-permute-start.19 = (bf16[80,512]{1,0:T(8,128)(2,1)S(1)}, bf16[80,512]{1,0:T(8,128)(2,1)S(1)}, u32[]{:S(2)}, u32[]{:S(2)}) collective-permute-start(bf16[80,512]{1,0:T(8,128)(2,1)S(1)} %activate.2.refs_3_), channel_id=1, source_target_pairs={{0,1},{1,0},{2,3},{3,2},{4,5},{5,4},{6,7},{7,6},{8,9},{9,8},{10,11... | collective-permute-start | bytes 245768 | tf_op jit(solution)/shard_map/ppermute | solution.py:17
  52.1 0.4 gate.10.refs_0_
  52.5 1.8 %collective-permute-done.13.refs_4_.refs_0_ = bf16[80,512]{1,0:T(8,128)(2,1)S(1)} collective-permute-done((bf16[80,512]{1,0:T(8,128)(2,1)S(1)}, bf16[80,512]{1,0:T(8,128)(2,1)S(1)}, u32[]{:S(2)}, u32[]{:S(2)}) %collective-permute-start.13) | collective-permute-done | bytes 81952 | tf_op jit(solution)/shard_map/ppermute | solution.py:17
  54.3 0.2 activate.3.refs_3_
  54.5 2.6 %collective-permute-start.14 = (bf16[80,512]{1,0:T(8,128)(2,1)S(1)}, bf16[80,512]{1,0:T(8,128)(2,1)S(1)}, u32[]{:S(2)}, u32[]{:S(2)}) collective-permute-start(bf16[80,512]{1,0:T(8,128)(2,1)S(1)} %activate.3.refs_3_), channel_id=1, source_target_pairs={{0,3},{1,2},{2,1},{3,0},{4,7},{5,6},{6,5},{7,4},{8,11},{9,10},{10,... | collective-permute-start | bytes 245768 | tf_op jit(solution)/shard_map/ppermute | solution.py:17
  57.2 1.8 %collective-permute-start.16 = (bf16[80,512]{1,0:T(8,128)(2,1)S(1)}, bf16[80,512]{1,0:T(8,128)(2,1)S(1)}, u32[]{:S(2)}, u32[]{:S(2)}) collective-permute-start(bf16[80,512]{1,0:T(8,128)(2,1)S(1)} %activate.3.refs_3_), channel_id=1, source_target_pairs={{0,1},{1,0},{2,3},{3,2},{4,5},{5,4},{6,7},{7,6},{8,9},{9,8},{10,11... | collective-permute-start | bytes 245768 | tf_op jit(solution)/shard_map/ppermute | solution.py:17
  59.0 1.4 %down.3 = (bf16[40,1792]{1,0:T(8,128)(2,1)S(1)}, bf16[40,1792]{1,0:T(8,128)(2,1)S(1)}) custom-call(s32[1]{0:T(128)} %bitcast.8.block_ref, bf16[1,2048,1792]{2,1,0:T(8,128)(2,1)S(1)} %bitcast.15, bf16[80,512]{1,0:T(8,128)(2,1)S(1)} %collective-permute-done.13.refs_4_.refs_0_, bf16[80,512]{1,0:T(8,128)(2,1)S(1)} %collective-permute-done.18.refs_1_, ...), custom_call_target="tpu_custom_call" | custom-call | flops 587202560 | bytes 7340032 | tf_op jit(solution)/shard_map/down/pallas_call | solution.py:347
  60.4 1.6 %collective-permute-start.20 = (bf16[40,1792]{1,0:T(8,128)(2,1)S(1)}, bf16[40,1792]{1,0:T(8,128)(2,1)S(1)}, u32[]{:S(2)}, u32[]{:S(2)}) collective-permute-start(bf16[40,1792]{1,0:T(8,128)(2,1)S(1)} %get-tuple-element.36), channel_id=1, source_target_pairs={{0,8},{4,12},{8,0},{12,4},{1,9},{5,13},{9,1},{13,5},{2,10},{6,14},... | collective-permute-start | bytes 430088 | tf_op jit(solution)/shard_map/ppermute | solution.py:17
  62.0 2.0 %collective-permute-done.15.refs_1_ = bf16[80,512]{1,0:T(8,128)(2,1)S(1)} collective-permute-done((bf16[80,512]{1,0:T(8,128)(2,1)S(1)}, bf16[80,512]{1,0:T(8,128)(2,1)S(1)}, u32[]{:S(2)}, u32[]{:S(2)}) %collective-permute-start.15) | collective-permute-done | bytes 81952 | tf_op jit(solution)/shard_map/ppermute | solution.py:17
  64.0 1.4 %down.2 = (bf16[40,1792]{1,0:T(8,128)(2,1)S(1)}, bf16[40,1792]{1,0:T(8,128)(2,1)S(1)}) custom-call(s32[1]{0:T(128)} %bitcast.8.block_ref, bf16[1,2048,1792]{2,1,0:T(8,128)(2,1)S(1)} %bitcast.15, bf16[80,512]{1,0:T(8,128)(2,1)S(1)} %collective-permute-done.14.refs_0_, bf16[80,512]{1,0:T(8,128)(2,1)S(1)} %collective-permute-done.15.refs_1_, ...), custom_call_target="tpu_custom_call" | custom-call | flops 587202560 | bytes 7340032 | tf_op jit(solution)/shard_map/down/pallas_call | solution.py:347
  65.4 0.8 %collective-permute-done.20.refs_2_ = bf16[40,1792]{1,0:T(8,128)(2,1)S(1)} collective-permute-done((bf16[40,1792]{1,0:T(8,128)(2,1)S(1)}, bf16[40,1792]{1,0:T(8,128)(2,1)S(1)}, u32[]{:S(2)}, u32[]{:S(2)}) %collective-permute-start.20) | collective-permute-done | bytes 143392 | tf_op jit(solution)/shard_map/ppermute | solution.py:17
  66.2 1.8 %collective-permute-done.21.refs_3_ = bf16[40,1792]{1,0:T(8,128)(2,1)S(1)} collective-permute-done((bf16[40,1792]{1,0:T(8,128)(2,1)S(1)}, bf16[40,1792]{1,0:T(8,128)(2,1)S(1)}, u32[]{:S(2)}, u32[]{:S(2)}) %collective-permute-start.21) | collective-permute-done | bytes 143392 | tf_op jit(solution)/shard_map/ppermute | solution.py:17
  68.0 1.0 %combine.1 = bf16[64,1792]{1,0:T(8,128)(2,1)} custom-call(bf16[64,160]{1,0:T(8,128)(2,1)S(1)} %get-tuple-element.32.high_ref, bf16[64,160]{1,0:T(8,128)(2,1)S(1)} %get-tuple-element.33.low_ref, bf16[40,1792]{1,0:T(8,128)(2,1)S(1)} %get-tuple-element.34.refs_0_, bf16[40,1792]{1,0:T(8,128)(2,1)S(1)} %collective-permute-done.17.refs_1_, ...), custom_call_target="tpu_custom_call" | custom-call | flops 73400320 | bytes 573440 | tf_op jit(solution)/shard_map/combine/pallas_call | solution.py:367
  (36 shorter events, 1.0 us)
Async XLA Ops:
  0.6 18.4 %copy-start.3 = (s32[64,2]{0,1:T(2,128)S(1)}, s32[64,2]{0,1:T(2,128)}, u32[]{:S(2)}) copy-start(s32[64,2]{0,1:T(2,128)} %param.10) | copy-start | bytes 1540
  0.6 26.8 %copy-start.4 = (bf16[1792]{0:T(1024)(128)(2,1)S(1)}, bf16[1792]{0:T(1024)(128)(2,1)}, u32[]{:S(2)}) copy-start(bf16[1792]{0:T(1024)(128)(2,1)} %param.9) | copy-start | bytes 10756
  2.1 9.5 %collective-permute-start.2 = (bf16[64,1792]{1,0:T(8,128)(2,1)S(1)}, bf16[64,1792]{1,0:T(8,128)(2,1)S(1)}, u32[]{:S(2)}, u32[]{:S(2)}) collective-permute-start(bf16[64,1792]{1,0:T(8,128)(2,1)S(1)} %get-tuple-element.38), channel_id=1, source_target_pairs={{0,1},{1,0},{2,3},{3,2},{4,5},{5,4},{6,7},{7,6},{8,9},{9,8},{10,11... | collective-permute-start | bytes 688136 | tf_op jit(solution)/shard_map/ppermute | solution.py:17
  5.2 14.3 %collective-permute-start = (bf16[64,1792]{1,0:T(8,128)(2,1)S(1)}, bf16[64,1792]{1,0:T(8,128)(2,1)S(1)}, u32[]{:S(2)}, u32[]{:S(2)}) collective-permute-start(bf16[64,1792]{1,0:T(8,128)(2,1)S(1)} %get-tuple-element.40), channel_id=1, source_target_pairs={{1,2},{2,1},{5,6},{6,5},{9,10},{10,9},{13,14},{14,13},{17,18},{18,... | collective-permute-start | bytes 688136 | tf_op jit(solution)/shard_map/ppermute | solution.py:221
  5.9 13.7 %collective-permute-start.1 = (bf16[64,1792]{1,0:T(8,128)(2,1)S(1)}, bf16[64,1792]{1,0:T(8,128)(2,1)S(1)}, u32[]{:S(2)}, u32[]{:S(2)}) collective-permute-start(bf16[64,1792]{1,0:T(8,128)(2,1)S(1)} %get-tuple-element.39.passing_ref), channel_id=1, source_target_pairs={{0,2},{3,1},{4,6},{7,5},{8,10},{11,9},{12,14},{15,13},{16,18},{19,... | collective-permute-start | bytes 688136 | tf_op jit(solution)/shard_map/ppermute | solution.py:222
  11.7 13.1 %collective-permute-start.3 = (bf16[64,1792]{1,0:T(8,128)(2,1)S(1)}, bf16[64,1792]{1,0:T(8,128)(2,1)S(1)}, u32[]{:S(2)}, u32[]{:S(2)}) collective-permute-start(bf16[64,1792]{1,0:T(8,128)(2,1)S(1)} %merge.1), channel_id=1, source_target_pairs={{0,1},{1,3},{2,0},{3,2},{4,5},{5,7},{6,4},{7,6},{8,9},{9,11},{10,8... | collective-permute-start | bytes 688136 | tf_op jit(solution)/shard_map/ppermute | solution.py:232
  14.2 3.1 %copy-start = (bf16[1,1792,2048]{2,1,0:T(8,128)(2,1)S(1)}, bf16[1,1792,2048]{2,1,0:T(8,128)(2,1)}, u32[]{:S(2)}) copy-start(bf16[1,1792,2048]{2,1,0:T(8,128)(2,1)} %refs_1_.1) | copy-start | bytes 22020100
  17.3 0.9 %copy-start.2 = (bf16[64,1792]{1,0:T(8,128)(2,1)S(1)}, bf16[64,1792]{1,0:T(8,128)(2,1)}, u32[]{:S(2)}) copy-start(bf16[64,1792]{1,0:T(8,128)(2,1)} %refs_0_.1) | copy-start | bytes 688132
  25.2 2.2 %collective-permute-start.6 = (bf16[40,1792]{1,0:T(8,128)(2,1)S(1)}, bf16[40,1792]{1,0:T(8,128)(2,1)S(1)}, u32[]{:S(2)}, u32[]{:S(2)}) collective-permute-start(bf16[40,1792]{1,0:T(8,128)(2,1)S(1)} %get-tuple-element.29), channel_id=1, source_target_pairs={{0,4},{4,0},{8,12},{12,8},{1,5},{5,1},{9,13},{13,9},{2,6},{6,2},{1... | collective-permute-start | bytes 430088 | tf_op jit(solution)/shard_map/ppermute | solution.py:17
  25.5 8.1 %collective-permute-start.4 = (bf16[40,1792]{1,0:T(8,128)(2,1)S(1)}, bf16[40,1792]{1,0:T(8,128)(2,1)S(1)}, u32[]{:S(2)}, u32[]{:S(2)}) collective-permute-start(bf16[40,1792]{1,0:T(8,128)(2,1)S(1)} %get-tuple-element.23), channel_id=1, source_target_pairs={{0,8},{4,12},{8,0},{12,4},{1,9},{5,13},{9,1},{13,5},{2,10},{6,14},... | collective-permute-start | bytes 430088 | tf_op jit(solution)/shard_map/ppermute | solution.py:17
  27.1 7.3 %collective-permute-start.5 = (bf16[40,1792]{1,0:T(8,128)(2,1)S(1)}, bf16[40,1792]{1,0:T(8,128)(2,1)S(1)}, u32[]{:S(2)}, u32[]{:S(2)}) collective-permute-start(bf16[40,1792]{1,0:T(8,128)(2,1)S(1)} %get-tuple-element.24), channel_id=1, source_target_pairs={{0,12},{4,8},{8,4},{12,0},{1,13},{5,9},{9,5},{13,1},{2,14},{6,10},... | collective-permute-start | bytes 430088 | tf_op jit(solution)/shard_map/ppermute | solution.py:17
  28.1 7.4 %collective-permute-start.9 = (bf16[88,512]{1,0:T(8,128)(2,1)S(1)}, bf16[88,512]{1,0:T(8,128)(2,1)S(1)}, u32[]{:S(2)}, u32[]{:S(2)}) collective-permute-start(bf16[88,512]{1,0:T(8,128)(2,1)S(1)} %gate.12), channel_id=1, source_target_pairs={{0,3},{1,2},{2,1},{3,0},{4,7},{5,6},{6,5},{7,4},{8,11},{9,10},{10,... | collective-permute-start | bytes 270344 | tf_op jit(solution)/shard_map/ppermute | solution.py:17
  31.3 7.5 %collective-permute-start.8 = (bf16[88,512]{1,0:T(8,128)(2,1)S(1)}, bf16[88,512]{1,0:T(8,128)(2,1)S(1)}, u32[]{:S(2)}, u32[]{:S(2)}) collective-permute-start(bf16[88,512]{1,0:T(8,128)(2,1)S(1)} %gate.11), channel_id=1, source_target_pairs={{0,2},{1,3},{2,0},{3,1},{4,6},{5,7},{6,4},{7,5},{8,10},{9,11},{10,... | collective-permute-start | bytes 270344 | tf_op jit(solution)/shard_map/ppermute | solution.py:17
  31.8 7.9 %collective-permute-start.7 = (bf16[88,512]{1,0:T(8,128)(2,1)S(1)}, bf16[88,512]{1,0:T(8,128)(2,1)S(1)}, u32[]{:S(2)}, u32[]{:S(2)}) collective-permute-start(bf16[88,512]{1,0:T(8,128)(2,1)S(1)} %gate.8), channel_id=1, source_target_pairs={{0,1},{1,0},{2,3},{3,2},{4,5},{5,4},{6,7},{7,6},{8,9},{9,8},{10,11... | collective-permute-start | bytes 270344 | tf_op jit(solution)/shard_map/ppermute | solution.py:17
  35.9 9.2 %collective-permute-start.12 = (bf16[88,512]{1,0:T(8,128)(2,1)S(1)}, bf16[88,512]{1,0:T(8,128)(2,1)S(1)}, u32[]{:S(2)}, u32[]{:S(2)}) collective-permute-start(bf16[88,512]{1,0:T(8,128)(2,1)S(1)} %gate.15), channel_id=1, source_target_pairs={{0,3},{1,2},{2,1},{3,0},{4,7},{5,6},{6,5},{7,4},{8,11},{9,10},{10,... | collective-permute-start | bytes 270344 | tf_op jit(solution)/shard_map/ppermute | solution.py:17
  39.3 7.4 %collective-permute-start.11 = (bf16[88,512]{1,0:T(8,128)(2,1)S(1)}, bf16[88,512]{1,0:T(8,128)(2,1)S(1)}, u32[]{:S(2)}, u32[]{:S(2)}) collective-permute-start(bf16[88,512]{1,0:T(8,128)(2,1)S(1)} %gate.14), channel_id=1, source_target_pairs={{0,2},{1,3},{2,0},{3,1},{4,6},{5,7},{6,4},{7,5},{8,10},{9,11},{10,... | collective-permute-start | bytes 270344 | tf_op jit(solution)/shard_map/ppermute | solution.py:17
  40.1 7.3 %collective-permute-start.10 = (bf16[88,512]{1,0:T(8,128)(2,1)S(1)}, bf16[88,512]{1,0:T(8,128)(2,1)S(1)}, u32[]{:S(2)}, u32[]{:S(2)}) collective-permute-start(bf16[88,512]{1,0:T(8,128)(2,1)S(1)} %gate.9.after_ref), channel_id=1, source_target_pairs={{0,1},{1,0},{2,3},{3,2},{4,5},{5,4},{6,7},{7,6},{8,9},{9,8},{10,11... | collective-permute-start | bytes 270344 | tf_op jit(solution)/shard_map/ppermute | solution.py:17
  43.7 0.9 %copy-start.1 = (bf16[64,1792]{1,0:T(8,128)(2,1)S(1)}, bf16[64,1792]{1,0:T(8,128)(2,1)}, u32[]{:S(2)}) copy-start(bf16[64,1792]{1,0:T(8,128)(2,1)} %store.1.refs_1_) | copy-start | bytes 688132
  44.6 14.3 %slice-start = ((s8[7340032]{0:T(1024)(128)(4,1)}), s8[4194304]{0:T(1024)(128)(4,1)S(1)}, s32[]{:S(2)}) async-start(s8[7340032]{0:T(1024)(128)(4,1)} %bitcast.14), calls=%async_computation | async-start | bytes 8388608
  45.1 13.9 %slice-start.1 = ((s8[7340032]{0:T(1024)(128)(4,1)}), s8[3145728]{0:T(1024)(128)(4,1)S(1)}, s32[]{:S(2)}) async-start(s8[7340032]{0:T(1024)(128)(4,1)} %bitcast.14), calls=%async_computation.1 | async-start | bytes 6291456
  47.6 6.7 %collective-permute-start.13 = (bf16[80,512]{1,0:T(8,128)(2,1)S(1)}, bf16[80,512]{1,0:T(8,128)(2,1)S(1)}, u32[]{:S(2)}, u32[]{:S(2)}) collective-permute-start(bf16[80,512]{1,0:T(8,128)(2,1)S(1)} %activate.2.refs_3_), channel_id=1, source_target_pairs={{0,3},{1,2},{2,1},{3,0},{4,7},{5,6},{6,5},{7,4},{8,11},{9,10},{10,... | collective-permute-start | bytes 245768 | tf_op jit(solution)/shard_map/ppermute | solution.py:17
  49.6 9.3 %collective-permute-start.18 = (bf16[80,512]{1,0:T(8,128)(2,1)S(1)}, bf16[80,512]{1,0:T(8,128)(2,1)S(1)}, u32[]{:S(2)}, u32[]{:S(2)}) collective-permute-start(bf16[80,512]{1,0:T(8,128)(2,1)S(1)} %activate.2.refs_3_), channel_id=1, source_target_pairs={{0,2},{1,3},{2,0},{3,1},{4,6},{5,7},{6,4},{7,5},{8,10},{9,11},{10,... | collective-permute-start | bytes 245768 | tf_op jit(solution)/shard_map/ppermute | solution.py:17
  49.6 9.3 %collective-permute-start.19 = (bf16[80,512]{1,0:T(8,128)(2,1)S(1)}, bf16[80,512]{1,0:T(8,128)(2,1)S(1)}, u32[]{:S(2)}, u32[]{:S(2)}) collective-permute-start(bf16[80,512]{1,0:T(8,128)(2,1)S(1)} %activate.2.refs_3_), channel_id=1, source_target_pairs={{0,1},{1,0},{2,3},{3,2},{4,5},{5,4},{6,7},{7,6},{8,9},{9,8},{10,11... | collective-permute-start | bytes 245768 | tf_op jit(solution)/shard_map/ppermute | solution.py:17
  54.5 7.4 %collective-permute-start.14 = (bf16[80,512]{1,0:T(8,128)(2,1)S(1)}, bf16[80,512]{1,0:T(8,128)(2,1)S(1)}, u32[]{:S(2)}, u32[]{:S(2)}) collective-permute-start(bf16[80,512]{1,0:T(8,128)(2,1)S(1)} %activate.3.refs_3_), channel_id=1, source_target_pairs={{0,3},{1,2},{2,1},{3,0},{4,7},{5,6},{6,5},{7,4},{8,11},{9,10},{10,... | collective-permute-start | bytes 245768 | tf_op jit(solution)/shard_map/ppermute | solution.py:17
  57.2 6.8 %collective-permute-start.15 = (bf16[80,512]{1,0:T(8,128)(2,1)S(1)}, bf16[80,512]{1,0:T(8,128)(2,1)S(1)}, u32[]{:S(2)}, u32[]{:S(2)}) collective-permute-start(bf16[80,512]{1,0:T(8,128)(2,1)S(1)} %activate.3.refs_3_), channel_id=1, source_target_pairs={{0,2},{1,3},{2,0},{3,1},{4,6},{5,7},{6,4},{7,5},{8,10},{9,11},{10,... | collective-permute-start | bytes 245768 | tf_op jit(solution)/shard_map/ppermute | solution.py:17
  57.2 6.8 %collective-permute-start.16 = (bf16[80,512]{1,0:T(8,128)(2,1)S(1)}, bf16[80,512]{1,0:T(8,128)(2,1)S(1)}, u32[]{:S(2)}, u32[]{:S(2)}) collective-permute-start(bf16[80,512]{1,0:T(8,128)(2,1)S(1)} %activate.3.refs_3_), channel_id=1, source_target_pairs={{0,1},{1,0},{2,3},{3,2},{4,5},{5,4},{6,7},{7,6},{8,9},{9,8},{10,11... | collective-permute-start | bytes 245768 | tf_op jit(solution)/shard_map/ppermute | solution.py:17
  60.4 5.8 %collective-permute-start.20 = (bf16[40,1792]{1,0:T(8,128)(2,1)S(1)}, bf16[40,1792]{1,0:T(8,128)(2,1)S(1)}, u32[]{:S(2)}, u32[]{:S(2)}) collective-permute-start(bf16[40,1792]{1,0:T(8,128)(2,1)S(1)} %get-tuple-element.36), channel_id=1, source_target_pairs={{0,8},{4,12},{8,0},{12,4},{1,9},{5,13},{9,1},{13,5},{2,10},{6,14},... | collective-permute-start | bytes 430088 | tf_op jit(solution)/shard_map/ppermute | solution.py:17
  61.9 6.0 %collective-permute-start.21 = (bf16[40,1792]{1,0:T(8,128)(2,1)S(1)}, bf16[40,1792]{1,0:T(8,128)(2,1)S(1)}, u32[]{:S(2)}, u32[]{:S(2)}) collective-permute-start(bf16[40,1792]{1,0:T(8,128)(2,1)S(1)} %get-tuple-element.37), channel_id=1, source_target_pairs={{0,12},{4,8},{8,4},{12,0},{1,13},{5,9},{9,5},{13,1},{2,14},{6,10},... | collective-permute-start | bytes 430088 | tf_op jit(solution)/shard_map/ppermute | solution.py:17
  65.4 2.6 %collective-permute-start.17 = (bf16[40,1792]{1,0:T(8,128)(2,1)S(1)}, bf16[40,1792]{1,0:T(8,128)(2,1)S(1)}, u32[]{:S(2)}, u32[]{:S(2)}) collective-permute-start(bf16[40,1792]{1,0:T(8,128)(2,1)S(1)} %get-tuple-element.35), channel_id=1, source_target_pairs={{0,4},{4,0},{8,12},{12,8},{1,5},{5,1},{9,13},{13,9},{2,6},{6,2},{1... | collective-permute-start | bytes 430088 | tf_op jit(solution)/shard_map/ppermute | solution.py:17

commit v5 on v4

--- a/solution.py
+++ b/solution.py
@@ -294,7 +294,7 @@
         )(norm_gain[None, :], *[arrived[k] for k in ks])
         tall = count + extra_rows(count, ff)
         gates = {}
-        for k in partners(nt):
+        for k in ([1, 3, 2, 0] if nt == 4 and after is not None else partners(nt)):
             earlier = [] if after is None else [after[k or 1]]
             if k == 0 and after is not None:
                 stored.append(

time: 69.3 us -> 68.8 us (level)
  starting transfers between devices: 33.6 us -> 32.5 us
    ppermute x19, starting transfers between devices: 26.2 us -> 25.1 us  [exchange(): return lax.ppermute(value, axis, [(i, i ^ step) for i in range(n)])]
where the time goes in v5:
time: 68.8 us; the launch traced here: 68.5 us
  starting transfers between devices  32.5 us (47%)
  waiting for transfers between devices  16.3 us (24%)
  Pallas kernels  10.8 us (16%)
  local copies, waits for them, and re-layouts  7.96 us (12%)
  between operations  0.94 us (1%)
    ppermute x19, starting transfers between devices, exchange(): return lax.ppermute(value, axis, [(i, i ^ step) for i in range(n)])  25.1 us
    ppermute x19, waiting for transfers between devices, exchange(): return lax.ppermute(value, axis, [(i, i ^ step) for i in range(n)])  11 us
    unnamed x16, local copies, waits for them, and re-layouts  6.52 us
    ppermute x1, starting transfers between devices, local(): parts.append(lax.ppermute(block(z ^ 2), 'tensor', [(0, 2), (3, 1)]))  5.75 us
    ppermute x1, waiting for transfers between devices, local(): lax.ppermute(merged, 'tensor', [(0, 1), (1, 3), (2, 0), (3, 2)])  5.28 us
    pallas_call x8, Pallas kernels, summed_gate(): pl.pallas_call(gate_kernel, out_shape=sds((tall, ff), bf16), grid_spec=pl...  3.58 us
    pallas_call x2, Pallas kernels, produced(): pl.pallas_call(functools.partial(down_kernel, nt, len(ks), cap), out_shap...  2.78 us
    dynamic_slice x1, local copies, waits for them, and re-layouts, block(): return lax.dynamic_slice(attn_partial[0], (0, k * share), (tokens, share))  1.44 us
  transfers between devices with their start and end apart: 22, of which 10 were waited for; matrix products, arithmetic and copies ran while one was open for 2% of the time, Pallas kernels for 13%

profile of v5, /device:TPU:0, one launch (start us, length us, event | category | flops | bytes accessed | tf_op | source)
XLA Modules:
  0.0 68.5 jit_solution(12353758934959674868)
XLA Ops:
  0.7 1.4 %dynamic-slice_bitcast_fusion = (bf16[64,1792]{1,0:T(8,128)(2,1)S(1)}, bf16[64,1792]{1,0:T(8,128)(2,1)S(1)}, bf16[64,1792]{1,0:T(8,128)(2,1)S(1)}, bf16[64,1792]{1,0:T(8,128)(2,1)S(1)}, bf16[64,1792]{1,0:T(8,128)(2,1)S(1)}) fusion(bf16[1,64,7168]{2,1,0:T(8,128)(2,1)} %param.8, s32[]{:T(128)S(6)} %select_n.30, s32[]{:T(128)S(6)} %select_n.27, s32[]{:T(128)S(6)} %select_n.26, ...), kind=kLoop, calls=%fused_computation | loop fusion | bytes 2293780 | tf_op jit(solution)/shard_map/dynamic_slice | solution.py:214
  2.1 3.1 %collective-permute-start.2 = (bf16[64,1792]{1,0:T(8,128)(2,1)S(1)}, bf16[64,1792]{1,0:T(8,128)(2,1)S(1)}, u32[]{:S(2)}, u32[]{:S(2)}) collective-permute-start(bf16[64,1792]{1,0:T(8,128)(2,1)S(1)} %get-tuple-element.38), channel_id=1, source_target_pairs={{0,1},{1,0},{2,3},{3,2},{4,5},{5,4},{6,7},{7,6},{8,9},{9,8},{10,11... | collective-permute-start | bytes 688136 | tf_op jit(solution)/shard_map/ppermute | solution.py:17
  5.2 0.7 collective-permute-start
  5.9 5.8 %collective-permute-start.1 = (bf16[64,1792]{1,0:T(8,128)(2,1)S(1)}, bf16[64,1792]{1,0:T(8,128)(2,1)S(1)}, u32[]{:S(2)}, u32[]{:S(2)}) collective-permute-start(bf16[64,1792]{1,0:T(8,128)(2,1)S(1)} %get-tuple-element.39.passing_ref), channel_id=1, source_target_pairs={{0,2},{3,1},{4,6},{7,5},{8,10},{11,9},{12,14},{15,13},{16,18},{19,... | collective-permute-start | bytes 688136 | tf_op jit(solution)/shard_map/ppermute | solution.py:222
  11.7 1.0 %collective-permute-start.3 = (bf16[64,1792]{1,0:T(8,128)(2,1)S(1)}, bf16[64,1792]{1,0:T(8,128)(2,1)S(1)}, u32[]{:S(2)}, u32[]{:S(2)}) collective-permute-start(bf16[64,1792]{1,0:T(8,128)(2,1)S(1)} %merge.1), channel_id=1, source_target_pairs={{0,1},{1,3},{2,0},{3,2},{4,5},{5,7},{6,4},{7,6},{8,9},{9,11},{10,8... | collective-permute-start | bytes 688136 | tf_op jit(solution)/shard_map/ppermute | solution.py:232
  12.7 0.8 %copy.10.scores_ref = f32[64,2]{1,0:T(8,128)S(1)} copy(f32[64,2]{0,1:T(2,128)} %param.11) | data formatting | bytes 1024 | tf_op args[4]
  13.4 0.8 %copy.9.ids_ref = s32[64,2]{1,0:T(8,128)S(1)} copy(s32[64,2]{0,1:T(2,128)} %param.10) | data formatting | bytes 1024 | tf_op args[3]
  14.2 3.1 %copy-done = bf16[1,1792,2048]{2,1,0:T(8,128)(2,1)S(1)} copy-done((bf16[1,1792,2048]{2,1,0:T(8,128)(2,1)S(1)}, bf16[1,1792,2048]{2,1,0:T(8,128)(2,1)}, u32[]{:S(2)}) %copy-start) | copy-done | bytes 7340056
  17.3 0.9 %copy-done.2 = bf16[64,1792]{1,0:T(8,128)(2,1)S(1)} copy-done((bf16[64,1792]{1,0:T(8,128)(2,1)S(1)}, bf16[64,1792]{1,0:T(8,128)(2,1)}, u32[]{:S(2)}) %copy-start.2) | copy-done | bytes 229400
  18.2 0.8 %fetch.1 = (bf16[64,1792]{1,0:T(8,128)(2,1)S(1)}, bf16[1,1792,2048]{2,1,0:T(8,128)(2,1)S(1)}) custom-call(bf16[64,1792]{1,0:T(8,128)(2,1)S(1)} %copy-done.2, bf16[1,1792,2048]{2,1,0:T(8,128)(2,1)S(1)} %copy-done), custom_call_target="tpu_custom_call" | custom-call | flops 1000000 | bytes 7569408 | tf_op jit(solution)/shard_map/fetch/pallas_call | solution.py:249
  19.0 0.5 routing.1
  19.6 5.3 %collective-permute-done.3.refs_3_ = bf16[64,1792]{1,0:T(8,128)(2,1)S(1)} collective-permute-done((bf16[64,1792]{1,0:T(8,128)(2,1)S(1)}, bf16[64,1792]{1,0:T(8,128)(2,1)S(1)}, u32[]{:S(2)}, u32[]{:S(2)}) %collective-permute-start.3) | collective-permute-done | bytes 229408 | tf_op jit(solution)/shard_map/ppermute | solution.py:232
  24.9 0.4 add.22
  25.3 0.2 pack.1
  25.5 1.6 %collective-permute-start.4 = (bf16[40,1792]{1,0:T(8,128)(2,1)S(1)}, bf16[40,1792]{1,0:T(8,128)(2,1)S(1)}, u32[]{:S(2)}, u32[]{:S(2)}) collective-permute-start(bf16[40,1792]{1,0:T(8,128)(2,1)S(1)} %get-tuple-element.23), channel_id=1, source_target_pairs={{0,8},{4,12},{8,0},{12,4},{1,9},{5,13},{9,1},{13,5},{2,10},{6,14},... | collective-permute-start | bytes 430088 | tf_op jit(solution)/shard_map/ppermute | solution.py:17
  27.1 0.4 collective-permute-start.5
  27.6 0.5 gate.12
  28.1 2.7 %collective-permute-start.9 = (bf16[88,512]{1,0:T(8,128)(2,1)S(1)}, bf16[88,512]{1,0:T(8,128)(2,1)S(1)}, u32[]{:S(2)}, u32[]{:S(2)}) collective-permute-start(bf16[88,512]{1,0:T(8,128)(2,1)S(1)} %gate.12), channel_id=1, source_target_pairs={{0,3},{1,2},{2,1},{3,0},{4,7},{5,6},{6,5},{7,4},{8,11},{9,10},{10,... | collective-permute-start | bytes 270344 | tf_op jit(solution)/shard_map/ppermute | solution.py:17
  30.8 0.4 gate.11
  31.4 0.4 gate.8
  31.8 1.8 %collective-permute-start.7 = (bf16[88,512]{1,0:T(8,128)(2,1)S(1)}, bf16[88,512]{1,0:T(8,128)(2,1)S(1)}, u32[]{:S(2)}, u32[]{:S(2)}) collective-permute-start(bf16[88,512]{1,0:T(8,128)(2,1)S(1)} %gate.8), channel_id=1, source_target_pairs={{0,2},{1,3},{2,0},{3,1},{4,6},{5,7},{6,4},{7,5},{8,10},{9,11},{10,... | collective-permute-start | bytes 270344 | tf_op jit(solution)/shard_map/ppermute | solution.py:17
  33.6 0.8 %collective-permute-done.5.refs_1_ = bf16[40,1792]{1,0:T(8,128)(2,1)S(1)} collective-permute-done((bf16[40,1792]{1,0:T(8,128)(2,1)S(1)}, bf16[40,1792]{1,0:T(8,128)(2,1)S(1)}, u32[]{:S(2)}, u32[]{:S(2)}) %collective-permute-start.5) | collective-permute-done | bytes 143392 | tf_op jit(solution)/shard_map/ppermute | solution.py:17
  34.6 0.8 %collective-permute-done.9.refs_0_.refs_3_ = bf16[88,512]{1,0:T(8,128)(2,1)S(1)} collective-permute-done((bf16[88,512]{1,0:T(8,128)(2,1)S(1)}, bf16[88,512]{1,0:T(8,128)(2,1)S(1)}, u32[]{:S(2)}, u32[]{:S(2)}) %collective-permute-start.9) | collective-permute-done | bytes 90144 | tf_op jit(solution)/shard_map/ppermute | solution.py:17
  35.4 0.4 gate.15
  35.9 2.7 %collective-permute-start.12 = (bf16[88,512]{1,0:T(8,128)(2,1)S(1)}, bf16[88,512]{1,0:T(8,128)(2,1)S(1)}, u32[]{:S(2)}, u32[]{:S(2)}) collective-permute-start(bf16[88,512]{1,0:T(8,128)(2,1)S(1)} %gate.15), channel_id=1, source_target_pairs={{0,3},{1,2},{2,1},{3,0},{4,7},{5,6},{6,5},{7,4},{8,11},{9,10},{10,... | collective-permute-start | bytes 270344 | tf_op jit(solution)/shard_map/ppermute | solution.py:17
  38.6 0.4 gate.14
  39.2 0.6 collective-permute-done.7.refs_0_.refs_2_
  39.8 0.4 gate.9.after_ref
  40.2 2.1 %collective-permute-start.11 = (bf16[88,512]{1,0:T(8,128)(2,1)S(1)}, bf16[88,512]{1,0:T(8,128)(2,1)S(1)}, u32[]{:S(2)}, u32[]{:S(2)}) collective-permute-start(bf16[88,512]{1,0:T(8,128)(2,1)S(1)} %gate.9.after_ref), channel_id=1, source_target_pairs={{0,2},{1,3},{2,0},{3,1},{4,6},{5,7},{6,4},{7,5},{8,10},{9,11},{10,... | collective-permute-start | bytes 270344 | tf_op jit(solution)/shard_map/ppermute | solution.py:17
  42.3 0.7 %store.1.refs_1_ = bf16[64,1792]{1,0:T(8,128)(2,1)} custom-call(bf16[64,1792]{1,0:T(8,128)(2,1)S(1)} %get-tuple-element.22.stream_ref.values_ref, bf16[88,512]{1,0:T(8,128)(2,1)S(1)} %gate.9.after_ref), custom_call_target="tpu_custom_call" | custom-call | flops 1000000 | bytes 458752 | tf_op jit(solution)/shard_map/store/pallas_call | solution.py:301
  43.0 0.9 %copy-done.1 = bf16[64,1792]{1,0:T(8,128)(2,1)S(1)} copy-done((bf16[64,1792]{1,0:T(8,128)(2,1)S(1)}, bf16[64,1792]{1,0:T(8,128)(2,1)}, u32[]{:S(2)}) %copy-start.1) | copy-done | bytes 229400
  44.0 0.4 gate.13.refs_0_
  44.5 0.6 collective-permute-done.10.refs_1_
  45.0 2.1 %collective-permute-done.11.refs_2_ = bf16[88,512]{1,0:T(8,128)(2,1)S(1)} collective-permute-done((bf16[88,512]{1,0:T(8,128)(2,1)S(1)}, bf16[88,512]{1,0:T(8,128)(2,1)S(1)}, u32[]{:S(2)}, u32[]{:S(2)}) %collective-permute-start.11) | collective-permute-done | bytes 90144 | tf_op jit(solution)/shard_map/ppermute | solution.py:17
  47.3 2.3 %collective-permute-start.13 = (bf16[80,512]{1,0:T(8,128)(2,1)S(1)}, bf16[80,512]{1,0:T(8,128)(2,1)S(1)}, u32[]{:S(2)}, u32[]{:S(2)}) collective-permute-start(bf16[80,512]{1,0:T(8,128)(2,1)S(1)} %activate.2.refs_3_), channel_id=1, source_target_pairs={{0,3},{1,2},{2,1},{3,0},{4,7},{5,6},{6,5},{7,4},{8,11},{9,10},{10,... | collective-permute-start | bytes 245768 | tf_op jit(solution)/shard_map/ppermute | solution.py:17
  49.6 2.1 %collective-permute-start.19 = (bf16[80,512]{1,0:T(8,128)(2,1)S(1)}, bf16[80,512]{1,0:T(8,128)(2,1)S(1)}, u32[]{:S(2)}, u32[]{:S(2)}) collective-permute-start(bf16[80,512]{1,0:T(8,128)(2,1)S(1)} %activate.2.refs_3_), channel_id=1, source_target_pairs={{0,1},{1,0},{2,3},{3,2},{4,5},{5,4},{6,7},{7,6},{8,9},{9,8},{10,11... | collective-permute-start | bytes 245768 | tf_op jit(solution)/shard_map/ppermute | solution.py:17
  51.8 0.4 gate.10.refs_0_
  52.2 1.5 %collective-permute-done.13.refs_4_.refs_0_ = bf16[80,512]{1,0:T(8,128)(2,1)S(1)} collective-permute-done((bf16[80,512]{1,0:T(8,128)(2,1)S(1)}, bf16[80,512]{1,0:T(8,128)(2,1)S(1)}, u32[]{:S(2)}, u32[]{:S(2)}) %collective-permute-start.13) | collective-permute-done | bytes 81952 | tf_op jit(solution)/shard_map/ppermute | solution.py:17
  54.0 2.3 %collective-permute-start.14 = (bf16[80,512]{1,0:T(8,128)(2,1)S(1)}, bf16[80,512]{1,0:T(8,128)(2,1)S(1)}, u32[]{:S(2)}, u32[]{:S(2)}) collective-permute-start(bf16[80,512]{1,0:T(8,128)(2,1)S(1)} %activate.3.refs_3_), channel_id=1, source_target_pairs={{0,3},{1,2},{2,1},{3,0},{4,7},{5,6},{6,5},{7,4},{8,11},{9,10},{10,... | collective-permute-start | bytes 245768 | tf_op jit(solution)/shard_map/ppermute | solution.py:17
  56.3 0.4 collective-permute-start.15
  56.7 1.7 %collective-permute-start.16 = (bf16[80,512]{1,0:T(8,128)(2,1)S(1)}, bf16[80,512]{1,0:T(8,128)(2,1)S(1)}, u32[]{:S(2)}, u32[]{:S(2)}) collective-permute-start(bf16[80,512]{1,0:T(8,128)(2,1)S(1)} %activate.3.refs_3_), channel_id=1, source_target_pairs={{0,1},{1,0},{2,3},{3,2},{4,5},{5,4},{6,7},{7,6},{8,9},{9,8},{10,11... | collective-permute-start | bytes 245768 | tf_op jit(solution)/shard_map/ppermute | solution.py:17
  58.5 1.4 %down.3 = (bf16[40,1792]{1,0:T(8,128)(2,1)S(1)}, bf16[40,1792]{1,0:T(8,128)(2,1)S(1)}) custom-call(s32[1]{0:T(128)} %bitcast.8.block_ref, bf16[1,2048,1792]{2,1,0:T(8,128)(2,1)S(1)} %bitcast.15, bf16[80,512]{1,0:T(8,128)(2,1)S(1)} %collective-permute-done.13.refs_4_.refs_0_, bf16[80,512]{1,0:T(8,128)(2,1)S(1)} %collective-permute-done.18.refs_1_, ...), custom_call_target="tpu_custom_call" | custom-call | flops 587202560 | bytes 7340032 | tf_op jit(solution)/shard_map/down/pallas_call | solution.py:347
  59.9 1.6 %collective-permute-start.20 = (bf16[40,1792]{1,0:T(8,128)(2,1)S(1)}, bf16[40,1792]{1,0:T(8,128)(2,1)S(1)}, u32[]{:S(2)}, u32[]{:S(2)}) collective-permute-start(bf16[40,1792]{1,0:T(8,128)(2,1)S(1)} %get-tuple-element.36), channel_id=1, source_target_pairs={{0,8},{4,12},{8,0},{12,4},{1,9},{5,13},{9,1},{13,5},{2,10},{6,14},... | collective-permute-start | bytes 430088 | tf_op jit(solution)/shard_map/ppermute | solution.py:17
  61.4 1.1 %collective-permute-done.15.refs_1_ = bf16[80,512]{1,0:T(8,128)(2,1)S(1)} collective-permute-done((bf16[80,512]{1,0:T(8,128)(2,1)S(1)}, bf16[80,512]{1,0:T(8,128)(2,1)S(1)}, u32[]{:S(2)}, u32[]{:S(2)}) %collective-permute-start.15) | collective-permute-done | bytes 81952 | tf_op jit(solution)/shard_map/ppermute | solution.py:17
  62.5 1.4 %down.2 = (bf16[40,1792]{1,0:T(8,128)(2,1)S(1)}, bf16[40,1792]{1,0:T(8,128)(2,1)S(1)}) custom-call(s32[1]{0:T(128)} %bitcast.8.block_ref, bf16[1,2048,1792]{2,1,0:T(8,128)(2,1)S(1)} %bitcast.15, bf16[80,512]{1,0:T(8,128)(2,1)S(1)} %collective-permute-done.14.refs_0_, bf16[80,512]{1,0:T(8,128)(2,1)S(1)} %collective-permute-done.15.refs_1_, ...), custom_call_target="tpu_custom_call" | custom-call | flops 587202560 | bytes 7340032 | tf_op jit(solution)/shard_map/down/pallas_call | solution.py:347
  64.0 1.7 %collective-permute-done.20.refs_2_ = bf16[40,1792]{1,0:T(8,128)(2,1)S(1)} collective-permute-done((bf16[40,1792]{1,0:T(8,128)(2,1)S(1)}, bf16[40,1792]{1,0:T(8,128)(2,1)S(1)}, u32[]{:S(2)}, u32[]{:S(2)}) %collective-permute-start.20) | collective-permute-done | bytes 143392 | tf_op jit(solution)/shard_map/ppermute | solution.py:17
  65.7 1.8 %collective-permute-done.21.refs_3_ = bf16[40,1792]{1,0:T(8,128)(2,1)S(1)} collective-permute-done((bf16[40,1792]{1,0:T(8,128)(2,1)S(1)}, bf16[40,1792]{1,0:T(8,128)(2,1)S(1)}, u32[]{:S(2)}, u32[]{:S(2)}) %collective-permute-start.21) | collective-permute-done | bytes 143392 | tf_op jit(solution)/shard_map/ppermute | solution.py:17
  67.5 1.0 %combine.1 = bf16[64,1792]{1,0:T(8,128)(2,1)} custom-call(bf16[64,160]{1,0:T(8,128)(2,1)S(1)} %get-tuple-element.32.high_ref, bf16[64,160]{1,0:T(8,128)(2,1)S(1)} %get-tuple-element.33.low_ref, bf16[40,1792]{1,0:T(8,128)(2,1)S(1)} %get-tuple-element.34.refs_0_, bf16[40,1792]{1,0:T(8,128)(2,1)S(1)} %collective-permute-done.17.refs_1_, ...), custom_call_target="tpu_custom_call" | custom-call | flops 73400320 | bytes 573440 | tf_op jit(solution)/shard_map/combine/pallas_call | solution.py:367
  (36 shorter events, 1.2 us)
Async XLA Ops:
  0.6 18.4 %copy-start.3 = (s32[64,2]{0,1:T(2,128)S(1)}, s32[64,2]{0,1:T(2,128)}, u32[]{:S(2)}) copy-start(s32[64,2]{0,1:T(2,128)} %param.10) | copy-start | bytes 1540
  0.6 26.8 %copy-start.4 = (bf16[1792]{0:T(1024)(128)(2,1)S(1)}, bf16[1792]{0:T(1024)(128)(2,1)}, u32[]{:S(2)}) copy-start(bf16[1792]{0:T(1024)(128)(2,1)} %param.9) | copy-start | bytes 10756
  2.1 9.5 %collective-permute-start.2 = (bf16[64,1792]{1,0:T(8,128)(2,1)S(1)}, bf16[64,1792]{1,0:T(8,128)(2,1)S(1)}, u32[]{:S(2)}, u32[]{:S(2)}) collective-permute-start(bf16[64,1792]{1,0:T(8,128)(2,1)S(1)} %get-tuple-element.38), channel_id=1, source_target_pairs={{0,1},{1,0},{2,3},{3,2},{4,5},{5,4},{6,7},{7,6},{8,9},{9,8},{10,11... | collective-permute-start | bytes 688136 | tf_op jit(solution)/shard_map/ppermute | solution.py:17
  5.2 14.3 %collective-permute-start = (bf16[64,1792]{1,0:T(8,128)(2,1)S(1)}, bf16[64,1792]{1,0:T(8,128)(2,1)S(1)}, u32[]{:S(2)}, u32[]{:S(2)}) collective-permute-start(bf16[64,1792]{1,0:T(8,128)(2,1)S(1)} %get-tuple-element.40), channel_id=1, source_target_pairs={{1,2},{2,1},{5,6},{6,5},{9,10},{10,9},{13,14},{14,13},{17,18},{18,... | collective-permute-start | bytes 688136 | tf_op jit(solution)/shard_map/ppermute | solution.py:221
  5.9 13.7 %collective-permute-start.1 = (bf16[64,1792]{1,0:T(8,128)(2,1)S(1)}, bf16[64,1792]{1,0:T(8,128)(2,1)S(1)}, u32[]{:S(2)}, u32[]{:S(2)}) collective-permute-start(bf16[64,1792]{1,0:T(8,128)(2,1)S(1)} %get-tuple-element.39.passing_ref), channel_id=1, source_target_pairs={{0,2},{3,1},{4,6},{7,5},{8,10},{11,9},{12,14},{15,13},{16,18},{19,... | collective-permute-start | bytes 688136 | tf_op jit(solution)/shard_map/ppermute | solution.py:222
  11.7 13.1 %collective-permute-start.3 = (bf16[64,1792]{1,0:T(8,128)(2,1)S(1)}, bf16[64,1792]{1,0:T(8,128)(2,1)S(1)}, u32[]{:S(2)}, u32[]{:S(2)}) collective-permute-start(bf16[64,1792]{1,0:T(8,128)(2,1)S(1)} %merge.1), channel_id=1, source_target_pairs={{0,1},{1,3},{2,0},{3,2},{4,5},{5,7},{6,4},{7,6},{8,9},{9,11},{10,8... | collective-permute-start | bytes 688136 | tf_op jit(solution)/shard_map/ppermute | solution.py:232
  14.2 3.1 %copy-start = (bf16[1,1792,2048]{2,1,0:T(8,128)(2,1)S(1)}, bf16[1,1792,2048]{2,1,0:T(8,128)(2,1)}, u32[]{:S(2)}) copy-start(bf16[1,1792,2048]{2,1,0:T(8,128)(2,1)} %refs_1_.1) | copy-start | bytes 22020100
  17.3 0.9 %copy-start.2 = (bf16[64,1792]{1,0:T(8,128)(2,1)S(1)}, bf16[64,1792]{1,0:T(8,128)(2,1)}, u32[]{:S(2)}) copy-start(bf16[64,1792]{1,0:T(8,128)(2,1)} %refs_0_.1) | copy-start | bytes 688132
  25.2 2.2 %collective-permute-start.6 = (bf16[40,1792]{1,0:T(8,128)(2,1)S(1)}, bf16[40,1792]{1,0:T(8,128)(2,1)S(1)}, u32[]{:S(2)}, u32[]{:S(2)}) collective-permute-start(bf16[40,1792]{1,0:T(8,128)(2,1)S(1)} %get-tuple-element.29), channel_id=1, source_target_pairs={{0,4},{4,0},{8,12},{12,8},{1,5},{5,1},{9,13},{13,9},{2,6},{6,2},{1... | collective-permute-start | bytes 430088 | tf_op jit(solution)/shard_map/ppermute | solution.py:17
  25.5 8.1 %collective-permute-start.4 = (bf16[40,1792]{1,0:T(8,128)(2,1)S(1)}, bf16[40,1792]{1,0:T(8,128)(2,1)S(1)}, u32[]{:S(2)}, u32[]{:S(2)}) collective-permute-start(bf16[40,1792]{1,0:T(8,128)(2,1)S(1)} %get-tuple-element.23), channel_id=1, source_target_pairs={{0,8},{4,12},{8,0},{12,4},{1,9},{5,13},{9,1},{13,5},{2,10},{6,14},... | collective-permute-start | bytes 430088 | tf_op jit(solution)/shard_map/ppermute | solution.py:17
  27.1 7.3 %collective-permute-start.5 = (bf16[40,1792]{1,0:T(8,128)(2,1)S(1)}, bf16[40,1792]{1,0:T(8,128)(2,1)S(1)}, u32[]{:S(2)}, u32[]{:S(2)}) collective-permute-start(bf16[40,1792]{1,0:T(8,128)(2,1)S(1)} %get-tuple-element.24), channel_id=1, source_target_pairs={{0,12},{4,8},{8,4},{12,0},{1,13},{5,9},{9,5},{13,1},{2,14},{6,10},... | collective-permute-start | bytes 430088 | tf_op jit(solution)/shard_map/ppermute | solution.py:17
  28.1 7.3 %collective-permute-start.9 = (bf16[88,512]{1,0:T(8,128)(2,1)S(1)}, bf16[88,512]{1,0:T(8,128)(2,1)S(1)}, u32[]{:S(2)}, u32[]{:S(2)}) collective-permute-start(bf16[88,512]{1,0:T(8,128)(2,1)S(1)} %gate.12), channel_id=1, source_target_pairs={{0,3},{1,2},{2,1},{3,0},{4,7},{5,6},{6,5},{7,4},{8,11},{9,10},{10,... | collective-permute-start | bytes 270344 | tf_op jit(solution)/shard_map/ppermute | solution.py:17
  31.3 7.4 %collective-permute-start.8 = (bf16[88,512]{1,0:T(8,128)(2,1)S(1)}, bf16[88,512]{1,0:T(8,128)(2,1)S(1)}, u32[]{:S(2)}, u32[]{:S(2)}) collective-permute-start(bf16[88,512]{1,0:T(8,128)(2,1)S(1)} %gate.11), channel_id=1, source_target_pairs={{0,1},{1,0},{2,3},{3,2},{4,5},{5,4},{6,7},{7,6},{8,9},{9,8},{10,11... | collective-permute-start | bytes 270344 | tf_op jit(solution)/shard_map/ppermute | solution.py:17
  31.8 8.0 %collective-permute-start.7 = (bf16[88,512]{1,0:T(8,128)(2,1)S(1)}, bf16[88,512]{1,0:T(8,128)(2,1)S(1)}, u32[]{:S(2)}, u32[]{:S(2)}) collective-permute-start(bf16[88,512]{1,0:T(8,128)(2,1)S(1)} %gate.8), channel_id=1, source_target_pairs={{0,2},{1,3},{2,0},{3,1},{4,6},{5,7},{6,4},{7,5},{8,10},{9,11},{10,... | collective-permute-start | bytes 270344 | tf_op jit(solution)/shard_map/ppermute | solution.py:17
  35.9 8.6 %collective-permute-start.12 = (bf16[88,512]{1,0:T(8,128)(2,1)S(1)}, bf16[88,512]{1,0:T(8,128)(2,1)S(1)}, u32[]{:S(2)}, u32[]{:S(2)}) collective-permute-start(bf16[88,512]{1,0:T(8,128)(2,1)S(1)} %gate.15), channel_id=1, source_target_pairs={{0,3},{1,2},{2,1},{3,0},{4,7},{5,6},{6,5},{7,4},{8,11},{9,10},{10,... | collective-permute-start | bytes 270344 | tf_op jit(solution)/shard_map/ppermute | solution.py:17
  39.1 5.9 %collective-permute-start.10 = (bf16[88,512]{1,0:T(8,128)(2,1)S(1)}, bf16[88,512]{1,0:T(8,128)(2,1)S(1)}, u32[]{:S(2)}, u32[]{:S(2)}) collective-permute-start(bf16[88,512]{1,0:T(8,128)(2,1)S(1)} %gate.14), channel_id=1, source_target_pairs={{0,1},{1,0},{2,3},{3,2},{4,5},{5,4},{6,7},{7,6},{8,9},{9,8},{10,11... | collective-permute-start | bytes 270344 | tf_op jit(solution)/shard_map/ppermute | solution.py:17
  40.2 6.9 %collective-permute-start.11 = (bf16[88,512]{1,0:T(8,128)(2,1)S(1)}, bf16[88,512]{1,0:T(8,128)(2,1)S(1)}, u32[]{:S(2)}, u32[]{:S(2)}) collective-permute-start(bf16[88,512]{1,0:T(8,128)(2,1)S(1)} %gate.9.after_ref), channel_id=1, source_target_pairs={{0,2},{1,3},{2,0},{3,1},{4,6},{5,7},{6,4},{7,5},{8,10},{9,11},{10,... | collective-permute-start | bytes 270344 | tf_op jit(solution)/shard_map/ppermute | solution.py:17
  43.0 0.9 %copy-start.1 = (bf16[64,1792]{1,0:T(8,128)(2,1)S(1)}, bf16[64,1792]{1,0:T(8,128)(2,1)}, u32[]{:S(2)}) copy-start(bf16[64,1792]{1,0:T(8,128)(2,1)} %store.1.refs_1_) | copy-start | bytes 688132
  44.0 14.5 %slice-start = ((s8[7340032]{0:T(1024)(128)(4,1)}), s8[4194304]{0:T(1024)(128)(4,1)S(1)}, s32[]{:S(2)}) async-start(s8[7340032]{0:T(1024)(128)(4,1)} %bitcast.14), calls=%async_computation | async-start | bytes 8388608
  44.4 14.0 %slice-start.1 = ((s8[7340032]{0:T(1024)(128)(4,1)}), s8[3145728]{0:T(1024)(128)(4,1)S(1)}, s32[]{:S(2)}) async-start(s8[7340032]{0:T(1024)(128)(4,1)} %bitcast.14), calls=%async_computation.1 | async-start | bytes 6291456
  47.3 6.4 %collective-permute-start.13 = (bf16[80,512]{1,0:T(8,128)(2,1)S(1)}, bf16[80,512]{1,0:T(8,128)(2,1)S(1)}, u32[]{:S(2)}, u32[]{:S(2)}) collective-permute-start(bf16[80,512]{1,0:T(8,128)(2,1)S(1)} %activate.2.refs_3_), channel_id=1, source_target_pairs={{0,3},{1,2},{2,1},{3,0},{4,7},{5,6},{6,5},{7,4},{8,11},{9,10},{10,... | collective-permute-start | bytes 245768 | tf_op jit(solution)/shard_map/ppermute | solution.py:17
  49.6 8.8 %collective-permute-start.18 = (bf16[80,512]{1,0:T(8,128)(2,1)S(1)}, bf16[80,512]{1,0:T(8,128)(2,1)S(1)}, u32[]{:S(2)}, u32[]{:S(2)}) collective-permute-start(bf16[80,512]{1,0:T(8,128)(2,1)S(1)} %activate.2.refs_3_), channel_id=1, source_target_pairs={{0,2},{1,3},{2,0},{3,1},{4,6},{5,7},{6,4},{7,5},{8,10},{9,11},{10,... | collective-permute-start | bytes 245768 | tf_op jit(solution)/shard_map/ppermute | solution.py:17
  49.6 8.8 %collective-permute-start.19 = (bf16[80,512]{1,0:T(8,128)(2,1)S(1)}, bf16[80,512]{1,0:T(8,128)(2,1)S(1)}, u32[]{:S(2)}, u32[]{:S(2)}) collective-permute-start(bf16[80,512]{1,0:T(8,128)(2,1)S(1)} %activate.2.refs_3_), channel_id=1, source_target_pairs={{0,1},{1,0},{2,3},{3,2},{4,5},{5,4},{6,7},{7,6},{8,9},{9,8},{10,11... | collective-permute-start | bytes 245768 | tf_op jit(solution)/shard_map/ppermute | solution.py:17
  54.0 7.4 %collective-permute-start.14 = (bf16[80,512]{1,0:T(8,128)(2,1)S(1)}, bf16[80,512]{1,0:T(8,128)(2,1)S(1)}, u32[]{:S(2)}, u32[]{:S(2)}) collective-permute-start(bf16[80,512]{1,0:T(8,128)(2,1)S(1)} %activate.3.refs_3_), channel_id=1, source_target_pairs={{0,3},{1,2},{2,1},{3,0},{4,7},{5,6},{6,5},{7,4},{8,11},{9,10},{10,... | collective-permute-start | bytes 245768 | tf_op jit(solution)/shard_map/ppermute | solution.py:17
  56.3 6.2 %collective-permute-start.15 = (bf16[80,512]{1,0:T(8,128)(2,1)S(1)}, bf16[80,512]{1,0:T(8,128)(2,1)S(1)}, u32[]{:S(2)}, u32[]{:S(2)}) collective-permute-start(bf16[80,512]{1,0:T(8,128)(2,1)S(1)} %activate.3.refs_3_), channel_id=1, source_target_pairs={{0,2},{1,3},{2,0},{3,1},{4,6},{5,7},{6,4},{7,5},{8,10},{9,11},{10,... | collective-permute-start | bytes 245768 | tf_op jit(solution)/shard_map/ppermute | solution.py:17
  56.7 5.8 %collective-permute-start.16 = (bf16[80,512]{1,0:T(8,128)(2,1)S(1)}, bf16[80,512]{1,0:T(8,128)(2,1)S(1)}, u32[]{:S(2)}, u32[]{:S(2)}) collective-permute-start(bf16[80,512]{1,0:T(8,128)(2,1)S(1)} %activate.3.refs_3_), channel_id=1, source_target_pairs={{0,1},{1,0},{2,3},{3,2},{4,5},{5,4},{6,7},{7,6},{8,9},{9,8},{10,11... | collective-permute-start | bytes 245768 | tf_op jit(solution)/shard_map/ppermute | solution.py:17
  59.9 5.8 %collective-permute-start.20 = (bf16[40,1792]{1,0:T(8,128)(2,1)S(1)}, bf16[40,1792]{1,0:T(8,128)(2,1)S(1)}, u32[]{:S(2)}, u32[]{:S(2)}) collective-permute-start(bf16[40,1792]{1,0:T(8,128)(2,1)S(1)} %get-tuple-element.36), channel_id=1, source_target_pairs={{0,8},{4,12},{8,0},{12,4},{1,9},{5,13},{9,1},{13,5},{2,10},{6,14},... | collective-permute-start | bytes 430088 | tf_op jit(solution)/shard_map/ppermute | solution.py:17
  61.4 6.0 %collective-permute-start.21 = (bf16[40,1792]{1,0:T(8,128)(2,1)S(1)}, bf16[40,1792]{1,0:T(8,128)(2,1)S(1)}, u32[]{:S(2)}, u32[]{:S(2)}) collective-permute-start(bf16[40,1792]{1,0:T(8,128)(2,1)S(1)} %get-tuple-element.37), channel_id=1, source_target_pairs={{0,12},{4,8},{8,4},{12,0},{1,13},{5,9},{9,5},{13,1},{2,14},{6,10},... | collective-permute-start | bytes 430088 | tf_op jit(solution)/shard_map/ppermute | solution.py:17
  63.9 3.6 %collective-permute-start.17 = (bf16[40,1792]{1,0:T(8,128)(2,1)S(1)}, bf16[40,1792]{1,0:T(8,128)(2,1)S(1)}, u32[]{:S(2)}, u32[]{:S(2)}) collective-permute-start(bf16[40,1792]{1,0:T(8,128)(2,1)S(1)} %get-tuple-element.35), channel_id=1, source_target_pairs={{0,4},{4,0},{8,12},{12,8},{1,5},{5,1},{9,13},{13,9},{2,6},{6,2},{1... | collective-permute-start | bytes 430088 | tf_op jit(solution)/shard_map/ppermute | solution.py:17

commit v6 on v5

--- a/solution.py
+++ b/solution.py
@@ -110,8 +110,13 @@
         out[...] = packed[i * cap : (i + 1) * cap, :].astype(jnp.bfloat16)
 
 
-def store_kernel(values_ref, after_ref, out_ref):
+def hold_kernel(value_ref, *refs):
+    refs[-1][...] = value_ref[...]
+
+
+def store_kernel(values_ref, after_ref, out_ref, token_ref):
     out_ref[...] = values_ref[...]
+    token_ref[...] = jnp.zeros(token_ref.shape, token_ref.dtype)
 
 
 def prepare_kernel(n, gain_ref, *refs):
@@ -297,18 +302,17 @@
         for k in ([1, 3, 2, 0] if nt == 4 and after is not None else partners(nt)):
             earlier = [] if after is None else [after[k or 1]]
             if k == 0 and after is not None:
-                stored.append(
-                    pl.pallas_call(
-                        store_kernel,
-                        out_shape=sds((tokens, share), bf16),
-                        in_specs=[whole(), anywhere()],
-                        out_specs=whole(),
-                        compiler_params=params(),
-                        cost_estimate=estimate(10**6, 4 * tokens * share),
-                        name="store",
-                    )(kept, partial_gate)
-                )
-                earlier.append(stored[0])
+                written, token = pl.pallas_call(
+                    store_kernel,
+                    out_shape=(sds((tokens, share), bf16), sds((8, 128), f32)),
+                    in_specs=[whole(), anywhere()],
+                    out_specs=(whole(), whole()),
+                    compiler_params=params(),
+                    cost_estimate=estimate(10**6, 4 * tokens * share),
+                    name="store",
+                )(kept, partial_gate)
+                stored.append(written)
+                earlier.append(token)
             partial_gate = pl.pallas_call(
                 gate_kernel,
                 out_shape=sds((tall, ff), bf16),
@@ -330,9 +334,9 @@
             gates[k] = exchange(partial_gate, "tensor", k) if k else partial_gate
         return gates
 
-    def gathered_hidden(ks, gates, after=()):
+    def activated(ks, gates, after=()):
         count = len(ks) * cap
-        own = pl.pallas_call(
+        return pl.pallas_call(
             functools.partial(activate_kernel, nt, count, float(share * nt)),
             out_shape=sds((count, ff), bf16),
             in_specs=[whole()] * nt + [anywhere()] * len(after),
@@ -341,7 +345,17 @@
             cost_estimate=estimate(20 * count * ff, 2 * count * ff * (nt + 1)),
             name="activate",
         )(*[gates[k] for k in range(nt)], *after)
-        return {k: exchange(own, "tensor", k) if k else own for k in partners(nt)}
+
+    def held(value, *after):
+        return pl.pallas_call(
+            hold_kernel,
+            out_shape=sds(value.shape, value.dtype),
+            in_specs=[whole()] + [anywhere()] * len(after),
+            out_specs=whole(),
+            compiler_params=params(),
+            cost_estimate=estimate(10**6, 4 * value.size),
+            name="hold",
+        )(value, *after)
 
     def produced(ks, hidden):
         outs = pl.pallas_call(
@@ -357,8 +371,12 @@
 
     near_gates = summed_gate(near)
     far_gates = summed_gate(far, near_gates)
-    far_hidden = gathered_hidden(far, far_gates)
-    near_hidden = gathered_hidden(near, near_gates, (far_hidden[3],))
+    near_own = activated(near, near_gates)
+    near_hidden = {0: near_own, 1: exchange(near_own, "tensor", 1)}
+    far_own = activated(far, far_gates, (near_own,))
+    far_hidden = {k: exchange(far_own, "tensor", k) if k else far_own for k in partners(nt)}
+    waiting = held(near_own, far_hidden[3], near_hidden[1])
+    near_hidden.update({k: exchange(waiting, "tensor", k) for k in partners(nt) if k > 1})
     returned = {}
     for ks, hidden in ((far, far_hidden), (near, near_hidden)):
         for k, value in produced(ks, hidden).items():

time: 68.8 us -> 68.5 us (level)
  waiting for transfers between devices: 16.3 us -> 18.1 us
  starting transfers between devices: 32.5 us -> 31.4 us
  local copies, waits for them, and re-layouts: 7.96 us -> 7.02 us
    ppermute x19, waiting for transfers between devices: 11 us -> 12.8 us  [exchange(): return lax.ppermute(value, axis, [(i, i ^ step) for i in range(n)])]
    ppermute x19, starting transfers between devices: 25.1 us -> 24 us  [exchange(): return lax.ppermute(value, axis, [(i, i ^ step) for i in range(n)])]
    unnamed x16 -> x14, local copies, waits for them, and re-layouts: 6.52 us -> 5.58 us
  transfers between devices with their start and end apart: 22 -> 22, of which waited for: 10 -> 11; matrix products, arithmetic and copies ran while one was open for 2% -> 2% of each run, Pallas kernels for 13% -> 14%
where the time goes in v6:
time: 68.5 us; the launch traced here: 68.2 us
  starting transfers between devices  31.4 us (46%)
  waiting for transfers between devices  18.1 us (26%)
  Pallas kernels  10.8 us (16%)
  local copies, waits for them, and re-layouts  7.02 us (10%)
  between operations  0.93 us (1%)
    ppermute x19, starting transfers between devices, exchange(): return lax.ppermute(value, axis, [(i, i ^ step) for i in range(n)])  24 us
    ppermute x19, waiting for transfers between devices, exchange(): return lax.ppermute(value, axis, [(i, i ^ step) for i in range(n)])  12.8 us
    ppermute x1, starting transfers between devices, local(): parts.append(lax.ppermute(block(z ^ 2), 'tensor', [(0, 2), (3, 1)]))  5.75 us
    unnamed x14, local copies, waits for them, and re-layouts  5.58 us
    ppermute x1, waiting for transfers between devices, local(): lax.ppermute(merged, 'tensor', [(0, 1), (1, 3), (2, 0), (3, 2)])  5.28 us
    pallas_call x8, Pallas kernels, summed_gate(): pl.pallas_call(gate_kernel, out_shape=sds((tall, ff), bf16), grid_spec=pl...  3.56 us
    pallas_call x2, Pallas kernels, produced(): pl.pallas_call(functools.partial(down_kernel, nt, len(ks), cap), out_shap...  2.78 us
    dynamic_slice x1, local copies, waits for them, and re-layouts, block(): return lax.dynamic_slice(attn_partial[0], (0, k * share), (tokens, share))  1.44 us
  transfers between devices with their start and end apart: 22, of which 11 were waited for; matrix products, arithmetic and copies ran while one was open for 2% of the time, Pallas kernels for 14%

profile of v6, /device:TPU:0, one launch (start us, length us, event | category | flops | bytes accessed | tf_op | source)
XLA Modules:
  0.0 68.2 jit_solution(6050373489242533985)
XLA Ops:
  0.7 1.4 %dynamic-slice_bitcast_fusion = (bf16[64,1792]{1,0:T(8,128)(2,1)S(1)}, bf16[64,1792]{1,0:T(8,128)(2,1)S(1)}, bf16[64,1792]{1,0:T(8,128)(2,1)S(1)}, bf16[64,1792]{1,0:T(8,128)(2,1)S(1)}, bf16[64,1792]{1,0:T(8,128)(2,1)S(1)}) fusion(bf16[1,64,7168]{2,1,0:T(8,128)(2,1)} %param.8, s32[]{:T(128)S(6)} %select_n.30, s32[]{:T(128)S(6)} %select_n.27, s32[]{:T(128)S(6)} %select_n.26, ...), kind=kLoop, calls=%fused_computation | loop fusion | bytes 2293780 | tf_op jit(solution)/shard_map/dynamic_slice | solution.py:219
  2.1 3.1 %collective-permute-start.2 = (bf16[64,1792]{1,0:T(8,128)(2,1)S(1)}, bf16[64,1792]{1,0:T(8,128)(2,1)S(1)}, u32[]{:S(2)}, u32[]{:S(2)}) collective-permute-start(bf16[64,1792]{1,0:T(8,128)(2,1)S(1)} %get-tuple-element.42), channel_id=1, source_target_pairs={{0,1},{1,0},{2,3},{3,2},{4,5},{5,4},{6,7},{7,6},{8,9},{9,8},{10,11... | collective-permute-start | bytes 688136 | tf_op jit(solution)/shard_map/ppermute | solution.py:17
  5.2 0.7 collective-permute-start
  5.9 5.8 %collective-permute-start.1 = (bf16[64,1792]{1,0:T(8,128)(2,1)S(1)}, bf16[64,1792]{1,0:T(8,128)(2,1)S(1)}, u32[]{:S(2)}, u32[]{:S(2)}) collective-permute-start(bf16[64,1792]{1,0:T(8,128)(2,1)S(1)} %get-tuple-element.43.passing_ref), channel_id=1, source_target_pairs={{0,2},{3,1},{4,6},{7,5},{8,10},{11,9},{12,14},{15,13},{16,18},{19,... | collective-permute-start | bytes 688136 | tf_op jit(solution)/shard_map/ppermute | solution.py:227
  11.7 1.0 %collective-permute-start.3 = (bf16[64,1792]{1,0:T(8,128)(2,1)S(1)}, bf16[64,1792]{1,0:T(8,128)(2,1)S(1)}, u32[]{:S(2)}, u32[]{:S(2)}) collective-permute-start(bf16[64,1792]{1,0:T(8,128)(2,1)S(1)} %merge.1), channel_id=1, source_target_pairs={{0,1},{1,3},{2,0},{3,2},{4,5},{5,7},{6,4},{7,6},{8,9},{9,11},{10,8... | collective-permute-start | bytes 688136 | tf_op jit(solution)/shard_map/ppermute | solution.py:237
  12.7 0.8 %copy.10.scores_ref = f32[64,2]{1,0:T(8,128)S(1)} copy(f32[64,2]{0,1:T(2,128)} %param.11) | data formatting | bytes 1024 | tf_op args[4]
  13.4 0.8 %copy.9.ids_ref = s32[64,2]{1,0:T(8,128)S(1)} copy(s32[64,2]{0,1:T(2,128)} %param.10) | data formatting | bytes 1024 | tf_op args[3]
  14.2 3.1 %copy-done = bf16[1,1792,2048]{2,1,0:T(8,128)(2,1)S(1)} copy-done((bf16[1,1792,2048]{2,1,0:T(8,128)(2,1)S(1)}, bf16[1,1792,2048]{2,1,0:T(8,128)(2,1)}, u32[]{:S(2)}) %copy-start) | copy-done | bytes 7340056
  17.3 0.9 %copy-done.1 = bf16[64,1792]{1,0:T(8,128)(2,1)S(1)} copy-done((bf16[64,1792]{1,0:T(8,128)(2,1)S(1)}, bf16[64,1792]{1,0:T(8,128)(2,1)}, u32[]{:S(2)}) %copy-start.1) | copy-done | bytes 229400
  18.2 0.8 %fetch.1 = (bf16[64,1792]{1,0:T(8,128)(2,1)S(1)}, bf16[1,1792,2048]{2,1,0:T(8,128)(2,1)S(1)}) custom-call(bf16[64,1792]{1,0:T(8,128)(2,1)S(1)} %copy-done.1, bf16[1,1792,2048]{2,1,0:T(8,128)(2,1)S(1)} %copy-done), custom_call_target="tpu_custom_call" | custom-call | flops 1000000 | bytes 7569408 | tf_op jit(solution)/shard_map/fetch/pallas_call | solution.py:254
  19.0 0.5 routing.1
  19.6 5.3 %collective-permute-done.3.refs_3_ = bf16[64,1792]{1,0:T(8,128)(2,1)S(1)} collective-permute-done((bf16[64,1792]{1,0:T(8,128)(2,1)S(1)}, bf16[64,1792]{1,0:T(8,128)(2,1)S(1)}, u32[]{:S(2)}, u32[]{:S(2)}) %collective-permute-start.3) | collective-permute-done | bytes 229408 | tf_op jit(solution)/shard_map/ppermute | solution.py:237
  24.9 0.4 add.22
  25.3 0.2 pack.1
  25.5 1.6 %collective-permute-start.4 = (bf16[40,1792]{1,0:T(8,128)(2,1)S(1)}, bf16[40,1792]{1,0:T(8,128)(2,1)S(1)}, u32[]{:S(2)}, u32[]{:S(2)}) collective-permute-start(bf16[40,1792]{1,0:T(8,128)(2,1)S(1)} %get-tuple-element.25), channel_id=1, source_target_pairs={{0,8},{4,12},{8,0},{12,4},{1,9},{5,13},{9,1},{13,5},{2,10},{6,14},... | collective-permute-start | bytes 430088 | tf_op jit(solution)/shard_map/ppermute | solution.py:17
  27.1 0.4 collective-permute-start.5
  27.6 0.5 gate.12
  28.1 2.7 %collective-permute-start.9 = (bf16[88,512]{1,0:T(8,128)(2,1)S(1)}, bf16[88,512]{1,0:T(8,128)(2,1)S(1)}, u32[]{:S(2)}, u32[]{:S(2)}) collective-permute-start(bf16[88,512]{1,0:T(8,128)(2,1)S(1)} %gate.12), channel_id=1, source_target_pairs={{0,3},{1,2},{2,1},{3,0},{4,7},{5,6},{6,5},{7,4},{8,11},{9,10},{10,... | collective-permute-start | bytes 270344 | tf_op jit(solution)/shard_map/ppermute | solution.py:17
  30.8 0.4 gate.11
  31.3 0.4 gate.8
  31.8 1.8 %collective-permute-start.7 = (bf16[88,512]{1,0:T(8,128)(2,1)S(1)}, bf16[88,512]{1,0:T(8,128)(2,1)S(1)}, u32[]{:S(2)}, u32[]{:S(2)}) collective-permute-start(bf16[88,512]{1,0:T(8,128)(2,1)S(1)} %gate.8), channel_id=1, source_target_pairs={{0,2},{1,3},{2,0},{3,1},{4,6},{5,7},{6,4},{7,5},{8,10},{9,11},{10,... | collective-permute-start | bytes 270344 | tf_op jit(solution)/shard_map/ppermute | solution.py:17
  33.6 0.8 %collective-permute-done.5.refs_1_ = bf16[40,1792]{1,0:T(8,128)(2,1)S(1)} collective-permute-done((bf16[40,1792]{1,0:T(8,128)(2,1)S(1)}, bf16[40,1792]{1,0:T(8,128)(2,1)S(1)}, u32[]{:S(2)}, u32[]{:S(2)}) %collective-permute-start.5) | collective-permute-done | bytes 143392 | tf_op jit(solution)/shard_map/ppermute | solution.py:17
  34.6 0.8 %collective-permute-done.9.refs_3_.refs_0_ = bf16[88,512]{1,0:T(8,128)(2,1)S(1)} collective-permute-done((bf16[88,512]{1,0:T(8,128)(2,1)S(1)}, bf16[88,512]{1,0:T(8,128)(2,1)S(1)}, u32[]{:S(2)}, u32[]{:S(2)}) %collective-permute-start.9) | collective-permute-done | bytes 90144 | tf_op jit(solution)/shard_map/ppermute | solution.py:17
  35.4 0.4 gate.15
  35.9 2.7 %collective-permute-start.12 = (bf16[88,512]{1,0:T(8,128)(2,1)S(1)}, bf16[88,512]{1,0:T(8,128)(2,1)S(1)}, u32[]{:S(2)}, u32[]{:S(2)}) collective-permute-start(bf16[88,512]{1,0:T(8,128)(2,1)S(1)} %gate.15), channel_id=1, source_target_pairs={{0,3},{1,2},{2,1},{3,0},{4,7},{5,6},{6,5},{7,4},{8,11},{9,10},{10,... | collective-permute-start | bytes 270344 | tf_op jit(solution)/shard_map/ppermute | solution.py:17
  38.6 0.4 gate.14
  39.2 0.6 collective-permute-done.7.refs_0_.refs_2_
  39.8 0.4 gate.9.after_ref
  40.2 2.1 %collective-permute-start.11 = (bf16[88,512]{1,0:T(8,128)(2,1)S(1)}, bf16[88,512]{1,0:T(8,128)(2,1)S(1)}, u32[]{:S(2)}, u32[]{:S(2)}) collective-permute-start(bf16[88,512]{1,0:T(8,128)(2,1)S(1)} %gate.9.after_ref), channel_id=1, source_target_pairs={{0,2},{1,3},{2,0},{3,1},{4,6},{5,7},{6,4},{7,5},{8,10},{9,11},{10,... | collective-permute-start | bytes 270344 | tf_op jit(solution)/shard_map/ppermute | solution.py:17
  42.3 0.4 gate.10.refs_0_
  43.0 0.6 collective-permute-start.14
  43.6 0.7 %store.1 = (bf16[64,1792]{1,0:T(8,128)(2,1)}, f32[8,128]{1,0:T(8,128)S(1)}) custom-call(bf16[64,1792]{1,0:T(8,128)(2,1)S(1)} %get-tuple-element.24.stream_ref.values_ref, bf16[88,512]{1,0:T(8,128)(2,1)S(1)} %gate.9.after_ref), custom_call_target="tpu_custom_call" | custom-call | flops 1000000 | bytes 458752 | tf_op jit(solution)/shard_map/store/pallas_call | solution.py:305
  44.3 0.4 gate.13.refs_0_
  44.8 0.5 collective-permute-done.10.refs_1_
  45.2 1.3 %collective-permute-done.11.refs_2_ = bf16[88,512]{1,0:T(8,128)(2,1)S(1)} collective-permute-done((bf16[88,512]{1,0:T(8,128)(2,1)S(1)}, bf16[88,512]{1,0:T(8,128)(2,1)S(1)}, u32[]{:S(2)}, u32[]{:S(2)}) %collective-permute-start.11) | collective-permute-done | bytes 90144 | tf_op jit(solution)/shard_map/ppermute | solution.py:17
  46.7 2.8 %collective-permute-start.13 = (bf16[80,512]{1,0:T(8,128)(2,1)S(1)}, bf16[80,512]{1,0:T(8,128)(2,1)S(1)}, u32[]{:S(2)}, u32[]{:S(2)}) collective-permute-start(bf16[80,512]{1,0:T(8,128)(2,1)S(1)} %activate.3.refs_3_), channel_id=1, source_target_pairs={{0,3},{1,2},{2,1},{3,0},{4,7},{5,6},{6,5},{7,4},{8,11},{9,10},{10,... | collective-permute-start | bytes 245768 | tf_op jit(solution)/shard_map/ppermute | solution.py:17
  49.6 1.6 %collective-permute-start.19 = (bf16[80,512]{1,0:T(8,128)(2,1)S(1)}, bf16[80,512]{1,0:T(8,128)(2,1)S(1)}, u32[]{:S(2)}, u32[]{:S(2)}) collective-permute-start(bf16[80,512]{1,0:T(8,128)(2,1)S(1)} %activate.3.refs_3_), channel_id=1, source_target_pairs={{0,1},{1,0},{2,3},{3,2},{4,5},{5,4},{6,7},{7,6},{8,9},{9,8},{10,11... | collective-permute-start | bytes 245768 | tf_op jit(solution)/shard_map/ppermute | solution.py:17
  51.2 2.6 %collective-permute-done.13.refs_0_ = bf16[80,512]{1,0:T(8,128)(2,1)S(1)} collective-permute-done((bf16[80,512]{1,0:T(8,128)(2,1)S(1)}, bf16[80,512]{1,0:T(8,128)(2,1)S(1)}, u32[]{:S(2)}, u32[]{:S(2)}) %collective-permute-start.13) | collective-permute-done | bytes 81952 | tf_op jit(solution)/shard_map/ppermute | solution.py:17
  53.8 2.2 %collective-permute-start.15 = (bf16[80,512]{1,0:T(8,128)(2,1)S(1)}, bf16[80,512]{1,0:T(8,128)(2,1)S(1)}, u32[]{:S(2)}, u32[]{:S(2)}) collective-permute-start(bf16[80,512]{1,0:T(8,128)(2,1)S(1)} %hold.1), channel_id=1, source_target_pairs={{0,3},{1,2},{2,1},{3,0},{4,7},{5,6},{6,5},{7,4},{8,11},{9,10},{10,... | collective-permute-start | bytes 245768 | tf_op jit(solution)/shard_map/ppermute | solution.py:17
  56.0 0.6 collective-permute-start.16
  56.6 1.6 %collective-permute-done.18.refs_1_ = bf16[80,512]{1,0:T(8,128)(2,1)S(1)} collective-permute-done((bf16[80,512]{1,0:T(8,128)(2,1)S(1)}, bf16[80,512]{1,0:T(8,128)(2,1)S(1)}, u32[]{:S(2)}, u32[]{:S(2)}) %collective-permute-start.18) | collective-permute-done | bytes 81952 | tf_op jit(solution)/shard_map/ppermute | solution.py:17
  58.2 1.4 %down.3 = (bf16[40,1792]{1,0:T(8,128)(2,1)S(1)}, bf16[40,1792]{1,0:T(8,128)(2,1)S(1)}) custom-call(s32[1]{0:T(128)} %bitcast.8.block_ref, bf16[1,2048,1792]{2,1,0:T(8,128)(2,1)S(1)} %bitcast.15, bf16[80,512]{1,0:T(8,128)(2,1)S(1)} %collective-permute-done.13.refs_0_, bf16[80,512]{1,0:T(8,128)(2,1)S(1)} %collective-permute-done.18.refs_1_, ...), custom_call_target="tpu_custom_call" | custom-call | flops 587202560 | bytes 7340032 | tf_op jit(solution)/shard_map/down/pallas_call | solution.py:361
  59.6 1.5 %collective-permute-start.20 = (bf16[40,1792]{1,0:T(8,128)(2,1)S(1)}, bf16[40,1792]{1,0:T(8,128)(2,1)S(1)}, u32[]{:S(2)}, u32[]{:S(2)}) collective-permute-start(bf16[40,1792]{1,0:T(8,128)(2,1)S(1)} %get-tuple-element.40), channel_id=1, source_target_pairs={{0,8},{4,12},{8,0},{12,4},{1,9},{5,13},{9,1},{13,5},{2,10},{6,14},... | collective-permute-start | bytes 430088 | tf_op jit(solution)/shard_map/ppermute | solution.py:17
  61.2 1.2 %collective-permute-done.16.refs_1_ = bf16[80,512]{1,0:T(8,128)(2,1)S(1)} collective-permute-done((bf16[80,512]{1,0:T(8,128)(2,1)S(1)}, bf16[80,512]{1,0:T(8,128)(2,1)S(1)}, u32[]{:S(2)}, u32[]{:S(2)}) %collective-permute-start.16) | collective-permute-done | bytes 81952 | tf_op jit(solution)/shard_map/ppermute | solution.py:17
  62.3 1.4 %down.2 = (bf16[40,1792]{1,0:T(8,128)(2,1)S(1)}, bf16[40,1792]{1,0:T(8,128)(2,1)S(1)}) custom-call(s32[1]{0:T(128)} %bitcast.8.block_ref, bf16[1,2048,1792]{2,1,0:T(8,128)(2,1)S(1)} %bitcast.15, bf16[80,512]{1,0:T(8,128)(2,1)S(1)} %collective-permute-done.15.refs_0_, bf16[80,512]{1,0:T(8,128)(2,1)S(1)} %collective-permute-done.16.refs_1_, ...), custom_call_target="tpu_custom_call" | custom-call | flops 587202560 | bytes 7340032 | tf_op jit(solution)/shard_map/down/pallas_call | solution.py:361
  63.8 1.6 %collective-permute-done.20.refs_2_ = bf16[40,1792]{1,0:T(8,128)(2,1)S(1)} collective-permute-done((bf16[40,1792]{1,0:T(8,128)(2,1)S(1)}, bf16[40,1792]{1,0:T(8,128)(2,1)S(1)}, u32[]{:S(2)}, u32[]{:S(2)}) %collective-permute-start.20) | collective-permute-done | bytes 143392 | tf_op jit(solution)/shard_map/ppermute | solution.py:17
  65.4 1.8 %collective-permute-done.21.refs_3_ = bf16[40,1792]{1,0:T(8,128)(2,1)S(1)} collective-permute-done((bf16[40,1792]{1,0:T(8,128)(2,1)S(1)}, bf16[40,1792]{1,0:T(8,128)(2,1)S(1)}, u32[]{:S(2)}, u32[]{:S(2)}) %collective-permute-start.21) | collective-permute-done | bytes 143392 | tf_op jit(solution)/shard_map/ppermute | solution.py:17
  67.2 1.0 %combine.1 = bf16[64,1792]{1,0:T(8,128)(2,1)} custom-call(bf16[64,160]{1,0:T(8,128)(2,1)S(1)} %get-tuple-element.35.high_ref, bf16[64,160]{1,0:T(8,128)(2,1)S(1)} %get-tuple-element.36.low_ref, bf16[40,1792]{1,0:T(8,128)(2,1)S(1)} %get-tuple-element.38.refs_0_, bf16[40,1792]{1,0:T(8,128)(2,1)S(1)} %collective-permute-done.17.refs_1_, ...), custom_call_target="tpu_custom_call" | custom-call | flops 73400320 | bytes 573440 | tf_op jit(solution)/shard_map/combine/pallas_call | solution.py:385
  (35 shorter events, 1.2 us)
Async XLA Ops:
  0.6 18.4 %copy-start.2 = (s32[64,2]{0,1:T(2,128)S(1)}, s32[64,2]{0,1:T(2,128)}, u32[]{:S(2)}) copy-start(s32[64,2]{0,1:T(2,128)} %param.10) | copy-start | bytes 1540
  0.6 26.8 %copy-start.3 = (bf16[1792]{0:T(1024)(128)(2,1)S(1)}, bf16[1792]{0:T(1024)(128)(2,1)}, u32[]{:S(2)}) copy-start(bf16[1792]{0:T(1024)(128)(2,1)} %param.9) | copy-start | bytes 10756
  2.1 9.5 %collective-permute-start.2 = (bf16[64,1792]{1,0:T(8,128)(2,1)S(1)}, bf16[64,1792]{1,0:T(8,128)(2,1)S(1)}, u32[]{:S(2)}, u32[]{:S(2)}) collective-permute-start(bf16[64,1792]{1,0:T(8,128)(2,1)S(1)} %get-tuple-element.42), channel_id=1, source_target_pairs={{0,1},{1,0},{2,3},{3,2},{4,5},{5,4},{6,7},{7,6},{8,9},{9,8},{10,11... | collective-permute-start | bytes 688136 | tf_op jit(solution)/shard_map/ppermute | solution.py:17
  5.2 14.3 %collective-permute-start = (bf16[64,1792]{1,0:T(8,128)(2,1)S(1)}, bf16[64,1792]{1,0:T(8,128)(2,1)S(1)}, u32[]{:S(2)}, u32[]{:S(2)}) collective-permute-start(bf16[64,1792]{1,0:T(8,128)(2,1)S(1)} %get-tuple-element.44), channel_id=1, source_target_pairs={{1,2},{2,1},{5,6},{6,5},{9,10},{10,9},{13,14},{14,13},{17,18},{18,... | collective-permute-start | bytes 688136 | tf_op jit(solution)/shard_map/ppermute | solution.py:226
  5.9 13.7 %collective-permute-start.1 = (bf16[64,1792]{1,0:T(8,128)(2,1)S(1)}, bf16[64,1792]{1,0:T(8,128)(2,1)S(1)}, u32[]{:S(2)}, u32[]{:S(2)}) collective-permute-start(bf16[64,1792]{1,0:T(8,128)(2,1)S(1)} %get-tuple-element.43.passing_ref), channel_id=1, source_target_pairs={{0,2},{3,1},{4,6},{7,5},{8,10},{11,9},{12,14},{15,13},{16,18},{19,... | collective-permute-start | bytes 688136 | tf_op jit(solution)/shard_map/ppermute | solution.py:227
  11.7 13.1 %collective-permute-start.3 = (bf16[64,1792]{1,0:T(8,128)(2,1)S(1)}, bf16[64,1792]{1,0:T(8,128)(2,1)S(1)}, u32[]{:S(2)}, u32[]{:S(2)}) collective-permute-start(bf16[64,1792]{1,0:T(8,128)(2,1)S(1)} %merge.1), channel_id=1, source_target_pairs={{0,1},{1,3},{2,0},{3,2},{4,5},{5,7},{6,4},{7,6},{8,9},{9,11},{10,8... | collective-permute-start | bytes 688136 | tf_op jit(solution)/shard_map/ppermute | solution.py:237
  14.2 3.1 %copy-start = (bf16[1,1792,2048]{2,1,0:T(8,128)(2,1)S(1)}, bf16[1,1792,2048]{2,1,0:T(8,128)(2,1)}, u32[]{:S(2)}) copy-start(bf16[1,1792,2048]{2,1,0:T(8,128)(2,1)} %refs_1_.1) | copy-start | bytes 22020100
  17.3 0.9 %copy-start.1 = (bf16[64,1792]{1,0:T(8,128)(2,1)S(1)}, bf16[64,1792]{1,0:T(8,128)(2,1)}, u32[]{:S(2)}) copy-start(bf16[64,1792]{1,0:T(8,128)(2,1)} %refs_0_.1) | copy-start | bytes 688132
  25.2 2.2 %collective-permute-start.6 = (bf16[40,1792]{1,0:T(8,128)(2,1)S(1)}, bf16[40,1792]{1,0:T(8,128)(2,1)S(1)}, u32[]{:S(2)}, u32[]{:S(2)}) collective-permute-start(bf16[40,1792]{1,0:T(8,128)(2,1)S(1)} %get-tuple-element.31), channel_id=1, source_target_pairs={{0,4},{4,0},{8,12},{12,8},{1,5},{5,1},{9,13},{13,9},{2,6},{6,2},{1... | collective-permute-start | bytes 430088 | tf_op jit(solution)/shard_map/ppermute | solution.py:17
  25.5 8.1 %collective-permute-start.4 = (bf16[40,1792]{1,0:T(8,128)(2,1)S(1)}, bf16[40,1792]{1,0:T(8,128)(2,1)S(1)}, u32[]{:S(2)}, u32[]{:S(2)}) collective-permute-start(bf16[40,1792]{1,0:T(8,128)(2,1)S(1)} %get-tuple-element.25), channel_id=1, source_target_pairs={{0,8},{4,12},{8,0},{12,4},{1,9},{5,13},{9,1},{13,5},{2,10},{6,14},... | collective-permute-start | bytes 430088 | tf_op jit(solution)/shard_map/ppermute | solution.py:17
  27.1 7.3 %collective-permute-start.5 = (bf16[40,1792]{1,0:T(8,128)(2,1)S(1)}, bf16[40,1792]{1,0:T(8,128)(2,1)S(1)}, u32[]{:S(2)}, u32[]{:S(2)}) collective-permute-start(bf16[40,1792]{1,0:T(8,128)(2,1)S(1)} %get-tuple-element.26), channel_id=1, source_target_pairs={{0,12},{4,8},{8,4},{12,0},{1,13},{5,9},{9,5},{13,1},{2,14},{6,10},... | collective-permute-start | bytes 430088 | tf_op jit(solution)/shard_map/ppermute | solution.py:17
  28.1 7.3 %collective-permute-start.9 = (bf16[88,512]{1,0:T(8,128)(2,1)S(1)}, bf16[88,512]{1,0:T(8,128)(2,1)S(1)}, u32[]{:S(2)}, u32[]{:S(2)}) collective-permute-start(bf16[88,512]{1,0:T(8,128)(2,1)S(1)} %gate.12), channel_id=1, source_target_pairs={{0,3},{1,2},{2,1},{3,0},{4,7},{5,6},{6,5},{7,4},{8,11},{9,10},{10,... | collective-permute-start | bytes 270344 | tf_op jit(solution)/shard_map/ppermute | solution.py:17
  31.3 7.4 %collective-permute-start.8 = (bf16[88,512]{1,0:T(8,128)(2,1)S(1)}, bf16[88,512]{1,0:T(8,128)(2,1)S(1)}, u32[]{:S(2)}, u32[]{:S(2)}) collective-permute-start(bf16[88,512]{1,0:T(8,128)(2,1)S(1)} %gate.11), channel_id=1, source_target_pairs={{0,1},{1,0},{2,3},{3,2},{4,5},{5,4},{6,7},{7,6},{8,9},{9,8},{10,11... | collective-permute-start | bytes 270344 | tf_op jit(solution)/shard_map/ppermute | solution.py:17
  31.8 8.0 %collective-permute-start.7 = (bf16[88,512]{1,0:T(8,128)(2,1)S(1)}, bf16[88,512]{1,0:T(8,128)(2,1)S(1)}, u32[]{:S(2)}, u32[]{:S(2)}) collective-permute-start(bf16[88,512]{1,0:T(8,128)(2,1)S(1)} %gate.8), channel_id=1, source_target_pairs={{0,2},{1,3},{2,0},{3,1},{4,6},{5,7},{6,4},{7,5},{8,10},{9,11},{10,... | collective-permute-start | bytes 270344 | tf_op jit(solution)/shard_map/ppermute | solution.py:17
  35.9 8.9 %collective-permute-start.12 = (bf16[88,512]{1,0:T(8,128)(2,1)S(1)}, bf16[88,512]{1,0:T(8,128)(2,1)S(1)}, u32[]{:S(2)}, u32[]{:S(2)}) collective-permute-start(bf16[88,512]{1,0:T(8,128)(2,1)S(1)} %gate.15), channel_id=1, source_target_pairs={{0,3},{1,2},{2,1},{3,0},{4,7},{5,6},{6,5},{7,4},{8,11},{9,10},{10,... | collective-permute-start | bytes 270344 | tf_op jit(solution)/shard_map/ppermute | solution.py:17
  39.1 6.1 %collective-permute-start.10 = (bf16[88,512]{1,0:T(8,128)(2,1)S(1)}, bf16[88,512]{1,0:T(8,128)(2,1)S(1)}, u32[]{:S(2)}, u32[]{:S(2)}) collective-permute-start(bf16[88,512]{1,0:T(8,128)(2,1)S(1)} %gate.14), channel_id=1, source_target_pairs={{0,1},{1,0},{2,3},{3,2},{4,5},{5,4},{6,7},{7,6},{8,9},{9,8},{10,11... | collective-permute-start | bytes 270344 | tf_op jit(solution)/shard_map/ppermute | solution.py:17
  40.2 18.0 %slice-start = ((s8[7340032]{0:T(1024)(128)(4,1)}), s8[4194304]{0:T(1024)(128)(4,1)S(1)}, s32[]{:S(2)}) async-start(s8[7340032]{0:T(1024)(128)(4,1)} %bitcast.14), calls=%async_computation | async-start | bytes 8388608
  40.2 6.3 %collective-permute-start.11 = (bf16[88,512]{1,0:T(8,128)(2,1)S(1)}, bf16[88,512]{1,0:T(8,128)(2,1)S(1)}, u32[]{:S(2)}, u32[]{:S(2)}) collective-permute-start(bf16[88,512]{1,0:T(8,128)(2,1)S(1)} %gate.9.after_ref), channel_id=1, source_target_pairs={{0,2},{1,3},{2,0},{3,1},{4,6},{5,7},{6,4},{7,5},{8,10},{9,11},{10,... | collective-permute-start | bytes 270344 | tf_op jit(solution)/shard_map/ppermute | solution.py:17
  43.0 8.2 %collective-permute-start.14 = (bf16[80,512]{1,0:T(8,128)(2,1)S(1)}, bf16[80,512]{1,0:T(8,128)(2,1)S(1)}, u32[]{:S(2)}, u32[]{:S(2)}) collective-permute-start(bf16[80,512]{1,0:T(8,128)(2,1)S(1)} %activate.2.refs_4_.value_ref.refs_3_), channel_id=1, source_target_pairs={{0,1},{1,0},{2,3},{3,2},{4,5},{5,4},{6,7},{7,6},{8,9},{9,8},{10,11... | collective-permute-start | bytes 245768 | tf_op jit(solution)/shard_map/ppermute | solution.py:17
  44.3 13.9 %slice-start.1 = ((s8[7340032]{0:T(1024)(128)(4,1)}), s8[3145728]{0:T(1024)(128)(4,1)S(1)}, s32[]{:S(2)}) async-start(s8[7340032]{0:T(1024)(128)(4,1)} %bitcast.14), calls=%async_computation.1 | async-start | bytes 6291456
  46.7 7.0 %collective-permute-start.13 = (bf16[80,512]{1,0:T(8,128)(2,1)S(1)}, bf16[80,512]{1,0:T(8,128)(2,1)S(1)}, u32[]{:S(2)}, u32[]{:S(2)}) collective-permute-start(bf16[80,512]{1,0:T(8,128)(2,1)S(1)} %activate.3.refs_3_), channel_id=1, source_target_pairs={{0,3},{1,2},{2,1},{3,0},{4,7},{5,6},{6,5},{7,4},{8,11},{9,10},{10,... | collective-permute-start | bytes 245768 | tf_op jit(solution)/shard_map/ppermute | solution.py:17
  49.6 8.6 %collective-permute-start.18 = (bf16[80,512]{1,0:T(8,128)(2,1)S(1)}, bf16[80,512]{1,0:T(8,128)(2,1)S(1)}, u32[]{:S(2)}, u32[]{:S(2)}) collective-permute-start(bf16[80,512]{1,0:T(8,128)(2,1)S(1)} %activate.3.refs_3_), channel_id=1, source_target_pairs={{0,2},{1,3},{2,0},{3,1},{4,6},{5,7},{6,4},{7,5},{8,10},{9,11},{10,... | collective-permute-start | bytes 245768 | tf_op jit(solution)/shard_map/ppermute | solution.py:17
  49.6 8.6 %collective-permute-start.19 = (bf16[80,512]{1,0:T(8,128)(2,1)S(1)}, bf16[80,512]{1,0:T(8,128)(2,1)S(1)}, u32[]{:S(2)}, u32[]{:S(2)}) collective-permute-start(bf16[80,512]{1,0:T(8,128)(2,1)S(1)} %activate.3.refs_3_), channel_id=1, source_target_pairs={{0,1},{1,0},{2,3},{3,2},{4,5},{5,4},{6,7},{7,6},{8,9},{9,8},{10,11... | collective-permute-start | bytes 245768 | tf_op jit(solution)/shard_map/ppermute | solution.py:17
  53.8 7.4 %collective-permute-start.15 = (bf16[80,512]{1,0:T(8,128)(2,1)S(1)}, bf16[80,512]{1,0:T(8,128)(2,1)S(1)}, u32[]{:S(2)}, u32[]{:S(2)}) collective-permute-start(bf16[80,512]{1,0:T(8,128)(2,1)S(1)} %hold.1), channel_id=1, source_target_pairs={{0,3},{1,2},{2,1},{3,0},{4,7},{5,6},{6,5},{7,4},{8,11},{9,10},{10,... | collective-permute-start | bytes 245768 | tf_op jit(solution)/shard_map/ppermute | solution.py:17
  56.0 6.3 %collective-permute-start.16 = (bf16[80,512]{1,0:T(8,128)(2,1)S(1)}, bf16[80,512]{1,0:T(8,128)(2,1)S(1)}, u32[]{:S(2)}, u32[]{:S(2)}) collective-permute-start(bf16[80,512]{1,0:T(8,128)(2,1)S(1)} %hold.1), channel_id=1, source_target_pairs={{0,2},{1,3},{2,0},{3,1},{4,6},{5,7},{6,4},{7,5},{8,10},{9,11},{10,... | collective-permute-start | bytes 245768 | tf_op jit(solution)/shard_map/ppermute | solution.py:17
  59.6 5.8 %collective-permute-start.20 = (bf16[40,1792]{1,0:T(8,128)(2,1)S(1)}, bf16[40,1792]{1,0:T(8,128)(2,1)S(1)}, u32[]{:S(2)}, u32[]{:S(2)}) collective-permute-start(bf16[40,1792]{1,0:T(8,128)(2,1)S(1)} %get-tuple-element.40), channel_id=1, source_target_pairs={{0,8},{4,12},{8,0},{12,4},{1,9},{5,13},{9,1},{13,5},{2,10},{6,14},... | collective-permute-start | bytes 430088 | tf_op jit(solution)/shard_map/ppermute | solution.py:17
  61.2 6.0 %collective-permute-start.21 = (bf16[40,1792]{1,0:T(8,128)(2,1)S(1)}, bf16[40,1792]{1,0:T(8,128)(2,1)S(1)}, u32[]{:S(2)}, u32[]{:S(2)}) collective-permute-start(bf16[40,1792]{1,0:T(8,128)(2,1)S(1)} %get-tuple-element.41), channel_id=1, source_target_pairs={{0,12},{4,8},{8,4},{12,0},{1,13},{5,9},{9,5},{13,1},{2,14},{6,10},... | collective-permute-start | bytes 430088 | tf_op jit(solution)/shard_map/ppermute | solution.py:17
  63.7 3.5 %collective-permute-start.17 = (bf16[40,1792]{1,0:T(8,128)(2,1)S(1)}, bf16[40,1792]{1,0:T(8,128)(2,1)S(1)}, u32[]{:S(2)}, u32[]{:S(2)}) collective-permute-start(bf16[40,1792]{1,0:T(8,128)(2,1)S(1)} %get-tuple-element.39), channel_id=1, source_target_pairs={{0,4},{4,0},{8,12},{12,8},{1,5},{5,1},{9,13},{13,9},{2,6},{6,2},{1... | collective-permute-start | bytes 430088 | tf_op jit(solution)/shard_map/ppermute | solution.py:17

commit v7 on v6

--- a/solution.py
+++ b/solution.py
@@ -177,16 +177,21 @@
     out_ref[...] = (gate / (1.0 + jnp.exp(-gate))).astype(bf16)
 
 
-def down_kernel(n_tensor, n, cap, block_ref, w_ref, *refs):
-    pieces, outs = refs[:n_tensor], refs[n_tensor:]
+def down_kernel(steps, cap, adds, block_ref, w_ref, *refs):
+    pieces, outs = refs[: len(steps)], refs[len(steps) :]
     width = pieces[0].shape[1]
     total = None
-    for i, k in enumerate(partners(n_tensor)):
+    if adds:
+        total, outs = outs[0][...], outs[1:]
+    for i, k in enumerate(steps):
         start = pl.multiple_of((block_ref[0] ^ k) * width, width)
         term = jnp.dot(pieces[i][...], w_ref[0, pl.ds(start, width), :], preferred_element_type=jnp.float32)
         total = term if total is None else total + term
-    for k in range(n):
-        outs[k][...] = total[k * cap : (k + 1) * cap, :].astype(jnp.bfloat16)
+    if cap is None:
+        outs[-1][...] = total
+    else:
+        for i, out in enumerate(outs):
+            out[...] = total[i * cap : (i + 1) * cap, :].astype(jnp.bfloat16)
 
 
 def combine_kernel(n, high_ref, low_ref, *refs):
@@ -357,17 +362,19 @@
             name="hold",
         )(value, *after)
 
-    def produced(ks, hidden):
+    def down(ks, hidden, steps, earlier=None, final=True, after=()):
+        count = len(ks) * cap
+        adds = earlier is not None
         outs = pl.pallas_call(
-            functools.partial(down_kernel, nt, len(ks), cap),
-            out_shape=(sds((cap, share), bf16),) * len(ks),
-            in_specs=[scalar(), whole()] + [whole()] * nt,
-            out_specs=(whole(),) * len(ks),
+            functools.partial(down_kernel, steps, cap if final else None, adds),
+            out_shape=(sds((cap, share), bf16),) * len(ks) if final else sds((count, share), f32),
+            in_specs=[scalar(), whole()] + [whole()] * (len(steps) + adds) + [anywhere()] * len(after),
+            out_specs=(whole(),) * len(ks) if final else whole(),
             compiler_params=params(),
-            cost_estimate=estimate(2 * len(ks) * cap * share * ff * nt, 2 * share * ff * nt),
+            cost_estimate=estimate(2 * count * share * ff * len(steps), 2 * share * ff * len(steps)),
             name="down",
-        )(z_arr, w_down, *[hidden[k] for k in partners(nt)])
-        return dict(zip(ks, outs))
+        )(z_arr, w_down, *[hidden[k] for k in steps], *[earlier] * adds, *after)
+        return dict(zip(ks, outs)) if final else outs
 
     near_gates = summed_gate(near)
     far_gates = summed_gate(far, near_gates)
@@ -375,12 +382,14 @@
     near_hidden = {0: near_own, 1: exchange(near_own, "tensor", 1)}
     far_own = activated(far, far_gates, (near_own,))
     far_hidden = {k: exchange(far_own, "tensor", k) if k else far_own for k in partners(nt)}
-    waiting = held(near_own, far_hidden[3], near_hidden[1])
+    early = [0, 3]
+    far_sum = down(far, far_hidden, early, final=False, after=(near_hidden[1],))
+    near_sum = down(near, near_hidden, [0, 1], final=False, after=(far_sum,))
+    waiting = held(near_own, far_sum, near_sum)
     near_hidden.update({k: exchange(waiting, "tensor", k) for k in partners(nt) if k > 1})
-    returned = {}
-    for ks, hidden in ((far, far_hidden), (near, near_hidden)):
-        for k, value in produced(ks, hidden).items():
-            returned[k] = exchange(value, "expert", k) if k else value
+    results = down(far, far_hidden, [k for k in partners(nt) if k not in early], far_sum)
+    results.update(down(near, near_hidden, [k for k in partners(nt) if k > 1], near_sum))
+    returned = {k: exchange(value, "expert", k) if k else value for k, value in results.items()}
 
     moe_out = pl.pallas_call(
         functools.partial(combine_kernel, ne),

time: 68.5 us -> 67.2 us (0.981)
  waiting for transfers between devices: 18.1 us -> 17.1 us
    ppermute x19, waiting for transfers between devices: 12.8 us -> 11.8 us  [exchange(): return lax.ppermute(value, axis, [(i, i ^ step) for i in range(n)])]
    pallas_call x2 -> x4, Pallas kernels: 2.78 us -> 3.03 us  [down(): pl.pallas_call(functools.partial(down_kernel, steps, cap if final else No...]
  transfers between devices with their start and end apart: 22 -> 22, of which waited for: 11 -> 10; matrix products, arithmetic and copies ran while one was open for 2% -> 2% of each run, Pallas kernels for 14% -> 14%
where the time goes in v7:
time: 67.2 us; the launch traced here: 67 us
  starting transfers between devices  30.9 us (46%)
  waiting for transfers between devices  17.1 us (25%)
  Pallas kernels  11 us (16%)
  local copies, waits for them, and re-layouts  7.03 us (10%)
  between operations  0.94 us (1%)
    ppermute x19, starting transfers between devices, exchange(): return lax.ppermute(value, axis, [(i, i ^ step) for i in range(n)])  23.5 us
    ppermute x19, waiting for transfers between devices, exchange(): return lax.ppermute(value, axis, [(i, i ^ step) for i in range(n)])  11.8 us
    ppermute x1, starting transfers between devices, local(): parts.append(lax.ppermute(block(z ^ 2), 'tensor', [(0, 2), (3, 1)]))  5.75 us
    unnamed x14, local copies, waits for them, and re-layouts  5.58 us
    ppermute x1, waiting for transfers between devices, local(): lax.ppermute(merged, 'tensor', [(0, 1), (1, 3), (2, 0), (3, 2)])  5.28 us
    pallas_call x8, Pallas kernels, summed_gate(): pl.pallas_call(gate_kernel, out_shape=sds((tall, ff), bf16), grid_spec=pl...  3.57 us
    pallas_call x4, Pallas kernels, down(): pl.pallas_call(functools.partial(down_kernel, steps, cap if final else No...  3.03 us
    dynamic_slice x1, local copies, waits for them, and re-layouts, block(): return lax.dynamic_slice(attn_partial[0], (0, k * share), (tokens, share))  1.44 us
  transfers between devices with their start and end apart: 22, of which 10 were waited for; matrix products, arithmetic and copies ran while one was open for 2% of the time, Pallas kernels for 14%

profile of v7, /device:TPU:0, one launch (start us, length us, event | category | flops | bytes accessed | tf_op | source)
XLA Modules:
  0.0 67.0 jit_solution(16650625573474374237)
XLA Ops:
  0.7 1.4 %dynamic-slice_bitcast_fusion = (bf16[64,1792]{1,0:T(8,128)(2,1)S(1)}, bf16[64,1792]{1,0:T(8,128)(2,1)S(1)}, bf16[64,1792]{1,0:T(8,128)(2,1)S(1)}, bf16[64,1792]{1,0:T(8,128)(2,1)S(1)}, bf16[64,1792]{1,0:T(8,128)(2,1)S(1)}) fusion(bf16[1,64,7168]{2,1,0:T(8,128)(2,1)} %param.8, s32[]{:T(128)S(6)} %select_n.30, s32[]{:T(128)S(6)} %select_n.27, s32[]{:T(128)S(6)} %select_n.26, ...), kind=kLoop, calls=%fused_computation | loop fusion | bytes 2293780 | tf_op jit(solution)/shard_map/dynamic_slice | solution.py:224
  2.1 3.1 %collective-permute-start.2 = (bf16[64,1792]{1,0:T(8,128)(2,1)S(1)}, bf16[64,1792]{1,0:T(8,128)(2,1)S(1)}, u32[]{:S(2)}, u32[]{:S(2)}) collective-permute-start(bf16[64,1792]{1,0:T(8,128)(2,1)S(1)} %get-tuple-element.42), channel_id=1, source_target_pairs={{0,1},{1,0},{2,3},{3,2},{4,5},{5,4},{6,7},{7,6},{8,9},{9,8},{10,11... | collective-permute-start | bytes 688136 | tf_op jit(solution)/shard_map/ppermute | solution.py:17
  5.2 0.7 collective-permute-start
  5.9 5.8 %collective-permute-start.1 = (bf16[64,1792]{1,0:T(8,128)(2,1)S(1)}, bf16[64,1792]{1,0:T(8,128)(2,1)S(1)}, u32[]{:S(2)}, u32[]{:S(2)}) collective-permute-start(bf16[64,1792]{1,0:T(8,128)(2,1)S(1)} %get-tuple-element.43.passing_ref), channel_id=1, source_target_pairs={{0,2},{3,1},{4,6},{7,5},{8,10},{11,9},{12,14},{15,13},{16,18},{19,... | collective-permute-start | bytes 688136 | tf_op jit(solution)/shard_map/ppermute | solution.py:232
  11.7 1.0 %collective-permute-start.3 = (bf16[64,1792]{1,0:T(8,128)(2,1)S(1)}, bf16[64,1792]{1,0:T(8,128)(2,1)S(1)}, u32[]{:S(2)}, u32[]{:S(2)}) collective-permute-start(bf16[64,1792]{1,0:T(8,128)(2,1)S(1)} %merge.1), channel_id=1, source_target_pairs={{0,1},{1,3},{2,0},{3,2},{4,5},{5,7},{6,4},{7,6},{8,9},{9,11},{10,8... | collective-permute-start | bytes 688136 | tf_op jit(solution)/shard_map/ppermute | solution.py:242
  12.7 0.8 %copy.10.scores_ref = f32[64,2]{1,0:T(8,128)S(1)} copy(f32[64,2]{0,1:T(2,128)} %param.11) | data formatting | bytes 1024 | tf_op args[4]
  13.4 0.8 %copy.9.ids_ref = s32[64,2]{1,0:T(8,128)S(1)} copy(s32[64,2]{0,1:T(2,128)} %param.10) | data formatting | bytes 1024 | tf_op args[3]
  14.2 3.1 %copy-done = bf16[1,1792,2048]{2,1,0:T(8,128)(2,1)S(1)} copy-done((bf16[1,1792,2048]{2,1,0:T(8,128)(2,1)S(1)}, bf16[1,1792,2048]{2,1,0:T(8,128)(2,1)}, u32[]{:S(2)}) %copy-start) | copy-done | bytes 7340056
  17.3 0.9 %copy-done.1 = bf16[64,1792]{1,0:T(8,128)(2,1)S(1)} copy-done((bf16[64,1792]{1,0:T(8,128)(2,1)S(1)}, bf16[64,1792]{1,0:T(8,128)(2,1)}, u32[]{:S(2)}) %copy-start.1) | copy-done | bytes 229400
  18.2 0.8 %fetch.1 = (bf16[64,1792]{1,0:T(8,128)(2,1)S(1)}, bf16[1,1792,2048]{2,1,0:T(8,128)(2,1)S(1)}) custom-call(bf16[64,1792]{1,0:T(8,128)(2,1)S(1)} %copy-done.1, bf16[1,1792,2048]{2,1,0:T(8,128)(2,1)S(1)} %copy-done), custom_call_target="tpu_custom_call" | custom-call | flops 1000000 | bytes 7569408 | tf_op jit(solution)/shard_map/fetch/pallas_call | solution.py:259
  19.0 0.5 routing.1
  19.6 5.3 %collective-permute-done.3.refs_3_ = bf16[64,1792]{1,0:T(8,128)(2,1)S(1)} collective-permute-done((bf16[64,1792]{1,0:T(8,128)(2,1)S(1)}, bf16[64,1792]{1,0:T(8,128)(2,1)S(1)}, u32[]{:S(2)}, u32[]{:S(2)}) %collective-permute-start.3) | collective-permute-done | bytes 229408 | tf_op jit(solution)/shard_map/ppermute | solution.py:242
  24.9 0.4 add.22
  25.3 0.2 pack.1
  25.5 1.6 %collective-permute-start.4 = (bf16[40,1792]{1,0:T(8,128)(2,1)S(1)}, bf16[40,1792]{1,0:T(8,128)(2,1)S(1)}, u32[]{:S(2)}, u32[]{:S(2)}) collective-permute-start(bf16[40,1792]{1,0:T(8,128)(2,1)S(1)} %get-tuple-element.25), channel_id=1, source_target_pairs={{0,8},{4,12},{8,0},{12,4},{1,9},{5,13},{9,1},{13,5},{2,10},{6,14},... | collective-permute-start | bytes 430088 | tf_op jit(solution)/shard_map/ppermute | solution.py:17
  27.1 0.4 collective-permute-start.5
  27.6 0.5 gate.12
  28.1 2.7 %collective-permute-start.9 = (bf16[88,512]{1,0:T(8,128)(2,1)S(1)}, bf16[88,512]{1,0:T(8,128)(2,1)S(1)}, u32[]{:S(2)}, u32[]{:S(2)}) collective-permute-start(bf16[88,512]{1,0:T(8,128)(2,1)S(1)} %gate.12), channel_id=1, source_target_pairs={{0,3},{1,2},{2,1},{3,0},{4,7},{5,6},{6,5},{7,4},{8,11},{9,10},{10,... | collective-permute-start | bytes 270344 | tf_op jit(solution)/shard_map/ppermute | solution.py:17
  30.8 0.4 gate.11
  31.3 0.4 gate.8
  31.8 1.8 %collective-permute-start.7 = (bf16[88,512]{1,0:T(8,128)(2,1)S(1)}, bf16[88,512]{1,0:T(8,128)(2,1)S(1)}, u32[]{:S(2)}, u32[]{:S(2)}) collective-permute-start(bf16[88,512]{1,0:T(8,128)(2,1)S(1)} %gate.8), channel_id=1, source_target_pairs={{0,2},{1,3},{2,0},{3,1},{4,6},{5,7},{6,4},{7,5},{8,10},{9,11},{10,... | collective-permute-start | bytes 270344 | tf_op jit(solution)/shard_map/ppermute | solution.py:17
  33.6 0.8 %collective-permute-done.5.refs_1_ = bf16[40,1792]{1,0:T(8,128)(2,1)S(1)} collective-permute-done((bf16[40,1792]{1,0:T(8,128)(2,1)S(1)}, bf16[40,1792]{1,0:T(8,128)(2,1)S(1)}, u32[]{:S(2)}, u32[]{:S(2)}) %collective-permute-start.5) | collective-permute-done | bytes 143392 | tf_op jit(solution)/shard_map/ppermute | solution.py:17
  34.6 0.8 %collective-permute-done.9.refs_3_.refs_0_ = bf16[88,512]{1,0:T(8,128)(2,1)S(1)} collective-permute-done((bf16[88,512]{1,0:T(8,128)(2,1)S(1)}, bf16[88,512]{1,0:T(8,128)(2,1)S(1)}, u32[]{:S(2)}, u32[]{:S(2)}) %collective-permute-start.9) | collective-permute-done | bytes 90144 | tf_op jit(solution)/shard_map/ppermute | solution.py:17
  35.4 0.4 gate.15
  35.9 2.7 %collective-permute-start.12 = (bf16[88,512]{1,0:T(8,128)(2,1)S(1)}, bf16[88,512]{1,0:T(8,128)(2,1)S(1)}, u32[]{:S(2)}, u32[]{:S(2)}) collective-permute-start(bf16[88,512]{1,0:T(8,128)(2,1)S(1)} %gate.15), channel_id=1, source_target_pairs={{0,3},{1,2},{2,1},{3,0},{4,7},{5,6},{6,5},{7,4},{8,11},{9,10},{10,... | collective-permute-start | bytes 270344 | tf_op jit(solution)/shard_map/ppermute | solution.py:17
  38.6 0.4 gate.14
  39.2 0.6 collective-permute-done.7.refs_0_.refs_2_
  39.8 0.4 gate.9.after_ref
  40.2 2.1 %collective-permute-start.11 = (bf16[88,512]{1,0:T(8,128)(2,1)S(1)}, bf16[88,512]{1,0:T(8,128)(2,1)S(1)}, u32[]{:S(2)}, u32[]{:S(2)}) collective-permute-start(bf16[88,512]{1,0:T(8,128)(2,1)S(1)} %gate.9.after_ref), channel_id=1, source_target_pairs={{0,2},{1,3},{2,0},{3,1},{4,6},{5,7},{6,4},{7,5},{8,10},{9,11},{10,... | collective-permute-start | bytes 270344 | tf_op jit(solution)/shard_map/ppermute | solution.py:17
  42.3 0.4 gate.10.refs_0_
  43.0 0.6 collective-permute-start.14
  43.6 0.7 %store.1 = (bf16[64,1792]{1,0:T(8,128)(2,1)}, f32[8,128]{1,0:T(8,128)S(1)}) custom-call(bf16[64,1792]{1,0:T(8,128)(2,1)S(1)} %get-tuple-element.24.stream_ref.values_ref, bf16[88,512]{1,0:T(8,128)(2,1)S(1)} %gate.9.after_ref), custom_call_target="tpu_custom_call" | custom-call | flops 1000000 | bytes 458752 | tf_op jit(solution)/shard_map/store/pallas_call | solution.py:310
  44.3 0.4 gate.13.refs_0_
  44.8 0.4 collective-permute-done.10.refs_1_
  45.2 1.3 %collective-permute-done.11.refs_2_ = bf16[88,512]{1,0:T(8,128)(2,1)S(1)} collective-permute-done((bf16[88,512]{1,0:T(8,128)(2,1)S(1)}, bf16[88,512]{1,0:T(8,128)(2,1)S(1)}, u32[]{:S(2)}, u32[]{:S(2)}) %collective-permute-start.11) | collective-permute-done | bytes 90144 | tf_op jit(solution)/shard_map/ppermute | solution.py:17
  46.7 2.8 %collective-permute-start.13 = (bf16[80,512]{1,0:T(8,128)(2,1)S(1)}, bf16[80,512]{1,0:T(8,128)(2,1)S(1)}, u32[]{:S(2)}, u32[]{:S(2)}) collective-permute-start(bf16[80,512]{1,0:T(8,128)(2,1)S(1)} %activate.3.refs_0_), channel_id=1, source_target_pairs={{0,3},{1,2},{2,1},{3,0},{4,7},{5,6},{6,5},{7,4},{8,11},{9,10},{10,... | collective-permute-start | bytes 245768 | tf_op jit(solution)/shard_map/ppermute | solution.py:17
  49.6 1.6 %collective-permute-start.19 = (bf16[80,512]{1,0:T(8,128)(2,1)S(1)}, bf16[80,512]{1,0:T(8,128)(2,1)S(1)}, u32[]{:S(2)}, u32[]{:S(2)}) collective-permute-start(bf16[80,512]{1,0:T(8,128)(2,1)S(1)} %activate.3.refs_0_), channel_id=1, source_target_pairs={{0,1},{1,0},{2,3},{3,2},{4,5},{5,4},{6,7},{7,6},{8,9},{9,8},{10,11... | collective-permute-start | bytes 245768 | tf_op jit(solution)/shard_map/ppermute | solution.py:17
  51.2 2.6 %collective-permute-done.13.refs_1_ = bf16[80,512]{1,0:T(8,128)(2,1)S(1)} collective-permute-done((bf16[80,512]{1,0:T(8,128)(2,1)S(1)}, bf16[80,512]{1,0:T(8,128)(2,1)S(1)}, u32[]{:S(2)}, u32[]{:S(2)}) %collective-permute-start.13) | collective-permute-done | bytes 81952 | tf_op jit(solution)/shard_map/ppermute | solution.py:17
  53.8 0.8 %down.4.refs_2_.refs_0_ = f32[80,1792]{1,0:T(8,128)S(1)} custom-call(s32[1]{0:T(128)} %bitcast.8.block_ref, bf16[1,2048,1792]{2,1,0:T(8,128)(2,1)S(1)} %bitcast.15, bf16[80,512]{1,0:T(8,128)(2,1)S(1)} %activate.3.refs_0_, bf16[80,512]{1,0:T(8,128)(2,1)S(1)} %collective-permute-done.13.refs_1_, bf16[80,512]{1,0:T(8,128)(2,1)S(1)} %collective-permute-done.14.refs_2_.refs_1_), custom_call_target="tpu_custom_call" | custom-call | flops 293601280 | bytes 3670016 | tf_op jit(solution)/shard_map/down/pallas_call | solution.py:368
  54.5 0.8 %down.5.refs_1_.refs_2_ = f32[80,1792]{1,0:T(8,128)S(1)} custom-call(s32[1]{0:T(128)} %bitcast.8.block_ref, bf16[1,2048,1792]{2,1,0:T(8,128)(2,1)S(1)} %bitcast.15, bf16[80,512]{1,0:T(8,128)(2,1)S(1)} %activate.2.refs_4_.refs_0_.value_ref, bf16[80,512]{1,0:T(8,128)(2,1)S(1)} %collective-permute-done.14.refs_2_.refs_1_, f32[80,1792]{1,0:T(8,128)S(1)} %down.4.refs_2_.refs_0_), custom_call_target="tpu_custom_call" | custom-call | flops 293601280 | bytes 3670016 | tf_op jit(solution)/shard_map/down/pallas_call | solution.py:368
  55.3 2.2 %collective-permute-start.15 = (bf16[80,512]{1,0:T(8,128)(2,1)S(1)}, bf16[80,512]{1,0:T(8,128)(2,1)S(1)}, u32[]{:S(2)}, u32[]{:S(2)}) collective-permute-start(bf16[80,512]{1,0:T(8,128)(2,1)S(1)} %hold.1), channel_id=1, source_target_pairs={{0,3},{1,2},{2,1},{3,0},{4,7},{5,6},{6,5},{7,4},{8,11},{9,10},{10,... | collective-permute-start | bytes 245768 | tf_op jit(solution)/shard_map/ppermute | solution.py:17
  57.6 0.8 %down.7 = (bf16[40,1792]{1,0:T(8,128)(2,1)S(1)}, bf16[40,1792]{1,0:T(8,128)(2,1)S(1)}) custom-call(s32[1]{0:T(128)} %bitcast.8.block_ref, bf16[1,2048,1792]{2,1,0:T(8,128)(2,1)S(1)} %bitcast.15, bf16[80,512]{1,0:T(8,128)(2,1)S(1)} %collective-permute-done.18.refs_0_, bf16[80,512]{1,0:T(8,128)(2,1)S(1)} %collective-permute-done.19.refs_1_, ...), custom_call_target="tpu_custom_call" | custom-call | flops 293601280 | bytes 3670016 | tf_op jit(solution)/shard_map/down/pallas_call | solution.py:368
  58.4 1.6 %collective-permute-start.20 = (bf16[40,1792]{1,0:T(8,128)(2,1)S(1)}, bf16[40,1792]{1,0:T(8,128)(2,1)S(1)}, u32[]{:S(2)}, u32[]{:S(2)}) collective-permute-start(bf16[40,1792]{1,0:T(8,128)(2,1)S(1)} %get-tuple-element.40), channel_id=1, source_target_pairs={{0,8},{4,12},{8,0},{12,4},{1,9},{5,13},{9,1},{13,5},{2,10},{6,14},... | collective-permute-start | bytes 430088 | tf_op jit(solution)/shard_map/ppermute | solution.py:17
  59.9 1.7 %collective-permute-done.15.refs_0_ = bf16[80,512]{1,0:T(8,128)(2,1)S(1)} collective-permute-done((bf16[80,512]{1,0:T(8,128)(2,1)S(1)}, bf16[80,512]{1,0:T(8,128)(2,1)S(1)}, u32[]{:S(2)}, u32[]{:S(2)}) %collective-permute-start.15) | collective-permute-done | bytes 81952 | tf_op jit(solution)/shard_map/ppermute | solution.py:17
  61.6 2.1 %collective-permute-done.16.refs_1_ = bf16[80,512]{1,0:T(8,128)(2,1)S(1)} collective-permute-done((bf16[80,512]{1,0:T(8,128)(2,1)S(1)}, bf16[80,512]{1,0:T(8,128)(2,1)S(1)}, u32[]{:S(2)}, u32[]{:S(2)}) %collective-permute-start.16) | collective-permute-done | bytes 81952 | tf_op jit(solution)/shard_map/ppermute | solution.py:17
  63.7 0.8 %down.6 = (bf16[40,1792]{1,0:T(8,128)(2,1)S(1)}, bf16[40,1792]{1,0:T(8,128)(2,1)S(1)}) custom-call(s32[1]{0:T(128)} %bitcast.8.block_ref, bf16[1,2048,1792]{2,1,0:T(8,128)(2,1)S(1)} %bitcast.15, bf16[80,512]{1,0:T(8,128)(2,1)S(1)} %collective-permute-done.15.refs_0_, bf16[80,512]{1,0:T(8,128)(2,1)S(1)} %collective-permute-done.16.refs_1_, ...), custom_call_target="tpu_custom_call" | custom-call | flops 293601280 | bytes 3670016 | tf_op jit(solution)/shard_map/down/pallas_call | solution.py:368
  64.6 1.4 %collective-permute-done.21.refs_3_ = bf16[40,1792]{1,0:T(8,128)(2,1)S(1)} collective-permute-done((bf16[40,1792]{1,0:T(8,128)(2,1)S(1)}, bf16[40,1792]{1,0:T(8,128)(2,1)S(1)}, u32[]{:S(2)}, u32[]{:S(2)}) %collective-permute-start.21) | collective-permute-done | bytes 143392 | tf_op jit(solution)/shard_map/ppermute | solution.py:17
  66.0 1.0 %combine.1 = bf16[64,1792]{1,0:T(8,128)(2,1)} custom-call(bf16[64,160]{1,0:T(8,128)(2,1)S(1)} %get-tuple-element.35.high_ref, bf16[64,160]{1,0:T(8,128)(2,1)S(1)} %get-tuple-element.36.low_ref, bf16[40,1792]{1,0:T(8,128)(2,1)S(1)} %get-tuple-element.38.refs_0_, bf16[40,1792]{1,0:T(8,128)(2,1)S(1)} %collective-permute-done.17.refs_1_, ...), custom_call_target="tpu_custom_call" | custom-call | flops 73400320 | bytes 573440 | tf_op jit(solution)/shard_map/combine/pallas_call | solution.py:394
  (37 shorter events, 1.2 us)
Async XLA Ops:
  0.6 18.4 %copy-start.2 = (s32[64,2]{0,1:T(2,128)S(1)}, s32[64,2]{0,1:T(2,128)}, u32[]{:S(2)}) copy-start(s32[64,2]{0,1:T(2,128)} %param.10) | copy-start | bytes 1540
  0.6 26.8 %copy-start.3 = (bf16[1792]{0:T(1024)(128)(2,1)S(1)}, bf16[1792]{0:T(1024)(128)(2,1)}, u32[]{:S(2)}) copy-start(bf16[1792]{0:T(1024)(128)(2,1)} %param.9) | copy-start | bytes 10756
  2.1 9.5 %collective-permute-start.2 = (bf16[64,1792]{1,0:T(8,128)(2,1)S(1)}, bf16[64,1792]{1,0:T(8,128)(2,1)S(1)}, u32[]{:S(2)}, u32[]{:S(2)}) collective-permute-start(bf16[64,1792]{1,0:T(8,128)(2,1)S(1)} %get-tuple-element.42), channel_id=1, source_target_pairs={{0,1},{1,0},{2,3},{3,2},{4,5},{5,4},{6,7},{7,6},{8,9},{9,8},{10,11... | collective-permute-start | bytes 688136 | tf_op jit(solution)/shard_map/ppermute | solution.py:17
  5.2 14.3 %collective-permute-start = (bf16[64,1792]{1,0:T(8,128)(2,1)S(1)}, bf16[64,1792]{1,0:T(8,128)(2,1)S(1)}, u32[]{:S(2)}, u32[]{:S(2)}) collective-permute-start(bf16[64,1792]{1,0:T(8,128)(2,1)S(1)} %get-tuple-element.44), channel_id=1, source_target_pairs={{1,2},{2,1},{5,6},{6,5},{9,10},{10,9},{13,14},{14,13},{17,18},{18,... | collective-permute-start | bytes 688136 | tf_op jit(solution)/shard_map/ppermute | solution.py:231
  5.9 13.7 %collective-permute-start.1 = (bf16[64,1792]{1,0:T(8,128)(2,1)S(1)}, bf16[64,1792]{1,0:T(8,128)(2,1)S(1)}, u32[]{:S(2)}, u32[]{:S(2)}) collective-permute-start(bf16[64,1792]{1,0:T(8,128)(2,1)S(1)} %get-tuple-element.43.passing_ref), channel_id=1, source_target_pairs={{0,2},{3,1},{4,6},{7,5},{8,10},{11,9},{12,14},{15,13},{16,18},{19,... | collective-permute-start | bytes 688136 | tf_op jit(solution)/shard_map/ppermute | solution.py:232
  11.7 13.1 %collective-permute-start.3 = (bf16[64,1792]{1,0:T(8,128)(2,1)S(1)}, bf16[64,1792]{1,0:T(8,128)(2,1)S(1)}, u32[]{:S(2)}, u32[]{:S(2)}) collective-permute-start(bf16[64,1792]{1,0:T(8,128)(2,1)S(1)} %merge.1), channel_id=1, source_target_pairs={{0,1},{1,3},{2,0},{3,2},{4,5},{5,7},{6,4},{7,6},{8,9},{9,11},{10,8... | collective-permute-start | bytes 688136 | tf_op jit(solution)/shard_map/ppermute | solution.py:242
  14.2 3.1 %copy-start = (bf16[1,1792,2048]{2,1,0:T(8,128)(2,1)S(1)}, bf16[1,1792,2048]{2,1,0:T(8,128)(2,1)}, u32[]{:S(2)}) copy-start(bf16[1,1792,2048]{2,1,0:T(8,128)(2,1)} %refs_1_.1) | copy-start | bytes 22020100
  17.3 0.9 %copy-start.1 = (bf16[64,1792]{1,0:T(8,128)(2,1)S(1)}, bf16[64,1792]{1,0:T(8,128)(2,1)}, u32[]{:S(2)}) copy-start(bf16[64,1792]{1,0:T(8,128)(2,1)} %refs_0_.1) | copy-start | bytes 688132
  25.2 2.2 %collective-permute-start.6 = (bf16[40,1792]{1,0:T(8,128)(2,1)S(1)}, bf16[40,1792]{1,0:T(8,128)(2,1)S(1)}, u32[]{:S(2)}, u32[]{:S(2)}) collective-permute-start(bf16[40,1792]{1,0:T(8,128)(2,1)S(1)} %get-tuple-element.31), channel_id=1, source_target_pairs={{0,4},{4,0},{8,12},{12,8},{1,5},{5,1},{9,13},{13,9},{2,6},{6,2},{1... | collective-permute-start | bytes 430088 | tf_op jit(solution)/shard_map/ppermute | solution.py:17
  25.5 8.1 %collective-permute-start.4 = (bf16[40,1792]{1,0:T(8,128)(2,1)S(1)}, bf16[40,1792]{1,0:T(8,128)(2,1)S(1)}, u32[]{:S(2)}, u32[]{:S(2)}) collective-permute-start(bf16[40,1792]{1,0:T(8,128)(2,1)S(1)} %get-tuple-element.25), channel_id=1, source_target_pairs={{0,8},{4,12},{8,0},{12,4},{1,9},{5,13},{9,1},{13,5},{2,10},{6,14},... | collective-permute-start | bytes 430088 | tf_op jit(solution)/shard_map/ppermute | solution.py:17
  27.1 7.3 %collective-permute-start.5 = (bf16[40,1792]{1,0:T(8,128)(2,1)S(1)}, bf16[40,1792]{1,0:T(8,128)(2,1)S(1)}, u32[]{:S(2)}, u32[]{:S(2)}) collective-permute-start(bf16[40,1792]{1,0:T(8,128)(2,1)S(1)} %get-tuple-element.26), channel_id=1, source_target_pairs={{0,12},{4,8},{8,4},{12,0},{1,13},{5,9},{9,5},{13,1},{2,14},{6,10},... | collective-permute-start | bytes 430088 | tf_op jit(solution)/shard_map/ppermute | solution.py:17
  28.1 7.3 %collective-permute-start.9 = (bf16[88,512]{1,0:T(8,128)(2,1)S(1)}, bf16[88,512]{1,0:T(8,128)(2,1)S(1)}, u32[]{:S(2)}, u32[]{:S(2)}) collective-permute-start(bf16[88,512]{1,0:T(8,128)(2,1)S(1)} %gate.12), channel_id=1, source_target_pairs={{0,3},{1,2},{2,1},{3,0},{4,7},{5,6},{6,5},{7,4},{8,11},{9,10},{10,... | collective-permute-start | bytes 270344 | tf_op jit(solution)/shard_map/ppermute | solution.py:17
  31.3 7.4 %collective-permute-start.8 = (bf16[88,512]{1,0:T(8,128)(2,1)S(1)}, bf16[88,512]{1,0:T(8,128)(2,1)S(1)}, u32[]{:S(2)}, u32[]{:S(2)}) collective-permute-start(bf16[88,512]{1,0:T(8,128)(2,1)S(1)} %gate.11), channel_id=1, source_target_pairs={{0,1},{1,0},{2,3},{3,2},{4,5},{5,4},{6,7},{7,6},{8,9},{9,8},{10,11... | collective-permute-start | bytes 270344 | tf_op jit(solution)/shard_map/ppermute | solution.py:17
  31.8 8.0 %collective-permute-start.7 = (bf16[88,512]{1,0:T(8,128)(2,1)S(1)}, bf16[88,512]{1,0:T(8,128)(2,1)S(1)}, u32[]{:S(2)}, u32[]{:S(2)}) collective-permute-start(bf16[88,512]{1,0:T(8,128)(2,1)S(1)} %gate.8), channel_id=1, source_target_pairs={{0,2},{1,3},{2,0},{3,1},{4,6},{5,7},{6,4},{7,5},{8,10},{9,11},{10,... | collective-permute-start | bytes 270344 | tf_op jit(solution)/shard_map/ppermute | solution.py:17
  35.9 8.9 %collective-permute-start.12 = (bf16[88,512]{1,0:T(8,128)(2,1)S(1)}, bf16[88,512]{1,0:T(8,128)(2,1)S(1)}, u32[]{:S(2)}, u32[]{:S(2)}) collective-permute-start(bf16[88,512]{1,0:T(8,128)(2,1)S(1)} %gate.15), channel_id=1, source_target_pairs={{0,3},{1,2},{2,1},{3,0},{4,7},{5,6},{6,5},{7,4},{8,11},{9,10},{10,... | collective-permute-start | bytes 270344 | tf_op jit(solution)/shard_map/ppermute | solution.py:17
  39.1 6.1 %collective-permute-start.10 = (bf16[88,512]{1,0:T(8,128)(2,1)S(1)}, bf16[88,512]{1,0:T(8,128)(2,1)S(1)}, u32[]{:S(2)}, u32[]{:S(2)}) collective-permute-start(bf16[88,512]{1,0:T(8,128)(2,1)S(1)} %gate.14), channel_id=1, source_target_pairs={{0,1},{1,0},{2,3},{3,2},{4,5},{5,4},{6,7},{7,6},{8,9},{9,8},{10,11... | collective-permute-start | bytes 270344 | tf_op jit(solution)/shard_map/ppermute | solution.py:17
  40.2 13.6 %slice-start = ((s8[7340032]{0:T(1024)(128)(4,1)}), s8[4194304]{0:T(1024)(128)(4,1)S(1)}, s32[]{:S(2)}) async-start(s8[7340032]{0:T(1024)(128)(4,1)} %bitcast.14), calls=%async_computation | async-start | bytes 8388608
  40.2 6.3 %collective-permute-start.11 = (bf16[88,512]{1,0:T(8,128)(2,1)S(1)}, bf16[88,512]{1,0:T(8,128)(2,1)S(1)}, u32[]{:S(2)}, u32[]{:S(2)}) collective-permute-start(bf16[88,512]{1,0:T(8,128)(2,1)S(1)} %gate.9.after_ref), channel_id=1, source_target_pairs={{0,2},{1,3},{2,0},{3,1},{4,6},{5,7},{6,4},{7,5},{8,10},{9,11},{10,... | collective-permute-start | bytes 270344 | tf_op jit(solution)/shard_map/ppermute | solution.py:17
  43.0 10.8 %slice-start.1 = ((s8[7340032]{0:T(1024)(128)(4,1)}), s8[3145728]{0:T(1024)(128)(4,1)S(1)}, s32[]{:S(2)}) async-start(s8[7340032]{0:T(1024)(128)(4,1)} %bitcast.14), calls=%async_computation.1 | async-start | bytes 6291456
  43.0 8.2 %collective-permute-start.14 = (bf16[80,512]{1,0:T(8,128)(2,1)S(1)}, bf16[80,512]{1,0:T(8,128)(2,1)S(1)}, u32[]{:S(2)}, u32[]{:S(2)}) collective-permute-start(bf16[80,512]{1,0:T(8,128)(2,1)S(1)} %activate.2.refs_4_.refs_0_.value_ref), channel_id=1, source_target_pairs={{0,1},{1,0},{2,3},{3,2},{4,5},{5,4},{6,7},{7,6},{8,9},{9,8},{10,11... | collective-permute-start | bytes 245768 | tf_op jit(solution)/shard_map/ppermute | solution.py:17
  46.7 7.0 %collective-permute-start.13 = (bf16[80,512]{1,0:T(8,128)(2,1)S(1)}, bf16[80,512]{1,0:T(8,128)(2,1)S(1)}, u32[]{:S(2)}, u32[]{:S(2)}) collective-permute-start(bf16[80,512]{1,0:T(8,128)(2,1)S(1)} %activate.3.refs_0_), channel_id=1, source_target_pairs={{0,3},{1,2},{2,1},{3,0},{4,7},{5,6},{6,5},{7,4},{8,11},{9,10},{10,... | collective-permute-start | bytes 245768 | tf_op jit(solution)/shard_map/ppermute | solution.py:17
  49.6 8.0 %collective-permute-start.18 = (bf16[80,512]{1,0:T(8,128)(2,1)S(1)}, bf16[80,512]{1,0:T(8,128)(2,1)S(1)}, u32[]{:S(2)}, u32[]{:S(2)}) collective-permute-start(bf16[80,512]{1,0:T(8,128)(2,1)S(1)} %activate.3.refs_0_), channel_id=1, source_target_pairs={{0,2},{1,3},{2,0},{3,1},{4,6},{5,7},{6,4},{7,5},{8,10},{9,11},{10,... | collective-permute-start | bytes 245768 | tf_op jit(solution)/shard_map/ppermute | solution.py:17
  49.6 8.0 %collective-permute-start.19 = (bf16[80,512]{1,0:T(8,128)(2,1)S(1)}, bf16[80,512]{1,0:T(8,128)(2,1)S(1)}, u32[]{:S(2)}, u32[]{:S(2)}) collective-permute-start(bf16[80,512]{1,0:T(8,128)(2,1)S(1)} %activate.3.refs_0_), channel_id=1, source_target_pairs={{0,1},{1,0},{2,3},{3,2},{4,5},{5,4},{6,7},{7,6},{8,9},{9,8},{10,11... | collective-permute-start | bytes 245768 | tf_op jit(solution)/shard_map/ppermute | solution.py:17
  55.3 6.3 %collective-permute-start.15 = (bf16[80,512]{1,0:T(8,128)(2,1)S(1)}, bf16[80,512]{1,0:T(8,128)(2,1)S(1)}, u32[]{:S(2)}, u32[]{:S(2)}) collective-permute-start(bf16[80,512]{1,0:T(8,128)(2,1)S(1)} %hold.1), channel_id=1, source_target_pairs={{0,3},{1,2},{2,1},{3,0},{4,7},{5,6},{6,5},{7,4},{8,11},{9,10},{10,... | collective-permute-start | bytes 245768 | tf_op jit(solution)/shard_map/ppermute | solution.py:17
  57.6 6.2 %collective-permute-start.16 = (bf16[80,512]{1,0:T(8,128)(2,1)S(1)}, bf16[80,512]{1,0:T(8,128)(2,1)S(1)}, u32[]{:S(2)}, u32[]{:S(2)}) collective-permute-start(bf16[80,512]{1,0:T(8,128)(2,1)S(1)} %hold.1), channel_id=1, source_target_pairs={{0,2},{1,3},{2,0},{3,1},{4,6},{5,7},{6,4},{7,5},{8,10},{9,11},{10,... | collective-permute-start | bytes 245768 | tf_op jit(solution)/shard_map/ppermute | solution.py:17
  58.4 6.2 %collective-permute-start.20 = (bf16[40,1792]{1,0:T(8,128)(2,1)S(1)}, bf16[40,1792]{1,0:T(8,128)(2,1)S(1)}, u32[]{:S(2)}, u32[]{:S(2)}) collective-permute-start(bf16[40,1792]{1,0:T(8,128)(2,1)S(1)} %get-tuple-element.40), channel_id=1, source_target_pairs={{0,8},{4,12},{8,0},{12,4},{1,9},{5,13},{9,1},{13,5},{2,10},{6,14},... | collective-permute-start | bytes 430088 | tf_op jit(solution)/shard_map/ppermute | solution.py:17
  59.9 6.0 %collective-permute-start.21 = (bf16[40,1792]{1,0:T(8,128)(2,1)S(1)}, bf16[40,1792]{1,0:T(8,128)(2,1)S(1)}, u32[]{:S(2)}, u32[]{:S(2)}) collective-permute-start(bf16[40,1792]{1,0:T(8,128)(2,1)S(1)} %get-tuple-element.41), channel_id=1, source_target_pairs={{0,12},{4,8},{8,4},{12,0},{1,13},{5,9},{9,5},{13,1},{2,14},{6,10},... | collective-permute-start | bytes 430088 | tf_op jit(solution)/shard_map/ppermute | solution.py:17
  64.5 1.5 %collective-permute-start.17 = (bf16[40,1792]{1,0:T(8,128)(2,1)S(1)}, bf16[40,1792]{1,0:T(8,128)(2,1)S(1)}, u32[]{:S(2)}, u32[]{:S(2)}) collective-permute-start(bf16[40,1792]{1,0:T(8,128)(2,1)S(1)} %get-tuple-element.39), channel_id=1, source_target_pairs={{0,4},{4,0},{8,12},{12,8},{1,5},{5,1},{9,13},{13,9},{2,6},{6,2},{1... | collective-permute-start | bytes 430088 | tf_op jit(solution)/shard_map/ppermute | solution.py:17

commit v8 on v7

--- a/solution.py
+++ b/solution.py
@@ -307,17 +307,7 @@
         for k in ([1, 3, 2, 0] if nt == 4 and after is not None else partners(nt)):
             earlier = [] if after is None else [after[k or 1]]
             if k == 0 and after is not None:
-                written, token = pl.pallas_call(
-                    store_kernel,
-                    out_shape=(sds((tokens, share), bf16), sds((8, 128), f32)),
-                    in_specs=[whole(), anywhere()],
-                    out_specs=(whole(), whole()),
-                    compiler_params=params(),
-                    cost_estimate=estimate(10**6, 4 * tokens * share),
-                    name="store",
-                )(kept, partial_gate)
-                stored.append(written)
-                earlier.append(token)
+                earlier.append(partial_gate)
             partial_gate = pl.pallas_call(
                 gate_kernel,
                 out_shape=sds((tall, ff), bf16),
@@ -380,12 +370,21 @@
     far_gates = summed_gate(far, near_gates)
     near_own = activated(near, near_gates)
     near_hidden = {0: near_own, 1: exchange(near_own, "tensor", 1)}
-    far_own = activated(far, far_gates, (near_own,))
+    far_own = activated(far, far_gates)
     far_hidden = {k: exchange(far_own, "tensor", k) if k else far_own for k in partners(nt)}
     early = [0, 3]
     far_sum = down(far, far_hidden, early, final=False, after=(near_hidden[1],))
-    near_sum = down(near, near_hidden, [0, 1], final=False, after=(far_sum,))
-    waiting = held(near_own, far_sum, near_sum)
+    near_sum = down(near, near_hidden, [0, 1], final=False, after=(far_own,))
+    stream, token = pl.pallas_call(
+        store_kernel,
+        out_shape=(sds((tokens, share), bf16), sds((8, 128), f32)),
+        in_specs=[whole(), anywhere()],
+        out_specs=(whole(), whole()),
+        compiler_params=params(),
+        cost_estimate=estimate(10**6, 4 * tokens * share),
+        name="store",
+    )(kept, far_sum)
+    waiting = held(near_own, far_sum, near_sum, token)
     near_hidden.update({k: exchange(waiting, "tensor", k) for k in partners(nt) if k > 1})
     results = down(far, far_hidden, [k for k in partners(nt) if k not in early], far_sum)
     results.update(down(near, near_hidden, [k for k in partners(nt) if k > 1], near_sum))
@@ -400,7 +399,7 @@
         cost_estimate=estimate(4 * rows * tokens * share, 2 * rows * share),
         name="combine",
     )(high, low, *[returned[k] for k in range(ne)])
-    return stored[0], moe_out
+    return stream, moe_out
 
 
 def solution(mesh):

time: 67.2 us -> 67.2 us (level)
  no operation moved by 1% of the time
where the time goes in v8:
time: 67.2 us; the launch traced here: 66.9 us
  starting transfers between devices  30.9 us (46%)
  waiting for transfers between devices  17 us (25%)
  Pallas kernels  11.1 us (17%)
  local copies, waits for them, and re-layouts  7.03 us (10%)
  between operations  0.94 us (1%)
    ppermute x19, starting transfers between devices, exchange(): return lax.ppermute(value, axis, [(i, i ^ step) for i in range(n)])  23.5 us
    ppermute x19, waiting for transfers between devices, exchange(): return lax.ppermute(value, axis, [(i, i ^ step) for i in range(n)])  11.7 us
    ppermute x1, starting transfers between devices, local(): parts.append(lax.ppermute(block(z ^ 2), 'tensor', [(0, 2), (3, 1)]))  5.75 us
    unnamed x14, local copies, waits for them, and re-layouts  5.58 us
    ppermute x1, waiting for transfers between devices, local(): lax.ppermute(merged, 'tensor', [(0, 1), (1, 3), (2, 0), (3, 2)])  5.28 us
    pallas_call x8, Pallas kernels, summed_gate(): pl.pallas_call(gate_kernel, out_shape=sds((tall, ff), bf16), grid_spec=pl...  3.6 us
    pallas_call x4, Pallas kernels, down(): pl.pallas_call(functools.partial(down_kernel, steps, cap if final else No...  3.04 us
    dynamic_slice x1, local copies, waits for them, and re-layouts, block(): return lax.dynamic_slice(attn_partial[0], (0, k * share), (tokens, share))  1.44 us
  transfers between devices with their start and end apart: 22, of which 10 were waited for; matrix products, arithmetic and copies ran while one was open for 2% of the time, Pallas kernels for 14%

profile of v8, /device:TPU:0, one launch (start us, length us, event | category | flops | bytes accessed | tf_op | source)
XLA Modules:
  0.0 66.9 jit_solution(1939384385702873952)
XLA Ops:
  0.7 1.4 %dynamic-slice_bitcast_fusion = (bf16[64,1792]{1,0:T(8,128)(2,1)S(1)}, bf16[64,1792]{1,0:T(8,128)(2,1)S(1)}, bf16[64,1792]{1,0:T(8,128)(2,1)S(1)}, bf16[64,1792]{1,0:T(8,128)(2,1)S(1)}, bf16[64,1792]{1,0:T(8,128)(2,1)S(1)}) fusion(bf16[1,64,7168]{2,1,0:T(8,128)(2,1)} %param.8, s32[]{:T(128)S(6)} %select_n.30, s32[]{:T(128)S(6)} %select_n.27, s32[]{:T(128)S(6)} %select_n.26, ...), kind=kLoop, calls=%fused_computation | loop fusion | bytes 2293780 | tf_op jit(solution)/shard_map/dynamic_slice | solution.py:224
  2.1 3.1 %collective-permute-start.2 = (bf16[64,1792]{1,0:T(8,128)(2,1)S(1)}, bf16[64,1792]{1,0:T(8,128)(2,1)S(1)}, u32[]{:S(2)}, u32[]{:S(2)}) collective-permute-start(bf16[64,1792]{1,0:T(8,128)(2,1)S(1)} %get-tuple-element.42), channel_id=1, source_target_pairs={{0,1},{1,0},{2,3},{3,2},{4,5},{5,4},{6,7},{7,6},{8,9},{9,8},{10,11... | collective-permute-start | bytes 688136 | tf_op jit(solution)/shard_map/ppermute | solution.py:17
  5.2 0.7 collective-permute-start
  5.9 5.8 %collective-permute-start.1 = (bf16[64,1792]{1,0:T(8,128)(2,1)S(1)}, bf16[64,1792]{1,0:T(8,128)(2,1)S(1)}, u32[]{:S(2)}, u32[]{:S(2)}) collective-permute-start(bf16[64,1792]{1,0:T(8,128)(2,1)S(1)} %get-tuple-element.43.passing_ref), channel_id=1, source_target_pairs={{0,2},{3,1},{4,6},{7,5},{8,10},{11,9},{12,14},{15,13},{16,18},{19,... | collective-permute-start | bytes 688136 | tf_op jit(solution)/shard_map/ppermute | solution.py:232
  11.7 1.0 %collective-permute-start.3 = (bf16[64,1792]{1,0:T(8,128)(2,1)S(1)}, bf16[64,1792]{1,0:T(8,128)(2,1)S(1)}, u32[]{:S(2)}, u32[]{:S(2)}) collective-permute-start(bf16[64,1792]{1,0:T(8,128)(2,1)S(1)} %merge.1), channel_id=1, source_target_pairs={{0,1},{1,3},{2,0},{3,2},{4,5},{5,7},{6,4},{7,6},{8,9},{9,11},{10,8... | collective-permute-start | bytes 688136 | tf_op jit(solution)/shard_map/ppermute | solution.py:242
  12.7 0.8 %copy.10.scores_ref = f32[64,2]{1,0:T(8,128)S(1)} copy(f32[64,2]{0,1:T(2,128)} %param.11) | data formatting | bytes 1024 | tf_op args[4]
  13.4 0.8 %copy.9.ids_ref = s32[64,2]{1,0:T(8,128)S(1)} copy(s32[64,2]{0,1:T(2,128)} %param.10) | data formatting | bytes 1024 | tf_op args[3]
  14.2 3.1 %copy-done = bf16[1,1792,2048]{2,1,0:T(8,128)(2,1)S(1)} copy-done((bf16[1,1792,2048]{2,1,0:T(8,128)(2,1)S(1)}, bf16[1,1792,2048]{2,1,0:T(8,128)(2,1)}, u32[]{:S(2)}) %copy-start) | copy-done | bytes 7340056
  17.3 0.9 %copy-done.1 = bf16[64,1792]{1,0:T(8,128)(2,1)S(1)} copy-done((bf16[64,1792]{1,0:T(8,128)(2,1)S(1)}, bf16[64,1792]{1,0:T(8,128)(2,1)}, u32[]{:S(2)}) %copy-start.1) | copy-done | bytes 229400
  18.2 0.8 %fetch.1 = (bf16[64,1792]{1,0:T(8,128)(2,1)S(1)}, bf16[1,1792,2048]{2,1,0:T(8,128)(2,1)S(1)}) custom-call(bf16[64,1792]{1,0:T(8,128)(2,1)S(1)} %copy-done.1, bf16[1,1792,2048]{2,1,0:T(8,128)(2,1)S(1)} %copy-done), custom_call_target="tpu_custom_call" | custom-call | flops 1000000 | bytes 7569408 | tf_op jit(solution)/shard_map/fetch/pallas_call | solution.py:259
  19.0 0.5 routing.1
  19.6 5.3 %collective-permute-done.3.refs_3_ = bf16[64,1792]{1,0:T(8,128)(2,1)S(1)} collective-permute-done((bf16[64,1792]{1,0:T(8,128)(2,1)S(1)}, bf16[64,1792]{1,0:T(8,128)(2,1)S(1)}, u32[]{:S(2)}, u32[]{:S(2)}) %collective-permute-start.3) | collective-permute-done | bytes 229408 | tf_op jit(solution)/shard_map/ppermute | solution.py:242
  24.9 0.4 add.22
  25.3 0.2 pack.1
  25.5 1.6 %collective-permute-start.4 = (bf16[40,1792]{1,0:T(8,128)(2,1)S(1)}, bf16[40,1792]{1,0:T(8,128)(2,1)S(1)}, u32[]{:S(2)}, u32[]{:S(2)}) collective-permute-start(bf16[40,1792]{1,0:T(8,128)(2,1)S(1)} %get-tuple-element.25), channel_id=1, source_target_pairs={{0,8},{4,12},{8,0},{12,4},{1,9},{5,13},{9,1},{13,5},{2,10},{6,14},... | collective-permute-start | bytes 430088 | tf_op jit(solution)/shard_map/ppermute | solution.py:17
  27.1 0.4 collective-permute-start.5
  27.6 0.5 gate.13
  28.1 2.7 %collective-permute-start.11 = (bf16[88,512]{1,0:T(8,128)(2,1)S(1)}, bf16[88,512]{1,0:T(8,128)(2,1)S(1)}, u32[]{:S(2)}, u32[]{:S(2)}) collective-permute-start(bf16[88,512]{1,0:T(8,128)(2,1)S(1)} %gate.13), channel_id=1, source_target_pairs={{0,3},{1,2},{2,1},{3,0},{4,7},{5,6},{6,5},{7,4},{8,11},{9,10},{10,... | collective-permute-start | bytes 270344 | tf_op jit(solution)/shard_map/ppermute | solution.py:17
  30.8 0.4 gate.8
  31.4 0.4 gate.9
  31.8 1.8 %collective-permute-start.8 = (bf16[88,512]{1,0:T(8,128)(2,1)S(1)}, bf16[88,512]{1,0:T(8,128)(2,1)S(1)}, u32[]{:S(2)}, u32[]{:S(2)}) collective-permute-start(bf16[88,512]{1,0:T(8,128)(2,1)S(1)} %gate.9), channel_id=1, source_target_pairs={{0,2},{1,3},{2,0},{3,1},{4,6},{5,7},{6,4},{7,5},{8,10},{9,11},{10,... | collective-permute-start | bytes 270344 | tf_op jit(solution)/shard_map/ppermute | solution.py:17
  33.6 0.8 %collective-permute-done.5.refs_1_ = bf16[40,1792]{1,0:T(8,128)(2,1)S(1)} collective-permute-done((bf16[40,1792]{1,0:T(8,128)(2,1)S(1)}, bf16[40,1792]{1,0:T(8,128)(2,1)S(1)}, u32[]{:S(2)}, u32[]{:S(2)}) %collective-permute-start.5) | collective-permute-done | bytes 143392 | tf_op jit(solution)/shard_map/ppermute | solution.py:17
  34.6 0.8 %collective-permute-done.11.refs_0_.refs_3_ = bf16[88,512]{1,0:T(8,128)(2,1)S(1)} collective-permute-done((bf16[88,512]{1,0:T(8,128)(2,1)S(1)}, bf16[88,512]{1,0:T(8,128)(2,1)S(1)}, u32[]{:S(2)}, u32[]{:S(2)}) %collective-permute-start.11) | collective-permute-done | bytes 90144 | tf_op jit(solution)/shard_map/ppermute | solution.py:17
  35.4 0.4 gate.14
  35.9 2.7 %collective-permute-start.12 = (bf16[88,512]{1,0:T(8,128)(2,1)S(1)}, bf16[88,512]{1,0:T(8,128)(2,1)S(1)}, u32[]{:S(2)}, u32[]{:S(2)}) collective-permute-start(bf16[88,512]{1,0:T(8,128)(2,1)S(1)} %gate.14), channel_id=1, source_target_pairs={{0,3},{1,2},{2,1},{3,0},{4,7},{5,6},{6,5},{7,4},{8,11},{9,10},{10,... | collective-permute-start | bytes 270344 | tf_op jit(solution)/shard_map/ppermute | solution.py:17
  38.6 0.4 gate.12
  39.2 0.6 collective-permute-done.8.refs_0_.refs_2_
  39.8 0.4 gate.10.refs_1_
  40.3 2.1 %collective-permute-start.10 = (bf16[88,512]{1,0:T(8,128)(2,1)S(1)}, bf16[88,512]{1,0:T(8,128)(2,1)S(1)}, u32[]{:S(2)}, u32[]{:S(2)}) collective-permute-start(bf16[88,512]{1,0:T(8,128)(2,1)S(1)} %gate.10.refs_1_), channel_id=1, source_target_pairs={{0,2},{1,3},{2,0},{3,1},{4,6},{5,7},{6,4},{7,5},{8,10},{9,11},{10,... | collective-permute-start | bytes 270344 | tf_op jit(solution)/shard_map/ppermute | solution.py:17
  42.4 0.4 gate.15.refs_0_
  43.0 0.6 collective-permute-start.14
  43.6 0.4 gate.11.refs_0_
  44.1 1.1 %collective-permute-done.9.refs_1_ = bf16[88,512]{1,0:T(8,128)(2,1)S(1)} collective-permute-done((bf16[88,512]{1,0:T(8,128)(2,1)S(1)}, bf16[88,512]{1,0:T(8,128)(2,1)S(1)}, u32[]{:S(2)}, u32[]{:S(2)}) %collective-permute-start.9) | collective-permute-done | bytes 90144 | tf_op jit(solution)/shard_map/ppermute | solution.py:17
  45.2 1.3 %collective-permute-done.10.refs_2_ = bf16[88,512]{1,0:T(8,128)(2,1)S(1)} collective-permute-done((bf16[88,512]{1,0:T(8,128)(2,1)S(1)}, bf16[88,512]{1,0:T(8,128)(2,1)S(1)}, u32[]{:S(2)}, u32[]{:S(2)}) %collective-permute-start.10) | collective-permute-done | bytes 90144 | tf_op jit(solution)/shard_map/ppermute | solution.py:17
  46.8 2.8 %collective-permute-start.13 = (bf16[80,512]{1,0:T(8,128)(2,1)S(1)}, bf16[80,512]{1,0:T(8,128)(2,1)S(1)}, u32[]{:S(2)}, u32[]{:S(2)}) collective-permute-start(bf16[80,512]{1,0:T(8,128)(2,1)S(1)} %activate.2.refs_0_.refs_2_), channel_id=1, source_target_pairs={{0,3},{1,2},{2,1},{3,0},{4,7},{5,6},{6,5},{7,4},{8,11},{9,10},{10,... | collective-permute-start | bytes 245768 | tf_op jit(solution)/shard_map/ppermute | solution.py:17
  49.6 1.6 %collective-permute-start.19 = (bf16[80,512]{1,0:T(8,128)(2,1)S(1)}, bf16[80,512]{1,0:T(8,128)(2,1)S(1)}, u32[]{:S(2)}, u32[]{:S(2)}) collective-permute-start(bf16[80,512]{1,0:T(8,128)(2,1)S(1)} %activate.2.refs_0_.refs_2_), channel_id=1, source_target_pairs={{0,1},{1,0},{2,3},{3,2},{4,5},{5,4},{6,7},{7,6},{8,9},{9,8},{10,11... | collective-permute-start | bytes 245768 | tf_op jit(solution)/shard_map/ppermute | solution.py:17
  51.2 0.8 %down.5.refs_1_.refs_2_ = f32[80,1792]{1,0:T(8,128)S(1)} custom-call(s32[1]{0:T(128)} %bitcast.8.block_ref, bf16[1,2048,1792]{2,1,0:T(8,128)(2,1)S(1)} %bitcast.15, bf16[80,512]{1,0:T(8,128)(2,1)S(1)} %activate.3.refs_0_.value_ref, bf16[80,512]{1,0:T(8,128)(2,1)S(1)} %collective-permute-done.14.refs_2_.refs_1_, bf16[80,512]{1,0:T(8,128)(2,1)S(1)} %activate.2.refs_0_.refs_2_), custom_call_target="tpu_custom_call" | custom-call | flops 293601280 | bytes 3670016 | tf_op jit(solution)/shard_map/down/pallas_call | solution.py:358
  52.0 1.8 %collective-permute-done.13.refs_1_ = bf16[80,512]{1,0:T(8,128)(2,1)S(1)} collective-permute-done((bf16[80,512]{1,0:T(8,128)(2,1)S(1)}, bf16[80,512]{1,0:T(8,128)(2,1)S(1)}, u32[]{:S(2)}, u32[]{:S(2)}) %collective-permute-start.13) | collective-permute-done | bytes 81952 | tf_op jit(solution)/shard_map/ppermute | solution.py:17
  53.8 0.8 %down.4.after_ref.refs_0_.refs_2_ = f32[80,1792]{1,0:T(8,128)S(1)} custom-call(s32[1]{0:T(128)} %bitcast.8.block_ref, bf16[1,2048,1792]{2,1,0:T(8,128)(2,1)S(1)} %bitcast.15, bf16[80,512]{1,0:T(8,128)(2,1)S(1)} %activate.2.refs_0_.refs_2_, bf16[80,512]{1,0:T(8,128)(2,1)S(1)} %collective-permute-done.13.refs_1_, ...), custom_call_target="tpu_custom_call" | custom-call | flops 293601280 | bytes 3670016 | tf_op jit(solution)/shard_map/down/pallas_call | solution.py:358
  54.5 0.7 %store.1 = (bf16[64,1792]{1,0:T(8,128)(2,1)}, f32[8,128]{1,0:T(8,128)S(1)}) custom-call(bf16[64,1792]{1,0:T(8,128)(2,1)S(1)} %get-tuple-element.24.stream_ref.values_ref, f32[80,1792]{1,0:T(8,128)S(1)} %down.4.after_ref.refs_0_.refs_2_), custom_call_target="tpu_custom_call" | custom-call | flops 1000000 | bytes 458752 | tf_op jit(solution)/shard_map/store/pallas_call | solution.py:378
  55.3 2.2 %collective-permute-start.15 = (bf16[80,512]{1,0:T(8,128)(2,1)S(1)}, bf16[80,512]{1,0:T(8,128)(2,1)S(1)}, u32[]{:S(2)}, u32[]{:S(2)}) collective-permute-start(bf16[80,512]{1,0:T(8,128)(2,1)S(1)} %hold.1), channel_id=1, source_target_pairs={{0,3},{1,2},{2,1},{3,0},{4,7},{5,6},{6,5},{7,4},{8,11},{9,10},{10,... | collective-permute-start | bytes 245768 | tf_op jit(solution)/shard_map/ppermute | solution.py:17
  57.5 0.8 %down.7 = (bf16[40,1792]{1,0:T(8,128)(2,1)S(1)}, bf16[40,1792]{1,0:T(8,128)(2,1)S(1)}) custom-call(s32[1]{0:T(128)} %bitcast.8.block_ref, bf16[1,2048,1792]{2,1,0:T(8,128)(2,1)S(1)} %bitcast.15, bf16[80,512]{1,0:T(8,128)(2,1)S(1)} %collective-permute-done.18.refs_0_, bf16[80,512]{1,0:T(8,128)(2,1)S(1)} %collective-permute-done.19.refs_1_, ...), custom_call_target="tpu_custom_call" | custom-call | flops 293601280 | bytes 3670016 | tf_op jit(solution)/shard_map/down/pallas_call | solution.py:358
  58.2 1.6 %collective-permute-start.20 = (bf16[40,1792]{1,0:T(8,128)(2,1)S(1)}, bf16[40,1792]{1,0:T(8,128)(2,1)S(1)}, u32[]{:S(2)}, u32[]{:S(2)}) collective-permute-start(bf16[40,1792]{1,0:T(8,128)(2,1)S(1)} %get-tuple-element.40), channel_id=1, source_target_pairs={{0,8},{4,12},{8,0},{12,4},{1,9},{5,13},{9,1},{13,5},{2,10},{6,14},... | collective-permute-start | bytes 430088 | tf_op jit(solution)/shard_map/ppermute | solution.py:17
  59.8 1.6 %collective-permute-done.15.refs_0_ = bf16[80,512]{1,0:T(8,128)(2,1)S(1)} collective-permute-done((bf16[80,512]{1,0:T(8,128)(2,1)S(1)}, bf16[80,512]{1,0:T(8,128)(2,1)S(1)}, u32[]{:S(2)}, u32[]{:S(2)}) %collective-permute-start.15) | collective-permute-done | bytes 81952 | tf_op jit(solution)/shard_map/ppermute | solution.py:17
  61.5 1.8 %collective-permute-done.16.refs_1_ = bf16[80,512]{1,0:T(8,128)(2,1)S(1)} collective-permute-done((bf16[80,512]{1,0:T(8,128)(2,1)S(1)}, bf16[80,512]{1,0:T(8,128)(2,1)S(1)}, u32[]{:S(2)}, u32[]{:S(2)}) %collective-permute-start.16) | collective-permute-done | bytes 81952 | tf_op jit(solution)/shard_map/ppermute | solution.py:17
  63.2 0.8 %down.6 = (bf16[40,1792]{1,0:T(8,128)(2,1)S(1)}, bf16[40,1792]{1,0:T(8,128)(2,1)S(1)}) custom-call(s32[1]{0:T(128)} %bitcast.8.block_ref, bf16[1,2048,1792]{2,1,0:T(8,128)(2,1)S(1)} %bitcast.15, bf16[80,512]{1,0:T(8,128)(2,1)S(1)} %collective-permute-done.15.refs_0_, bf16[80,512]{1,0:T(8,128)(2,1)S(1)} %collective-permute-done.16.refs_1_, ...), custom_call_target="tpu_custom_call" | custom-call | flops 293601280 | bytes 3670016 | tf_op jit(solution)/shard_map/down/pallas_call | solution.py:358
  64.1 1.8 %collective-permute-done.21.refs_3_ = bf16[40,1792]{1,0:T(8,128)(2,1)S(1)} collective-permute-done((bf16[40,1792]{1,0:T(8,128)(2,1)S(1)}, bf16[40,1792]{1,0:T(8,128)(2,1)S(1)}, u32[]{:S(2)}, u32[]{:S(2)}) %collective-permute-start.21) | collective-permute-done | bytes 143392 | tf_op jit(solution)/shard_map/ppermute | solution.py:17
  65.9 1.0 %combine.1 = bf16[64,1792]{1,0:T(8,128)(2,1)} custom-call(bf16[64,160]{1,0:T(8,128)(2,1)S(1)} %get-tuple-element.35.high_ref, bf16[64,160]{1,0:T(8,128)(2,1)S(1)} %get-tuple-element.36.low_ref, bf16[40,1792]{1,0:T(8,128)(2,1)S(1)} %get-tuple-element.38.refs_0_, bf16[40,1792]{1,0:T(8,128)(2,1)S(1)} %collective-permute-done.17.refs_1_, ...), custom_call_target="tpu_custom_call" | custom-call | flops 73400320 | bytes 573440 | tf_op jit(solution)/shard_map/combine/pallas_call | solution.py:393
  (37 shorter events, 1.2 us)
Async XLA Ops:
  0.6 18.4 %copy-start.2 = (s32[64,2]{0,1:T(2,128)S(1)}, s32[64,2]{0,1:T(2,128)}, u32[]{:S(2)}) copy-start(s32[64,2]{0,1:T(2,128)} %param.10) | copy-start | bytes 1540
  0.6 26.8 %copy-start.3 = (bf16[1792]{0:T(1024)(128)(2,1)S(1)}, bf16[1792]{0:T(1024)(128)(2,1)}, u32[]{:S(2)}) copy-start(bf16[1792]{0:T(1024)(128)(2,1)} %param.9) | copy-start | bytes 10756
  2.1 9.5 %collective-permute-start.2 = (bf16[64,1792]{1,0:T(8,128)(2,1)S(1)}, bf16[64,1792]{1,0:T(8,128)(2,1)S(1)}, u32[]{:S(2)}, u32[]{:S(2)}) collective-permute-start(bf16[64,1792]{1,0:T(8,128)(2,1)S(1)} %get-tuple-element.42), channel_id=1, source_target_pairs={{0,1},{1,0},{2,3},{3,2},{4,5},{5,4},{6,7},{7,6},{8,9},{9,8},{10,11... | collective-permute-start | bytes 688136 | tf_op jit(solution)/shard_map/ppermute | solution.py:17
  5.2 14.3 %collective-permute-start = (bf16[64,1792]{1,0:T(8,128)(2,1)S(1)}, bf16[64,1792]{1,0:T(8,128)(2,1)S(1)}, u32[]{:S(2)}, u32[]{:S(2)}) collective-permute-start(bf16[64,1792]{1,0:T(8,128)(2,1)S(1)} %get-tuple-element.44), channel_id=1, source_target_pairs={{1,2},{2,1},{5,6},{6,5},{9,10},{10,9},{13,14},{14,13},{17,18},{18,... | collective-permute-start | bytes 688136 | tf_op jit(solution)/shard_map/ppermute | solution.py:231
  5.9 13.7 %collective-permute-start.1 = (bf16[64,1792]{1,0:T(8,128)(2,1)S(1)}, bf16[64,1792]{1,0:T(8,128)(2,1)S(1)}, u32[]{:S(2)}, u32[]{:S(2)}) collective-permute-start(bf16[64,1792]{1,0:T(8,128)(2,1)S(1)} %get-tuple-element.43.passing_ref), channel_id=1, source_target_pairs={{0,2},{3,1},{4,6},{7,5},{8,10},{11,9},{12,14},{15,13},{16,18},{19,... | collective-permute-start | bytes 688136 | tf_op jit(solution)/shard_map/ppermute | solution.py:232
  11.7 13.1 %collective-permute-start.3 = (bf16[64,1792]{1,0:T(8,128)(2,1)S(1)}, bf16[64,1792]{1,0:T(8,128)(2,1)S(1)}, u32[]{:S(2)}, u32[]{:S(2)}) collective-permute-start(bf16[64,1792]{1,0:T(8,128)(2,1)S(1)} %merge.1), channel_id=1, source_target_pairs={{0,1},{1,3},{2,0},{3,2},{4,5},{5,7},{6,4},{7,6},{8,9},{9,11},{10,8... | collective-permute-start | bytes 688136 | tf_op jit(solution)/shard_map/ppermute | solution.py:242
  14.2 3.1 %copy-start = (bf16[1,1792,2048]{2,1,0:T(8,128)(2,1)S(1)}, bf16[1,1792,2048]{2,1,0:T(8,128)(2,1)}, u32[]{:S(2)}) copy-start(bf16[1,1792,2048]{2,1,0:T(8,128)(2,1)} %refs_1_.1) | copy-start | bytes 22020100
  17.3 0.9 %copy-start.1 = (bf16[64,1792]{1,0:T(8,128)(2,1)S(1)}, bf16[64,1792]{1,0:T(8,128)(2,1)}, u32[]{:S(2)}) copy-start(bf16[64,1792]{1,0:T(8,128)(2,1)} %refs_0_.1) | copy-start | bytes 688132
  25.2 2.2 %collective-permute-start.6 = (bf16[40,1792]{1,0:T(8,128)(2,1)S(1)}, bf16[40,1792]{1,0:T(8,128)(2,1)S(1)}, u32[]{:S(2)}, u32[]{:S(2)}) collective-permute-start(bf16[40,1792]{1,0:T(8,128)(2,1)S(1)} %get-tuple-element.31), channel_id=1, source_target_pairs={{0,4},{4,0},{8,12},{12,8},{1,5},{5,1},{9,13},{13,9},{2,6},{6,2},{1... | collective-permute-start | bytes 430088 | tf_op jit(solution)/shard_map/ppermute | solution.py:17
  25.5 8.1 %collective-permute-start.4 = (bf16[40,1792]{1,0:T(8,128)(2,1)S(1)}, bf16[40,1792]{1,0:T(8,128)(2,1)S(1)}, u32[]{:S(2)}, u32[]{:S(2)}) collective-permute-start(bf16[40,1792]{1,0:T(8,128)(2,1)S(1)} %get-tuple-element.25), channel_id=1, source_target_pairs={{0,8},{4,12},{8,0},{12,4},{1,9},{5,13},{9,1},{13,5},{2,10},{6,14},... | collective-permute-start | bytes 430088 | tf_op jit(solution)/shard_map/ppermute | solution.py:17
  27.1 7.3 %collective-permute-start.5 = (bf16[40,1792]{1,0:T(8,128)(2,1)S(1)}, bf16[40,1792]{1,0:T(8,128)(2,1)S(1)}, u32[]{:S(2)}, u32[]{:S(2)}) collective-permute-start(bf16[40,1792]{1,0:T(8,128)(2,1)S(1)} %get-tuple-element.26), channel_id=1, source_target_pairs={{0,12},{4,8},{8,4},{12,0},{1,13},{5,9},{9,5},{13,1},{2,14},{6,10},... | collective-permute-start | bytes 430088 | tf_op jit(solution)/shard_map/ppermute | solution.py:17
  28.1 7.3 %collective-permute-start.11 = (bf16[88,512]{1,0:T(8,128)(2,1)S(1)}, bf16[88,512]{1,0:T(8,128)(2,1)S(1)}, u32[]{:S(2)}, u32[]{:S(2)}) collective-permute-start(bf16[88,512]{1,0:T(8,128)(2,1)S(1)} %gate.13), channel_id=1, source_target_pairs={{0,3},{1,2},{2,1},{3,0},{4,7},{5,6},{6,5},{7,4},{8,11},{9,10},{10,... | collective-permute-start | bytes 270344 | tf_op jit(solution)/shard_map/ppermute | solution.py:17
  31.3 7.4 %collective-permute-start.7 = (bf16[88,512]{1,0:T(8,128)(2,1)S(1)}, bf16[88,512]{1,0:T(8,128)(2,1)S(1)}, u32[]{:S(2)}, u32[]{:S(2)}) collective-permute-start(bf16[88,512]{1,0:T(8,128)(2,1)S(1)} %gate.8), channel_id=1, source_target_pairs={{0,1},{1,0},{2,3},{3,2},{4,5},{5,4},{6,7},{7,6},{8,9},{9,8},{10,11... | collective-permute-start | bytes 270344 | tf_op jit(solution)/shard_map/ppermute | solution.py:17
  31.8 8.0 %collective-permute-start.8 = (bf16[88,512]{1,0:T(8,128)(2,1)S(1)}, bf16[88,512]{1,0:T(8,128)(2,1)S(1)}, u32[]{:S(2)}, u32[]{:S(2)}) collective-permute-start(bf16[88,512]{1,0:T(8,128)(2,1)S(1)} %gate.9), channel_id=1, source_target_pairs={{0,2},{1,3},{2,0},{3,1},{4,6},{5,7},{6,4},{7,5},{8,10},{9,11},{10,... | collective-permute-start | bytes 270344 | tf_op jit(solution)/shard_map/ppermute | solution.py:17
  35.9 8.2 %collective-permute-start.12 = (bf16[88,512]{1,0:T(8,128)(2,1)S(1)}, bf16[88,512]{1,0:T(8,128)(2,1)S(1)}, u32[]{:S(2)}, u32[]{:S(2)}) collective-permute-start(bf16[88,512]{1,0:T(8,128)(2,1)S(1)} %gate.14), channel_id=1, source_target_pairs={{0,3},{1,2},{2,1},{3,0},{4,7},{5,6},{6,5},{7,4},{8,11},{9,10},{10,... | collective-permute-start | bytes 270344 | tf_op jit(solution)/shard_map/ppermute | solution.py:17
  39.1 6.1 %collective-permute-start.9 = (bf16[88,512]{1,0:T(8,128)(2,1)S(1)}, bf16[88,512]{1,0:T(8,128)(2,1)S(1)}, u32[]{:S(2)}, u32[]{:S(2)}) collective-permute-start(bf16[88,512]{1,0:T(8,128)(2,1)S(1)} %gate.12), channel_id=1, source_target_pairs={{0,1},{1,0},{2,3},{3,2},{4,5},{5,4},{6,7},{7,6},{8,9},{9,8},{10,11... | collective-permute-start | bytes 270344 | tf_op jit(solution)/shard_map/ppermute | solution.py:17
  40.2 11.0 %slice-start = ((s8[7340032]{0:T(1024)(128)(4,1)}), s8[4194304]{0:T(1024)(128)(4,1)S(1)}, s32[]{:S(2)}) async-start(s8[7340032]{0:T(1024)(128)(4,1)} %bitcast.14), calls=%async_computation | async-start | bytes 8388608
  40.3 6.3 %collective-permute-start.10 = (bf16[88,512]{1,0:T(8,128)(2,1)S(1)}, bf16[88,512]{1,0:T(8,128)(2,1)S(1)}, u32[]{:S(2)}, u32[]{:S(2)}) collective-permute-start(bf16[88,512]{1,0:T(8,128)(2,1)S(1)} %gate.10.refs_1_), channel_id=1, source_target_pairs={{0,2},{1,3},{2,0},{3,1},{4,6},{5,7},{6,4},{7,5},{8,10},{9,11},{10,... | collective-permute-start | bytes 270344 | tf_op jit(solution)/shard_map/ppermute | solution.py:17
  43.0 8.2 %slice-start.1 = ((s8[7340032]{0:T(1024)(128)(4,1)}), s8[3145728]{0:T(1024)(128)(4,1)S(1)}, s32[]{:S(2)}) async-start(s8[7340032]{0:T(1024)(128)(4,1)} %bitcast.14), calls=%async_computation.1 | async-start | bytes 6291456
  43.0 8.2 %collective-permute-start.14 = (bf16[80,512]{1,0:T(8,128)(2,1)S(1)}, bf16[80,512]{1,0:T(8,128)(2,1)S(1)}, u32[]{:S(2)}, u32[]{:S(2)}) collective-permute-start(bf16[80,512]{1,0:T(8,128)(2,1)S(1)} %activate.3.refs_0_.value_ref), channel_id=1, source_target_pairs={{0,1},{1,0},{2,3},{3,2},{4,5},{5,4},{6,7},{7,6},{8,9},{9,8},{10,11... | collective-permute-start | bytes 245768 | tf_op jit(solution)/shard_map/ppermute | solution.py:17
  46.8 7.0 %collective-permute-start.13 = (bf16[80,512]{1,0:T(8,128)(2,1)S(1)}, bf16[80,512]{1,0:T(8,128)(2,1)S(1)}, u32[]{:S(2)}, u32[]{:S(2)}) collective-permute-start(bf16[80,512]{1,0:T(8,128)(2,1)S(1)} %activate.2.refs_0_.refs_2_), channel_id=1, source_target_pairs={{0,3},{1,2},{2,1},{3,0},{4,7},{5,6},{6,5},{7,4},{8,11},{9,10},{10,... | collective-permute-start | bytes 245768 | tf_op jit(solution)/shard_map/ppermute | solution.py:17
  49.6 7.9 %collective-permute-start.18 = (bf16[80,512]{1,0:T(8,128)(2,1)S(1)}, bf16[80,512]{1,0:T(8,128)(2,1)S(1)}, u32[]{:S(2)}, u32[]{:S(2)}) collective-permute-start(bf16[80,512]{1,0:T(8,128)(2,1)S(1)} %activate.2.refs_0_.refs_2_), channel_id=1, source_target_pairs={{0,2},{1,3},{2,0},{3,1},{4,6},{5,7},{6,4},{7,5},{8,10},{9,11},{10,... | collective-permute-start | bytes 245768 | tf_op jit(solution)/shard_map/ppermute | solution.py:17
  49.6 7.9 %collective-permute-start.19 = (bf16[80,512]{1,0:T(8,128)(2,1)S(1)}, bf16[80,512]{1,0:T(8,128)(2,1)S(1)}, u32[]{:S(2)}, u32[]{:S(2)}) collective-permute-start(bf16[80,512]{1,0:T(8,128)(2,1)S(1)} %activate.2.refs_0_.refs_2_), channel_id=1, source_target_pairs={{0,1},{1,0},{2,3},{3,2},{4,5},{5,4},{6,7},{7,6},{8,9},{9,8},{10,11... | collective-permute-start | bytes 245768 | tf_op jit(solution)/shard_map/ppermute | solution.py:17
  55.3 6.2 %collective-permute-start.15 = (bf16[80,512]{1,0:T(8,128)(2,1)S(1)}, bf16[80,512]{1,0:T(8,128)(2,1)S(1)}, u32[]{:S(2)}, u32[]{:S(2)}) collective-permute-start(bf16[80,512]{1,0:T(8,128)(2,1)S(1)} %hold.1), channel_id=1, source_target_pairs={{0,3},{1,2},{2,1},{3,0},{4,7},{5,6},{6,5},{7,4},{8,11},{9,10},{10,... | collective-permute-start | bytes 245768 | tf_op jit(solution)/shard_map/ppermute | solution.py:17
  57.4 5.8 %collective-permute-start.16 = (bf16[80,512]{1,0:T(8,128)(2,1)S(1)}, bf16[80,512]{1,0:T(8,128)(2,1)S(1)}, u32[]{:S(2)}, u32[]{:S(2)}) collective-permute-start(bf16[80,512]{1,0:T(8,128)(2,1)S(1)} %hold.1), channel_id=1, source_target_pairs={{0,2},{1,3},{2,0},{3,1},{4,6},{5,7},{6,4},{7,5},{8,10},{9,11},{10,... | collective-permute-start | bytes 245768 | tf_op jit(solution)/shard_map/ppermute | solution.py:17
  58.2 5.9 %collective-permute-start.20 = (bf16[40,1792]{1,0:T(8,128)(2,1)S(1)}, bf16[40,1792]{1,0:T(8,128)(2,1)S(1)}, u32[]{:S(2)}, u32[]{:S(2)}) collective-permute-start(bf16[40,1792]{1,0:T(8,128)(2,1)S(1)} %get-tuple-element.40), channel_id=1, source_target_pairs={{0,8},{4,12},{8,0},{12,4},{1,9},{5,13},{9,1},{13,5},{2,10},{6,14},... | collective-permute-start | bytes 430088 | tf_op jit(solution)/shard_map/ppermute | solution.py:17
  59.8 6.1 %collective-permute-start.21 = (bf16[40,1792]{1,0:T(8,128)(2,1)S(1)}, bf16[40,1792]{1,0:T(8,128)(2,1)S(1)}, u32[]{:S(2)}, u32[]{:S(2)}) collective-permute-start(bf16[40,1792]{1,0:T(8,128)(2,1)S(1)} %get-tuple-element.41), channel_id=1, source_target_pairs={{0,12},{4,8},{8,4},{12,0},{1,13},{5,9},{9,5},{13,1},{2,14},{6,10},... | collective-permute-start | bytes 430088 | tf_op jit(solution)/shard_map/ppermute | solution.py:17
  64.0 1.9 %collective-permute-start.17 = (bf16[40,1792]{1,0:T(8,128)(2,1)S(1)}, bf16[40,1792]{1,0:T(8,128)(2,1)S(1)}, u32[]{:S(2)}, u32[]{:S(2)}) collective-permute-start(bf16[40,1792]{1,0:T(8,128)(2,1)S(1)} %get-tuple-element.39), channel_id=1, source_target_pairs={{0,4},{4,0},{8,12},{12,8},{1,5},{5,1},{9,13},{13,9},{2,6},{6,2},{1... | collective-permute-start | bytes 430088 | tf_op jit(solution)/shard_map/ppermute | solution.py:17

commit v9 on v8

--- a/solution.py
+++ b/solution.py
@@ -6,6 +6,9 @@
 from jax.experimental import pallas as pl
 from jax.experimental.pallas import tpu as pltpu
 from jax.sharding import PartitionSpec as P
+
+
+SCALE = 2.0**-20
 
 
 def partners(n):
@@ -122,11 +125,12 @@
 def prepare_kernel(n, gain_ref, *refs):
     pieces, lhs_ref, squares_ref = refs[:n], refs[-2], refs[-1]
     rows = jnp.concatenate([p[...].astype(jnp.float32) for p in pieces], axis=0)
-    squared = (rows * rows).astype(jnp.bfloat16)
+    scaled = rows * SCALE
+    squared = (scaled * scaled).astype(jnp.bfloat16)
     ones = jnp.ones((8, rows.shape[1]), jnp.bfloat16)
     sums = lax.dot_general(ones, squared, (((1,), (1,)), ((), ())), preferred_element_type=jnp.float32)
     high = sums.astype(jnp.bfloat16).astype(jnp.float32)
-    low = sums - high
+    low = jnp.where(high < jnp.inf, sums - high, 0.0)
     which = lax.broadcasted_iota(jnp.int32, sums.shape, 0)
     squares_ref[...] = jnp.where(which == 0, high, jnp.where(which == 1, low, 0.0))
     lhs_ref[...] = (rows * gain_ref[...].astype(jnp.float32)).astype(jnp.bfloat16)
@@ -171,9 +175,9 @@
     pieces = -(-rows // width)
     lines = [squares[2 * i : 2 * i + 1] + squares[2 * i + 1 : 2 * i + 2] for i in range(pieces)]
     line = (lines[0] if pieces == 1 else jnp.concatenate(lines, axis=1))[:, :rows]
-    inverse = lax.rsqrt(line / features + 1e-06)
+    inverse = lax.rsqrt(line * (1.0 / SCALE**2) / features + 1e-06)
     column = jnp.transpose(jnp.broadcast_to(inverse, (8, rows)))[:, 0:1]
-    gate = total * column
+    gate = jnp.where(column > 0.0, total * column, 0.0)
     out_ref[...] = (gate / (1.0 + jnp.exp(-gate))).astype(bf16)
 
 

time: 67.2 us -> 67.2 us (level)
  transfers between devices with their start and end apart: 22 -> 22, of which waited for: 10 -> 10; matrix products, arithmetic and copies ran while one was open for 2% -> 2% of each run, Pallas kernels for 14% -> 15%
where the time goes in v9:
time: 67.2 us; the launch traced here: 66.9 us
  starting transfers between devices  30.9 us (46%)
  waiting for transfers between devices  17 us (25%)
  Pallas kernels  11.1 us (17%)
  local copies, waits for them, and re-layouts  7.03 us (10%)
  between operations  0.93 us (1%)
    ppermute x19, starting transfers between devices, exchange(): return lax.ppermute(value, axis, [(i, i ^ step) for i in range(n)])  23.5 us
    ppermute x19, waiting for transfers between devices, exchange(): return lax.ppermute(value, axis, [(i, i ^ step) for i in range(n)])  11.7 us
    ppermute x1, starting transfers between devices, local(): parts.append(lax.ppermute(block(z ^ 2), 'tensor', [(0, 2), (3, 1)]))  5.75 us
    unnamed x14, local copies, waits for them, and re-layouts  5.58 us
    ppermute x1, waiting for transfers between devices, local(): lax.ppermute(merged, 'tensor', [(0, 1), (1, 3), (2, 0), (3, 2)])  5.28 us
    pallas_call x8, Pallas kernels, summed_gate(): pl.pallas_call(gate_kernel, out_shape=sds((tall, ff), bf16), grid_spec=pl...  3.6 us
    pallas_call x4, Pallas kernels, down(): pl.pallas_call(functools.partial(down_kernel, steps, cap if final else No...  3.04 us
    dynamic_slice x1, local copies, waits for them, and re-layouts, block(): return lax.dynamic_slice(attn_partial[0], (0, k * share), (tokens, share))  1.44 us
  transfers between devices with their start and end apart: 22, of which 10 were waited for; matrix products, arithmetic and copies ran while one was open for 2% of the time, Pallas kernels for 15%

profile of v9, /device:TPU:0, one launch (start us, length us, event | category | flops | bytes accessed | tf_op | source)
XLA Modules:
  0.0 66.9 jit_solution(13321787695808756723)
XLA Ops:
  0.7 1.4 %dynamic-slice_bitcast_fusion = (bf16[64,1792]{1,0:T(8,128)(2,1)S(1)}, bf16[64,1792]{1,0:T(8,128)(2,1)S(1)}, bf16[64,1792]{1,0:T(8,128)(2,1)S(1)}, bf16[64,1792]{1,0:T(8,128)(2,1)S(1)}, bf16[64,1792]{1,0:T(8,128)(2,1)S(1)}) fusion(bf16[1,64,7168]{2,1,0:T(8,128)(2,1)} %param.8, s32[]{:T(128)S(6)} %select_n.30, s32[]{:T(128)S(6)} %select_n.27, s32[]{:T(128)S(6)} %select_n.26, ...), kind=kLoop, calls=%fused_computation | loop fusion | bytes 2293780 | tf_op jit(solution)/shard_map/dynamic_slice | solution.py:228
  2.1 3.1 %collective-permute-start.2 = (bf16[64,1792]{1,0:T(8,128)(2,1)S(1)}, bf16[64,1792]{1,0:T(8,128)(2,1)S(1)}, u32[]{:S(2)}, u32[]{:S(2)}) collective-permute-start(bf16[64,1792]{1,0:T(8,128)(2,1)S(1)} %get-tuple-element.42), channel_id=1, source_target_pairs={{0,1},{1,0},{2,3},{3,2},{4,5},{5,4},{6,7},{7,6},{8,9},{9,8},{10,11... | collective-permute-start | bytes 688136 | tf_op jit(solution)/shard_map/ppermute | solution.py:20
  5.2 0.7 collective-permute-start
  5.9 5.8 %collective-permute-start.1 = (bf16[64,1792]{1,0:T(8,128)(2,1)S(1)}, bf16[64,1792]{1,0:T(8,128)(2,1)S(1)}, u32[]{:S(2)}, u32[]{:S(2)}) collective-permute-start(bf16[64,1792]{1,0:T(8,128)(2,1)S(1)} %get-tuple-element.43.passing_ref), channel_id=1, source_target_pairs={{0,2},{3,1},{4,6},{7,5},{8,10},{11,9},{12,14},{15,13},{16,18},{19,... | collective-permute-start | bytes 688136 | tf_op jit(solution)/shard_map/ppermute | solution.py:236
  11.7 1.0 %collective-permute-start.3 = (bf16[64,1792]{1,0:T(8,128)(2,1)S(1)}, bf16[64,1792]{1,0:T(8,128)(2,1)S(1)}, u32[]{:S(2)}, u32[]{:S(2)}) collective-permute-start(bf16[64,1792]{1,0:T(8,128)(2,1)S(1)} %merge.1), channel_id=1, source_target_pairs={{0,1},{1,3},{2,0},{3,2},{4,5},{5,7},{6,4},{7,6},{8,9},{9,11},{10,8... | collective-permute-start | bytes 688136 | tf_op jit(solution)/shard_map/ppermute | solution.py:246
  12.7 0.8 %copy.10.scores_ref = f32[64,2]{1,0:T(8,128)S(1)} copy(f32[64,2]{0,1:T(2,128)} %param.11) | data formatting | bytes 1024 | tf_op args[4]
  13.4 0.8 %copy.9.ids_ref = s32[64,2]{1,0:T(8,128)S(1)} copy(s32[64,2]{0,1:T(2,128)} %param.10) | data formatting | bytes 1024 | tf_op args[3]
  14.2 3.1 %copy-done = bf16[1,1792,2048]{2,1,0:T(8,128)(2,1)S(1)} copy-done((bf16[1,1792,2048]{2,1,0:T(8,128)(2,1)S(1)}, bf16[1,1792,2048]{2,1,0:T(8,128)(2,1)}, u32[]{:S(2)}) %copy-start) | copy-done | bytes 7340056
  17.3 0.9 %copy-done.1 = bf16[64,1792]{1,0:T(8,128)(2,1)S(1)} copy-done((bf16[64,1792]{1,0:T(8,128)(2,1)S(1)}, bf16[64,1792]{1,0:T(8,128)(2,1)}, u32[]{:S(2)}) %copy-start.1) | copy-done | bytes 229400
  18.2 0.8 %fetch.1 = (bf16[64,1792]{1,0:T(8,128)(2,1)S(1)}, bf16[1,1792,2048]{2,1,0:T(8,128)(2,1)S(1)}) custom-call(bf16[64,1792]{1,0:T(8,128)(2,1)S(1)} %copy-done.1, bf16[1,1792,2048]{2,1,0:T(8,128)(2,1)S(1)} %copy-done), custom_call_target="tpu_custom_call" | custom-call | flops 1000000 | bytes 7569408 | tf_op jit(solution)/shard_map/fetch/pallas_call | solution.py:263
  19.0 0.5 routing.1
  19.6 5.3 %collective-permute-done.3.refs_3_ = bf16[64,1792]{1,0:T(8,128)(2,1)S(1)} collective-permute-done((bf16[64,1792]{1,0:T(8,128)(2,1)S(1)}, bf16[64,1792]{1,0:T(8,128)(2,1)S(1)}, u32[]{:S(2)}, u32[]{:S(2)}) %collective-permute-start.3) | collective-permute-done | bytes 229408 | tf_op jit(solution)/shard_map/ppermute | solution.py:246
  24.9 0.4 add.22
  25.5 1.6 %collective-permute-start.4 = (bf16[40,1792]{1,0:T(8,128)(2,1)S(1)}, bf16[40,1792]{1,0:T(8,128)(2,1)S(1)}, u32[]{:S(2)}, u32[]{:S(2)}) collective-permute-start(bf16[40,1792]{1,0:T(8,128)(2,1)S(1)} %get-tuple-element.25), channel_id=1, source_target_pairs={{0,8},{4,12},{8,0},{12,4},{1,9},{5,13},{9,1},{13,5},{2,10},{6,14},... | collective-permute-start | bytes 430088 | tf_op jit(solution)/shard_map/ppermute | solution.py:20
  27.1 0.4 collective-permute-start.5
  27.7 0.5 gate.13
  28.1 2.7 %collective-permute-start.11 = (bf16[88,512]{1,0:T(8,128)(2,1)S(1)}, bf16[88,512]{1,0:T(8,128)(2,1)S(1)}, u32[]{:S(2)}, u32[]{:S(2)}) collective-permute-start(bf16[88,512]{1,0:T(8,128)(2,1)S(1)} %gate.13), channel_id=1, source_target_pairs={{0,3},{1,2},{2,1},{3,0},{4,7},{5,6},{6,5},{7,4},{8,11},{9,10},{10,... | collective-permute-start | bytes 270344 | tf_op jit(solution)/shard_map/ppermute | solution.py:20
  30.8 0.4 gate.8
  31.4 0.4 gate.9
  31.8 1.8 %collective-permute-start.8 = (bf16[88,512]{1,0:T(8,128)(2,1)S(1)}, bf16[88,512]{1,0:T(8,128)(2,1)S(1)}, u32[]{:S(2)}, u32[]{:S(2)}) collective-permute-start(bf16[88,512]{1,0:T(8,128)(2,1)S(1)} %gate.9), channel_id=1, source_target_pairs={{0,2},{1,3},{2,0},{3,1},{4,6},{5,7},{6,4},{7,5},{8,10},{9,11},{10,... | collective-permute-start | bytes 270344 | tf_op jit(solution)/shard_map/ppermute | solution.py:20
  33.6 0.8 %collective-permute-done.5.refs_1_ = bf16[40,1792]{1,0:T(8,128)(2,1)S(1)} collective-permute-done((bf16[40,1792]{1,0:T(8,128)(2,1)S(1)}, bf16[40,1792]{1,0:T(8,128)(2,1)S(1)}, u32[]{:S(2)}, u32[]{:S(2)}) %collective-permute-start.5) | collective-permute-done | bytes 143392 | tf_op jit(solution)/shard_map/ppermute | solution.py:20
  34.6 0.8 %collective-permute-done.11.refs_0_.refs_3_ = bf16[88,512]{1,0:T(8,128)(2,1)S(1)} collective-permute-done((bf16[88,512]{1,0:T(8,128)(2,1)S(1)}, bf16[88,512]{1,0:T(8,128)(2,1)S(1)}, u32[]{:S(2)}, u32[]{:S(2)}) %collective-permute-start.11) | collective-permute-done | bytes 90144 | tf_op jit(solution)/shard_map/ppermute | solution.py:20
  35.5 0.4 gate.14
  35.9 2.7 %collective-permute-start.12 = (bf16[88,512]{1,0:T(8,128)(2,1)S(1)}, bf16[88,512]{1,0:T(8,128)(2,1)S(1)}, u32[]{:S(2)}, u32[]{:S(2)}) collective-permute-start(bf16[88,512]{1,0:T(8,128)(2,1)S(1)} %gate.14), channel_id=1, source_target_pairs={{0,3},{1,2},{2,1},{3,0},{4,7},{5,6},{6,5},{7,4},{8,11},{9,10},{10,... | collective-permute-start | bytes 270344 | tf_op jit(solution)/shard_map/ppermute | solution.py:20
  38.7 0.4 gate.12
  39.2 0.6 collective-permute-done.8.refs_0_.refs_2_
  39.8 0.4 gate.10.refs_1_
  40.3 2.1 %collective-permute-start.10 = (bf16[88,512]{1,0:T(8,128)(2,1)S(1)}, bf16[88,512]{1,0:T(8,128)(2,1)S(1)}, u32[]{:S(2)}, u32[]{:S(2)}) collective-permute-start(bf16[88,512]{1,0:T(8,128)(2,1)S(1)} %gate.10.refs_1_), channel_id=1, source_target_pairs={{0,2},{1,3},{2,0},{3,1},{4,6},{5,7},{6,4},{7,5},{8,10},{9,11},{10,... | collective-permute-start | bytes 270344 | tf_op jit(solution)/shard_map/ppermute | solution.py:20
  42.4 0.4 gate.15.refs_0_
  42.8 0.2 activate.3.refs_0_.value_ref
  43.1 0.6 collective-permute-start.14
  43.6 0.4 gate.11.refs_0_
  44.1 1.1 %collective-permute-done.9.refs_1_ = bf16[88,512]{1,0:T(8,128)(2,1)S(1)} collective-permute-done((bf16[88,512]{1,0:T(8,128)(2,1)S(1)}, bf16[88,512]{1,0:T(8,128)(2,1)S(1)}, u32[]{:S(2)}, u32[]{:S(2)}) %collective-permute-start.9) | collective-permute-done | bytes 90144 | tf_op jit(solution)/shard_map/ppermute | solution.py:20
  45.2 1.4 %collective-permute-done.10.refs_2_ = bf16[88,512]{1,0:T(8,128)(2,1)S(1)} collective-permute-done((bf16[88,512]{1,0:T(8,128)(2,1)S(1)}, bf16[88,512]{1,0:T(8,128)(2,1)S(1)}, u32[]{:S(2)}, u32[]{:S(2)}) %collective-permute-start.10) | collective-permute-done | bytes 90144 | tf_op jit(solution)/shard_map/ppermute | solution.py:20
  46.8 2.9 %collective-permute-start.13 = (bf16[80,512]{1,0:T(8,128)(2,1)S(1)}, bf16[80,512]{1,0:T(8,128)(2,1)S(1)}, u32[]{:S(2)}, u32[]{:S(2)}) collective-permute-start(bf16[80,512]{1,0:T(8,128)(2,1)S(1)} %activate.2.refs_0_.refs_2_), channel_id=1, source_target_pairs={{0,3},{1,2},{2,1},{3,0},{4,7},{5,6},{6,5},{7,4},{8,11},{9,10},{10,... | collective-permute-start | bytes 245768 | tf_op jit(solution)/shard_map/ppermute | solution.py:20
  49.7 1.5 %collective-permute-start.19 = (bf16[80,512]{1,0:T(8,128)(2,1)S(1)}, bf16[80,512]{1,0:T(8,128)(2,1)S(1)}, u32[]{:S(2)}, u32[]{:S(2)}) collective-permute-start(bf16[80,512]{1,0:T(8,128)(2,1)S(1)} %activate.2.refs_0_.refs_2_), channel_id=1, source_target_pairs={{0,1},{1,0},{2,3},{3,2},{4,5},{5,4},{6,7},{7,6},{8,9},{9,8},{10,11... | collective-permute-start | bytes 245768 | tf_op jit(solution)/shard_map/ppermute | solution.py:20
  51.2 0.8 %down.5.refs_1_.refs_2_ = f32[80,1792]{1,0:T(8,128)S(1)} custom-call(s32[1]{0:T(128)} %bitcast.8.block_ref, bf16[1,2048,1792]{2,1,0:T(8,128)(2,1)S(1)} %bitcast.15, bf16[80,512]{1,0:T(8,128)(2,1)S(1)} %activate.3.refs_0_.value_ref, bf16[80,512]{1,0:T(8,128)(2,1)S(1)} %collective-permute-done.14.refs_2_.refs_1_, bf16[80,512]{1,0:T(8,128)(2,1)S(1)} %activate.2.refs_0_.refs_2_), custom_call_target="tpu_custom_call" | custom-call | flops 293601280 | bytes 3670016 | tf_op jit(solution)/shard_map/down/pallas_call | solution.py:362
  52.0 1.8 %collective-permute-done.13.refs_1_ = bf16[80,512]{1,0:T(8,128)(2,1)S(1)} collective-permute-done((bf16[80,512]{1,0:T(8,128)(2,1)S(1)}, bf16[80,512]{1,0:T(8,128)(2,1)S(1)}, u32[]{:S(2)}, u32[]{:S(2)}) %collective-permute-start.13) | collective-permute-done | bytes 81952 | tf_op jit(solution)/shard_map/ppermute | solution.py:20
  53.8 0.8 %down.4.after_ref.refs_0_.refs_2_ = f32[80,1792]{1,0:T(8,128)S(1)} custom-call(s32[1]{0:T(128)} %bitcast.8.block_ref, bf16[1,2048,1792]{2,1,0:T(8,128)(2,1)S(1)} %bitcast.15, bf16[80,512]{1,0:T(8,128)(2,1)S(1)} %activate.2.refs_0_.refs_2_, bf16[80,512]{1,0:T(8,128)(2,1)S(1)} %collective-permute-done.13.refs_1_, ...), custom_call_target="tpu_custom_call" | custom-call | flops 293601280 | bytes 3670016 | tf_op jit(solution)/shard_map/down/pallas_call | solution.py:362
  54.5 0.7 %store.1 = (bf16[64,1792]{1,0:T(8,128)(2,1)}, f32[8,128]{1,0:T(8,128)S(1)}) custom-call(bf16[64,1792]{1,0:T(8,128)(2,1)S(1)} %get-tuple-element.24.stream_ref.values_ref, f32[80,1792]{1,0:T(8,128)S(1)} %down.4.after_ref.refs_0_.refs_2_), custom_call_target="tpu_custom_call" | custom-call | flops 1000000 | bytes 458752 | tf_op jit(solution)/shard_map/store/pallas_call | solution.py:382
  55.3 2.2 %collective-permute-start.15 = (bf16[80,512]{1,0:T(8,128)(2,1)S(1)}, bf16[80,512]{1,0:T(8,128)(2,1)S(1)}, u32[]{:S(2)}, u32[]{:S(2)}) collective-permute-start(bf16[80,512]{1,0:T(8,128)(2,1)S(1)} %hold.1), channel_id=1, source_target_pairs={{0,3},{1,2},{2,1},{3,0},{4,7},{5,6},{6,5},{7,4},{8,11},{9,10},{10,... | collective-permute-start | bytes 245768 | tf_op jit(solution)/shard_map/ppermute | solution.py:20
  57.5 0.8 %down.7 = (bf16[40,1792]{1,0:T(8,128)(2,1)S(1)}, bf16[40,1792]{1,0:T(8,128)(2,1)S(1)}) custom-call(s32[1]{0:T(128)} %bitcast.8.block_ref, bf16[1,2048,1792]{2,1,0:T(8,128)(2,1)S(1)} %bitcast.15, bf16[80,512]{1,0:T(8,128)(2,1)S(1)} %collective-permute-done.18.refs_0_, bf16[80,512]{1,0:T(8,128)(2,1)S(1)} %collective-permute-done.19.refs_1_, ...), custom_call_target="tpu_custom_call" | custom-call | flops 293601280 | bytes 3670016 | tf_op jit(solution)/shard_map/down/pallas_call | solution.py:362
  58.3 1.6 %collective-permute-start.20 = (bf16[40,1792]{1,0:T(8,128)(2,1)S(1)}, bf16[40,1792]{1,0:T(8,128)(2,1)S(1)}, u32[]{:S(2)}, u32[]{:S(2)}) collective-permute-start(bf16[40,1792]{1,0:T(8,128)(2,1)S(1)} %get-tuple-element.40), channel_id=1, source_target_pairs={{0,8},{4,12},{8,0},{12,4},{1,9},{5,13},{9,1},{13,5},{2,10},{6,14},... | collective-permute-start | bytes 430088 | tf_op jit(solution)/shard_map/ppermute | solution.py:20
  59.9 1.6 %collective-permute-done.15.refs_0_ = bf16[80,512]{1,0:T(8,128)(2,1)S(1)} collective-permute-done((bf16[80,512]{1,0:T(8,128)(2,1)S(1)}, bf16[80,512]{1,0:T(8,128)(2,1)S(1)}, u32[]{:S(2)}, u32[]{:S(2)}) %collective-permute-start.15) | collective-permute-done | bytes 81952 | tf_op jit(solution)/shard_map/ppermute | solution.py:20
  61.5 1.8 %collective-permute-done.16.refs_1_ = bf16[80,512]{1,0:T(8,128)(2,1)S(1)} collective-permute-done((bf16[80,512]{1,0:T(8,128)(2,1)S(1)}, bf16[80,512]{1,0:T(8,128)(2,1)S(1)}, u32[]{:S(2)}, u32[]{:S(2)}) %collective-permute-start.16) | collective-permute-done | bytes 81952 | tf_op jit(solution)/shard_map/ppermute | solution.py:20
  63.3 0.8 %down.6 = (bf16[40,1792]{1,0:T(8,128)(2,1)S(1)}, bf16[40,1792]{1,0:T(8,128)(2,1)S(1)}) custom-call(s32[1]{0:T(128)} %bitcast.8.block_ref, bf16[1,2048,1792]{2,1,0:T(8,128)(2,1)S(1)} %bitcast.15, bf16[80,512]{1,0:T(8,128)(2,1)S(1)} %collective-permute-done.15.refs_0_, bf16[80,512]{1,0:T(8,128)(2,1)S(1)} %collective-permute-done.16.refs_1_, ...), custom_call_target="tpu_custom_call" | custom-call | flops 293601280 | bytes 3670016 | tf_op jit(solution)/shard_map/down/pallas_call | solution.py:362
  64.1 1.8 %collective-permute-done.21.refs_3_ = bf16[40,1792]{1,0:T(8,128)(2,1)S(1)} collective-permute-done((bf16[40,1792]{1,0:T(8,128)(2,1)S(1)}, bf16[40,1792]{1,0:T(8,128)(2,1)S(1)}, u32[]{:S(2)}, u32[]{:S(2)}) %collective-permute-start.21) | collective-permute-done | bytes 143392 | tf_op jit(solution)/shard_map/ppermute | solution.py:20
  65.9 1.0 %combine.1 = bf16[64,1792]{1,0:T(8,128)(2,1)} custom-call(bf16[64,160]{1,0:T(8,128)(2,1)S(1)} %get-tuple-element.35.high_ref, bf16[64,160]{1,0:T(8,128)(2,1)S(1)} %get-tuple-element.36.low_ref, bf16[40,1792]{1,0:T(8,128)(2,1)S(1)} %get-tuple-element.38.refs_0_, bf16[40,1792]{1,0:T(8,128)(2,1)S(1)} %collective-permute-done.17.refs_1_, ...), custom_call_target="tpu_custom_call" | custom-call | flops 73400320 | bytes 573440 | tf_op jit(solution)/shard_map/combine/pallas_call | solution.py:397
  (37 shorter events, 1.2 us)
Async XLA Ops:
  0.6 18.4 %copy-start.2 = (s32[64,2]{0,1:T(2,128)S(1)}, s32[64,2]{0,1:T(2,128)}, u32[]{:S(2)}) copy-start(s32[64,2]{0,1:T(2,128)} %param.10) | copy-start | bytes 1540
  0.6 26.8 %copy-start.3 = (bf16[1792]{0:T(1024)(128)(2,1)S(1)}, bf16[1792]{0:T(1024)(128)(2,1)}, u32[]{:S(2)}) copy-start(bf16[1792]{0:T(1024)(128)(2,1)} %param.9) | copy-start | bytes 10756
  2.1 9.5 %collective-permute-start.2 = (bf16[64,1792]{1,0:T(8,128)(2,1)S(1)}, bf16[64,1792]{1,0:T(8,128)(2,1)S(1)}, u32[]{:S(2)}, u32[]{:S(2)}) collective-permute-start(bf16[64,1792]{1,0:T(8,128)(2,1)S(1)} %get-tuple-element.42), channel_id=1, source_target_pairs={{0,1},{1,0},{2,3},{3,2},{4,5},{5,4},{6,7},{7,6},{8,9},{9,8},{10,11... | collective-permute-start | bytes 688136 | tf_op jit(solution)/shard_map/ppermute | solution.py:20
  5.2 14.3 %collective-permute-start = (bf16[64,1792]{1,0:T(8,128)(2,1)S(1)}, bf16[64,1792]{1,0:T(8,128)(2,1)S(1)}, u32[]{:S(2)}, u32[]{:S(2)}) collective-permute-start(bf16[64,1792]{1,0:T(8,128)(2,1)S(1)} %get-tuple-element.44), channel_id=1, source_target_pairs={{1,2},{2,1},{5,6},{6,5},{9,10},{10,9},{13,14},{14,13},{17,18},{18,... | collective-permute-start | bytes 688136 | tf_op jit(solution)/shard_map/ppermute | solution.py:235
  5.9 13.7 %collective-permute-start.1 = (bf16[64,1792]{1,0:T(8,128)(2,1)S(1)}, bf16[64,1792]{1,0:T(8,128)(2,1)S(1)}, u32[]{:S(2)}, u32[]{:S(2)}) collective-permute-start(bf16[64,1792]{1,0:T(8,128)(2,1)S(1)} %get-tuple-element.43.passing_ref), channel_id=1, source_target_pairs={{0,2},{3,1},{4,6},{7,5},{8,10},{11,9},{12,14},{15,13},{16,18},{19,... | collective-permute-start | bytes 688136 | tf_op jit(solution)/shard_map/ppermute | solution.py:236
  11.7 13.1 %collective-permute-start.3 = (bf16[64,1792]{1,0:T(8,128)(2,1)S(1)}, bf16[64,1792]{1,0:T(8,128)(2,1)S(1)}, u32[]{:S(2)}, u32[]{:S(2)}) collective-permute-start(bf16[64,1792]{1,0:T(8,128)(2,1)S(1)} %merge.1), channel_id=1, source_target_pairs={{0,1},{1,3},{2,0},{3,2},{4,5},{5,7},{6,4},{7,6},{8,9},{9,11},{10,8... | collective-permute-start | bytes 688136 | tf_op jit(solution)/shard_map/ppermute | solution.py:246
  14.2 3.1 %copy-start = (bf16[1,1792,2048]{2,1,0:T(8,128)(2,1)S(1)}, bf16[1,1792,2048]{2,1,0:T(8,128)(2,1)}, u32[]{:S(2)}) copy-start(bf16[1,1792,2048]{2,1,0:T(8,128)(2,1)} %refs_1_.1) | copy-start | bytes 22020100
  17.3 0.9 %copy-start.1 = (bf16[64,1792]{1,0:T(8,128)(2,1)S(1)}, bf16[64,1792]{1,0:T(8,128)(2,1)}, u32[]{:S(2)}) copy-start(bf16[64,1792]{1,0:T(8,128)(2,1)} %refs_0_.1) | copy-start | bytes 688132
  25.2 2.2 %collective-permute-start.6 = (bf16[40,1792]{1,0:T(8,128)(2,1)S(1)}, bf16[40,1792]{1,0:T(8,128)(2,1)S(1)}, u32[]{:S(2)}, u32[]{:S(2)}) collective-permute-start(bf16[40,1792]{1,0:T(8,128)(2,1)S(1)} %get-tuple-element.31), channel_id=1, source_target_pairs={{0,4},{4,0},{8,12},{12,8},{1,5},{5,1},{9,13},{13,9},{2,6},{6,2},{1... | collective-permute-start | bytes 430088 | tf_op jit(solution)/shard_map/ppermute | solution.py:20
  25.5 8.1 %collective-permute-start.4 = (bf16[40,1792]{1,0:T(8,128)(2,1)S(1)}, bf16[40,1792]{1,0:T(8,128)(2,1)S(1)}, u32[]{:S(2)}, u32[]{:S(2)}) collective-permute-start(bf16[40,1792]{1,0:T(8,128)(2,1)S(1)} %get-tuple-element.25), channel_id=1, source_target_pairs={{0,8},{4,12},{8,0},{12,4},{1,9},{5,13},{9,1},{13,5},{2,10},{6,14},... | collective-permute-start | bytes 430088 | tf_op jit(solution)/shard_map/ppermute | solution.py:20
  27.1 7.3 %collective-permute-start.5 = (bf16[40,1792]{1,0:T(8,128)(2,1)S(1)}, bf16[40,1792]{1,0:T(8,128)(2,1)S(1)}, u32[]{:S(2)}, u32[]{:S(2)}) collective-permute-start(bf16[40,1792]{1,0:T(8,128)(2,1)S(1)} %get-tuple-element.26), channel_id=1, source_target_pairs={{0,12},{4,8},{8,4},{12,0},{1,13},{5,9},{9,5},{13,1},{2,14},{6,10},... | collective-permute-start | bytes 430088 | tf_op jit(solution)/shard_map/ppermute | solution.py:20
  28.1 7.3 %collective-permute-start.11 = (bf16[88,512]{1,0:T(8,128)(2,1)S(1)}, bf16[88,512]{1,0:T(8,128)(2,1)S(1)}, u32[]{:S(2)}, u32[]{:S(2)}) collective-permute-start(bf16[88,512]{1,0:T(8,128)(2,1)S(1)} %gate.13), channel_id=1, source_target_pairs={{0,3},{1,2},{2,1},{3,0},{4,7},{5,6},{6,5},{7,4},{8,11},{9,10},{10,... | collective-permute-start | bytes 270344 | tf_op jit(solution)/shard_map/ppermute | solution.py:20
  31.3 7.4 %collective-permute-start.7 = (bf16[88,512]{1,0:T(8,128)(2,1)S(1)}, bf16[88,512]{1,0:T(8,128)(2,1)S(1)}, u32[]{:S(2)}, u32[]{:S(2)}) collective-permute-start(bf16[88,512]{1,0:T(8,128)(2,1)S(1)} %gate.8), channel_id=1, source_target_pairs={{0,1},{1,0},{2,3},{3,2},{4,5},{5,4},{6,7},{7,6},{8,9},{9,8},{10,11... | collective-permute-start | bytes 270344 | tf_op jit(solution)/shard_map/ppermute | solution.py:20
  31.8 8.0 %collective-permute-start.8 = (bf16[88,512]{1,0:T(8,128)(2,1)S(1)}, bf16[88,512]{1,0:T(8,128)(2,1)S(1)}, u32[]{:S(2)}, u32[]{:S(2)}) collective-permute-start(bf16[88,512]{1,0:T(8,128)(2,1)S(1)} %gate.9), channel_id=1, source_target_pairs={{0,2},{1,3},{2,0},{3,1},{4,6},{5,7},{6,4},{7,5},{8,10},{9,11},{10,... | collective-permute-start | bytes 270344 | tf_op jit(solution)/shard_map/ppermute | solution.py:20
  35.9 8.2 %collective-permute-start.12 = (bf16[88,512]{1,0:T(8,128)(2,1)S(1)}, bf16[88,512]{1,0:T(8,128)(2,1)S(1)}, u32[]{:S(2)}, u32[]{:S(2)}) collective-permute-start(bf16[88,512]{1,0:T(8,128)(2,1)S(1)} %gate.14), channel_id=1, source_target_pairs={{0,3},{1,2},{2,1},{3,0},{4,7},{5,6},{6,5},{7,4},{8,11},{9,10},{10,... | collective-permute-start | bytes 270344 | tf_op jit(solution)/shard_map/ppermute | solution.py:20
  39.1 6.1 %collective-permute-start.9 = (bf16[88,512]{1,0:T(8,128)(2,1)S(1)}, bf16[88,512]{1,0:T(8,128)(2,1)S(1)}, u32[]{:S(2)}, u32[]{:S(2)}) collective-permute-start(bf16[88,512]{1,0:T(8,128)(2,1)S(1)} %gate.12), channel_id=1, source_target_pairs={{0,1},{1,0},{2,3},{3,2},{4,5},{5,4},{6,7},{7,6},{8,9},{9,8},{10,11... | collective-permute-start | bytes 270344 | tf_op jit(solution)/shard_map/ppermute | solution.py:20
  40.3 11.0 %slice-start = ((s8[7340032]{0:T(1024)(128)(4,1)}), s8[4194304]{0:T(1024)(128)(4,1)S(1)}, s32[]{:S(2)}) async-start(s8[7340032]{0:T(1024)(128)(4,1)} %bitcast.14), calls=%async_computation | async-start | bytes 8388608
  40.3 6.3 %collective-permute-start.10 = (bf16[88,512]{1,0:T(8,128)(2,1)S(1)}, bf16[88,512]{1,0:T(8,128)(2,1)S(1)}, u32[]{:S(2)}, u32[]{:S(2)}) collective-permute-start(bf16[88,512]{1,0:T(8,128)(2,1)S(1)} %gate.10.refs_1_), channel_id=1, source_target_pairs={{0,2},{1,3},{2,0},{3,1},{4,6},{5,7},{6,4},{7,5},{8,10},{9,11},{10,... | collective-permute-start | bytes 270344 | tf_op jit(solution)/shard_map/ppermute | solution.py:20
  43.0 8.2 %slice-start.1 = ((s8[7340032]{0:T(1024)(128)(4,1)}), s8[3145728]{0:T(1024)(128)(4,1)S(1)}, s32[]{:S(2)}) async-start(s8[7340032]{0:T(1024)(128)(4,1)} %bitcast.14), calls=%async_computation.1 | async-start | bytes 6291456
  43.1 8.2 %collective-permute-start.14 = (bf16[80,512]{1,0:T(8,128)(2,1)S(1)}, bf16[80,512]{1,0:T(8,128)(2,1)S(1)}, u32[]{:S(2)}, u32[]{:S(2)}) collective-permute-start(bf16[80,512]{1,0:T(8,128)(2,1)S(1)} %activate.3.refs_0_.value_ref), channel_id=1, source_target_pairs={{0,1},{1,0},{2,3},{3,2},{4,5},{5,4},{6,7},{7,6},{8,9},{9,8},{10,11... | collective-permute-start | bytes 245768 | tf_op jit(solution)/shard_map/ppermute | solution.py:20
  46.8 7.0 %collective-permute-start.13 = (bf16[80,512]{1,0:T(8,128)(2,1)S(1)}, bf16[80,512]{1,0:T(8,128)(2,1)S(1)}, u32[]{:S(2)}, u32[]{:S(2)}) collective-permute-start(bf16[80,512]{1,0:T(8,128)(2,1)S(1)} %activate.2.refs_0_.refs_2_), channel_id=1, source_target_pairs={{0,3},{1,2},{2,1},{3,0},{4,7},{5,6},{6,5},{7,4},{8,11},{9,10},{10,... | collective-permute-start | bytes 245768 | tf_op jit(solution)/shard_map/ppermute | solution.py:20
  49.7 7.8 %collective-permute-start.18 = (bf16[80,512]{1,0:T(8,128)(2,1)S(1)}, bf16[80,512]{1,0:T(8,128)(2,1)S(1)}, u32[]{:S(2)}, u32[]{:S(2)}) collective-permute-start(bf16[80,512]{1,0:T(8,128)(2,1)S(1)} %activate.2.refs_0_.refs_2_), channel_id=1, source_target_pairs={{0,2},{1,3},{2,0},{3,1},{4,6},{5,7},{6,4},{7,5},{8,10},{9,11},{10,... | collective-permute-start | bytes 245768 | tf_op jit(solution)/shard_map/ppermute | solution.py:20
  49.7 7.8 %collective-permute-start.19 = (bf16[80,512]{1,0:T(8,128)(2,1)S(1)}, bf16[80,512]{1,0:T(8,128)(2,1)S(1)}, u32[]{:S(2)}, u32[]{:S(2)}) collective-permute-start(bf16[80,512]{1,0:T(8,128)(2,1)S(1)} %activate.2.refs_0_.refs_2_), channel_id=1, source_target_pairs={{0,1},{1,0},{2,3},{3,2},{4,5},{5,4},{6,7},{7,6},{8,9},{9,8},{10,11... | collective-permute-start | bytes 245768 | tf_op jit(solution)/shard_map/ppermute | solution.py:20
  55.3 6.2 %collective-permute-start.15 = (bf16[80,512]{1,0:T(8,128)(2,1)S(1)}, bf16[80,512]{1,0:T(8,128)(2,1)S(1)}, u32[]{:S(2)}, u32[]{:S(2)}) collective-permute-start(bf16[80,512]{1,0:T(8,128)(2,1)S(1)} %hold.1), channel_id=1, source_target_pairs={{0,3},{1,2},{2,1},{3,0},{4,7},{5,6},{6,5},{7,4},{8,11},{9,10},{10,... | collective-permute-start | bytes 245768 | tf_op jit(solution)/shard_map/ppermute | solution.py:20
  57.5 5.7 %collective-permute-start.16 = (bf16[80,512]{1,0:T(8,128)(2,1)S(1)}, bf16[80,512]{1,0:T(8,128)(2,1)S(1)}, u32[]{:S(2)}, u32[]{:S(2)}) collective-permute-start(bf16[80,512]{1,0:T(8,128)(2,1)S(1)} %hold.1), channel_id=1, source_target_pairs={{0,2},{1,3},{2,0},{3,1},{4,6},{5,7},{6,4},{7,5},{8,10},{9,11},{10,... | collective-permute-start | bytes 245768 | tf_op jit(solution)/shard_map/ppermute | solution.py:20
  58.3 5.8 %collective-permute-start.20 = (bf16[40,1792]{1,0:T(8,128)(2,1)S(1)}, bf16[40,1792]{1,0:T(8,128)(2,1)S(1)}, u32[]{:S(2)}, u32[]{:S(2)}) collective-permute-start(bf16[40,1792]{1,0:T(8,128)(2,1)S(1)} %get-tuple-element.40), channel_id=1, source_target_pairs={{0,8},{4,12},{8,0},{12,4},{1,9},{5,13},{9,1},{13,5},{2,10},{6,14},... | collective-permute-start | bytes 430088 | tf_op jit(solution)/shard_map/ppermute | solution.py:20
  59.9 6.0 %collective-permute-start.21 = (bf16[40,1792]{1,0:T(8,128)(2,1)S(1)}, bf16[40,1792]{1,0:T(8,128)(2,1)S(1)}, u32[]{:S(2)}, u32[]{:S(2)}) collective-permute-start(bf16[40,1792]{1,0:T(8,128)(2,1)S(1)} %get-tuple-element.41), channel_id=1, source_target_pairs={{0,12},{4,8},{8,4},{12,0},{1,13},{5,9},{9,5},{13,1},{2,14},{6,10},... | collective-permute-start | bytes 430088 | tf_op jit(solution)/shard_map/ppermute | solution.py:20
  64.0 1.9 %collective-permute-start.17 = (bf16[40,1792]{1,0:T(8,128)(2,1)S(1)}, bf16[40,1792]{1,0:T(8,128)(2,1)S(1)}, u32[]{:S(2)}, u32[]{:S(2)}) collective-permute-start(bf16[40,1792]{1,0:T(8,128)(2,1)S(1)} %get-tuple-element.39), channel_id=1, source_target_pairs={{0,4},{4,0},{8,12},{12,8},{1,5},{5,1},{9,13},{13,9},{2,6},{6,2},{1... | collective-permute-start | bytes 430088 | tf_op jit(solution)/shard_map/ppermute | solution.py:20

commit v10 on v9

--- a/solution.py
+++ b/solution.py
@@ -36,7 +36,7 @@
     return pl.BlockSpec(memory_space=pltpu.SMEM)
 
 
-def routing_kernel(n, cap, me_ref, ids_ref, idst_ref, scores_ref, select_ref, high_ref, low_ref):
+def routing_kernel(n, cap, me_ref, ids_ref, idst_ref, scores_ref, select_ref, weigh_ref):
     me = me_ref[0]
     tokens, top = ids_ref.shape
     f32, bf16 = jnp.float32, jnp.bfloat16
@@ -71,8 +71,8 @@
         highs.append(high)
         lows.append(full - high)
     select_ref[...] = jnp.concatenate(selects, axis=0).astype(bf16)
-    high_ref[...] = jnp.concatenate(highs, axis=1).astype(bf16)
-    low_ref[...] = jnp.concatenate(lows, axis=1).astype(bf16)
+    weigh_ref[:tokens, :] = jnp.concatenate(highs, axis=1).astype(bf16)
+    weigh_ref[tokens:, :] = jnp.concatenate(lows, axis=1).astype(bf16)
 
 
 def fetch_kernel(*refs):
@@ -198,12 +198,20 @@
             out[...] = total[i * cap : (i + 1) * cap, :].astype(jnp.bfloat16)
 
 
-def combine_kernel(n, high_ref, low_ref, *refs):
-    pieces, out_ref = refs[:n], refs[n]
-    rows = jnp.concatenate([p[...].astype(jnp.float32) for p in pieces], axis=0).astype(jnp.bfloat16)
-    total = jnp.dot(high_ref[...], rows, preferred_element_type=jnp.float32)
-    total += jnp.dot(low_ref[...], rows, preferred_element_type=jnp.float32)
-    out_ref[...] = total.astype(jnp.bfloat16)
+def combine_kernel(n, n_chunks, weigh_ref, *refs):
+    pieces, (out_ref, result_ref, sems) = refs[:n], refs[n:]
+    tokens, share = out_ref.shape
+    width = share // n_chunks
+    copies = []
+    for i in range(n_chunks):
+        columns = pl.ds(i * width, width)
+        rows = jnp.concatenate([p[:, columns].astype(jnp.float32) for p in pieces], axis=0).astype(jnp.bfloat16)
+        total = jnp.dot(weigh_ref[...], rows, preferred_element_type=jnp.float32)
+        result_ref[:, columns] = (total[:tokens] + total[tokens:]).astype(jnp.bfloat16)
+        copies.append(pltpu.make_async_copy(result_ref.at[:, columns], out_ref.at[:, columns], sems.at[i]))
+        copies[i].start()
+    for copy in copies:
+        copy.wait()
 
 
 def estimate(flops, moved):
@@ -249,11 +257,11 @@
         end_arr = jnp.ones((1,), jnp.int32)
         parts = [exchange(block(z ^ k), "tensor", k) if k else block(z) for k in partners(nt)]
 
-    select, high, low = pl.pallas_call(
+    select, weigh = pl.pallas_call(
         functools.partial(routing_kernel, ne, cap),
-        out_shape=(sds((rows, tokens), bf16), sds((tokens, rows), bf16), sds((tokens, rows), bf16)),
+        out_shape=(sds((rows, tokens), bf16), sds((2 * tokens, rows), bf16)),
         in_specs=[scalar(), whole(), whole(), whole()],
-        out_specs=(whole(),) * 3,
+        out_specs=(whole(),) * 2,
         compiler_params=params(),
         cost_estimate=estimate(10**6, 2**16),
         name="routing",
@@ -272,24 +280,16 @@
     )(*fetched)
 
     kept, *near_rows = pl.pallas_call(
-        functools.partial(add_kernel, len(parts), cap, near),
-        out_shape=(sds((tokens, share), bf16),) + (sds((cap, share), bf16),) * len(near),
+        functools.partial(add_kernel, len(parts), cap, near + far),
+        out_shape=(sds((tokens, share), bf16),) + (sds((cap, share), bf16),) * ne,
         in_specs=[scalar()] + [whole()] * (2 + len(parts)),
-        out_specs=(whole(),) * (1 + len(near)),
+        out_specs=(whole(),) * (1 + ne),
         compiler_params=params(),
         cost_estimate=estimate(2 * rows * tokens * share, 4 * tokens * share * nt),
         name="add",
     )(end_arr, residual, select, *parts)
     arrived = {0: near_rows[0], 1: exchange(near_rows[1], "expert", 1)}
-    far_rows = pl.pallas_call(
-        functools.partial(pack_kernel, cap, far),
-        out_shape=(sds((cap, share), bf16),) * len(far),
-        in_specs=[whole()] * 2,
-        out_specs=(whole(),) * len(far),
-        compiler_params=params(),
-        cost_estimate=estimate(2 * rows * tokens * share, 4 * tokens * share),
-        name="pack",
-    )(kept, select)
+    far_rows = near_rows[len(near) :]
     for k, value in zip(far, far_rows):
         arrived[k] = exchange(value, "expert", k)
 
@@ -394,15 +394,17 @@
     results.update(down(near, near_hidden, [k for k in partners(nt) if k > 1], near_sum))
     returned = {k: exchange(value, "expert", k) if k else value for k, value in results.items()}
 
+    n_chunks = 7 if share % (128 * 7) == 0 else 1
     moe_out = pl.pallas_call(
-        functools.partial(combine_kernel, ne),
+        functools.partial(combine_kernel, ne, n_chunks),
         out_shape=sds((tokens, share), bf16),
-        in_specs=[whole()] * (2 + ne),
-        out_specs=whole(),
+        in_specs=[whole()] * (1 + ne),
+        out_specs=anywhere(),
+        scratch_shapes=[pltpu.VMEM((tokens, share), bf16), pltpu.SemaphoreType.DMA((n_chunks,))],
         compiler_params=params(),
         cost_estimate=estimate(4 * rows * tokens * share, 2 * rows * share),
         name="combine",
-    )(high, low, *[returned[k] for k in range(ne)])
+    )(weigh, *[returned[k] for k in range(ne)])
     return stream, moe_out
 
 

time: 67.2 us -> 67 us (level)
    pallas_call x3 -> x2, Pallas kernels: 1.61 us -> 1.37 us  [the longest x1 0.96 us: local(): pl.pallas_call(functools.partial(combine_kernel, ne, n_chunks), out_shape...]
  transfers between devices with their start and end apart: 22 -> 22, of which waited for: 10 -> 10; matrix products, arithmetic and copies ran while one was open for 2% -> 2% of each run, Pallas kernels for 15% -> 14%
where the time goes in v10:
time: 67 us; the launch traced here: 66.8 us
  starting transfers between devices  31 us (46%)
  waiting for transfers between devices  16.9 us (25%)
  Pallas kernels  10.8 us (16%)
  local copies, waits for them, and re-layouts  7.03 us (10%)
  between operations  0.94 us (1%)
    ppermute x19, starting transfers between devices, exchange(): return lax.ppermute(value, axis, [(i, i ^ step) for i in range(n)])  23.7 us
    ppermute x19, waiting for transfers between devices, exchange(): return lax.ppermute(value, axis, [(i, i ^ step) for i in range(n)])  11.6 us
    ppermute x1, starting transfers between devices, local(): parts.append(lax.ppermute(block(z ^ 2), 'tensor', [(0, 2), (3, 1)]))  5.75 us
    unnamed x14, local copies, waits for them, and re-layouts  5.58 us
    ppermute x1, waiting for transfers between devices, local(): lax.ppermute(merged, 'tensor', [(0, 1), (1, 3), (2, 0), (3, 2)])  5.28 us
    pallas_call x8, Pallas kernels, summed_gate(): pl.pallas_call(gate_kernel, out_shape=sds((tall, ff), bf16), grid_spec=pl...  3.59 us
    pallas_call x4, Pallas kernels, down(): pl.pallas_call(functools.partial(down_kernel, steps, cap if final else No...  3.03 us
    dynamic_slice x1, local copies, waits for them, and re-layouts, block(): return lax.dynamic_slice(attn_partial[0], (0, k * share), (tokens, share))  1.44 us
  transfers between devices with their start and end apart: 22, of which 10 were waited for; matrix products, arithmetic and copies ran while one was open for 2% of the time, Pallas kernels for 14%

profile of v10, /device:TPU:0, one launch (start us, length us, event | category | flops | bytes accessed | tf_op | source)
XLA Modules:
  0.0 66.8 jit_solution(4166115909858474049)
XLA Ops:
  0.7 1.4 %dynamic-slice_bitcast_fusion = (bf16[64,1792]{1,0:T(8,128)(2,1)S(1)}, bf16[64,1792]{1,0:T(8,128)(2,1)S(1)}, bf16[64,1792]{1,0:T(8,128)(2,1)S(1)}, bf16[64,1792]{1,0:T(8,128)(2,1)S(1)}, bf16[64,1792]{1,0:T(8,128)(2,1)S(1)}) fusion(bf16[1,64,7168]{2,1,0:T(8,128)(2,1)} %param.8, s32[]{:T(128)S(6)} %select_n.30, s32[]{:T(128)S(6)} %select_n.27, s32[]{:T(128)S(6)} %select_n.26, ...), kind=kLoop, calls=%fused_computation | loop fusion | bytes 2293780 | tf_op jit(solution)/shard_map/dynamic_slice | solution.py:236
  2.1 3.1 %collective-permute-start.2 = (bf16[64,1792]{1,0:T(8,128)(2,1)S(1)}, bf16[64,1792]{1,0:T(8,128)(2,1)S(1)}, u32[]{:S(2)}, u32[]{:S(2)}) collective-permute-start(bf16[64,1792]{1,0:T(8,128)(2,1)S(1)} %get-tuple-element.40), channel_id=1, source_target_pairs={{0,1},{1,0},{2,3},{3,2},{4,5},{5,4},{6,7},{7,6},{8,9},{9,8},{10,11... | collective-permute-start | bytes 688136 | tf_op jit(solution)/shard_map/ppermute | solution.py:20
  5.2 0.7 collective-permute-start
  5.9 5.8 %collective-permute-start.1 = (bf16[64,1792]{1,0:T(8,128)(2,1)S(1)}, bf16[64,1792]{1,0:T(8,128)(2,1)S(1)}, u32[]{:S(2)}, u32[]{:S(2)}) collective-permute-start(bf16[64,1792]{1,0:T(8,128)(2,1)S(1)} %get-tuple-element.41.passing_ref), channel_id=1, source_target_pairs={{0,2},{3,1},{4,6},{7,5},{8,10},{11,9},{12,14},{15,13},{16,18},{19,... | collective-permute-start | bytes 688136 | tf_op jit(solution)/shard_map/ppermute | solution.py:244
  11.7 1.0 %collective-permute-start.3 = (bf16[64,1792]{1,0:T(8,128)(2,1)S(1)}, bf16[64,1792]{1,0:T(8,128)(2,1)S(1)}, u32[]{:S(2)}, u32[]{:S(2)}) collective-permute-start(bf16[64,1792]{1,0:T(8,128)(2,1)S(1)} %merge.1), channel_id=1, source_target_pairs={{0,1},{1,3},{2,0},{3,2},{4,5},{5,7},{6,4},{7,6},{8,9},{9,11},{10,8... | collective-permute-start | bytes 688136 | tf_op jit(solution)/shard_map/ppermute | solution.py:254
  12.7 0.8 %copy.10.scores_ref = f32[64,2]{1,0:T(8,128)S(1)} copy(f32[64,2]{0,1:T(2,128)} %param.11) | data formatting | bytes 1024 | tf_op args[4]
  13.4 0.8 %copy.9.ids_ref = s32[64,2]{1,0:T(8,128)S(1)} copy(s32[64,2]{0,1:T(2,128)} %param.10) | data formatting | bytes 1024 | tf_op args[3]
  14.2 3.1 %copy-done = bf16[1,1792,2048]{2,1,0:T(8,128)(2,1)S(1)} copy-done((bf16[1,1792,2048]{2,1,0:T(8,128)(2,1)S(1)}, bf16[1,1792,2048]{2,1,0:T(8,128)(2,1)}, u32[]{:S(2)}) %copy-start) | copy-done | bytes 7340056
  17.3 0.9 %copy-done.1 = bf16[64,1792]{1,0:T(8,128)(2,1)S(1)} copy-done((bf16[64,1792]{1,0:T(8,128)(2,1)S(1)}, bf16[64,1792]{1,0:T(8,128)(2,1)}, u32[]{:S(2)}) %copy-start.1) | copy-done | bytes 229400
  18.2 0.8 %fetch.1 = (bf16[64,1792]{1,0:T(8,128)(2,1)S(1)}, bf16[1,1792,2048]{2,1,0:T(8,128)(2,1)S(1)}) custom-call(bf16[64,1792]{1,0:T(8,128)(2,1)S(1)} %copy-done.1, bf16[1,1792,2048]{2,1,0:T(8,128)(2,1)S(1)} %copy-done), custom_call_target="tpu_custom_call" | custom-call | flops 1000000 | bytes 7569408 | tf_op jit(solution)/shard_map/fetch/pallas_call | solution.py:271
  19.0 0.5 routing.1
  19.6 5.3 %collective-permute-done.3.refs_3_ = bf16[64,1792]{1,0:T(8,128)(2,1)S(1)} collective-permute-done((bf16[64,1792]{1,0:T(8,128)(2,1)S(1)}, bf16[64,1792]{1,0:T(8,128)(2,1)S(1)}, u32[]{:S(2)}, u32[]{:S(2)}) %collective-permute-start.3) | collective-permute-done | bytes 229408 | tf_op jit(solution)/shard_map/ppermute | solution.py:254
  24.9 0.4 add.22
  25.3 1.6 %collective-permute-start.4 = (bf16[40,1792]{1,0:T(8,128)(2,1)S(1)}, bf16[40,1792]{1,0:T(8,128)(2,1)S(1)}, u32[]{:S(2)}, u32[]{:S(2)}) collective-permute-start(bf16[40,1792]{1,0:T(8,128)(2,1)S(1)} %get-tuple-element.24), channel_id=1, source_target_pairs={{0,8},{4,12},{8,0},{12,4},{1,9},{5,13},{9,1},{13,5},{2,10},{6,14},... | collective-permute-start | bytes 430088 | tf_op jit(solution)/shard_map/ppermute | solution.py:20
  26.9 0.3 collective-permute-start.5
  27.4 0.5 gate.13
  27.9 2.7 %collective-permute-start.11 = (bf16[88,512]{1,0:T(8,128)(2,1)S(1)}, bf16[88,512]{1,0:T(8,128)(2,1)S(1)}, u32[]{:S(2)}, u32[]{:S(2)}) collective-permute-start(bf16[88,512]{1,0:T(8,128)(2,1)S(1)} %gate.13), channel_id=1, source_target_pairs={{0,3},{1,2},{2,1},{3,0},{4,7},{5,6},{6,5},{7,4},{8,11},{9,10},{10,... | collective-permute-start | bytes 270344 | tf_op jit(solution)/shard_map/ppermute | solution.py:20
  30.6 0.4 gate.8
  31.1 0.4 gate.9
  31.6 1.8 %collective-permute-start.8 = (bf16[88,512]{1,0:T(8,128)(2,1)S(1)}, bf16[88,512]{1,0:T(8,128)(2,1)S(1)}, u32[]{:S(2)}, u32[]{:S(2)}) collective-permute-start(bf16[88,512]{1,0:T(8,128)(2,1)S(1)} %gate.9), channel_id=1, source_target_pairs={{0,2},{1,3},{2,0},{3,1},{4,6},{5,7},{6,4},{7,5},{8,10},{9,11},{10,... | collective-permute-start | bytes 270344 | tf_op jit(solution)/shard_map/ppermute | solution.py:20
  33.4 0.7 %collective-permute-done.5.refs_1_ = bf16[40,1792]{1,0:T(8,128)(2,1)S(1)} collective-permute-done((bf16[40,1792]{1,0:T(8,128)(2,1)S(1)}, bf16[40,1792]{1,0:T(8,128)(2,1)S(1)}, u32[]{:S(2)}, u32[]{:S(2)}) %collective-permute-start.5) | collective-permute-done | bytes 143392 | tf_op jit(solution)/shard_map/ppermute | solution.py:20
  34.3 0.9 %collective-permute-done.11.refs_0_.refs_3_ = bf16[88,512]{1,0:T(8,128)(2,1)S(1)} collective-permute-done((bf16[88,512]{1,0:T(8,128)(2,1)S(1)}, bf16[88,512]{1,0:T(8,128)(2,1)S(1)}, u32[]{:S(2)}, u32[]{:S(2)}) %collective-permute-start.11) | collective-permute-done | bytes 90144 | tf_op jit(solution)/shard_map/ppermute | solution.py:20
  35.2 0.4 gate.14
  35.7 2.7 %collective-permute-start.12 = (bf16[88,512]{1,0:T(8,128)(2,1)S(1)}, bf16[88,512]{1,0:T(8,128)(2,1)S(1)}, u32[]{:S(2)}, u32[]{:S(2)}) collective-permute-start(bf16[88,512]{1,0:T(8,128)(2,1)S(1)} %gate.14), channel_id=1, source_target_pairs={{0,3},{1,2},{2,1},{3,0},{4,7},{5,6},{6,5},{7,4},{8,11},{9,10},{10,... | collective-permute-start | bytes 270344 | tf_op jit(solution)/shard_map/ppermute | solution.py:20
  38.4 0.4 gate.12
  38.9 0.6 collective-permute-done.8.refs_0_.refs_2_
  39.6 0.4 gate.10.refs_1_
  40.0 2.2 %collective-permute-start.10 = (bf16[88,512]{1,0:T(8,128)(2,1)S(1)}, bf16[88,512]{1,0:T(8,128)(2,1)S(1)}, u32[]{:S(2)}, u32[]{:S(2)}) collective-permute-start(bf16[88,512]{1,0:T(8,128)(2,1)S(1)} %gate.10.refs_1_), channel_id=1, source_target_pairs={{0,2},{1,3},{2,0},{3,1},{4,6},{5,7},{6,4},{7,5},{8,10},{9,11},{10,... | collective-permute-start | bytes 270344 | tf_op jit(solution)/shard_map/ppermute | solution.py:20
  42.2 0.4 gate.15.refs_0_
  42.7 0.2 activate.3.refs_0_.value_ref
  42.9 0.5 collective-permute-start.14
  43.4 0.4 gate.11.refs_0_
  43.8 1.0 %collective-permute-done.9.refs_1_ = bf16[88,512]{1,0:T(8,128)(2,1)S(1)} collective-permute-done((bf16[88,512]{1,0:T(8,128)(2,1)S(1)}, bf16[88,512]{1,0:T(8,128)(2,1)S(1)}, u32[]{:S(2)}, u32[]{:S(2)}) %collective-permute-start.9) | collective-permute-done | bytes 90144 | tf_op jit(solution)/shard_map/ppermute | solution.py:20
  44.9 1.4 %collective-permute-done.10.refs_2_ = bf16[88,512]{1,0:T(8,128)(2,1)S(1)} collective-permute-done((bf16[88,512]{1,0:T(8,128)(2,1)S(1)}, bf16[88,512]{1,0:T(8,128)(2,1)S(1)}, u32[]{:S(2)}, u32[]{:S(2)}) %collective-permute-start.10) | collective-permute-done | bytes 90144 | tf_op jit(solution)/shard_map/ppermute | solution.py:20
  46.5 2.9 %collective-permute-start.13 = (bf16[80,512]{1,0:T(8,128)(2,1)S(1)}, bf16[80,512]{1,0:T(8,128)(2,1)S(1)}, u32[]{:S(2)}, u32[]{:S(2)}) collective-permute-start(bf16[80,512]{1,0:T(8,128)(2,1)S(1)} %activate.2.refs_0_.refs_2_), channel_id=1, source_target_pairs={{0,3},{1,2},{2,1},{3,0},{4,7},{5,6},{6,5},{7,4},{8,11},{9,10},{10,... | collective-permute-start | bytes 245768 | tf_op jit(solution)/shard_map/ppermute | solution.py:20
  49.5 1.5 %collective-permute-start.19 = (bf16[80,512]{1,0:T(8,128)(2,1)S(1)}, bf16[80,512]{1,0:T(8,128)(2,1)S(1)}, u32[]{:S(2)}, u32[]{:S(2)}) collective-permute-start(bf16[80,512]{1,0:T(8,128)(2,1)S(1)} %activate.2.refs_0_.refs_2_), channel_id=1, source_target_pairs={{0,1},{1,0},{2,3},{3,2},{4,5},{5,4},{6,7},{7,6},{8,9},{9,8},{10,11... | collective-permute-start | bytes 245768 | tf_op jit(solution)/shard_map/ppermute | solution.py:20
  51.0 0.8 %down.5.refs_1_.refs_2_ = f32[80,1792]{1,0:T(8,128)S(1)} custom-call(s32[1]{0:T(128)} %bitcast.8.block_ref, bf16[1,2048,1792]{2,1,0:T(8,128)(2,1)S(1)} %bitcast.15, bf16[80,512]{1,0:T(8,128)(2,1)S(1)} %activate.3.refs_0_.value_ref, bf16[80,512]{1,0:T(8,128)(2,1)S(1)} %collective-permute-done.14.refs_2_.refs_1_, bf16[80,512]{1,0:T(8,128)(2,1)S(1)} %activate.2.refs_0_.refs_2_), custom_call_target="tpu_custom_call" | custom-call | flops 293601280 | bytes 3670016 | tf_op jit(solution)/shard_map/down/pallas_call | solution.py:362
  51.8 1.7 %collective-permute-done.13.refs_1_ = bf16[80,512]{1,0:T(8,128)(2,1)S(1)} collective-permute-done((bf16[80,512]{1,0:T(8,128)(2,1)S(1)}, bf16[80,512]{1,0:T(8,128)(2,1)S(1)}, u32[]{:S(2)}, u32[]{:S(2)}) %collective-permute-start.13) | collective-permute-done | bytes 81952 | tf_op jit(solution)/shard_map/ppermute | solution.py:20
  53.5 0.8 %down.4.after_ref.refs_0_.refs_2_ = f32[80,1792]{1,0:T(8,128)S(1)} custom-call(s32[1]{0:T(128)} %bitcast.8.block_ref, bf16[1,2048,1792]{2,1,0:T(8,128)(2,1)S(1)} %bitcast.15, bf16[80,512]{1,0:T(8,128)(2,1)S(1)} %activate.2.refs_0_.refs_2_, bf16[80,512]{1,0:T(8,128)(2,1)S(1)} %collective-permute-done.13.refs_1_, ...), custom_call_target="tpu_custom_call" | custom-call | flops 293601280 | bytes 3670016 | tf_op jit(solution)/shard_map/down/pallas_call | solution.py:362
  54.2 0.7 %store.1 = (bf16[64,1792]{1,0:T(8,128)(2,1)}, f32[8,128]{1,0:T(8,128)S(1)}) custom-call(bf16[64,1792]{1,0:T(8,128)(2,1)S(1)} %get-tuple-element.23.values_ref, f32[80,1792]{1,0:T(8,128)S(1)} %down.4.after_ref.refs_0_.refs_2_), custom_call_target="tpu_custom_call" | custom-call | flops 1000000 | bytes 458752 | tf_op jit(solution)/shard_map/store/pallas_call | solution.py:382
  54.9 2.4 %collective-permute-start.15 = (bf16[80,512]{1,0:T(8,128)(2,1)S(1)}, bf16[80,512]{1,0:T(8,128)(2,1)S(1)}, u32[]{:S(2)}, u32[]{:S(2)}) collective-permute-start(bf16[80,512]{1,0:T(8,128)(2,1)S(1)} %hold.1), channel_id=1, source_target_pairs={{0,3},{1,2},{2,1},{3,0},{4,7},{5,6},{6,5},{7,4},{8,11},{9,10},{10,... | collective-permute-start | bytes 245768 | tf_op jit(solution)/shard_map/ppermute | solution.py:20
  57.4 0.8 %down.7 = (bf16[40,1792]{1,0:T(8,128)(2,1)S(1)}, bf16[40,1792]{1,0:T(8,128)(2,1)S(1)}) custom-call(s32[1]{0:T(128)} %bitcast.8.block_ref, bf16[1,2048,1792]{2,1,0:T(8,128)(2,1)S(1)} %bitcast.15, bf16[80,512]{1,0:T(8,128)(2,1)S(1)} %collective-permute-done.18.refs_0_, bf16[80,512]{1,0:T(8,128)(2,1)S(1)} %collective-permute-done.19.refs_1_, ...), custom_call_target="tpu_custom_call" | custom-call | flops 293601280 | bytes 3670016 | tf_op jit(solution)/shard_map/down/pallas_call | solution.py:362
  58.2 1.6 %collective-permute-start.20 = (bf16[40,1792]{1,0:T(8,128)(2,1)S(1)}, bf16[40,1792]{1,0:T(8,128)(2,1)S(1)}, u32[]{:S(2)}, u32[]{:S(2)}) collective-permute-start(bf16[40,1792]{1,0:T(8,128)(2,1)S(1)} %get-tuple-element.38), channel_id=1, source_target_pairs={{0,8},{4,12},{8,0},{12,4},{1,9},{5,13},{9,1},{13,5},{2,10},{6,14},... | collective-permute-start | bytes 430088 | tf_op jit(solution)/shard_map/ppermute | solution.py:20
  59.7 1.4 %collective-permute-done.15.refs_0_ = bf16[80,512]{1,0:T(8,128)(2,1)S(1)} collective-permute-done((bf16[80,512]{1,0:T(8,128)(2,1)S(1)}, bf16[80,512]{1,0:T(8,128)(2,1)S(1)}, u32[]{:S(2)}, u32[]{:S(2)}) %collective-permute-start.15) | collective-permute-done | bytes 81952 | tf_op jit(solution)/shard_map/ppermute | solution.py:20
  61.2 2.4 %collective-permute-done.16.refs_1_ = bf16[80,512]{1,0:T(8,128)(2,1)S(1)} collective-permute-done((bf16[80,512]{1,0:T(8,128)(2,1)S(1)}, bf16[80,512]{1,0:T(8,128)(2,1)S(1)}, u32[]{:S(2)}, u32[]{:S(2)}) %collective-permute-start.16) | collective-permute-done | bytes 81952 | tf_op jit(solution)/shard_map/ppermute | solution.py:20
  63.6 0.8 %down.6 = (bf16[40,1792]{1,0:T(8,128)(2,1)S(1)}, bf16[40,1792]{1,0:T(8,128)(2,1)S(1)}) custom-call(s32[1]{0:T(128)} %bitcast.8.block_ref, bf16[1,2048,1792]{2,1,0:T(8,128)(2,1)S(1)} %bitcast.15, bf16[80,512]{1,0:T(8,128)(2,1)S(1)} %collective-permute-done.15.refs_0_, bf16[80,512]{1,0:T(8,128)(2,1)S(1)} %collective-permute-done.16.refs_1_, ...), custom_call_target="tpu_custom_call" | custom-call | flops 293601280 | bytes 3670016 | tf_op jit(solution)/shard_map/down/pallas_call | solution.py:362
  64.4 1.4 %collective-permute-done.21.refs_3_ = bf16[40,1792]{1,0:T(8,128)(2,1)S(1)} collective-permute-done((bf16[40,1792]{1,0:T(8,128)(2,1)S(1)}, bf16[40,1792]{1,0:T(8,128)(2,1)S(1)}, u32[]{:S(2)}, u32[]{:S(2)}) %collective-permute-start.21) | collective-permute-done | bytes 143392 | tf_op jit(solution)/shard_map/ppermute | solution.py:20
  65.8 1.0 %combine.1 = bf16[64,1792]{1,0:T(8,128)(2,1)} custom-call(bf16[128,160]{1,0:T(8,128)(2,1)S(1)} %get-tuple-element.34.weigh_ref, bf16[40,1792]{1,0:T(8,128)(2,1)S(1)} %get-tuple-element.36.refs_0_, bf16[40,1792]{1,0:T(8,128)(2,1)S(1)} %collective-permute-done.17.refs_1_, bf16[40,1792]{1,0:T(8,128)(2,1)S(1)} %collective-permute-done.20.refs_2_, ...), custom_call_target="tpu_custom_call" | custom-call | flops 73400320 | bytes 573440 | tf_op jit(solution)/shard_map/combine/pallas_call | solution.py:398
  (36 shorter events, 1.1 us)
Async XLA Ops:
  0.6 18.4 %copy-start.2 = (s32[64,2]{0,1:T(2,128)S(1)}, s32[64,2]{0,1:T(2,128)}, u32[]{:S(2)}) copy-start(s32[64,2]{0,1:T(2,128)} %param.10) | copy-start | bytes 1540
  0.6 26.6 %copy-start.3 = (bf16[1792]{0:T(1024)(128)(2,1)S(1)}, bf16[1792]{0:T(1024)(128)(2,1)}, u32[]{:S(2)}) copy-start(bf16[1792]{0:T(1024)(128)(2,1)} %param.9) | copy-start | bytes 10756
  2.1 9.5 %collective-permute-start.2 = (bf16[64,1792]{1,0:T(8,128)(2,1)S(1)}, bf16[64,1792]{1,0:T(8,128)(2,1)S(1)}, u32[]{:S(2)}, u32[]{:S(2)}) collective-permute-start(bf16[64,1792]{1,0:T(8,128)(2,1)S(1)} %get-tuple-element.40), channel_id=1, source_target_pairs={{0,1},{1,0},{2,3},{3,2},{4,5},{5,4},{6,7},{7,6},{8,9},{9,8},{10,11... | collective-permute-start | bytes 688136 | tf_op jit(solution)/shard_map/ppermute | solution.py:20
  5.2 14.3 %collective-permute-start = (bf16[64,1792]{1,0:T(8,128)(2,1)S(1)}, bf16[64,1792]{1,0:T(8,128)(2,1)S(1)}, u32[]{:S(2)}, u32[]{:S(2)}) collective-permute-start(bf16[64,1792]{1,0:T(8,128)(2,1)S(1)} %get-tuple-element.42), channel_id=1, source_target_pairs={{1,2},{2,1},{5,6},{6,5},{9,10},{10,9},{13,14},{14,13},{17,18},{18,... | collective-permute-start | bytes 688136 | tf_op jit(solution)/shard_map/ppermute | solution.py:243
  5.9 13.7 %collective-permute-start.1 = (bf16[64,1792]{1,0:T(8,128)(2,1)S(1)}, bf16[64,1792]{1,0:T(8,128)(2,1)S(1)}, u32[]{:S(2)}, u32[]{:S(2)}) collective-permute-start(bf16[64,1792]{1,0:T(8,128)(2,1)S(1)} %get-tuple-element.41.passing_ref), channel_id=1, source_target_pairs={{0,2},{3,1},{4,6},{7,5},{8,10},{11,9},{12,14},{15,13},{16,18},{19,... | collective-permute-start | bytes 688136 | tf_op jit(solution)/shard_map/ppermute | solution.py:244
  11.7 13.1 %collective-permute-start.3 = (bf16[64,1792]{1,0:T(8,128)(2,1)S(1)}, bf16[64,1792]{1,0:T(8,128)(2,1)S(1)}, u32[]{:S(2)}, u32[]{:S(2)}) collective-permute-start(bf16[64,1792]{1,0:T(8,128)(2,1)S(1)} %merge.1), channel_id=1, source_target_pairs={{0,1},{1,3},{2,0},{3,2},{4,5},{5,7},{6,4},{7,6},{8,9},{9,11},{10,8... | collective-permute-start | bytes 688136 | tf_op jit(solution)/shard_map/ppermute | solution.py:254
  14.2 3.1 %copy-start = (bf16[1,1792,2048]{2,1,0:T(8,128)(2,1)S(1)}, bf16[1,1792,2048]{2,1,0:T(8,128)(2,1)}, u32[]{:S(2)}) copy-start(bf16[1,1792,2048]{2,1,0:T(8,128)(2,1)} %refs_1_.1) | copy-start | bytes 22020100
  17.3 0.9 %copy-start.1 = (bf16[64,1792]{1,0:T(8,128)(2,1)S(1)}, bf16[64,1792]{1,0:T(8,128)(2,1)}, u32[]{:S(2)}) copy-start(bf16[64,1792]{1,0:T(8,128)(2,1)} %refs_0_.1) | copy-start | bytes 688132
  25.3 2.0 %collective-permute-start.6 = (bf16[40,1792]{1,0:T(8,128)(2,1)S(1)}, bf16[40,1792]{1,0:T(8,128)(2,1)S(1)}, u32[]{:S(2)}, u32[]{:S(2)}) collective-permute-start(bf16[40,1792]{1,0:T(8,128)(2,1)S(1)} %get-tuple-element.30), channel_id=1, source_target_pairs={{0,4},{4,0},{8,12},{12,8},{1,5},{5,1},{9,13},{13,9},{2,6},{6,2},{1... | collective-permute-start | bytes 430088 | tf_op jit(solution)/shard_map/ppermute | solution.py:20
  25.3 8.1 %collective-permute-start.4 = (bf16[40,1792]{1,0:T(8,128)(2,1)S(1)}, bf16[40,1792]{1,0:T(8,128)(2,1)S(1)}, u32[]{:S(2)}, u32[]{:S(2)}) collective-permute-start(bf16[40,1792]{1,0:T(8,128)(2,1)S(1)} %get-tuple-element.24), channel_id=1, source_target_pairs={{0,8},{4,12},{8,0},{12,4},{1,9},{5,13},{9,1},{13,5},{2,10},{6,14},... | collective-permute-start | bytes 430088 | tf_op jit(solution)/shard_map/ppermute | solution.py:20
  26.9 7.2 %collective-permute-start.5 = (bf16[40,1792]{1,0:T(8,128)(2,1)S(1)}, bf16[40,1792]{1,0:T(8,128)(2,1)S(1)}, u32[]{:S(2)}, u32[]{:S(2)}) collective-permute-start(bf16[40,1792]{1,0:T(8,128)(2,1)S(1)} %get-tuple-element.25), channel_id=1, source_target_pairs={{0,12},{4,8},{8,4},{12,0},{1,13},{5,9},{9,5},{13,1},{2,14},{6,10},... | collective-permute-start | bytes 430088 | tf_op jit(solution)/shard_map/ppermute | solution.py:20
  27.9 7.3 %collective-permute-start.11 = (bf16[88,512]{1,0:T(8,128)(2,1)S(1)}, bf16[88,512]{1,0:T(8,128)(2,1)S(1)}, u32[]{:S(2)}, u32[]{:S(2)}) collective-permute-start(bf16[88,512]{1,0:T(8,128)(2,1)S(1)} %gate.13), channel_id=1, source_target_pairs={{0,3},{1,2},{2,1},{3,0},{4,7},{5,6},{6,5},{7,4},{8,11},{9,10},{10,... | collective-permute-start | bytes 270344 | tf_op jit(solution)/shard_map/ppermute | solution.py:20
  31.1 7.4 %collective-permute-start.7 = (bf16[88,512]{1,0:T(8,128)(2,1)S(1)}, bf16[88,512]{1,0:T(8,128)(2,1)S(1)}, u32[]{:S(2)}, u32[]{:S(2)}) collective-permute-start(bf16[88,512]{1,0:T(8,128)(2,1)S(1)} %gate.8), channel_id=1, source_target_pairs={{0,1},{1,0},{2,3},{3,2},{4,5},{5,4},{6,7},{7,6},{8,9},{9,8},{10,11... | collective-permute-start | bytes 270344 | tf_op jit(solution)/shard_map/ppermute | solution.py:20
  31.6 8.0 %collective-permute-start.8 = (bf16[88,512]{1,0:T(8,128)(2,1)S(1)}, bf16[88,512]{1,0:T(8,128)(2,1)S(1)}, u32[]{:S(2)}, u32[]{:S(2)}) collective-permute-start(bf16[88,512]{1,0:T(8,128)(2,1)S(1)} %gate.9), channel_id=1, source_target_pairs={{0,2},{1,3},{2,0},{3,1},{4,6},{5,7},{6,4},{7,5},{8,10},{9,11},{10,... | collective-permute-start | bytes 270344 | tf_op jit(solution)/shard_map/ppermute | solution.py:20
  35.7 8.2 %collective-permute-start.12 = (bf16[88,512]{1,0:T(8,128)(2,1)S(1)}, bf16[88,512]{1,0:T(8,128)(2,1)S(1)}, u32[]{:S(2)}, u32[]{:S(2)}) collective-permute-start(bf16[88,512]{1,0:T(8,128)(2,1)S(1)} %gate.14), channel_id=1, source_target_pairs={{0,3},{1,2},{2,1},{3,0},{4,7},{5,6},{6,5},{7,4},{8,11},{9,10},{10,... | collective-permute-start | bytes 270344 | tf_op jit(solution)/shard_map/ppermute | solution.py:20
  38.9 6.0 %collective-permute-start.9 = (bf16[88,512]{1,0:T(8,128)(2,1)S(1)}, bf16[88,512]{1,0:T(8,128)(2,1)S(1)}, u32[]{:S(2)}, u32[]{:S(2)}) collective-permute-start(bf16[88,512]{1,0:T(8,128)(2,1)S(1)} %gate.12), channel_id=1, source_target_pairs={{0,1},{1,0},{2,3},{3,2},{4,5},{5,4},{6,7},{7,6},{8,9},{9,8},{10,11... | collective-permute-start | bytes 270344 | tf_op jit(solution)/shard_map/ppermute | solution.py:20
  40.0 11.0 %slice-start = ((s8[7340032]{0:T(1024)(128)(4,1)}), s8[4194304]{0:T(1024)(128)(4,1)S(1)}, s32[]{:S(2)}) async-start(s8[7340032]{0:T(1024)(128)(4,1)} %bitcast.14), calls=%async_computation | async-start | bytes 8388608
  40.0 6.3 %collective-permute-start.10 = (bf16[88,512]{1,0:T(8,128)(2,1)S(1)}, bf16[88,512]{1,0:T(8,128)(2,1)S(1)}, u32[]{:S(2)}, u32[]{:S(2)}) collective-permute-start(bf16[88,512]{1,0:T(8,128)(2,1)S(1)} %gate.10.refs_1_), channel_id=1, source_target_pairs={{0,2},{1,3},{2,0},{3,1},{4,6},{5,7},{6,4},{7,5},{8,10},{9,11},{10,... | collective-permute-start | bytes 270344 | tf_op jit(solution)/shard_map/ppermute | solution.py:20
  42.9 8.1 %slice-start.1 = ((s8[7340032]{0:T(1024)(128)(4,1)}), s8[3145728]{0:T(1024)(128)(4,1)S(1)}, s32[]{:S(2)}) async-start(s8[7340032]{0:T(1024)(128)(4,1)} %bitcast.14), calls=%async_computation.1 | async-start | bytes 6291456
  42.9 8.1 %collective-permute-start.14 = (bf16[80,512]{1,0:T(8,128)(2,1)S(1)}, bf16[80,512]{1,0:T(8,128)(2,1)S(1)}, u32[]{:S(2)}, u32[]{:S(2)}) collective-permute-start(bf16[80,512]{1,0:T(8,128)(2,1)S(1)} %activate.3.refs_0_.value_ref), channel_id=1, source_target_pairs={{0,1},{1,0},{2,3},{3,2},{4,5},{5,4},{6,7},{7,6},{8,9},{9,8},{10,11... | collective-permute-start | bytes 245768 | tf_op jit(solution)/shard_map/ppermute | solution.py:20
  46.5 6.9 %collective-permute-start.13 = (bf16[80,512]{1,0:T(8,128)(2,1)S(1)}, bf16[80,512]{1,0:T(8,128)(2,1)S(1)}, u32[]{:S(2)}, u32[]{:S(2)}) collective-permute-start(bf16[80,512]{1,0:T(8,128)(2,1)S(1)} %activate.2.refs_0_.refs_2_), channel_id=1, source_target_pairs={{0,3},{1,2},{2,1},{3,0},{4,7},{5,6},{6,5},{7,4},{8,11},{9,10},{10,... | collective-permute-start | bytes 245768 | tf_op jit(solution)/shard_map/ppermute | solution.py:20
  49.5 7.9 %collective-permute-start.18 = (bf16[80,512]{1,0:T(8,128)(2,1)S(1)}, bf16[80,512]{1,0:T(8,128)(2,1)S(1)}, u32[]{:S(2)}, u32[]{:S(2)}) collective-permute-start(bf16[80,512]{1,0:T(8,128)(2,1)S(1)} %activate.2.refs_0_.refs_2_), channel_id=1, source_target_pairs={{0,2},{1,3},{2,0},{3,1},{4,6},{5,7},{6,4},{7,5},{8,10},{9,11},{10,... | collective-permute-start | bytes 245768 | tf_op jit(solution)/shard_map/ppermute | solution.py:20
  49.5 7.9 %collective-permute-start.19 = (bf16[80,512]{1,0:T(8,128)(2,1)S(1)}, bf16[80,512]{1,0:T(8,128)(2,1)S(1)}, u32[]{:S(2)}, u32[]{:S(2)}) collective-permute-start(bf16[80,512]{1,0:T(8,128)(2,1)S(1)} %activate.2.refs_0_.refs_2_), channel_id=1, source_target_pairs={{0,1},{1,0},{2,3},{3,2},{4,5},{5,4},{6,7},{7,6},{8,9},{9,8},{10,11... | collective-permute-start | bytes 245768 | tf_op jit(solution)/shard_map/ppermute | solution.py:20
  54.9 6.2 %collective-permute-start.15 = (bf16[80,512]{1,0:T(8,128)(2,1)S(1)}, bf16[80,512]{1,0:T(8,128)(2,1)S(1)}, u32[]{:S(2)}, u32[]{:S(2)}) collective-permute-start(bf16[80,512]{1,0:T(8,128)(2,1)S(1)} %hold.1), channel_id=1, source_target_pairs={{0,3},{1,2},{2,1},{3,0},{4,7},{5,6},{6,5},{7,4},{8,11},{9,10},{10,... | collective-permute-start | bytes 245768 | tf_op jit(solution)/shard_map/ppermute | solution.py:20
  57.3 6.2 %collective-permute-start.16 = (bf16[80,512]{1,0:T(8,128)(2,1)S(1)}, bf16[80,512]{1,0:T(8,128)(2,1)S(1)}, u32[]{:S(2)}, u32[]{:S(2)}) collective-permute-start(bf16[80,512]{1,0:T(8,128)(2,1)S(1)} %hold.1), channel_id=1, source_target_pairs={{0,2},{1,3},{2,0},{3,1},{4,6},{5,7},{6,4},{7,5},{8,10},{9,11},{10,... | collective-permute-start | bytes 245768 | tf_op jit(solution)/shard_map/ppermute | solution.py:20
  58.2 6.2 %collective-permute-start.20 = (bf16[40,1792]{1,0:T(8,128)(2,1)S(1)}, bf16[40,1792]{1,0:T(8,128)(2,1)S(1)}, u32[]{:S(2)}, u32[]{:S(2)}) collective-permute-start(bf16[40,1792]{1,0:T(8,128)(2,1)S(1)} %get-tuple-element.38), channel_id=1, source_target_pairs={{0,8},{4,12},{8,0},{12,4},{1,9},{5,13},{9,1},{13,5},{2,10},{6,14},... | collective-permute-start | bytes 430088 | tf_op jit(solution)/shard_map/ppermute | solution.py:20
  59.7 6.0 %collective-permute-start.21 = (bf16[40,1792]{1,0:T(8,128)(2,1)S(1)}, bf16[40,1792]{1,0:T(8,128)(2,1)S(1)}, u32[]{:S(2)}, u32[]{:S(2)}) collective-permute-start(bf16[40,1792]{1,0:T(8,128)(2,1)S(1)} %get-tuple-element.39), channel_id=1, source_target_pairs={{0,12},{4,8},{8,4},{12,0},{1,13},{5,9},{9,5},{13,1},{2,14},{6,10},... | collective-permute-start | bytes 430088 | tf_op jit(solution)/shard_map/ppermute | solution.py:20
  64.3 1.5 %collective-permute-start.17 = (bf16[40,1792]{1,0:T(8,128)(2,1)S(1)}, bf16[40,1792]{1,0:T(8,128)(2,1)S(1)}, u32[]{:S(2)}, u32[]{:S(2)}) collective-permute-start(bf16[40,1792]{1,0:T(8,128)(2,1)S(1)} %get-tuple-element.37), channel_id=1, source_target_pairs={{0,4},{4,0},{8,12},{12,8},{1,5},{5,1},{9,13},{13,9},{2,6},{6,2},{1... | collective-permute-start | bytes 430088 | tf_op jit(solution)/shard_map/ppermute | solution.py:20
